TPU v7x, 256 devices: a whole 4x4x8 slice. The times are simulated.
256 devices in a mesh: row: 32 (over z_lo, y, core), col: 8 (over z_hi, x).
Axes of the slice: x: 4, y: 4, z: 8 (z_hi: 2, z_lo: 4; z = z_hi * 4 + z_lo), core: 2. Of those that a mesh axis runs over, the one named last changes fastest.
Arguments:
- queries: bfloat16 [256, 32, 3072], P('row', None, 'col'), may hold values from -50 to 50
- keys: bfloat16 [256, 32, 3072], P('row', None, 'col'), may hold values from -6 to 6
- values: bfloat16 [256, 32, 3072], P('row', None, 'col'), may hold values from -6 to 6
- out_grad: bfloat16 [256, 32, 3072], P('row', None, 'col'), may hold values from -6 to 6
- outputs: bfloat16 [256, 32, 3072], P('row', None, 'col'), may hold values from -6 to 6
- bias: bfloat16 [3072, 3072], P('row', 'col'), may hold values from -6 to 6
- key_mask: int32 [3072], P('col'), may hold values 0 or 1
Outputs:
- query_grad: bfloat16 [256, 32, 3072], P('row', None, 'col')
- key_grad: bfloat16 [256, 32, 3072], P('row', None, 'col')
- value_grad: bfloat16 [256, 32, 3072], P('row', None, 'col')
- bias_grad: float32 [3072, 3072], P('row', 'col')
All inputs are finite; a program needn't handle non-finite values. No bound on the sum of `key_mask` on one device may be relied on, other than what follows from the above.
Results may differ from a plain program's by a relative error of at most 0.005.
Values may be sent and summed in bfloat16 or wider, within the bound.
No kernel may reach another device: no remote copies, remote signals or barrier semaphores. Data moves between devices by JAX's collectives and lax.ppermute only.
A program may use at most 128 MiB of HBM per device.

v0:
```python
import jax
import jax.numpy as jnp
from jax import lax
from jax.sharding import PartitionSpec as P


def joined(x, axis, combine):
    everything = jax.tree.map(lambda part: lax.all_gather(part, axis), x)
    leading = jax.tree.map(lambda part: part[0], everything)

    def hop(k, so_far):
        return combine(so_far, jax.tree.map(lambda part: part[k], everything))

    return lax.fori_loop(1, lax.axis_size(axis), hop, leading)


def finish_query(partial_sums, scale):
    summed = lax.psum_scatter(partial_sums, "col", scatter_dimension=2, tiled=True)
    return (scale * summed).astype(jnp.bfloat16)


def finish_bias(partial_bias):
    return lax.psum_scatter(partial_bias, "row", scatter_dimension=0, tiled=True)


def combine_totals(first, second):
    top = jnp.maximum(first[0], second[0])
    summed = first[1] * jnp.exp(first[0] - top) + second[1] * jnp.exp(second[0] - top)
    return (top, summed, first[2] + second[2])


def per_device(queries, keys, values, out_grad, outputs, bias, key_mask):
    rows, head, key_count = keys.shape
    scale = head ** (-0.5)
    q_whole, g_whole = (
        lax.all_gather(queries, "col", axis=2, tiled=True),
        lax.all_gather(out_grad, "col", axis=2, tiled=True),
    )
    total = q_whole.shape[2]
    bias_cols = lax.all_gather(bias, "row", axis=0, tiled=True)
    offset = jnp.where(key_mask == 0, -1000000000.0, 0.0).astype(jnp.float32)
    full_bias = bias_cols.astype(jnp.float32) + offset[None, :]

    def scores_of(query, keyrow):
        product = jnp.einsum("cj,ct->jt", query, keyrow, preferred_element_type=jnp.float32)
        return product * scale + full_bias

    def partial_stats(pair):
        scores = scores_of(pair[0], pair[1])
        top = jnp.max(scores, axis=1)
        return (top, jnp.sum(jnp.exp(scores - top[:, None]), axis=1))

    tops, sums = lax.map(partial_stats, (q_whole, keys))
    own_delta = jnp.sum(out_grad.astype(jnp.float32) * outputs.astype(jnp.float32), axis=1)
    placed = lax.dynamic_update_slice_in_dim(
        jnp.zeros((rows, total), jnp.float32), own_delta, lax.axis_index("col") * key_count, 1
    )
    top, summed, delta = joined((tops, sums, placed), "col", combine_totals)
    lse = top + jnp.log(summed)
    inputs = (q_whole, g_whole, keys, values, lse, delta)

    def dscores_of(query, gradrow, keyrow, valrow, lse_row, delta_row):
        probs = jnp.exp(scores_of(query, keyrow) - lse_row[:, None])
        dprobs = jnp.einsum("cj,ct->jt", gradrow, valrow, preferred_element_type=jnp.float32)
        dscores = probs * (dprobs - delta_row[:, None])
        return (probs, dscores, dscores.astype(jnp.bfloat16))

    start = jnp.zeros((total, key_count), jnp.float32)

    def joint_step(acc, parts):
        query, gradrow, keyrow, valrow, lse_row, delta_row = parts
        probs, dscores, dscores_low = dscores_of(query, gradrow, keyrow, valrow, lse_row, delta_row)
        probs_low = probs.astype(jnp.bfloat16)
        value_part = jnp.einsum("jt,cj->ct", probs_low, gradrow, preferred_element_type=jnp.float32)
        key_part = jnp.einsum("jt,cj->ct", dscores_low, query, preferred_element_type=jnp.float32)
        local_out = ((scale * key_part).astype(jnp.bfloat16), value_part.astype(jnp.bfloat16))
        query_part = jnp.einsum(
            "jt,ct->cj", dscores_low, keyrow, preferred_element_type=jnp.float32
        )
        return (acc + dscores, local_out + (query_part,))

    partial_bias, results = lax.scan(joint_step, start, inputs)
    key_grad, value_grad = (results[0], results[1])
    query_grad = finish_query(results[2], scale)
    bias_grad = finish_bias(partial_bias)
    return (query_grad, key_grad, value_grad, bias_grad)


def solution(mesh):
    in_specs = (
        P("row", None, "col"),
        P("row", None, "col"),
        P("row", None, "col"),
        P("row", None, "col"),
        P("row", None, "col"),
        P("row", "col"),
        P("col"),
    )
    out_specs = (
        P("row", None, "col"),
        P("row", None, "col"),
        P("row", None, "col"),
        P("row", "col"),
    )
    return jax.shard_map(
        per_device, mesh=mesh, in_specs=in_specs, out_specs=out_specs, check_vma=False
    )
```

profile of v0, /device:TPU:2, one launch (start us, length us, event | category | flops | bytes accessed | tf_op | source)
XLA Modules:
  0.0 703.1 jit_solution(12278153400581564329)
XLA Ops:
  7.9 0.7 all-gather.6.cloned.1.call-update
  9.5 1.1 multiply_reduce_fusion
  10.6 48.9 %all_gather.37 = f32[8,8,3072]{2,1,0:T(8,128)S(1)} all-gather(f32[1,8,3072]{2,1,0:T(8,128)S(1)} %bitcast_dynamic-update-slice_fusion), channel_id=1, replica_groups=mesh['row'=32,'col'=8] {'col'}, dimensions={0}, use_global_device_ids=true | all-gather | bytes 884736 | tf_op jit(solution)/shard_map/all_gather | solution.py:8
  59.6 0.7 compare_select_fusion
  60.3 13.3 %all-gather.8.cloned.1.call-done = bf16[3072,384]{1,0:T(8,128)(2,1)} async-done(((bf16[96,384]{1,0:T(8,128)(2,1)}), bf16[3072,384]{1,0:T(8,128)(2,1)}) %all-gather.8.cloned.1.call-update) | async-done | bytes 2359312 | tf_op jit(solution)/shard_map/all_gather | solution.py:40
  73.5 4.1 convert_add_fusion
  77.7 6.1 copy.12
  83.7 61.5 %all-gather.6.cloned.1.call-done = bf16[8,32,3072]{2,1,0:T(8,128)(2,1)} async-done(((bf16[8,32,384]{2,1,0:T(8,128)(2,1)}), bf16[8,32,3072]{2,1,0:T(8,128)(2,1)}) %all-gather.6.cloned.1.call-update) | async-done | bytes 1572880 | tf_op jit(solution)/shard_map/all_gather | solution.py:36
  145.2 36.9 %while.48 = (s32[]{:T(128)}, f32[8,3072]{1,0:T(8,128)S(1)}, f32[8,3072]{1,0:T(8,128)S(1)}, bf16[8,32,3072]{2,1,0:T(8,128)(2,1)}, bf16[8,32,384]{2,1,0:T(8,128)(2...) while((s32[]{:T(128)}, f32[8,3072]{1,0:T(8,128)S(1)}, f32[8,3072]{1,0:T(8,128)S(1)}, ...), condition=%wide.region_3.4_spmd, body=%wide.region_0.3_spmd.sunk | while | flops 81389568 | bytes 14464093 | solution.py:53
  145.2 3.3 fusion.69
  149.8 3.3 fusion.69
  154.4 3.4 fusion.69
  159.1 3.3 fusion.69
  163.7 3.3 fusion.69
  168.3 3.3 fusion.69
  172.9 3.3 fusion.69
  177.5 3.3 fusion.69
  182.1 45.7 %all-gather = f32[64,3072]{1,0:T(8,128)S(1)} all-gather(f32[8,3072]{1,0:T(8,128)S(1)} %get-tuple-element.280), channel_id=2, replica_groups=mesh['row'=32,'col'=8] {'col'}, dimensions={0}, use_global_device_ids=true | all-gather | bytes 884736 | tf_op jit(solution)/shard_map/all_gather | solution.py:8
  227.8 46.0 %all-gather.1 = f32[64,3072]{1,0:T(8,128)S(1)} all-gather(f32[8,3072]{1,0:T(8,128)S(1)} %get-tuple-element.281), channel_id=3, replica_groups=mesh['row'=32,'col'=8] {'col'}, dimensions={0}, use_global_device_ids=true | all-gather | bytes 884736 | tf_op jit(solution)/shard_map/all_gather | solution.py:8
  273.8 0.8 while.49
  274.6 155.9 %while.50 = (s32[]{:T(128)}, f32[3072,384]{1,0:T(8,128)}, bf16[8,32,384]{2,1,0:T(8,128)(2,1)}, bf16[8,32,384]{2,1,0:T(8,128)(2,1)}, f32[8,32,3072]{2,1,0:T(8,128...) while((s32[]{:T(128)}, f32[3072,384]{1,0:T(8,128)}, ...), condition=%wide.region_8.9_spmd.clone, body=%wide.region_7.8_spmd.clone.sunk | while | flops 388141056 | bytes 50926784 | solution.py:82
  274.6 5.9 subtract_exponential_fusion.2
  280.5 6.0 select_add_fusion.2
  286.6 2.3 fusion.81
  288.9 2.0 fusion.79
  290.9 2.0 fusion.80
  292.9 5.9 subtract_exponential_fusion.2
  298.8 7.4 %select_add_fusion.2 = (f32[3072,384]{1,0:T(8,128)}, bf16[3072,384]{1,0:T(8,128)(2,1)S(1)}) fusion(f32[3072,384]{1,0:T(8,128)} %get-tuple-element.641, pred[]{:T(512)S(6)} %compare.3, f32[3072,384]{1,0:T(8,128)} %subtract_exponential_fusion.2, f32[3072]{0:T(1024)S(1)} %bitcast.114, bf16[8,32,384]{2,1,0:T(8,128)(2,1)} %get-tuple-element.664, ...), kind=kOutput, calls=%fused_computation.13.clone.1 | convolution fusion | flops 81395712 | bytes 16749569 | tf_op jit(solution)/shard_map/while/body/eval_jaxpr/cj,ct->jt/dot_general | solution.py:64
  306.2 2.3 fusion.81
  308.5 2.0 fusion.79
  310.5 2.0 fusion.80
  312.5 5.9 subtract_exponential_fusion.2
  318.5 7.4 %select_add_fusion.2 = (f32[3072,384]{1,0:T(8,128)}, bf16[3072,384]{1,0:T(8,128)(2,1)S(1)}) fusion(f32[3072,384]{1,0:T(8,128)} %get-tuple-element.641, pred[]{:T(512)S(6)} %compare.3, f32[3072,384]{1,0:T(8,128)} %subtract_exponential_fusion.2, f32[3072]{0:T(1024)S(1)} %bitcast.114, bf16[8,32,384]{2,1,0:T(8,128)(2,1)} %get-tuple-element.664, ...), kind=kOutput, calls=%fused_computation.13.clone.1 | convolution fusion | flops 81395712 | bytes 16749569 | tf_op jit(solution)/shard_map/while/body/eval_jaxpr/cj,ct->jt/dot_general | solution.py:64
  325.9 2.3 fusion.81
  328.2 2.0 fusion.79
  330.2 2.0 fusion.80
  332.2 5.9 subtract_exponential_fusion.2
  338.1 7.4 %select_add_fusion.2 = (f32[3072,384]{1,0:T(8,128)}, bf16[3072,384]{1,0:T(8,128)(2,1)S(1)}) fusion(f32[3072,384]{1,0:T(8,128)} %get-tuple-element.641, pred[]{:T(512)S(6)} %compare.3, f32[3072,384]{1,0:T(8,128)} %subtract_exponential_fusion.2, f32[3072]{0:T(1024)S(1)} %bitcast.114, bf16[8,32,384]{2,1,0:T(8,128)(2,1)} %get-tuple-element.664, ...), kind=kOutput, calls=%fused_computation.13.clone.1 | convolution fusion | flops 81395712 | bytes 16749569 | tf_op jit(solution)/shard_map/while/body/eval_jaxpr/cj,ct->jt/dot_general | solution.py:64
  345.5 2.3 fusion.81
  347.9 2.0 fusion.79
  349.9 2.0 fusion.80
  351.9 5.9 subtract_exponential_fusion.2
  357.8 7.4 %select_add_fusion.2 = (f32[3072,384]{1,0:T(8,128)}, bf16[3072,384]{1,0:T(8,128)(2,1)S(1)}) fusion(f32[3072,384]{1,0:T(8,128)} %get-tuple-element.641, pred[]{:T(512)S(6)} %compare.3, f32[3072,384]{1,0:T(8,128)} %subtract_exponential_fusion.2, f32[3072]{0:T(1024)S(1)} %bitcast.114, bf16[8,32,384]{2,1,0:T(8,128)(2,1)} %get-tuple-element.664, ...), kind=kOutput, calls=%fused_computation.13.clone.1 | convolution fusion | flops 81395712 | bytes 16749569 | tf_op jit(solution)/shard_map/while/body/eval_jaxpr/cj,ct->jt/dot_general | solution.py:64
  365.2 2.3 fusion.81
  367.5 2.0 fusion.79
  369.5 2.0 fusion.80
  371.5 5.9 subtract_exponential_fusion.2
  377.5 7.4 %select_add_fusion.2 = (f32[3072,384]{1,0:T(8,128)}, bf16[3072,384]{1,0:T(8,128)(2,1)S(1)}) fusion(f32[3072,384]{1,0:T(8,128)} %get-tuple-element.641, pred[]{:T(512)S(6)} %compare.3, f32[3072,384]{1,0:T(8,128)} %subtract_exponential_fusion.2, f32[3072]{0:T(1024)S(1)} %bitcast.114, bf16[8,32,384]{2,1,0:T(8,128)(2,1)} %get-tuple-element.664, ...), kind=kOutput, calls=%fused_computation.13.clone.1 | convolution fusion | flops 81395712 | bytes 16749569 | tf_op jit(solution)/shard_map/while/body/eval_jaxpr/cj,ct->jt/dot_general | solution.py:64
  384.9 2.3 fusion.81
  387.2 2.0 fusion.79
  389.2 2.0 fusion.80
  391.2 5.9 subtract_exponential_fusion.2
  397.1 7.4 %select_add_fusion.2 = (f32[3072,384]{1,0:T(8,128)}, bf16[3072,384]{1,0:T(8,128)(2,1)S(1)}) fusion(f32[3072,384]{1,0:T(8,128)} %get-tuple-element.641, pred[]{:T(512)S(6)} %compare.3, f32[3072,384]{1,0:T(8,128)} %subtract_exponential_fusion.2, f32[3072]{0:T(1024)S(1)} %bitcast.114, bf16[8,32,384]{2,1,0:T(8,128)(2,1)} %get-tuple-element.664, ...), kind=kOutput, calls=%fused_computation.13.clone.1 | convolution fusion | flops 81395712 | bytes 16749569 | tf_op jit(solution)/shard_map/while/body/eval_jaxpr/cj,ct->jt/dot_general | solution.py:64
  404.5 2.3 fusion.81
  406.8 2.0 fusion.79
  408.8 2.0 fusion.80
  410.9 5.9 subtract_exponential_fusion.2
  416.8 7.4 %select_add_fusion.2 = (f32[3072,384]{1,0:T(8,128)}, bf16[3072,384]{1,0:T(8,128)(2,1)S(1)}) fusion(f32[3072,384]{1,0:T(8,128)} %get-tuple-element.641, pred[]{:T(512)S(6)} %compare.3, f32[3072,384]{1,0:T(8,128)} %subtract_exponential_fusion.2, f32[3072]{0:T(1024)S(1)} %bitcast.114, bf16[8,32,384]{2,1,0:T(8,128)(2,1)} %get-tuple-element.664, ...), kind=kOutput, calls=%fused_computation.13.clone.1 | convolution fusion | flops 81395712 | bytes 16749569 | tf_op jit(solution)/shard_map/while/body/eval_jaxpr/cj,ct->jt/dot_general | solution.py:64
  424.2 2.3 fusion.81
  426.5 2.0 fusion.79
  428.5 2.0 fusion.80
  431.1 114.6 %reduce-scatter.3.cloned.1.call-done = f32[8,32,384]{2,1,0:T(8,128)} async-done(((f32[8,32,3072]{2,1,0:T(8,128)}), f32[8,32,384]{2,1,0:T(8,128)}) %reduce-scatter.3.cloned.1.call-update) | async-done | bytes 393232 | tf_op jit(solution)/shard_map/reduce_scatter | solution.py:18
  545.7 1.7 multiply_convert_fusion
  547.4 149.2 %reduce-scatter.5.cloned.1.call-done = f32[96,384]{1,0:T(8,128)} async-done(((f32[3072,384]{1,0:T(8,128)}), f32[96,384]{1,0:T(8,128)}) %reduce-scatter.5.cloned.1.call-update) | async-done | bytes 147472 | tf_op jit(solution)/shard_map/reduce_scatter | solution.py:23
  (101 shorter events, 13.1 us)
Async XLA Ops:
  7.2 66.4 %all-gather.8.cloned.1.call-start = ((), (), s32[]{:S(2)}) async-start(), calls=%async_computation.3 | async-start | bytes 2433024 | tf_op jit(solution)/shard_map/all_gather | solution.py:40
  7.9 137.3 %all-gather.6.cloned.1.call-start = ((), (), s32[]{:S(2)}) async-start(), calls=%async_computation.2 | async-start | bytes 1769472 | tf_op jit(solution)/shard_map/all_gather | solution.py:36
  8.6 265.9 %all-gather.10.cloned.1.call-start = ((), (), s32[]{:S(2)}) async-start(), calls=%async_computation.4 | async-start | bytes 1769472 | tf_op jit(solution)/shard_map/all_gather | solution.py:37
  9.4 536.3 %reduce-scatter.3.cloned.1.call-start = ((), (), s32[]{:S(2)}) async-start(), calls=%async_computation.5 | async-start | bytes 3538944 | tf_op jit(solution)/shard_map/reduce_scatter | solution.py:18
  280.5 10.3 %slice-start = ((s8[4718592]{0:T(1024)(128)(4,1)}), s8[4194304]{0:T(1024)(128)(4,1)S(1)}, s32[]{:S(2)}) async-start(s8[4718592]{0:T(1024)(128)(4,1)} %bitcast.108), calls=%async_computation.7 | async-start | bytes 8388608 | tf_op jit(solution)/shard_map/while
  280.5 10.3 %slice-start.1 = ((s8[4718592]{0:T(1024)(128)(4,1)}), s8[524288]{0:T(1024)(128)(4,1)S(1)}, s32[]{:S(2)}) async-start(s8[4718592]{0:T(1024)(128)(4,1)} %bitcast.108), calls=%async_computation.8 | async-start | bytes 1048576 | tf_op jit(solution)/shard_map/while
  298.8 11.7 %slice-start = ((s8[4718592]{0:T(1024)(128)(4,1)}), s8[4194304]{0:T(1024)(128)(4,1)S(1)}, s32[]{:S(2)}) async-start(s8[4718592]{0:T(1024)(128)(4,1)} %bitcast.108), calls=%async_computation.7 | async-start | bytes 8388608 | tf_op jit(solution)/shard_map/while
  298.8 11.7 %slice-start.1 = ((s8[4718592]{0:T(1024)(128)(4,1)}), s8[524288]{0:T(1024)(128)(4,1)S(1)}, s32[]{:S(2)}) async-start(s8[4718592]{0:T(1024)(128)(4,1)} %bitcast.108), calls=%async_computation.8 | async-start | bytes 1048576 | tf_op jit(solution)/shard_map/while
  318.5 11.7 %slice-start = ((s8[4718592]{0:T(1024)(128)(4,1)}), s8[4194304]{0:T(1024)(128)(4,1)S(1)}, s32[]{:S(2)}) async-start(s8[4718592]{0:T(1024)(128)(4,1)} %bitcast.108), calls=%async_computation.7 | async-start | bytes 8388608 | tf_op jit(solution)/shard_map/while
  318.5 11.7 %slice-start.1 = ((s8[4718592]{0:T(1024)(128)(4,1)}), s8[524288]{0:T(1024)(128)(4,1)S(1)}, s32[]{:S(2)}) async-start(s8[4718592]{0:T(1024)(128)(4,1)} %bitcast.108), calls=%async_computation.8 | async-start | bytes 1048576 | tf_op jit(solution)/shard_map/while
  338.1 11.8 %slice-start = ((s8[4718592]{0:T(1024)(128)(4,1)}), s8[4194304]{0:T(1024)(128)(4,1)S(1)}, s32[]{:S(2)}) async-start(s8[4718592]{0:T(1024)(128)(4,1)} %bitcast.108), calls=%async_computation.7 | async-start | bytes 8388608 | tf_op jit(solution)/shard_map/while
  338.1 11.8 %slice-start.1 = ((s8[4718592]{0:T(1024)(128)(4,1)}), s8[524288]{0:T(1024)(128)(4,1)S(1)}, s32[]{:S(2)}) async-start(s8[4718592]{0:T(1024)(128)(4,1)} %bitcast.108), calls=%async_computation.8 | async-start | bytes 1048576 | tf_op jit(solution)/shard_map/while
  357.8 11.7 %slice-start = ((s8[4718592]{0:T(1024)(128)(4,1)}), s8[4194304]{0:T(1024)(128)(4,1)S(1)}, s32[]{:S(2)}) async-start(s8[4718592]{0:T(1024)(128)(4,1)} %bitcast.108), calls=%async_computation.7 | async-start | bytes 8388608 | tf_op jit(solution)/shard_map/while
  357.8 11.7 %slice-start.1 = ((s8[4718592]{0:T(1024)(128)(4,1)}), s8[524288]{0:T(1024)(128)(4,1)S(1)}, s32[]{:S(2)}) async-start(s8[4718592]{0:T(1024)(128)(4,1)} %bitcast.108), calls=%async_computation.8 | async-start | bytes 1048576 | tf_op jit(solution)/shard_map/while
  377.4 11.7 %slice-start = ((s8[4718592]{0:T(1024)(128)(4,1)}), s8[4194304]{0:T(1024)(128)(4,1)S(1)}, s32[]{:S(2)}) async-start(s8[4718592]{0:T(1024)(128)(4,1)} %bitcast.108), calls=%async_computation.7 | async-start | bytes 8388608 | tf_op jit(solution)/shard_map/while
  377.4 11.7 %slice-start.1 = ((s8[4718592]{0:T(1024)(128)(4,1)}), s8[524288]{0:T(1024)(128)(4,1)S(1)}, s32[]{:S(2)}) async-start(s8[4718592]{0:T(1024)(128)(4,1)} %bitcast.108), calls=%async_computation.8 | async-start | bytes 1048576 | tf_op jit(solution)/shard_map/while
  397.1 11.7 %slice-start = ((s8[4718592]{0:T(1024)(128)(4,1)}), s8[4194304]{0:T(1024)(128)(4,1)S(1)}, s32[]{:S(2)}) async-start(s8[4718592]{0:T(1024)(128)(4,1)} %bitcast.108), calls=%async_computation.7 | async-start | bytes 8388608 | tf_op jit(solution)/shard_map/while
  397.1 11.7 %slice-start.1 = ((s8[4718592]{0:T(1024)(128)(4,1)}), s8[524288]{0:T(1024)(128)(4,1)S(1)}, s32[]{:S(2)}) async-start(s8[4718592]{0:T(1024)(128)(4,1)} %bitcast.108), calls=%async_computation.8 | async-start | bytes 1048576 | tf_op jit(solution)/shard_map/while
  416.8 11.7 %slice-start = ((s8[4718592]{0:T(1024)(128)(4,1)}), s8[4194304]{0:T(1024)(128)(4,1)S(1)}, s32[]{:S(2)}) async-start(s8[4718592]{0:T(1024)(128)(4,1)} %bitcast.108), calls=%async_computation.7 | async-start | bytes 8388608 | tf_op jit(solution)/shard_map/while
  416.8 11.7 %slice-start.1 = ((s8[4718592]{0:T(1024)(128)(4,1)}), s8[524288]{0:T(1024)(128)(4,1)S(1)}, s32[]{:S(2)}) async-start(s8[4718592]{0:T(1024)(128)(4,1)} %bitcast.108), calls=%async_computation.8 | async-start | bytes 1048576 | tf_op jit(solution)/shard_map/while
  430.5 266.1 %reduce-scatter.5.cloned.1.call-start = ((), (), s32[]{:S(2)}) async-start(), calls=%async_computation.6 | async-start | bytes 4866048 | tf_op jit(solution)/shard_map/reduce_scatter | solution.py:23
Sparse Core Ops, SparseCore 0:
  9.9 63.6 all-gather.7
  76.0 69.1 all-gather.5
  147.7 73.4 all-gather.9
  430.6 114.9 reduce-scatter.2
  548.8 147.7 reduce-scatter.4
where the time goes:
time: 705 us; the launch traced here: 703 us
  waiting for transfers between devices  341 us (48%)
  matrix products  182 us (26%)
  blocking collectives  141 us (20%)
  between operations  13.9 us (2%)
  other arithmetic  13.6 us (2%)
  local copies, waits for them, and re-layouts  11 us (2%)
    reduce_scatter x1, waiting for transfers between devices, finish_bias(): lax.psum_scatter(partial_bias, 'row', scatter_dimension=0, tiled=True)  149 us
    all_gather x3, blocking collectives, joined(): everything = jax.tree.map(lambda part: lax.all_gather(part, axis), x)  141 us
    reduce_scatter x1, waiting for transfers between devices, finish_query(): lax.psum_scatter(partial_sums, 'col', scatter_dimension=2, tiled=True)  115 us
    dot_general x16, matrix products, scores_of(): jnp.einsum('cj,ct->jt', query, keyrow, preferred_element_type=jnp.float32)  73.7 us
    all_gather x1, waiting for transfers between devices, per_device(): lax.all_gather(queries, 'col', axis=2, tiled=True)  61.5 us
    dot_general x8, matrix products, dscores_of(): jnp.einsum('cj,ct->jt', gradrow, valrow, preferred_element_type=jnp.float32)  58 us
    dot_general x8, matrix products, joint_step(): jnp.einsum('jt,ct->cj', dscores_low, keyrow, preferred_element_type=jnp.f...  18.5 us
    dot_general x8, matrix products, joint_step(): jnp.einsum('jt,cj->ct', probs_low, gradrow, preferred_element_type=jnp.fl...  16 us
  transfers between devices with their start and end apart: 5, of which 4 were waited for; matrix products, arithmetic and copies ran while one was open for 7% of the time, Pallas kernels for 0%

commit v1 on v0

v1 whole, which is shorter than its diff:
```python
import math

import jax
import jax.numpy as jnp
from jax import lax
from jax.experimental import pallas as pl
from jax.experimental.pallas import tpu as pltpu
from jax.sharding import Mesh, PartitionSpec as P

FINE = ("zlo", "y", "core", "zhi", "x")
ZLO, Y, CORE, ZHI, X = 4, 4, 2, 2, 4
LOG2E = math.log2(math.e)
MASKED = -8192.0
BF16, F32 = jnp.bfloat16, jnp.float32


def dot(a, b, ca, cb):
    return lax.dot_general(a, b, (((ca,), (cb,)), ((), ())), preferred_element_type=F32)


def split3(x):
    high = x.astype(BF16).astype(F32)
    rest = x - high
    middle = rest.astype(BF16).astype(F32)
    return high, middle, rest - middle


def rows_of(parts, count, width):
    row = lax.broadcasted_iota(jnp.int32, (count, width), 0)
    out = jnp.zeros((count, width), F32)
    for at, part in enumerate(parts):
        out = jnp.where(row == at, part, out)
    return out


def put_keys(refs, masks, place, scale):
    rows, head, width = refs[0].shape
    for slot, (ref, mask) in enumerate(zip(refs, masks)):
        offset = jnp.where(mask[...] == 0.0, MASKED, 0.0)
        extra = rows_of((-1.0, -1.0, -1.0, offset), head, width)

        def prepare(i, carry):
            parts = split3(ref[i].astype(F32) * scale)
            whole = jnp.concatenate(parts + (extra,), axis=0)
            place[i, slot * width : (slot + 1) * width, :] = whole.T.astype(BF16)
            return carry

        lax.fori_loop(0, rows, prepare, 0)


def put_values(refs, place):
    rows, head, width = refs[0].shape
    extra = rows_of((-1.0, -1.0, -1.0), 128 - head, width)
    for slot, ref in enumerate(refs):

        def prepare(i, carry):
            whole = jnp.concatenate((ref[i].astype(F32), extra), axis=0)
            place[i, slot * width : (slot + 1) * width, :] = whole.T.astype(BF16)
            return carry

        lax.fori_loop(0, rows, prepare, 0)


def bias_pieces(at):
    zlo, y, core, zhi, x = (at[n] for n in range(5))
    for yd in range(Y):
        row = lax.rem(y + yd, Y)
        for zd in range(ZLO):
            piece = lax.rem(zlo + zd, ZLO)
            half, part = lax.div(piece, 2), lax.rem(piece, 2)
            slot = lax.rem(half + zhi, 2)
            chunk = lax.rem(part * 2 + lax.div(row, 2) - x + X, X)
            for other in range(CORE):
                which = lax.rem(core + other, 2)
                first = chunk * 384 + lax.rem(row, 2) * 192 + which * 96
                yield yd, zd, other, slot, pl.multiple_of(first, 32)


def stats_kernel(scale, at, *refs):
    q = refs[0:4]
    keys, masks = refs[4:6], refs[6:8]
    grad, outs = refs[8:10]
    pieces = (refs[10:14], refs[14:18])
    stat, bias_t = refs[18:20]
    bias_n, bias_f, key_t = refs[20:]
    rows, head, width = q[0].shape
    total = X * width
    put_keys(keys, masks, key_t, scale * LOG2E)
    for yd, zd, other, slot, first in bias_pieces(at):
        bias_n[slot, pl.ds(first, 96), :] = pieces[other][yd][zd]
    for slot in range(2):
        for j in range(0, total, 128):
            tile = bias_n[slot, j : j + 128, :].astype(F32).T
            bias_t[slot * width : (slot + 1) * width, j : j + 128] = tile.astype(BF16)
            bias_f[slot * width : (slot + 1) * width, j : j + 128] = tile * LOG2E
    ones = rows_of((0.0, 0.0, 0.0, 1.0), 16, width).astype(BF16)

    def row_step(i, carry):
        for d in range(X):
            query = q[d][i]
            augmented = jnp.concatenate((query, query, query, ones), axis=0)
            cols = slice(d * width, (d + 1) * width)
            top, total_sum = None, None
            for k in range(0, 2 * width, 128):
                scores = dot(key_t[i, k : k + 128, :112], augmented, 1, 0)
                scores = (scores + bias_f[k : k + 128, cols]).reshape(16, 8, width)
                here = jnp.max(scores, axis=0)
                if top is None:
                    top = here
                    total_sum = jnp.sum(jnp.exp2(scores - top), axis=0)
                else:
                    new = jnp.maximum(top, here)
                    total_sum = total_sum * jnp.exp2(top - new) + jnp.sum(
                        jnp.exp2(scores - new), axis=0
                    )
                    top = new
            most = jnp.max(top, axis=0, keepdims=True)
            summed = jnp.sum(total_sum * jnp.exp2(top - most), axis=0, keepdims=True)
            stat[pl.ds(i, 1), cols] = most
            stat[pl.ds(i, 1), total + d * width : total + (d + 1) * width] = summed
        product = grad[i].astype(F32) * outs[i].astype(F32)
        stat[pl.ds(i, 1), 2 * total :] = jnp.sum(product, axis=0, keepdims=True)
        return carry

    lax.fori_loop(0, rows, row_step, 0)


def main_kernel(scale, at, *refs):
    q, g = refs[0:4], refs[4:8]
    keys, values, masks = refs[8:10], refs[10:12], refs[12:14]
    stats = refs[14:18]
    bias_t = refs[18]
    dq = refs[19:23]
    dk_own, dv_own, dkv_away = refs[23:26]
    bias_own, bias_away = refs[26:30], refs[30:34]
    bias_f, acc, turned, key_t, value_t, lse, delta = refs[34:]
    rows, head, width = q[0].shape
    total = X * width
    put_keys(keys, masks, key_t, scale * LOG2E)
    put_values(values, value_t)
    for d in range(X):
        cols = slice(d * width, (d + 1) * width)
        there = [(d - e) % X for e in range(X)]
        tops = [stats[e][:, n * width : (n + 1) * width] for e, n in enumerate(there)]
        sums = [stats[e][:, total + n * width : total + (n + 1) * width] for e, n in enumerate(there)]
        top = jnp.maximum(jnp.maximum(tops[0], tops[1]), jnp.maximum(tops[2], tops[3]))
        summed = sum(s * jnp.exp2(t - top) for s, t in zip(sums, tops))
        lse[:, cols] = top + jnp.log(summed) * LOG2E
        delta[:, cols] = stats[d][:, 2 * total :]
    bias_f[...] = bias_t[...].astype(F32) * LOG2E
    acc[...] = jnp.zeros_like(acc)

    def row_step(i, carry):
        dk_row, dv_row = None, None
        for d in range(X):
            cols = slice(d * width, (d + 1) * width)
            query, gradient = q[d][i], g[d][i]
            high, middle, low = split3(lse[pl.ds(i, 1), cols])
            extra = rows_of((high, middle, low, 1.0), 16, width).astype(BF16)
            query_all = jnp.concatenate((query, query, query, extra), axis=0)
            extra = rows_of(split3(delta[pl.ds(i, 1), cols]), 16, width).astype(BF16)
            gradient_all = jnp.concatenate((gradient, extra), axis=0)
            probs = jnp.exp2(dot(key_t[i, :, :112], query_all, 1, 0) + bias_f[:, cols])
            dscores = probs * dot(value_t[i, :, :48], gradient_all, 1, 0)
            acc[:, cols] += dscores
            probs_low, dscores_low = probs.astype(BF16), dscores.astype(BF16)
            dv_part = dot(gradient, probs_low, 1, 1)
            dk_part = dot(query, dscores_low, 1, 1)
            dv_row = dv_part if d == 0 else dv_row + dv_part
            dk_row = dk_part if d == 0 else dk_row + dk_part
            dq_part = dot(keys[0][i], dscores_low[:width], 1, 0) + dot(
                keys[1][i], dscores_low[width:], 1, 0
            )
            dq[d][i] = dq_part.astype(dq[d].dtype)
        dk_own[i], dv_own[i] = dk_row[:, :width], dv_row[:, :width]
        dkv_away[i] = dk_row[:, width:].astype(BF16)
        dkv_away[rows + i] = dv_row[:, width:].astype(BF16)
        return carry

    lax.fori_loop(0, rows, row_step, 0)
    for slot in range(2):
        for j in range(0, total, 128):
            tile = acc[slot * width : (slot + 1) * width, j : j + 128].T
            turned[slot, j : j + 128, :] = tile
    for yd, zd, other, slot, first in bias_pieces(at):
        place = bias_own if other == 0 else bias_away
        place[yd][zd] = turned[slot, pl.ds(first, 96), :].astype(place[yd].dtype)


VMEM = pl.BlockSpec(memory_space=pltpu.VMEM)
SMEM = pl.BlockSpec(memory_space=pltpu.SMEM)


def call(kernel, name, args, outs, scratch):
    return pl.pallas_call(
        kernel,
        in_specs=[SMEM] + [VMEM] * (len(args) - 1),
        out_specs=[VMEM] * len(outs),
        out_shape=[jax.ShapeDtypeStruct(shape, dtype) for shape, dtype in outs],
        scratch_shapes=[pltpu.VMEM(shape, dtype) for shape, dtype in scratch],
        compiler_params=pltpu.CompilerParams(vmem_limit_bytes=52 * 2**20),
        name=name,
    )(*args)


def fetch(x, axis, size, distance):
    return lax.ppermute(x, axis, [((n + distance) % size, n) for n in range(size)])


def deliver(x, axis, size, distance):
    return lax.ppermute(x, axis, [(n, (n + distance) % size) for n in range(size)])


def z_pairs(distance):
    pairs = []
    for group in range(ZHI):
        for place in range(ZLO):
            half, part = divmod((place + distance) % ZLO, 2)
            pairs.append(((2 * group + part) * ZHI + half, place * ZHI + group))
    return pairs


def per_device(queries, keys, values, out_grad, outputs, bias, key_mask):
    rows, head, width = keys.shape
    scale = head ** (-0.5)
    total = X * width
    z_axes = ("zlo", "zhi")
    at = jnp.stack([lax.axis_index(name) for name in FINE]).astype(jnp.int32)
    mask = key_mask.astype(F32)[None, :]

    from_z = jnp.stack([lax.ppermute(bias, z_axes, z_pairs(d)) for d in range(ZLO)])
    q = [queries] + [fetch(queries, "x", X, d) for d in range(1, X)]
    away = [fetch(a, "zhi", ZHI, 1) for a in (keys, values, mask)]
    here = [from_z] + [fetch(from_z, "y", Y, d) for d in range(1, Y)]
    there = [fetch(a, "core", CORE, 1) for a in here]
    g = [out_grad] + [fetch(out_grad, "x", X, d) for d in range(1, X)]

    both = 2 * width
    stat, bias_t = call(
        lambda *refs: stats_kernel(scale, *refs),
        "softmax_statistics",
        [at, *q, keys, away[0], mask, away[2], out_grad, outputs, *here, *there],
        [((rows, 2 * total + width), F32), ((both, total), BF16)],
        [((2, total, width), BF16), ((both, total), F32), ((rows, both, 128), BF16)],
    )
    stats = [stat] + [fetch(stat, "x", X, d) for d in range(1, X)]

    block, piece = (rows, head, width), (ZLO, 96, width)
    results = call(
        lambda *refs: main_kernel(scale, *refs),
        "attention_gradients",
        [at, *q, *g, keys, away[0], values, away[1], mask, away[2], *stats, bias_t],
        [(block, F32)]
        + [(block, BF16)] * 3
        + [(block, F32)] * 2
        + [((2 * rows, head, width), BF16)]
        + [(piece, F32)] * 4
        + [(piece, BF16)] * 4,
        [
            ((both, total), F32),
            ((both, total), F32),
            ((2, total, width), F32),
            ((rows, both, 128), BF16),
            ((rows, both, 128), BF16),
            ((rows, total), F32),
            ((rows, total), F32),
        ],
    )
    dq, (dk, dv, dkv_away) = results[0:4], results[4:7]
    bias_own, bias_away = results[7:11], results[11:15]

    near = [
        own + fetch(other, "core", CORE, 1).astype(F32)
        for own, other in zip(bias_own, bias_away)
    ]
    along_y = near[0]
    for d in range(1, Y):
        along_y = along_y + deliver(near[d].astype(BF16), "y", Y, d).astype(F32)
    low = along_y.astype(BF16)
    bias_grad = None
    for d in range(ZLO):
        pairs = [(worker, owner) for owner, worker in z_pairs(d)]
        part = lax.ppermute(low[d], z_axes, pairs).astype(F32)
        bias_grad = part if bias_grad is None else bias_grad + part

    query_sum = dq[0]
    for d in range(1, X):
        query_sum = query_sum + deliver(dq[d], "x", X, d).astype(F32)
    arrived = fetch(dkv_away, "zhi", ZHI, 1).astype(F32)
    query_grad = (scale * query_sum).astype(BF16)
    key_grad = (scale * (dk + arrived[:rows])).astype(BF16)
    value_grad = (dv + arrived[rows:]).astype(BF16)
    return query_grad, key_grad, value_grad, bias_grad


def solution(mesh):
    fine = Mesh(mesh.devices.reshape(ZLO, Y, CORE, ZHI, X), FINE)
    row, col = ("zlo", "y", "core"), ("zhi", "x")
    pair, flat = P(row, None, col), P(row, col)
    return jax.shard_map(
        per_device,
        mesh=fine,
        in_specs=(pair,) * 5 + (flat, P(col)),
        out_specs=(pair,) * 3 + (flat,),
        check_vma=False,
    )
```

time: 705 us -> 168 us (0.24)
  the two profiles are of different devices: /device:TPU:2 before, /device:TPU:64 now
where the time goes in v1:
time: 168 us; the launch traced here: 167 us
  starting transfers between devices  66.6 us (40%)
  Pallas kernels  48.9 us (29%)
  waiting for transfers between devices  39.6 us (24%)
  other arithmetic  5.7 us (3%)
  local copies, waits for them, and re-layouts  5.17 us (3%)
    pallas_call x2, Pallas kernels, call(): pl.pallas_call(kernel, in_specs=[SMEM] + [VMEM] * (len(args) - 1), out_sp...  48.9 us
    ppermute x24, starting transfers between devices, fetch(): lax.ppermute(x, axis, [((n + distance) % size, n) for n in range(size)])  38 us
    ppermute x24, waiting for transfers between devices, fetch(): lax.ppermute(x, axis, [((n + distance) % size, n) for n in range(size)])  25.7 us
    ppermute x4, starting transfers between devices, per_device(): lax.ppermute(bias, z_axes, z_pairs(d))  10.7 us
    ppermute x4, starting transfers between devices, per_device(): part = lax.ppermute(low[d], z_axes, pairs).astype(F32)  9.37 us
    ppermute x6, starting transfers between devices, deliver(): lax.ppermute(x, axis, [(n, (n + distance) % size) for n in range(size)])  8.47 us
    ppermute x4, waiting for transfers between devices, per_device(): part = lax.ppermute(low[d], z_axes, pairs).astype(F32)  6.5 us
    unnamed x40, local copies, waits for them, and re-layouts  5.05 us
  transfers between devices with their start and end apart: 38, of which 11 were waited for; matrix products, arithmetic and copies ran while one was open for 3% of the time, Pallas kernels for 8%

profile of v1, /device:TPU:64, one launch (start us, length us, event | category | flops | bytes accessed | tf_op | source)
XLA Modules:
  0.0 166.8 jit_solution(8592919843637923707)
XLA Ops:
  0.6 0.0 copy-start.2
  0.6 5.0 %collective-permute-start.10 = (bf16[96,384]{1,0:T(8,128)(2,1)}, bf16[96,384]{1,0:T(8,128)(2,1)S(1)}, u32[]{:S(2)}, u32[]{:S(2)}) collective-permute-start(bf16[96,384]{1,0:T(8,128)(2,1)} %param.12), channel_id=1, source_target_pairs={{64,0},{4,64},{68,128},{0,192},{192,4},{132,68},{196,132},{128,196... | collective-permute-start | bytes 221192 | tf_op jit(solution)/shard_map/ppermute | solution.py:231
  5.7 1.9 %collective-permute-start.9 = (bf16[96,384]{1,0:T(8,128)(2,1)}, bf16[96,384]{1,0:T(8,128)(2,1)S(1)}, u32[]{:S(2)}, u32[]{:S(2)}) collective-permute-start(bf16[96,384]{1,0:T(8,128)(2,1)} %param.12), channel_id=1, source_target_pairs={{0,0},{64,64},{4,128},{68,192},{128,4},{192,68},{132,132},{196,196... | collective-permute-start | bytes 221192 | tf_op jit(solution)/shard_map/ppermute | solution.py:231
  7.6 3.7 %collective-permute-start.12 = (bf16[96,384]{1,0:T(8,128)(2,1)}, bf16[96,384]{1,0:T(8,128)(2,1)S(1)}, u32[]{:S(2)}, u32[]{:S(2)}) collective-permute-start(bf16[96,384]{1,0:T(8,128)(2,1)} %param.12), channel_id=1, source_target_pairs={{68,0},{0,64},{64,128},{4,192},{196,4},{128,68},{192,132},{132,196... | collective-permute-start | bytes 221192 | tf_op jit(solution)/shard_map/ppermute | solution.py:231
  11.3 2.9 %collective-permute-start.6 = (bf16[8,32,384]{2,1,0:T(8,128)(2,1)}, bf16[8,32,384]{2,1,0:T(8,128)(2,1)S(1)}, u32[]{:S(2)}, u32[]{:S(2)}) collective-permute-start(bf16[8,32,384]{2,1,0:T(8,128)(2,1)} %refs_9_.3), channel_id=1, source_target_pairs={{4,0},{0,4},{5,1},{1,5},{6,2},{2,6},{7,3},{3,7},{12,8},{8,12},{13,... | collective-permute-start | bytes 589832 | tf_op jit(solution)/shard_map/ppermute | solution.py:207
  14.2 0.0 collective-permute-done.10
  14.2 1.5 collective-permute-start.2
  15.7 4.6 %collective-permute-done.11 = bf16[96,384]{1,0:T(8,128)(2,1)S(1)} collective-permute-done((bf16[96,384]{1,0:T(8,128)(2,1)}, bf16[96,384]{1,0:T(8,128)(2,1)S(1)}, u32[]{:S(2)}, u32[]{:S(2)}) %collective-permute-start.11) | collective-permute-done | bytes 73760 | tf_op jit(solution)/shard_map/ppermute | solution.py:231
  20.4 1.7 collective-permute-start.15
  22.1 2.9 %collective-permute-start.14 = (bf16[4,96,384]{2,1,0:T(8,128)(2,1)S(1)}, bf16[4,96,384]{2,1,0:T(8,128)(2,1)S(1)}, u32[]{:S(2)}, u32[]{:S(2)}) collective-permute-start(bf16[4,96,384]{2,1,0:T(8,128)(2,1)S(1)} %pad_maximum_fusion.refs_11_), channel_id=1, source_target_pairs={{32,0},{48,16},{0,32},{16,48},{33,1},{49,17},{1,33},{17,49},{34,2}... | collective-permute-start | bytes 884744 | tf_op jit(solution)/shard_map/ppermute | solution.py:207
  24.9 0.7 convert_element_type.69
  25.6 3.7 %collective-permute-start.8 = (f32[1,384]{1,0:T(1,128)S(1)}, f32[1,384]{1,0:T(1,128)S(1)}, u32[]{:S(2)}, u32[]{:S(2)}) collective-permute-start(f32[1,384]{1,0:T(1,128)S(1)} %broadcast_in_dim.3.refs_7_.refs_13_), channel_id=1, source_target_pairs={{4,0},{0,4},{5,1},{1,5},{6,2},{2,6},{7,3},{3,7},{12,8},{8,12},{13,... | collective-permute-start | bytes 4616 | tf_op jit(solution)/shard_map/ppermute | solution.py:207
  29.4 3.8 %collective-permute-done.8.refs_8_.refs_14_ = f32[1,384]{1,0:T(1,128)S(1)} collective-permute-done((f32[1,384]{1,0:T(1,128)S(1)}, f32[1,384]{1,0:T(1,128)S(1)}, u32[]{:S(2)}, u32[]{:S(2)}) %collective-permute-start.8) | collective-permute-done | bytes 1568 | tf_op jit(solution)/shard_map/ppermute | solution.py:207
  33.1 1.3 collective-permute-start.13
  34.5 3.0 %collective-permute-start.1 = (bf16[8,32,384]{2,1,0:T(8,128)(2,1)}, bf16[8,32,384]{2,1,0:T(8,128)(2,1)S(1)}, u32[]{:S(2)}, u32[]{:S(2)}) collective-permute-start(bf16[8,32,384]{2,1,0:T(8,128)(2,1)} %refs_1_.3), channel_id=1, source_target_pairs={{2,0},{3,1},{0,2},{1,3},{6,4},{7,5},{4,6},{5,7},{10,8},{11,9},{8,1... | collective-permute-start | bytes 589832 | tf_op jit(solution)/shard_map/ppermute | solution.py:207
  37.5 4.4 %collective-permute-done.1.refs_3_ = bf16[8,32,384]{2,1,0:T(8,128)(2,1)S(1)} collective-permute-done((bf16[8,32,384]{2,1,0:T(8,128)(2,1)}, bf16[8,32,384]{2,1,0:T(8,128)(2,1)S(1)}, u32[]{:S(2)}, u32[]{:S(2)}) %collective-permute-start.1) | collective-permute-done | bytes 196640 | tf_op jit(solution)/shard_map/ppermute | solution.py:207
  41.9 3.9 %collective-permute-start = (bf16[8,32,384]{2,1,0:T(8,128)(2,1)}, bf16[8,32,384]{2,1,0:T(8,128)(2,1)S(1)}, u32[]{:S(2)}, u32[]{:S(2)}) collective-permute-start(bf16[8,32,384]{2,1,0:T(8,128)(2,1)} %refs_1_.3), channel_id=1, source_target_pairs={{1,0},{2,1},{3,2},{0,3},{5,4},{6,5},{7,6},{4,7},{9,8},{10,9},{11,1... | collective-permute-start | bytes 589832 | tf_op jit(solution)/shard_map/ppermute | solution.py:207
  45.8 0.5 collective-permute-start.18
  46.3 0.1 collective-permute-start.17
  46.4 2.9 %collective-permute-done.refs_2_ = bf16[8,32,384]{2,1,0:T(8,128)(2,1)S(1)} collective-permute-done((bf16[8,32,384]{2,1,0:T(8,128)(2,1)}, bf16[8,32,384]{2,1,0:T(8,128)(2,1)S(1)}, u32[]{:S(2)}, u32[]{:S(2)}) %collective-permute-start) | collective-permute-done | bytes 196640 | tf_op jit(solution)/shard_map/ppermute | solution.py:207
  49.3 3.7 %collective-permute-start.7 = (bf16[8,32,384]{2,1,0:T(8,128)(2,1)}, bf16[8,32,384]{2,1,0:T(8,128)(2,1)S(1)}, u32[]{:S(2)}, u32[]{:S(2)}) collective-permute-start(bf16[8,32,384]{2,1,0:T(8,128)(2,1)} %refs_11_.1), channel_id=1, source_target_pairs={{4,0},{0,4},{5,1},{1,5},{6,2},{2,6},{7,3},{3,7},{12,8},{8,12},{13,... | collective-permute-start | bytes 589832 | tf_op jit(solution)/shard_map/ppermute | solution.py:207
  53.0 2.0 %collective-permute-start.5 = (bf16[8,32,384]{2,1,0:T(8,128)(2,1)}, bf16[8,32,384]{2,1,0:T(8,128)(2,1)}, u32[]{:S(2)}, u32[]{:S(2)}) collective-permute-start(bf16[8,32,384]{2,1,0:T(8,128)(2,1)} %refs_5_.3), channel_id=1, source_target_pairs={{3,0},{0,1},{1,2},{2,3},{7,4},{4,5},{5,6},{6,7},{11,8},{8,9},{9,10... | collective-permute-start | bytes 589832 | tf_op jit(solution)/shard_map/ppermute | solution.py:207
  55.0 3.0 %collective-permute-start.4 = (bf16[8,32,384]{2,1,0:T(8,128)(2,1)}, bf16[8,32,384]{2,1,0:T(8,128)(2,1)}, u32[]{:S(2)}, u32[]{:S(2)}) collective-permute-start(bf16[8,32,384]{2,1,0:T(8,128)(2,1)} %refs_5_.3), channel_id=1, source_target_pairs={{2,0},{3,1},{0,2},{1,3},{6,4},{7,5},{4,6},{5,7},{10,8},{11,9},{8,1... | collective-permute-start | bytes 589832 | tf_op jit(solution)/shard_map/ppermute | solution.py:207
  58.0 0.0 collective-permute-start.3
  58.1 0.1 stack.38.refs_0_
  58.2 0.6 copy-done.16
  58.8 0.7 copy-done.17
  59.5 0.9 copy-done
  60.4 0.9 copy-done.1
  61.3 0.9 copy-done.3
  62.3 0.9 copy-done.5
  63.2 14.1 %softmax_statistics.1 = (f32[8,3456]{1,0:T(8,128)S(1)}, bf16[768,1536]{1,0:T(8,128)(2,1)}) custom-call(s32[5]{0:T(128)S(1)} %stack.38.refs_0_, bf16[8,32,384]{2,1,0:T(8,128)(2,1)S(1)} %copy-done, bf16[8,32,384]{2,1,0:T(8,128)(2,1)S(1)} %collective-permute-done.refs_2_, bf16[8,32,384]{2,1,0:T(8,128)(2,1)S(1)} %collective-permute-done.1.refs_3_, ...), custom_call_target="tpu_custom_call" | custom-call | tf_op jit(solution)/shard_map/softmax_statistics/pallas_call | solution.py:195
  77.3 1.4 collective-permute-start.22
  78.7 0.5 collective-permute-start.21
  79.3 2.3 %collective-permute-start.20 = (f32[8,3456]{1,0:T(8,128)S(1)}, f32[8,3456]{1,0:T(8,128)S(1)}, u32[]{:S(2)}, u32[]{:S(2)}) collective-permute-start(f32[8,3456]{1,0:T(8,128)S(1)} %get-tuple-element.21.refs_15_), channel_id=1, source_target_pairs={{1,0},{2,1},{3,2},{0,3},{5,4},{6,5},{7,6},{4,7},{9,8},{10,9},{11,1... | collective-permute-start | bytes 331784 | tf_op jit(solution)/shard_map/ppermute | solution.py:207
  81.5 1.7 %collective-permute-done.22.refs_18_ = f32[8,3456]{1,0:T(8,128)S(1)} collective-permute-done((f32[8,3456]{1,0:T(8,128)S(1)}, f32[8,3456]{1,0:T(8,128)S(1)}, u32[]{:S(2)}, u32[]{:S(2)}) %collective-permute-start.22) | collective-permute-done | bytes 110624 | tf_op jit(solution)/shard_map/ppermute | solution.py:207
  83.3 1.7 %collective-permute-done.21.refs_17_ = f32[8,3456]{1,0:T(8,128)S(1)} collective-permute-done((f32[8,3456]{1,0:T(8,128)S(1)}, f32[8,3456]{1,0:T(8,128)S(1)}, u32[]{:S(2)}, u32[]{:S(2)}) %collective-permute-start.21) | collective-permute-done | bytes 110624 | tf_op jit(solution)/shard_map/ppermute | solution.py:207
  85.0 0.3 collective-permute-done.20.refs_16_
  85.3 34.8 %attention_gradients.1 = (f32[8,32,384]{2,1,0:T(8,128)}, bf16[8,32,384]{2,1,0:T(8,128)(2,1)S(1)}, bf16[8,32,384]{2,1,0:T(8,128)(2,1)S(1)}, bf16[8,32,384]{2,1,0:...) custom-call(s32[5]{0:T(128)S(1)} %stack.38.refs_0_, ...), custom_call_target="tpu_custom_call" | custom-call | tf_op jit(solution)/shard_map/attention_gradients/pallas_call | solution.py:195
  120.1 0.1 collective-permute-start.28
  120.2 0.5 collective-permute-start.30
  120.7 1.0 collective-permute-start.23
  121.7 3.1 %collective-permute-start.24 = (bf16[8,32,384]{2,1,0:T(8,128)(2,1)S(1)}, bf16[8,32,384]{2,1,0:T(8,128)(2,1)S(1)}, u32[]{:S(2)}, u32[]{:S(2)}) collective-permute-start(bf16[8,32,384]{2,1,0:T(8,128)(2,1)S(1)} %get-tuple-element.25), channel_id=1, source_target_pairs={{0,2},{1,3},{2,0},{3,1},{4,6},{5,7},{6,4},{7,5},{8,10},{9,11},{10,... | collective-permute-start | bytes 589832 | tf_op jit(solution)/shard_map/ppermute | solution.py:211
  124.9 0.2 collective-permute-start.25
  125.1 1.1 add_convert_fusion.3
  126.2 0.6 collective-permute-start.27
  126.8 1.2 add_convert_fusion.2
  128.0 2.3 %collective-permute-start.26 = (bf16[16,32,384]{2,1,0:T(8,128)(2,1)S(1)}, bf16[16,32,384]{2,1,0:T(8,128)(2,1)S(1)}, u32[]{:S(2)}, u32[]{:S(2)}) collective-permute-start(bf16[16,32,384]{2,1,0:T(8,128)(2,1)S(1)} %copy-done.19), channel_id=1, source_target_pairs={{4,0},{0,4},{5,1},{1,5},{6,2},{2,6},{7,3},{3,7},{12,8},{8,12},{13,... | collective-permute-start | bytes 1179656 | tf_op jit(solution)/shard_map/ppermute | solution.py:207
  130.4 0.1 add_convert_fusion.1
  130.5 0.7 collective-permute-start.29
  131.2 2.8 %collective-permute-done.24 = bf16[8,32,384]{2,1,0:T(8,128)(2,1)S(1)} collective-permute-done((bf16[8,32,384]{2,1,0:T(8,128)(2,1)S(1)}, bf16[8,32,384]{2,1,0:T(8,128)(2,1)S(1)}, u32[]{:S(2)}, u32[]{:S(2)}) %collective-permute-start.24) | collective-permute-done | bytes 196640 | tf_op jit(solution)/shard_map/ppermute | solution.py:211
  134.0 0.3 collective-permute-start.31
  134.3 3.0 %collective-permute-start.33 = (bf16[4,96,384]{2,1,0:T(8,128)(2,1)S(1)}, bf16[4,96,384]{2,1,0:T(8,128)(2,1)S(1)}, u32[]{:S(2)}, u32[]{:S(2)}) collective-permute-start(bf16[4,96,384]{2,1,0:T(8,128)(2,1)S(1)} %add_convert_fusion.1), channel_id=1, source_target_pairs={{0,48},{16,0},{32,16},{48,32},{1,49},{17,1},{33,17},{49,33},{2,50}... | collective-permute-start | bytes 884744 | tf_op jit(solution)/shard_map/ppermute | solution.py:211
  137.3 0.8 multiply_convert_fusion
  138.1 10.9 %collective-permute-done.26 = bf16[16,32,384]{2,1,0:T(8,128)(2,1)S(1)} collective-permute-done((bf16[16,32,384]{2,1,0:T(8,128)(2,1)S(1)}, bf16[16,32,384]{2,1,0:T(8,128)(2,1)S(1)}, u32[]{:S(2)}, u32[]{:S(2)}) %collective-permute-start.26) | collective-permute-done | bytes 393248 | tf_op jit(solution)/shard_map/ppermute | solution.py:207
  149.1 0.1 convert_element_type.74
  149.2 0.2 add_convert_fusion
  149.4 1.9 %collective-permute-start.34 = (bf16[96,384]{1,0:T(8,128)(2,1)S(1)}, bf16[96,384]{1,0:T(8,128)(2,1)S(1)}, u32[]{:S(2)}, u32[]{:S(2)}) collective-permute-start(bf16[96,384]{1,0:T(8,128)(2,1)S(1)} %get-tuple-element.40), channel_id=1, source_target_pairs={{0,0},{64,64},{128,4},{192,68},{4,128},{68,192},{132,132},{196,196... | collective-permute-start | bytes 221192 | tf_op jit(solution)/shard_map/ppermute | solution.py:283
  151.3 0.1 collective-permute-start.37
  151.4 7.4 %collective-permute-start.36 = (bf16[96,384]{1,0:T(8,128)(2,1)S(1)}, bf16[96,384]{1,0:T(8,128)(2,1)S(1)}, u32[]{:S(2)}, u32[]{:S(2)}) collective-permute-start(bf16[96,384]{1,0:T(8,128)(2,1)S(1)} %get-tuple-element.42), channel_id=1, source_target_pairs={{0,4},{64,68},{128,0},{192,64},{4,132},{68,196},{132,128},{196,192... | collective-permute-start | bytes 221192 | tf_op jit(solution)/shard_map/ppermute | solution.py:283
  158.8 0.8 fusion
  159.6 3.9 %collective-permute-done.37 = bf16[96,384]{1,0:T(8,128)(2,1)S(1)} collective-permute-done((bf16[96,384]{1,0:T(8,128)(2,1)S(1)}, bf16[96,384]{1,0:T(8,128)(2,1)S(1)}, u32[]{:S(2)}, u32[]{:S(2)}) %collective-permute-start.37) | collective-permute-done | bytes 73760 | tf_op jit(solution)/shard_map/ppermute | solution.py:283
  163.5 2.6 %collective-permute-done.35 = bf16[96,384]{1,0:T(8,128)(2,1)S(1)} collective-permute-done((bf16[96,384]{1,0:T(8,128)(2,1)S(1)}, bf16[96,384]{1,0:T(8,128)(2,1)S(1)}, u32[]{:S(2)}, u32[]{:S(2)}) %collective-permute-start.35) | collective-permute-done | bytes 73760 | tf_op jit(solution)/shard_map/ppermute | solution.py:283
  166.1 0.7 convert_add_fusion
  (67 shorter events, 0.2 us)
Async XLA Ops:
  0.6 84.7 %copy-start.2 = (bf16[8,32,384]{2,1,0:T(8,128)(2,1)S(1)}, bf16[8,32,384]{2,1,0:T(8,128)(2,1)}, u32[]{:S(2)}) copy-start(bf16[8,32,384]{2,1,0:T(8,128)(2,1)} %refs_5_.3) | copy-start | bytes 589828
  0.6 13.6 %collective-permute-start.10 = (bf16[96,384]{1,0:T(8,128)(2,1)}, bf16[96,384]{1,0:T(8,128)(2,1)S(1)}, u32[]{:S(2)}, u32[]{:S(2)}) collective-permute-start(bf16[96,384]{1,0:T(8,128)(2,1)} %param.12), channel_id=1, source_target_pairs={{64,0},{4,64},{68,128},{0,192},{192,4},{132,68},{196,132},{128,196... | collective-permute-start | bytes 221192 | tf_op jit(solution)/shard_map/ppermute | solution.py:231
  5.7 10.1 %collective-permute-start.9 = (bf16[96,384]{1,0:T(8,128)(2,1)}, bf16[96,384]{1,0:T(8,128)(2,1)S(1)}, u32[]{:S(2)}, u32[]{:S(2)}) collective-permute-start(bf16[96,384]{1,0:T(8,128)(2,1)} %param.12), channel_id=1, source_target_pairs={{0,0},{64,64},{4,128},{68,192},{128,4},{192,68},{132,132},{196,196... | collective-permute-start | bytes 221192 | tf_op jit(solution)/shard_map/ppermute | solution.py:231
  7.6 8.2 %collective-permute-start.12 = (bf16[96,384]{1,0:T(8,128)(2,1)}, bf16[96,384]{1,0:T(8,128)(2,1)S(1)}, u32[]{:S(2)}, u32[]{:S(2)}) collective-permute-start(bf16[96,384]{1,0:T(8,128)(2,1)} %param.12), channel_id=1, source_target_pairs={{68,0},{0,64},{64,128},{4,192},{196,4},{128,68},{192,132},{132,196... | collective-permute-start | bytes 221192 | tf_op jit(solution)/shard_map/ppermute | solution.py:231
  11.3 9.0 %collective-permute-start.11 = (bf16[96,384]{1,0:T(8,128)(2,1)}, bf16[96,384]{1,0:T(8,128)(2,1)S(1)}, u32[]{:S(2)}, u32[]{:S(2)}) collective-permute-start(bf16[96,384]{1,0:T(8,128)(2,1)} %param.12), channel_id=1, source_target_pairs={{4,0},{68,64},{0,128},{64,192},{132,4},{196,68},{128,132},{192,196... | collective-permute-start | bytes 221192 | tf_op jit(solution)/shard_map/ppermute | solution.py:231
  11.3 23.2 %collective-permute-start.6 = (bf16[8,32,384]{2,1,0:T(8,128)(2,1)}, bf16[8,32,384]{2,1,0:T(8,128)(2,1)S(1)}, u32[]{:S(2)}, u32[]{:S(2)}) collective-permute-start(bf16[8,32,384]{2,1,0:T(8,128)(2,1)} %refs_9_.3), channel_id=1, source_target_pairs={{4,0},{0,4},{5,1},{1,5},{6,2},{2,6},{7,3},{3,7},{12,8},{8,12},{13,... | collective-permute-start | bytes 589832 | tf_op jit(solution)/shard_map/ppermute | solution.py:207
  14.2 23.3 %collective-permute-start.2 = (bf16[8,32,384]{2,1,0:T(8,128)(2,1)}, bf16[8,32,384]{2,1,0:T(8,128)(2,1)S(1)}, u32[]{:S(2)}, u32[]{:S(2)}) collective-permute-start(bf16[8,32,384]{2,1,0:T(8,128)(2,1)} %refs_1_.3), channel_id=1, source_target_pairs={{3,0},{0,1},{1,2},{2,3},{7,4},{4,5},{5,6},{6,7},{11,8},{8,9},{9,10... | collective-permute-start | bytes 589832 | tf_op jit(solution)/shard_map/ppermute | solution.py:207
  20.4 25.4 %collective-permute-start.15 = (bf16[4,96,384]{2,1,0:T(8,128)(2,1)S(1)}, bf16[4,96,384]{2,1,0:T(8,128)(2,1)S(1)}, u32[]{:S(2)}, u32[]{:S(2)}) collective-permute-start(bf16[4,96,384]{2,1,0:T(8,128)(2,1)S(1)} %pad_maximum_fusion.refs_11_), channel_id=1, source_target_pairs={{48,0},{0,16},{16,32},{32,48},{49,1},{1,17},{17,33},{33,49},{50,2}... | collective-permute-start | bytes 884744 | tf_op jit(solution)/shard_map/ppermute | solution.py:207
  22.1 23.7 %collective-permute-start.14 = (bf16[4,96,384]{2,1,0:T(8,128)(2,1)S(1)}, bf16[4,96,384]{2,1,0:T(8,128)(2,1)S(1)}, u32[]{:S(2)}, u32[]{:S(2)}) collective-permute-start(bf16[4,96,384]{2,1,0:T(8,128)(2,1)S(1)} %pad_maximum_fusion.refs_11_), channel_id=1, source_target_pairs={{32,0},{48,16},{0,32},{16,48},{33,1},{49,17},{1,33},{17,49},{34,2}... | collective-permute-start | bytes 884744 | tf_op jit(solution)/shard_map/ppermute | solution.py:207
  25.6 7.5 %collective-permute-start.8 = (f32[1,384]{1,0:T(1,128)S(1)}, f32[1,384]{1,0:T(1,128)S(1)}, u32[]{:S(2)}, u32[]{:S(2)}) collective-permute-start(f32[1,384]{1,0:T(1,128)S(1)} %broadcast_in_dim.3.refs_7_.refs_13_), channel_id=1, source_target_pairs={{4,0},{0,4},{5,1},{1,5},{6,2},{2,6},{7,3},{3,7},{12,8},{8,12},{13,... | collective-permute-start | bytes 4616 | tf_op jit(solution)/shard_map/ppermute | solution.py:207
  33.1 13.1 %collective-permute-start.13 = (bf16[4,96,384]{2,1,0:T(8,128)(2,1)S(1)}, bf16[4,96,384]{2,1,0:T(8,128)(2,1)S(1)}, u32[]{:S(2)}, u32[]{:S(2)}) collective-permute-start(bf16[4,96,384]{2,1,0:T(8,128)(2,1)S(1)} %pad_maximum_fusion.refs_11_), channel_id=1, source_target_pairs={{16,0},{32,16},{48,32},{0,48},{17,1},{33,17},{49,33},{1,49},{18,2}... | collective-permute-start | bytes 884744 | tf_op jit(solution)/shard_map/ppermute | solution.py:207
  34.5 50.8 %copy-start.4 = (bf16[8,32,384]{2,1,0:T(8,128)(2,1)}, bf16[8,32,384]{2,1,0:T(8,128)(2,1)S(1)}, u32[]{:S(2)}) copy-start(bf16[8,32,384]{2,1,0:T(8,128)(2,1)S(1)} %collective-permute-done.6.refs_6_.refs_10_) | copy-start | bytes 589828
  34.5 7.4 %collective-permute-start.1 = (bf16[8,32,384]{2,1,0:T(8,128)(2,1)}, bf16[8,32,384]{2,1,0:T(8,128)(2,1)S(1)}, u32[]{:S(2)}, u32[]{:S(2)}) collective-permute-start(bf16[8,32,384]{2,1,0:T(8,128)(2,1)} %refs_1_.3), channel_id=1, source_target_pairs={{2,0},{3,1},{0,2},{1,3},{6,4},{7,5},{4,6},{5,7},{10,8},{11,9},{8,1... | collective-permute-start | bytes 589832 | tf_op jit(solution)/shard_map/ppermute | solution.py:207
  37.5 15.5 %collective-permute-start.16 = (bf16[4,96,384]{2,1,0:T(8,128)(2,1)S(1)}, bf16[4,96,384]{2,1,0:T(8,128)(2,1)S(1)}, u32[]{:S(2)}, u32[]{:S(2)}) collective-permute-start(bf16[4,96,384]{2,1,0:T(8,128)(2,1)S(1)} %pad_maximum_fusion.refs_11_), channel_id=1, source_target_pairs={{8,0},{0,8},{9,1},{1,9},{10,2},{2,10},{11,3},{3,11},{12,4},{4,12},... | collective-permute-start | bytes 884744 | tf_op jit(solution)/shard_map/ppermute | solution.py:207
  41.9 7.4 %collective-permute-start = (bf16[8,32,384]{2,1,0:T(8,128)(2,1)}, bf16[8,32,384]{2,1,0:T(8,128)(2,1)S(1)}, u32[]{:S(2)}, u32[]{:S(2)}) collective-permute-start(bf16[8,32,384]{2,1,0:T(8,128)(2,1)} %refs_1_.3), channel_id=1, source_target_pairs={{1,0},{2,1},{3,2},{0,3},{5,4},{6,5},{7,6},{4,7},{9,8},{10,9},{11,1... | collective-permute-start | bytes 589832 | tf_op jit(solution)/shard_map/ppermute | solution.py:207
  45.8 12.4 %copy-start.11 = (bf16[4,96,384]{2,1,0:T(8,128)(2,1)}, bf16[4,96,384]{2,1,0:T(8,128)(2,1)S(1)}, u32[]{:S(2)}) copy-start(bf16[4,96,384]{2,1,0:T(8,128)(2,1)S(1)} %collective-permute-done.15.refs_14_) | copy-start | bytes 884740
  45.8 9.3 %collective-permute-start.19 = (bf16[4,96,384]{2,1,0:T(8,128)(2,1)S(1)}, bf16[4,96,384]{2,1,0:T(8,128)(2,1)S(1)}, u32[]{:S(2)}, u32[]{:S(2)}) collective-permute-start(bf16[4,96,384]{2,1,0:T(8,128)(2,1)S(1)} %collective-permute-done.15.refs_14_), channel_id=1, source_target_pairs={{8,0},{0,8},{9,1},{1,9},{10,2},{2,10},{11,3},{3,11},{12,4},{4,12},... | collective-permute-start | bytes 884744 | tf_op jit(solution)/shard_map/ppermute | solution.py:207
  45.8 12.4 %copy-start.12 = (bf16[4,96,384]{2,1,0:T(8,128)(2,1)}, bf16[4,96,384]{2,1,0:T(8,128)(2,1)S(1)}, u32[]{:S(2)}) copy-start(bf16[4,96,384]{2,1,0:T(8,128)(2,1)S(1)} %collective-permute-done.14.refs_13_) | copy-start | bytes 884740
  45.8 12.3 %collective-permute-start.18 = (bf16[4,96,384]{2,1,0:T(8,128)(2,1)S(1)}, bf16[4,96,384]{2,1,0:T(8,128)(2,1)S(1)}, u32[]{:S(2)}, u32[]{:S(2)}) collective-permute-start(bf16[4,96,384]{2,1,0:T(8,128)(2,1)S(1)} %collective-permute-done.14.refs_13_), channel_id=1, source_target_pairs={{8,0},{0,8},{9,1},{1,9},{10,2},{2,10},{11,3},{3,11},{12,4},{4,12},... | collective-permute-start | bytes 884744 | tf_op jit(solution)/shard_map/ppermute | solution.py:207
  46.3 11.9 %copy-start.13 = (bf16[4,96,384]{2,1,0:T(8,128)(2,1)}, bf16[4,96,384]{2,1,0:T(8,128)(2,1)S(1)}, u32[]{:S(2)}) copy-start(bf16[4,96,384]{2,1,0:T(8,128)(2,1)S(1)} %collective-permute-done.13.refs_12_) | copy-start | bytes 884740
  46.3 11.9 %collective-permute-start.17 = (bf16[4,96,384]{2,1,0:T(8,128)(2,1)S(1)}, bf16[4,96,384]{2,1,0:T(8,128)(2,1)S(1)}, u32[]{:S(2)}, u32[]{:S(2)}) collective-permute-start(bf16[4,96,384]{2,1,0:T(8,128)(2,1)S(1)} %collective-permute-done.13.refs_12_), channel_id=1, source_target_pairs={{8,0},{0,8},{9,1},{1,9},{10,2},{2,10},{11,3},{3,11},{12,4},{4,12},... | collective-permute-start | bytes 884744 | tf_op jit(solution)/shard_map/ppermute | solution.py:207
  49.3 29.5 %collective-permute-start.7 = (bf16[8,32,384]{2,1,0:T(8,128)(2,1)}, bf16[8,32,384]{2,1,0:T(8,128)(2,1)S(1)}, u32[]{:S(2)}, u32[]{:S(2)}) collective-permute-start(bf16[8,32,384]{2,1,0:T(8,128)(2,1)} %refs_11_.1), channel_id=1, source_target_pairs={{4,0},{0,4},{5,1},{1,5},{6,2},{2,6},{7,3},{3,7},{12,8},{8,12},{13,... | collective-permute-start | bytes 589832 | tf_op jit(solution)/shard_map/ppermute | solution.py:207
  53.0 5.2 %copy-start.14 = (bf16[4,96,384]{2,1,0:T(8,128)(2,1)}, bf16[4,96,384]{2,1,0:T(8,128)(2,1)S(1)}, u32[]{:S(2)}) copy-start(bf16[4,96,384]{2,1,0:T(8,128)(2,1)S(1)} %collective-permute-done.16.refs_15_) | copy-start | bytes 884740
  53.0 26.3 %collective-permute-start.5 = (bf16[8,32,384]{2,1,0:T(8,128)(2,1)}, bf16[8,32,384]{2,1,0:T(8,128)(2,1)}, u32[]{:S(2)}, u32[]{:S(2)}) collective-permute-start(bf16[8,32,384]{2,1,0:T(8,128)(2,1)} %refs_5_.3), channel_id=1, source_target_pairs={{3,0},{0,1},{1,2},{2,3},{7,4},{4,5},{5,6},{6,7},{11,8},{8,9},{9,10... | collective-permute-start | bytes 589832 | tf_op jit(solution)/shard_map/ppermute | solution.py:207
  55.0 3.2 %copy-start.15 = (bf16[4,96,384]{2,1,0:T(8,128)(2,1)}, bf16[4,96,384]{2,1,0:T(8,128)(2,1)S(1)}, u32[]{:S(2)}) copy-start(bf16[4,96,384]{2,1,0:T(8,128)(2,1)S(1)} %collective-permute-done.19.refs_18_) | copy-start | bytes 884740
  55.0 26.5 %collective-permute-start.4 = (bf16[8,32,384]{2,1,0:T(8,128)(2,1)}, bf16[8,32,384]{2,1,0:T(8,128)(2,1)}, u32[]{:S(2)}, u32[]{:S(2)}) collective-permute-start(bf16[8,32,384]{2,1,0:T(8,128)(2,1)} %refs_5_.3), channel_id=1, source_target_pairs={{2,0},{3,1},{0,2},{1,3},{6,4},{7,5},{4,6},{5,7},{10,8},{11,9},{8,1... | collective-permute-start | bytes 589832 | tf_op jit(solution)/shard_map/ppermute | solution.py:207
  58.0 0.7 copy-start.16
  58.0 23.5 %collective-permute-start.3 = (bf16[8,32,384]{2,1,0:T(8,128)(2,1)}, bf16[8,32,384]{2,1,0:T(8,128)(2,1)}, u32[]{:S(2)}, u32[]{:S(2)}) collective-permute-start(bf16[8,32,384]{2,1,0:T(8,128)(2,1)} %refs_5_.3), channel_id=1, source_target_pairs={{1,0},{2,1},{3,2},{0,3},{5,4},{6,5},{7,6},{4,7},{9,8},{10,9},{11,1... | collective-permute-start | bytes 589832 | tf_op jit(solution)/shard_map/ppermute | solution.py:207
  58.8 0.7 copy-start.17
  59.5 0.9 copy-start
  60.4 0.9 copy-start.1
  61.3 0.9 copy-start.3
  62.3 0.9 copy-start.5
  77.3 6.0 %collective-permute-start.22 = (f32[8,3456]{1,0:T(8,128)S(1)}, f32[8,3456]{1,0:T(8,128)S(1)}, u32[]{:S(2)}, u32[]{:S(2)}) collective-permute-start(f32[8,3456]{1,0:T(8,128)S(1)} %get-tuple-element.21.refs_15_), channel_id=1, source_target_pairs={{3,0},{0,1},{1,2},{2,3},{7,4},{4,5},{5,6},{6,7},{11,8},{8,9},{9,10... | collective-permute-start | bytes 331784 | tf_op jit(solution)/shard_map/ppermute | solution.py:207
  78.7 6.6 %copy-start.18 = (bf16[8,32,384]{2,1,0:T(8,128)(2,1)}, bf16[8,32,384]{2,1,0:T(8,128)(2,1)S(1)}, u32[]{:S(2)}) copy-start(bf16[8,32,384]{2,1,0:T(8,128)(2,1)S(1)} %collective-permute-done.7.refs_12_) | copy-start | bytes 589828
  78.7 6.3 %collective-permute-start.21 = (f32[8,3456]{1,0:T(8,128)S(1)}, f32[8,3456]{1,0:T(8,128)S(1)}, u32[]{:S(2)}, u32[]{:S(2)}) collective-permute-start(f32[8,3456]{1,0:T(8,128)S(1)} %get-tuple-element.21.refs_15_), channel_id=1, source_target_pairs={{2,0},{3,1},{0,2},{1,3},{6,4},{7,5},{4,6},{5,7},{10,8},{11,9},{8,1... | collective-permute-start | bytes 331784 | tf_op jit(solution)/shard_map/ppermute | solution.py:207
  79.3 6.0 %collective-permute-start.20 = (f32[8,3456]{1,0:T(8,128)S(1)}, f32[8,3456]{1,0:T(8,128)S(1)}, u32[]{:S(2)}, u32[]{:S(2)}) collective-permute-start(f32[8,3456]{1,0:T(8,128)S(1)} %get-tuple-element.21.refs_15_), channel_id=1, source_target_pairs={{1,0},{2,1},{3,2},{0,3},{5,4},{6,5},{7,6},{4,7},{9,8},{10,9},{11,1... | collective-permute-start | bytes 331784 | tf_op jit(solution)/shard_map/ppermute | solution.py:207
  120.1 7.9 %copy-start.19 = (bf16[16,32,384]{2,1,0:T(8,128)(2,1)S(1)}, bf16[16,32,384]{2,1,0:T(8,128)(2,1)}, u32[]{:S(2)}) copy-start(bf16[16,32,384]{2,1,0:T(8,128)(2,1)} %get-tuple-element.28) | copy-start | bytes 1179652
  120.1 10.3 %copy-start.6 = (f32[4,96,384]{2,1,0:T(8,128)S(1)}, f32[4,96,384]{2,1,0:T(8,128)}, u32[]{:S(2)}) copy-start(f32[4,96,384]{2,1,0:T(8,128)} %get-tuple-element.36) | copy-start | bytes 1769476
  120.1 17.2 %copy-start.8 = (f32[8,32,384]{2,1,0:T(8,128)S(1)}, f32[8,32,384]{2,1,0:T(8,128)}, u32[]{:S(2)}) copy-start(f32[8,32,384]{2,1,0:T(8,128)} %get-tuple-element.23) | copy-start | bytes 1179652
  120.1 5.0 %collective-permute-start.28 = (bf16[4,96,384]{2,1,0:T(8,128)(2,1)}, bf16[4,96,384]{2,1,0:T(8,128)(2,1)S(1)}, u32[]{:S(2)}, u32[]{:S(2)}) collective-permute-start(bf16[4,96,384]{2,1,0:T(8,128)(2,1)} %get-tuple-element.33), channel_id=1, source_target_pairs={{8,0},{0,8},{9,1},{1,9},{10,2},{2,10},{11,3},{3,11},{12,4},{4,12},... | collective-permute-start | bytes 884744 | tf_op jit(solution)/shard_map/ppermute | solution.py:207
  120.2 6.0 %collective-permute-start.30 = (bf16[4,96,384]{2,1,0:T(8,128)(2,1)}, bf16[4,96,384]{2,1,0:T(8,128)(2,1)S(1)}, u32[]{:S(2)}, u32[]{:S(2)}) collective-permute-start(bf16[4,96,384]{2,1,0:T(8,128)(2,1)} %get-tuple-element.35), channel_id=1, source_target_pairs={{8,0},{0,8},{9,1},{1,9},{10,2},{2,10},{11,3},{3,11},{12,4},{4,12},... | collective-permute-start | bytes 884744 | tf_op jit(solution)/shard_map/ppermute | solution.py:207
  120.7 9.7 %collective-permute-start.23 = (bf16[8,32,384]{2,1,0:T(8,128)(2,1)S(1)}, bf16[8,32,384]{2,1,0:T(8,128)(2,1)S(1)}, u32[]{:S(2)}, u32[]{:S(2)}) collective-permute-start(bf16[8,32,384]{2,1,0:T(8,128)(2,1)S(1)} %get-tuple-element.24), channel_id=1, source_target_pairs={{0,1},{1,2},{2,3},{3,0},{4,5},{5,6},{6,7},{7,4},{8,9},{9,10},{10,1... | collective-permute-start | bytes 589832 | tf_op jit(solution)/shard_map/ppermute | solution.py:211
  121.7 12.2 %collective-permute-start.24 = (bf16[8,32,384]{2,1,0:T(8,128)(2,1)S(1)}, bf16[8,32,384]{2,1,0:T(8,128)(2,1)S(1)}, u32[]{:S(2)}, u32[]{:S(2)}) collective-permute-start(bf16[8,32,384]{2,1,0:T(8,128)(2,1)S(1)} %get-tuple-element.25), channel_id=1, source_target_pairs={{0,2},{1,3},{2,0},{3,1},{4,6},{5,7},{6,4},{7,5},{8,10},{9,11},{10,... | collective-permute-start | bytes 589832 | tf_op jit(solution)/shard_map/ppermute | solution.py:211
  124.9 9.4 %collective-permute-start.25 = (bf16[8,32,384]{2,1,0:T(8,128)(2,1)S(1)}, bf16[8,32,384]{2,1,0:T(8,128)(2,1)S(1)}, u32[]{:S(2)}, u32[]{:S(2)}) collective-permute-start(bf16[8,32,384]{2,1,0:T(8,128)(2,1)S(1)} %get-tuple-element.26), channel_id=1, source_target_pairs={{0,3},{1,0},{2,1},{3,2},{4,7},{5,4},{6,5},{7,6},{8,11},{9,8},{10,9... | collective-permute-start | bytes 589832 | tf_op jit(solution)/shard_map/ppermute | solution.py:211
  125.1 2.9 %collective-permute-start.32 = (bf16[4,96,384]{2,1,0:T(8,128)(2,1)}, bf16[4,96,384]{2,1,0:T(8,128)(2,1)S(1)}, u32[]{:S(2)}, u32[]{:S(2)}) collective-permute-start(bf16[4,96,384]{2,1,0:T(8,128)(2,1)} %get-tuple-element.37), channel_id=1, source_target_pairs={{8,0},{0,8},{9,1},{1,9},{10,2},{2,10},{11,3},{3,11},{12,4},{4,12},... | collective-permute-start | bytes 884744 | tf_op jit(solution)/shard_map/ppermute | solution.py:207
  126.2 22.9 %collective-permute-start.27 = (bf16[4,96,384]{2,1,0:T(8,128)(2,1)}, bf16[4,96,384]{2,1,0:T(8,128)(2,1)S(1)}, u32[]{:S(2)}, u32[]{:S(2)}) collective-permute-start(bf16[4,96,384]{2,1,0:T(8,128)(2,1)} %get-tuple-element.31), channel_id=1, source_target_pairs={{8,0},{0,8},{9,1},{1,9},{10,2},{2,10},{11,3},{3,11},{12,4},{4,12},... | collective-permute-start | bytes 884744 | tf_op jit(solution)/shard_map/ppermute | solution.py:207
  126.8 22.4 %copy-start.7 = (f32[4,96,384]{2,1,0:T(8,128)S(1)}, f32[4,96,384]{2,1,0:T(8,128)}, u32[]{:S(2)}) copy-start(f32[4,96,384]{2,1,0:T(8,128)} %get-tuple-element.30) | copy-start | bytes 1769476
  128.0 21.0 %collective-permute-start.26 = (bf16[16,32,384]{2,1,0:T(8,128)(2,1)S(1)}, bf16[16,32,384]{2,1,0:T(8,128)(2,1)S(1)}, u32[]{:S(2)}, u32[]{:S(2)}) collective-permute-start(bf16[16,32,384]{2,1,0:T(8,128)(2,1)S(1)} %copy-done.19), channel_id=1, source_target_pairs={{4,0},{0,4},{5,1},{1,5},{6,2},{2,6},{7,3},{3,7},{12,8},{8,12},{13,... | collective-permute-start | bytes 1179656 | tf_op jit(solution)/shard_map/ppermute | solution.py:207
  130.5 18.7 %collective-permute-start.29 = (bf16[4,96,384]{2,1,0:T(8,128)(2,1)S(1)}, bf16[4,96,384]{2,1,0:T(8,128)(2,1)S(1)}, u32[]{:S(2)}, u32[]{:S(2)}) collective-permute-start(bf16[4,96,384]{2,1,0:T(8,128)(2,1)S(1)} %add_convert_fusion.3), channel_id=1, source_target_pairs={{0,16},{16,32},{32,48},{48,0},{1,17},{17,33},{33,49},{49,1},{2,18}... | collective-permute-start | bytes 884744 | tf_op jit(solution)/shard_map/ppermute | solution.py:211
  134.0 15.2 %collective-permute-start.31 = (bf16[4,96,384]{2,1,0:T(8,128)(2,1)S(1)}, bf16[4,96,384]{2,1,0:T(8,128)(2,1)S(1)}, u32[]{:S(2)}, u32[]{:S(2)}) collective-permute-start(bf16[4,96,384]{2,1,0:T(8,128)(2,1)S(1)} %add_convert_fusion.2), channel_id=1, source_target_pairs={{0,32},{16,48},{32,0},{48,16},{1,33},{17,49},{33,1},{49,17},{2,34}... | collective-permute-start | bytes 884744 | tf_op jit(solution)/shard_map/ppermute | solution.py:211
  134.3 14.9 %collective-permute-start.33 = (bf16[4,96,384]{2,1,0:T(8,128)(2,1)S(1)}, bf16[4,96,384]{2,1,0:T(8,128)(2,1)S(1)}, u32[]{:S(2)}, u32[]{:S(2)}) collective-permute-start(bf16[4,96,384]{2,1,0:T(8,128)(2,1)S(1)} %add_convert_fusion.1), channel_id=1, source_target_pairs={{0,48},{16,0},{32,16},{48,32},{1,49},{17,1},{33,17},{49,33},{2,50}... | collective-permute-start | bytes 884744 | tf_op jit(solution)/shard_map/ppermute | solution.py:211
  137.3 21.4 %copy-start.9 = (f32[8,32,384]{2,1,0:T(8,128)S(1)}, f32[8,32,384]{2,1,0:T(8,128)}, u32[]{:S(2)}) copy-start(f32[8,32,384]{2,1,0:T(8,128)} %get-tuple-element.27) | copy-start | bytes 1179652
  137.3 21.4 %copy-start.10 = (f32[8,32,384]{2,1,0:T(8,128)S(1)}, f32[8,32,384]{2,1,0:T(8,128)}, u32[]{:S(2)}) copy-start(f32[8,32,384]{2,1,0:T(8,128)} %get-tuple-element.29) | copy-start | bytes 1179652
  149.4 10.2 %collective-permute-start.34 = (bf16[96,384]{1,0:T(8,128)(2,1)S(1)}, bf16[96,384]{1,0:T(8,128)(2,1)S(1)}, u32[]{:S(2)}, u32[]{:S(2)}) collective-permute-start(bf16[96,384]{1,0:T(8,128)(2,1)S(1)} %get-tuple-element.40), channel_id=1, source_target_pairs={{0,0},{64,64},{128,4},{192,68},{4,128},{68,192},{132,132},{196,196... | collective-permute-start | bytes 221192 | tf_op jit(solution)/shard_map/ppermute | solution.py:283
  151.3 12.2 %collective-permute-start.37 = (bf16[96,384]{1,0:T(8,128)(2,1)S(1)}, bf16[96,384]{1,0:T(8,128)(2,1)S(1)}, u32[]{:S(2)}, u32[]{:S(2)}) collective-permute-start(bf16[96,384]{1,0:T(8,128)(2,1)S(1)} %get-tuple-element.41), channel_id=1, source_target_pairs={{0,68},{64,0},{128,64},{192,4},{4,196},{68,128},{132,192},{196,132... | collective-permute-start | bytes 221192 | tf_op jit(solution)/shard_map/ppermute | solution.py:283
  151.4 12.1 %collective-permute-start.36 = (bf16[96,384]{1,0:T(8,128)(2,1)S(1)}, bf16[96,384]{1,0:T(8,128)(2,1)S(1)}, u32[]{:S(2)}, u32[]{:S(2)}) collective-permute-start(bf16[96,384]{1,0:T(8,128)(2,1)S(1)} %get-tuple-element.42), channel_id=1, source_target_pairs={{0,4},{64,68},{128,0},{192,64},{4,132},{68,196},{132,128},{196,192... | collective-permute-start | bytes 221192 | tf_op jit(solution)/shard_map/ppermute | solution.py:283
  158.8 7.4 %collective-permute-start.35 = (bf16[96,384]{1,0:T(8,128)(2,1)S(1)}, bf16[96,384]{1,0:T(8,128)(2,1)S(1)}, u32[]{:S(2)}, u32[]{:S(2)}) collective-permute-start(bf16[96,384]{1,0:T(8,128)(2,1)S(1)} %get-tuple-element.43), channel_id=1, source_target_pairs={{0,64},{64,4},{128,68},{192,0},{4,192},{68,132},{132,196},{196,128... | collective-permute-start | bytes 221192 | tf_op jit(solution)/shard_map/ppermute | solution.py:283

commit v2 on v1

v2 whole, which is shorter than its diff:
```python
import math

import jax
import jax.numpy as jnp
from jax import lax
from jax.experimental import pallas as pl
from jax.experimental.pallas import tpu as pltpu
from jax.sharding import Mesh, PartitionSpec as P

FINE = ("zlo", "y", "core", "zhi", "x")
ZLO, Y, CORE, ZHI, X = 4, 4, 2, 2, 4
LOG2E = math.log2(math.e)
MASKED = -8192.0
BF16, F32 = jnp.bfloat16, jnp.float32


def dot(a, b, ca, cb):
    return lax.dot_general(a, b, (((ca,), (cb,)), ((), ())), preferred_element_type=F32)


def split3(x):
    high = x.astype(BF16).astype(F32)
    rest = x - high
    middle = rest.astype(BF16).astype(F32)
    return high, middle, rest - middle


def rows_of(parts, count, width):
    row = lax.broadcasted_iota(jnp.int32, (count, width), 0)
    out = jnp.zeros((count, width), F32)
    for at, part in enumerate(parts):
        out = jnp.where(row == at, part, out)
    return out


def put_keys(refs, masks, place, scale):
    rows, head, width = refs[0].shape
    for slot, (ref, mask) in enumerate(zip(refs, masks)):
        offset = jnp.where(mask == 0.0, MASKED, 0.0)
        extra = rows_of((-1.0, -1.0, -1.0, offset), head, width)

        def prepare(i, carry):
            parts = split3(ref[i].astype(F32) * scale)
            whole = jnp.concatenate(parts + (extra,), axis=0)
            place[i, slot * width : (slot + 1) * width, :] = whole.T.astype(BF16)
            return carry

        lax.fori_loop(0, rows, prepare, 0)


def put_values(refs, place):
    rows, head, width = refs[0].shape
    extra = rows_of((-1.0, -1.0, -1.0), 128 - head, width)
    for slot, ref in enumerate(refs):

        def prepare(i, carry):
            whole = jnp.concatenate((ref[i].astype(F32), extra), axis=0)
            place[i, slot * width : (slot + 1) * width, :] = whole.T.astype(BF16)
            return carry

        lax.fori_loop(0, rows, prepare, 0)


def bias_pieces(at, half):
    zlo, y, core, zhi, x = (at[n] for n in range(5))
    for yd in range(Y):
        row = lax.rem(y + yd, Y)
        for key_half in range(ZHI):
            zd = lax.rem(key_half * 2 + half - zlo + ZLO, ZLO)
            slot = lax.rem(key_half + zhi, 2)
            for other in range(CORE):
                which = lax.rem(core + other, 2)
                first = pl.multiple_of(row * 192 + which * 96, 32)
                yield yd, key_half, zd, other, slot, first


def stats_kernel(scale, half, at, *refs):
    both_qg, keys, away, mask = refs[0:4]
    pieces = (refs[4:8], refs[8:12])
    refs = refs[12:]
    rows, head, width = keys.shape
    span = 2 * width
    if half == 0:
        values, grad, outs, stat, bias_t, key_t, value_t, bias_n, bias_f = refs
        put_keys((keys, away), (mask[...], away[2 * rows, 0:1, :].astype(F32)), key_t, scale * LOG2E)
        put_values((values, away.at[rows : 2 * rows]), value_t)
    else:
        key_t, stat, bias_t, bias_n, bias_f = refs
    for yd, _, zd, other, slot, first in bias_pieces(at, half):
        bias_n[slot, pl.ds(first, 96), :] = pieces[other][yd][zd]
    for slot in range(2):
        for j in range(0, span, 128):
            tile = bias_n[slot, j : j + 128, :].astype(F32).T
            bias_t[slot * width : (slot + 1) * width, j : j + 128] = tile.astype(BF16)
            bias_f[slot * width : (slot + 1) * width, j : j + 128] = tile * LOG2E
    ones = rows_of((0.0, 0.0, 0.0, 1.0), 16, width).astype(BF16)

    def row_step(i, carry):
        for d in range(2):
            query = both_qg[2 * half + d, i]
            augmented = jnp.concatenate((query, query, query, ones), axis=0)
            cols = slice(d * width, (d + 1) * width)
            top, total_sum = None, None
            for k in range(0, 2 * width, 128):
                scores = dot(key_t[i, k : k + 128, :112], augmented, 1, 0)
                scores = (scores + bias_f[k : k + 128, cols]).reshape(16, 8, width)
                here = jnp.max(scores, axis=0)
                if top is None:
                    top = here
                    total_sum = jnp.sum(jnp.exp2(scores - top), axis=0)
                else:
                    new = jnp.maximum(top, here)
                    total_sum = total_sum * jnp.exp2(top - new) + jnp.sum(
                        jnp.exp2(scores - new), axis=0
                    )
                    top = new
            most = jnp.max(top, axis=0, keepdims=True)
            summed = jnp.sum(total_sum * jnp.exp2(top - most), axis=0, keepdims=True)
            stat[pl.ds(i, 1), cols] = most
            stat[pl.ds(i, 1), span + d * width : span + (d + 1) * width] = summed
        if half == 0:
            product = grad[i].astype(F32) * outs[i].astype(F32)
            stat[pl.ds(i, 1), 2 * span :] = jnp.sum(product, axis=0, keepdims=True)
        return carry

    lax.fori_loop(0, rows, row_step, 0)


def main_kernel(half, at, *refs):
    both_qg, keys, away, key_t, value_t, bias_t = refs[0:6]
    stats, first_stats = refs[6:10], refs[10:14]
    refs = refs[14:]
    rows, head, width = keys.shape
    span = 2 * width
    if half == 0:
        dk_sum, dv_sum, dq, bias_own, bias_away = refs[:5]
    else:
        dk_before, dv_before, dk_own, dv_own, dkv_away, dq, bias_own, bias_away = refs[:8]
    bias_f, acc, turned, lse, delta = refs[-5:]
    for e in range(X):
        delta[lax.rem(at[4] + e, X)] = first_stats[e][:, 2 * span :]
    tops = [stats[e][:, :span] for e in range(X)]
    sums = [stats[e][:, span : 2 * span] for e in range(X)]
    top = jnp.maximum(jnp.maximum(tops[0], tops[1]), jnp.maximum(tops[2], tops[3]))
    summed = sum(s * jnp.exp2(t - top) for s, t in zip(sums, tops))
    lse[...] = top + jnp.log(summed) * LOG2E
    bias_f[...] = bias_t[...].astype(F32) * LOG2E
    acc[...] = jnp.zeros_like(acc)

    def row_step(i, carry):
        dk_row, dv_row = None, None
        for d in range(2):
            chunk = 2 * half + d
            cols = slice(d * width, (d + 1) * width)
            query, gradient = both_qg[chunk, i], both_qg[chunk, rows + i]
            high, middle, low = split3(lse[pl.ds(i, 1), cols])
            extra = rows_of((high, middle, low, 1.0), 16, width).astype(BF16)
            query_all = jnp.concatenate((query, query, query, extra), axis=0)
            extra = rows_of(split3(delta[chunk, pl.ds(i, 1), :]), 16, width).astype(BF16)
            gradient_all = jnp.concatenate((gradient, extra), axis=0)
            probs = jnp.exp2(dot(key_t[i, :, :112], query_all, 1, 0) + bias_f[:, cols])
            dscores = probs * dot(value_t[i, :, :48], gradient_all, 1, 0)
            acc[:, cols] += dscores
            probs_low, dscores_low = probs.astype(BF16), dscores.astype(BF16)
            dv_part = dot(gradient, probs_low, 1, 1)
            dk_part = dot(query, dscores_low, 1, 1)
            dv_row = dv_part if d == 0 else dv_row + dv_part
            dk_row = dk_part if d == 0 else dk_row + dk_part
            dq_part = dot(keys[i], dscores_low[:width], 1, 0) + dot(
                away[i], dscores_low[width:], 1, 0
            )
            dq[d, i] = dq_part
        if half == 0:
            dk_sum[i], dv_sum[i] = dk_row, dv_row
        else:
            dk_row, dv_row = dk_row + dk_before[i], dv_row + dv_before[i]
            dk_own[i], dv_own[i] = dk_row[:, :width], dv_row[:, :width]
            dkv_away[i] = dk_row[:, width:].astype(BF16)
            dkv_away[rows + i] = dv_row[:, width:].astype(BF16)
        return carry

    lax.fori_loop(0, rows, row_step, 0)
    for slot in range(2):
        for j in range(0, span, 128):
            turned[slot, j : j + 128, :] = acc[slot * width : (slot + 1) * width, j : j + 128].T
    for yd, key_half, _, other, slot, first in bias_pieces(at, half):
        place = bias_own if other == 0 else bias_away
        place[yd, key_half] = turned[slot, pl.ds(first, 96), :].astype(place.dtype)


VMEM = pl.BlockSpec(memory_space=pltpu.VMEM)
SMEM = pl.BlockSpec(memory_space=pltpu.SMEM)


def call(kernel, name, args, outs, scratch, mebibytes):
    return pl.pallas_call(
        kernel,
        in_specs=[SMEM] + [VMEM] * (len(args) - 1),
        out_specs=[VMEM] * len(outs),
        out_shape=[jax.ShapeDtypeStruct(shape, dtype) for shape, dtype in outs],
        scratch_shapes=[pltpu.VMEM(shape, dtype) for shape, dtype in scratch],
        compiler_params=pltpu.CompilerParams(vmem_limit_bytes=mebibytes * 2**20),
        name=name,
    )(*args)


def fetch(x, axis, size, distance):
    return lax.ppermute(x, axis, [((n + distance) % size, n) for n in range(size)])


def deliver(x, axis, size, distance):
    return lax.ppermute(x, axis, [(n, (n + distance) % size) for n in range(size)])


def z_pairs(distance):
    pairs = []
    for group in range(ZHI):
        for place in range(ZLO):
            half, part = divmod((place + distance) % ZLO, 2)
            pairs.append(((2 * group + part) * ZHI + half, place * ZHI + group))
    return pairs


def per_device(queries, keys, values, out_grad, outputs, bias, key_mask):
    rows, head, width = keys.shape
    scale = head ** (-0.5)
    span, both = 2 * width, 2 * width
    z_axes = ("zlo", "zhi")
    at = jnp.stack([lax.axis_index(name) for name in FINE]).astype(jnp.int32)
    mask = key_mask.astype(F32)[None, :]

    both_qg = lax.all_gather(jnp.concatenate([queries, out_grad], axis=0), "x")
    from_z = jnp.stack([lax.ppermute(bias, z_axes, z_pairs(d)) for d in range(ZLO)])
    mask_rows = jnp.broadcast_to(key_mask.astype(BF16), (1, head, width))
    away = fetch(jnp.concatenate([keys, values, mask_rows], axis=0), "zhi", ZHI, 1)
    here = [from_z] + [fetch(from_z, "y", Y, d) for d in range(1, Y)]
    there = [fetch(a, "core", CORE, 1) for a in here]

    bias_shapes = [((2, span, width), BF16), ((both, span), F32)]
    transposed = ((rows, both, 128), BF16)
    stat0, bias0, key_t, value_t = call(
        lambda *refs: stats_kernel(scale, 0, *refs),
        "softmax_statistics_0",
        [at, both_qg, keys, away, mask, *here, *there, values, out_grad, outputs],
        [((rows, 2 * span + width), F32), ((both, span), BF16), transposed, transposed],
        bias_shapes,
        24,
    )
    stats0 = [stat0] + [fetch(stat0, "x", X, d) for d in range(1, X)]
    stat1, bias1 = call(
        lambda *refs: stats_kernel(scale, 1, *refs),
        "softmax_statistics_1",
        [at, both_qg, keys, away, mask, *here, *there, key_t],
        [((rows, 2 * span), F32), ((both, span), BF16)],
        bias_shapes,
        24,
    )
    stats1 = [stat1] + [fetch(stat1, "x", X, d) for d in range(1, X)]

    block, whole = ((rows, head, width), F32), ((rows, head, both), F32)
    pair, pieces = ((2, rows, head, width), F32), (Y, ZHI, 96, width)
    scratch = [
        ((both, span), F32),
        ((both, span), F32),
        ((2, span, width), F32),
        ((rows, span), F32),
        ((X, rows, width), F32),
    ]
    dk, dv, dq0, own0, away0 = call(
        lambda *refs: main_kernel(0, *refs),
        "attention_gradients_0",
        [at, both_qg, keys, away, key_t, value_t, bias0, *stats0, *stats0],
        [whole, whole, pair, (pieces, F32), (pieces, BF16)],
        scratch,
        32,
    )
    near0 = own0 + fetch(away0, "core", CORE, 1).astype(F32)
    sent0 = [near0[d].astype(BF16) for d in range(1, Y)]
    sent0, dk, dv = lax.optimization_barrier((sent0, dk, dv))
    far0 = [deliver(sent0[d - 1], "y", Y, d) for d in range(1, Y)]
    dk, dv, dkv_away, dq1, own1, away1 = call(
        lambda *refs: main_kernel(1, *refs),
        "attention_gradients_1",
        [at, both_qg, keys, away, key_t, value_t, bias1, *stats1, *stats0, dk, dv],
        [block, block, ((2 * rows, head, width), BF16), pair, (pieces, F32), (pieces, BF16)],
        scratch,
        32,
    )
    near1 = own1 + fetch(away1, "core", CORE, 1).astype(F32)
    sent1 = [near1[d].astype(BF16) for d in range(1, Y)]
    dq = jnp.concatenate([dq0, dq1], axis=0)
    sent1, dkv_away, dq = lax.optimization_barrier((sent1, dkv_away, dq))
    far1 = [deliver(sent1[d - 1], "y", Y, d) for d in range(1, Y)]

    def along_y(near, far):
        total = near[0]
        for part in far:
            total = total + part.astype(F32)
        return total.astype(BF16)

    x_at, zlo = lax.axis_index("x"), lax.axis_index("zlo")
    arrived = fetch(dkv_away, "zhi", ZHI, 1).astype(F32)
    mine = lax.dynamic_index_in_dim(dq, x_at, 0, False)
    for d in range(1, X):
        part = lax.dynamic_index_in_dim(dq, lax.rem(x_at + d, X), 0, False).astype(BF16)
        mine = mine + deliver(part, "x", X, d).astype(F32)
    low = jnp.stack([along_y(near0, far0), along_y(near1, far1)], axis=1)
    low = low.reshape(ZLO, 96, width)
    bias_grad = None
    for d in range(ZLO):
        pairs = [(worker, owner) for owner, worker in z_pairs(d)]
        part = lax.dynamic_index_in_dim(low, lax.rem(zlo + d, ZLO), 0, False)
        part = lax.ppermute(part, z_axes, pairs).astype(F32)
        bias_grad = part if bias_grad is None else bias_grad + part

    query_grad = (scale * mine).astype(BF16)
    key_grad = (scale * (dk + arrived[:rows])).astype(BF16)
    value_grad = (dv + arrived[rows:]).astype(BF16)
    return query_grad, key_grad, value_grad, bias_grad


def solution(mesh):
    fine = Mesh(mesh.devices.reshape(ZLO, Y, CORE, ZHI, X), FINE)
    row, col = ("zlo", "y", "core"), ("zhi", "x")
    pair, flat = P(row, None, col), P(row, col)
    return jax.shard_map(
        per_device,
        mesh=fine,
        in_specs=(pair,) * 5 + (flat, P(col)),
        out_specs=(pair,) * 3 + (flat,),
        check_vma=False,
    )
```

time: 168 us -> 175 us (1.042)
  starting transfers between devices: 66.6 us -> 51.8 us
  between operations: 0.91 us -> 14.3 us
  waiting for transfers between devices: 39.6 us -> 44.9 us
  other arithmetic: 5.7 us -> 7.98 us
    ppermute x24 -> x17, starting transfers between devices: 38 us -> 24.8 us  [fetch(): lax.ppermute(x, axis, [((n + distance) % size, n) for n in range(size)])]
    ppermute x6 -> x9, waiting for transfers between devices: 2.77 us -> 9.17 us  [deliver(): lax.ppermute(x, axis, [(n, (n + distance) % size) for n in range(size)])]
    ppermute x4, starting transfers between devices: 9.37 us -> 5.12 us  [per_device(): part = lax.ppermute(part, z_axes, pairs).astype(F32)]
    concatenate x0 -> x3, other arithmetic: none -> 2.9 us  [the longest x1 1.98 us: per_device(): both_qg = lax.all_gather(jnp.concatenate([queries, out_grad], axis=0), 'x')]
    another operation x0 -> x5, other arithmetic: none -> 2.6 us
    convert_element_type x5 -> x1, other arithmetic: 3.35 us -> 0.8 us  [per_device(): query_grad = (scale * mine).astype(BF16)]
    ppermute x6 -> x9, starting transfers between devices: 8.47 us -> 10.4 us  [deliver(): lax.ppermute(x, axis, [(n, (n + distance) % size) for n in range(size)])]
    ppermute x24 -> x17, waiting for transfers between devices: 25.7 us -> 23.8 us  [fetch(): lax.ppermute(x, axis, [((n + distance) % size, n) for n in range(size)])]
  transfers between devices with their start and end apart: 38 -> 35, of which waited for: 11 -> 16; matrix products, arithmetic and copies ran while one was open for 3% -> 4% of each run, Pallas kernels for 8% -> 4%
where the time goes in v2:
time: 175 us; the launch traced here: 173 us
  starting transfers between devices  51.8 us (30%)
  Pallas kernels  47.9 us (27%)
  waiting for transfers between devices  44.9 us (26%)
  between operations  14.3 us (8%)
  other arithmetic  7.98 us (5%)
  local copies, waits for them, and re-layouts  5.66 us (3%)
    pallas_call x4, Pallas kernels, call(): pl.pallas_call(kernel, in_specs=[SMEM] + [VMEM] * (len(args) - 1), out_sp...  47.9 us
    ppermute x17, starting transfers between devices, fetch(): lax.ppermute(x, axis, [((n + distance) % size, n) for n in range(size)])  24.8 us
    ppermute x17, waiting for transfers between devices, fetch(): lax.ppermute(x, axis, [((n + distance) % size, n) for n in range(size)])  23.8 us
    ppermute x4, starting transfers between devices, per_device(): lax.ppermute(bias, z_axes, z_pairs(d))  11.5 us
    ppermute x9, starting transfers between devices, deliver(): lax.ppermute(x, axis, [(n, (n + distance) % size) for n in range(size)])  10.4 us
    ppermute x9, waiting for transfers between devices, deliver(): lax.ppermute(x, axis, [(n, (n + distance) % size) for n in range(size)])  9.17 us
    ppermute x4, waiting for transfers between devices, per_device(): part = lax.ppermute(part, z_axes, pairs).astype(F32)  7.79 us
    ppermute x4, starting transfers between devices, per_device(): part = lax.ppermute(part, z_axes, pairs).astype(F32)  5.12 us
  transfers between devices with their start and end apart: 35, of which 16 were waited for; matrix products, arithmetic and copies ran while one was open for 4% of the time, Pallas kernels for 4%

profile of v2, /device:TPU:64, one launch (start us, length us, event | category | flops | bytes accessed | tf_op | source)
XLA Modules:
  0.0 172.6 jit_solution(10521654204847595759)
XLA Ops:
  7.3 2.0 %pad_maximum_fusion.2 = bf16[16,32,384]{2,1,0:T(8,128)(2,1)} fusion(bf16[8,32,384]{2,1,0:T(8,128)(2,1)} %refs_14_.1, bf16[8,32,384]{2,1,0:T(8,128)(2,1)} %param.7), kind=kLoop, calls=%fused_computation.9 | loop fusion | flops 196608 | bytes 786432 | tf_op jit(solution)/shard_map/concatenate | solution.py:232
  9.3 6.4 %collective-permute-start.1 = (bf16[96,384]{1,0:T(8,128)(2,1)S(1)}, bf16[96,384]{1,0:T(8,128)(2,1)S(1)}, u32[]{:S(2)}, u32[]{:S(2)}) collective-permute-start(bf16[96,384]{1,0:T(8,128)(2,1)S(1)} %copy-done.15), channel_id=1, source_target_pairs={{0,0},{64,64},{4,128},{68,192},{128,4},{192,68},{132,132},{196,196... | collective-permute-start | bytes 221192 | tf_op jit(solution)/shard_map/ppermute | solution.py:233
  15.8 2.5 %collective-permute-start.3 = (bf16[96,384]{1,0:T(8,128)(2,1)S(1)}, bf16[96,384]{1,0:T(8,128)(2,1)S(1)}, u32[]{:S(2)}, u32[]{:S(2)}) collective-permute-start(bf16[96,384]{1,0:T(8,128)(2,1)S(1)} %copy-done.15), channel_id=1, source_target_pairs={{4,0},{68,64},{0,128},{64,192},{132,4},{196,68},{128,132},{192,196... | collective-permute-start | bytes 221192 | tf_op jit(solution)/shard_map/ppermute | solution.py:233
  18.2 2.6 %collective-permute-start.4 = (bf16[96,384]{1,0:T(8,128)(2,1)S(1)}, bf16[96,384]{1,0:T(8,128)(2,1)S(1)}, u32[]{:S(2)}, u32[]{:S(2)}) collective-permute-start(bf16[96,384]{1,0:T(8,128)(2,1)S(1)} %copy-done.15), channel_id=1, source_target_pairs={{68,0},{0,64},{64,128},{4,192},{196,4},{128,68},{192,132},{132,196... | collective-permute-start | bytes 221192 | tf_op jit(solution)/shard_map/ppermute | solution.py:233
  20.8 3.2 %collective-permute-done.2 = bf16[96,384]{1,0:T(8,128)(2,1)S(1)} collective-permute-done((bf16[96,384]{1,0:T(8,128)(2,1)S(1)}, bf16[96,384]{1,0:T(8,128)(2,1)S(1)}, u32[]{:S(2)}, u32[]{:S(2)}) %collective-permute-start.2) | collective-permute-done | bytes 73760 | tf_op jit(solution)/shard_map/ppermute | solution.py:233
  24.0 0.8 collective-permute-done.4
  24.9 3.3 %collective-permute-start.6 = (bf16[4,96,384]{2,1,0:T(8,128)(2,1)S(1)}, bf16[4,96,384]{2,1,0:T(8,128)(2,1)S(1)}, u32[]{:S(2)}, u32[]{:S(2)}) collective-permute-start(bf16[4,96,384]{2,1,0:T(8,128)(2,1)S(1)} %pad_maximum_fusion.3.refs_5_), channel_id=1, source_target_pairs={{32,0},{48,16},{0,32},{16,48},{33,1},{49,17},{1,33},{17,49},{34,2}... | collective-permute-start | bytes 884744 | tf_op jit(solution)/shard_map/ppermute | solution.py:208
  28.1 0.7 collective-permute-start.7
  28.8 2.6 %collective-permute-start.5 = (bf16[4,96,384]{2,1,0:T(8,128)(2,1)S(1)}, bf16[4,96,384]{2,1,0:T(8,128)(2,1)S(1)}, u32[]{:S(2)}, u32[]{:S(2)}) collective-permute-start(bf16[4,96,384]{2,1,0:T(8,128)(2,1)S(1)} %pad_maximum_fusion.3.refs_5_), channel_id=1, source_target_pairs={{16,0},{32,16},{48,32},{0,48},{17,1},{33,17},{49,33},{1,49},{18,2}... | collective-permute-start | bytes 884744 | tf_op jit(solution)/shard_map/ppermute | solution.py:208
  31.4 0.8 pad_maximum_fusion.1
  32.2 6.2 %collective-permute-start = (bf16[17,32,384]{2,1,0:T(8,128)(2,1)}, bf16[17,32,384]{2,1,0:T(8,128)(2,1)S(1)}, u32[]{:S(2)}, u32[]{:S(2)}) collective-permute-start(bf16[17,32,384]{2,1,0:T(8,128)(2,1)} %pad_maximum_fusion.1), channel_id=1, source_target_pairs={{4,0},{0,4},{5,1},{1,5},{6,2},{2,6},{7,3},{3,7},{12,8},{8,12},{13,... | collective-permute-start | bytes 1253384 | tf_op jit(solution)/shard_map/ppermute | solution.py:208
  38.5 0.5 collective-permute-start.10
  39.0 1.9 %collective-permute-done.7.refs_8_ = bf16[4,96,384]{2,1,0:T(8,128)(2,1)S(1)} collective-permute-done((bf16[4,96,384]{2,1,0:T(8,128)(2,1)S(1)}, bf16[4,96,384]{2,1,0:T(8,128)(2,1)S(1)}, u32[]{:S(2)}, u32[]{:S(2)}) %collective-permute-start.7) | collective-permute-done | bytes 294944 | tf_op jit(solution)/shard_map/ppermute | solution.py:208
  40.9 0.1 collective-permute-start.11
  40.9 0.3 collective-permute-done.5.refs_6_
  41.2 0.1 collective-permute-start.9
  41.5 14.7 %collective-permute-done.refs_3_ = bf16[17,32,384]{2,1,0:T(8,128)(2,1)S(1)} collective-permute-done((bf16[17,32,384]{2,1,0:T(8,128)(2,1)}, bf16[17,32,384]{2,1,0:T(8,128)(2,1)S(1)}, u32[]{:S(2)}, u32[]{:S(2)}) %collective-permute-start) | collective-permute-done | bytes 417824 | tf_op jit(solution)/shard_map/ppermute | solution.py:208
  56.2 1.4 copy-done
  57.6 0.9 copy-done.11
  58.5 9.8 %softmax_statistics_0.1 = (f32[8,1920]{1,0:T(8,128)S(1)}, bf16[768,768]{1,0:T(8,128)(2,1)S(1)}, bf16[8,768,128]{2,1,0:T(8,128)(2,1)S(1)}, bf16[8,768,128]{2,1,0:T(8,128)(2,1)S(1)}) custom-call(s32[5]{0:T(128)S(1)} %stack.47.refs_0_, bf16[4,16,32,384]{3,2,1,0:T(8,128)(2,1)S(1)} %bitcast.75, bf16[8,32,384]{2,1,0:T(8,128)(2,1)S(1)} %copy-done.2, ...), custom_call_target="tpu_custom_call" | custom-call | tf_op jit(solution)/shard_map/softmax_statistics_0/pallas_call | solution.py:196
  68.3 2.8 %collective-permute-start.15 = (f32[8,1920]{1,0:T(8,128)S(1)}, f32[8,1920]{1,0:T(8,128)S(1)}, u32[]{:S(2)}, u32[]{:S(2)}) collective-permute-start(f32[8,1920]{1,0:T(8,128)S(1)} %get-tuple-element.35.refs_7_.refs_11_), channel_id=1, source_target_pairs={{1,0},{2,1},{3,2},{0,3},{5,4},{6,5},{7,6},{4,7},{9,8},{10,9},{11,1... | collective-permute-start | bytes 184328 | tf_op jit(solution)/shard_map/ppermute | solution.py:208
  71.1 0.8 collective-permute-start.16
  71.9 0.9 collective-permute-start.17
  72.8 0.2 collective-permute-done.15.refs_8_.refs_12_
  73.0 3.9 %collective-permute-done.16.refs_9_.refs_13_ = f32[8,1920]{1,0:T(8,128)S(1)} collective-permute-done((f32[8,1920]{1,0:T(8,128)S(1)}, f32[8,1920]{1,0:T(8,128)S(1)}, u32[]{:S(2)}, u32[]{:S(2)}) %collective-permute-start.16) | collective-permute-done | bytes 61472 | tf_op jit(solution)/shard_map/ppermute | solution.py:208
  76.9 0.6 collective-permute-done.17.refs_10_.refs_14_
  77.5 15.5 %attention_gradients_0.1 = (f32[8,32,768]{2,1,0:T(8,128)S(1)}, f32[8,32,768]{2,1,0:T(8,128)S(1)}, f32[2,8,32,384]{3,2,1,0:T(8,128)S(1)}, f32[4,2,96,384]{3,2,1,0:T(8,128)S(1)}, bf16[4,2,96,384]{3,2,1,0:T(8,128)(2,1)S(1)}) custom-call(s32[5]{0:T(128)S(1)} %stack.47.refs_0_, bf16[4,16,32,384]{3,2,1,0:T(8,128)(2,1)S(1)} %bitcast.76, ...), custom_call_target="tpu_custom_call" | custom-call | tf_op jit(solution)/shard_map/attention_gradients_0/pallas_call | solution.py:196
  93.1 0.1 collective-permute-start.18
  93.2 6.3 %softmax_statistics_1.1 = (f32[8,1536]{1,0:T(8,128)S(1)}, bf16[768,768]{1,0:T(8,128)(2,1)S(1)}) custom-call(s32[5]{0:T(128)S(1)} %stack.47.refs_0_, bf16[4,16,32,384]{3,2,1,0:T(8,128)(2,1)S(1)} %bitcast.77, bf16[8,32,384]{2,1,0:T(8,128)(2,1)S(1)} %copy-done.2, bf16[17,32,384]{2,1,0:T(8,128)(2,1)S(1)} %collective-permute-done.refs_3_, ...), custom_call_target="tpu_custom_call" | custom-call | tf_op jit(solution)/shard_map/softmax_statistics_1/pallas_call | solution.py:196
  99.4 0.6 collective-permute-start.12
  100.1 1.0 collective-permute-start.13
  101.1 1.2 collective-permute-start.14
  102.3 1.3 fusion.21
  103.6 0.8 slice_bitcast_fusion.5
  104.3 1.5 collective-permute-done.13.refs_9_
  105.8 0.8 collective-permute-done.14.refs_10_
  106.6 16.4 %attention_gradients_1.1 = (f32[8,32,384]{2,1,0:T(8,128)S(1)}, f32[8,32,384]{2,1,0:T(8,128)S(1)}, bf16[16,32,384]{2,1,0:T(8,128)(2,1)S(1)}, f32[2,8,32,384]{3,2,...) custom-call(s32[5]{0:T(128)S(1)} %stack.47.refs_0_, ...), custom_call_target="tpu_custom_call" | custom-call | tf_op jit(solution)/shard_map/attention_gradients_1/pallas_call | solution.py:196
  122.9 0.7 copy-done.7
  123.7 0.7 copy-done.9
  124.4 0.8 copy-done.12
  125.2 1.8 %collective-permute-start.25 = (bf16[2,96,384]{2,1,0:T(8,128)(2,1)}, bf16[2,96,384]{2,1,0:T(8,128)(2,1)S(1)}, u32[]{:S(2)}, u32[]{:S(2)}) collective-permute-start(bf16[2,96,384]{2,1,0:T(8,128)(2,1)} %get-tuple-element.53), channel_id=1, source_target_pairs={{0,32},{16,48},{32,0},{48,16},{1,33},{17,49},{33,1},{49,17},{2,34}... | collective-permute-start | bytes 442376 | tf_op jit(solution)/shard_map/ppermute | solution.py:212
  127.0 1.5 collective-permute-start.26
  128.4 0.1 pad_maximum_fusion
  128.6 0.2 fusion.20
  128.8 1.2 collective-permute-start.27
  130.0 2.2 %collective-permute-start.28 = (bf16[2,96,384]{2,1,0:T(8,128)(2,1)S(1)}, bf16[2,96,384]{2,1,0:T(8,128)(2,1)S(1)}, u32[]{:S(2)}, u32[]{:S(2)}) collective-permute-start(bf16[2,96,384]{2,1,0:T(8,128)(2,1)S(1)} %get-tuple-element.56), channel_id=1, source_target_pairs={{0,32},{16,48},{32,0},{48,16},{1,33},{17,49},{33,1},{49,17},{2,34}... | collective-permute-start | bytes 442376 | tf_op jit(solution)/shard_map/ppermute | solution.py:212
  132.1 4.3 %collective-permute-done.24 = bf16[2,96,384]{2,1,0:T(8,128)(2,1)S(1)} collective-permute-done((bf16[2,96,384]{2,1,0:T(8,128)(2,1)}, bf16[2,96,384]{2,1,0:T(8,128)(2,1)S(1)}, u32[]{:S(2)}, u32[]{:S(2)}) %collective-permute-start.24) | collective-permute-done | bytes 147488 | tf_op jit(solution)/shard_map/ppermute | solution.py:212
  136.4 0.9 collective-permute-done.26
  137.4 1.0 fusion.18
  138.4 3.8 %collective-permute-start.23 = (bf16[16,32,384]{2,1,0:T(8,128)(2,1)S(1)}, bf16[16,32,384]{2,1,0:T(8,128)(2,1)S(1)}, u32[]{:S(2)}, u32[]{:S(2)}) collective-permute-start(bf16[16,32,384]{2,1,0:T(8,128)(2,1)S(1)} %copy-done.13), channel_id=1, source_target_pairs={{4,0},{0,4},{5,1},{1,5},{6,2},{2,6},{7,3},{3,7},{12,8},{8,12},{13,... | collective-permute-start | bytes 1179656 | tf_op jit(solution)/shard_map/ppermute | solution.py:208
  142.3 0.6 collective-permute-start.20
  143.0 2.6 %collective-permute-start.21 = (bf16[8,32,384]{2,1,0:T(8,128)(2,1)S(1)}, bf16[8,32,384]{2,1,0:T(8,128)(2,1)S(1)}, u32[]{:S(2)}, u32[]{:S(2)}) collective-permute-start(bf16[8,32,384]{2,1,0:T(8,128)(2,1)S(1)} %get-tuple-element.64), channel_id=1, source_target_pairs={{0,2},{1,3},{2,0},{3,1},{4,6},{5,7},{6,4},{7,5},{8,10},{9,11},{10,... | collective-permute-start | bytes 589832 | tf_op jit(solution)/shard_map/ppermute | solution.py:212
  145.6 0.6 collective-permute-start.22
  146.2 0.1 fusion.19
  146.4 1.9 %collective-permute-start.30 = (bf16[96,384]{1,0:T(8,128)(2,1)S(1)}, bf16[96,384]{1,0:T(8,128)(2,1)S(1)}, u32[]{:S(2)}, u32[]{:S(2)}) collective-permute-start(bf16[96,384]{1,0:T(8,128)(2,1)S(1)} %get-tuple-element.73), channel_id=1, source_target_pairs={{0,0},{64,64},{128,4},{192,68},{4,128},{68,192},{132,132},{196,196... | collective-permute-start | bytes 221192 | tf_op jit(solution)/shard_map/ppermute | solution.py:313
  148.4 3.1 %collective-permute-done.20 = bf16[8,32,384]{2,1,0:T(8,128)(2,1)S(1)} collective-permute-done((bf16[8,32,384]{2,1,0:T(8,128)(2,1)S(1)}, bf16[8,32,384]{2,1,0:T(8,128)(2,1)S(1)}, u32[]{:S(2)}, u32[]{:S(2)}) %collective-permute-start.20) | collective-permute-done | bytes 196640 | tf_op jit(solution)/shard_map/ppermute | solution.py:212
  151.4 1.4 collective-permute-start.31
  152.8 0.3 collective-permute-done.21
  153.1 0.6 collective-permute-done.22
  153.7 1.8 %collective-permute-start.33 = (bf16[96,384]{1,0:T(8,128)(2,1)S(1)}, bf16[96,384]{1,0:T(8,128)(2,1)S(1)}, u32[]{:S(2)}, u32[]{:S(2)}) collective-permute-start(bf16[96,384]{1,0:T(8,128)(2,1)S(1)} %get-tuple-element.74), channel_id=1, source_target_pairs={{0,68},{64,0},{128,64},{192,4},{4,196},{68,128},{132,192},{196,132... | collective-permute-start | bytes 221192 | tf_op jit(solution)/shard_map/ppermute | solution.py:313
  155.5 0.8 fusion.6
  156.3 7.8 %collective-permute-done.30 = bf16[96,384]{1,0:T(8,128)(2,1)S(1)} collective-permute-done((bf16[96,384]{1,0:T(8,128)(2,1)S(1)}, bf16[96,384]{1,0:T(8,128)(2,1)S(1)}, u32[]{:S(2)}, u32[]{:S(2)}) %collective-permute-start.30) | collective-permute-done | bytes 73760 | tf_op jit(solution)/shard_map/ppermute | solution.py:313
  164.1 0.7 convert_add_fusion.2
  164.9 0.8 fusion
  (65 shorter events, 0.7 us)
Async XLA Ops:
  7.2 49.0 %copy-start.3 = (bf16[8,32,384]{2,1,0:T(8,128)(2,1)S(1)}, bf16[8,32,384]{2,1,0:T(8,128)(2,1)}, u32[]{:S(2)}) copy-start(bf16[8,32,384]{2,1,0:T(8,128)(2,1)} %refs_14_.1) | copy-start | bytes 589828
  7.2 2.1 %copy-start.15 = (bf16[96,384]{1,0:T(8,128)(2,1)S(1)}, bf16[96,384]{1,0:T(8,128)(2,1)}, u32[]{:S(2)}) copy-start(bf16[96,384]{1,0:T(8,128)(2,1)} %param.12) | copy-start | bytes 221188
  7.2 24.2 %copy-start.14 = (s32[384]{0:T(512)S(1)}, s32[384]{0:T(512)}, u32[]{:S(2)}) copy-start(s32[384]{0:T(512)} %param.13) | copy-start | bytes 4612
  7.2 24.2 %copy-start.2 = (bf16[8,32,384]{2,1,0:T(8,128)(2,1)S(1)}, bf16[8,32,384]{2,1,0:T(8,128)(2,1)}, u32[]{:S(2)}) copy-start(bf16[8,32,384]{2,1,0:T(8,128)(2,1)} %refs_2_.7) | copy-start | bytes 589828
  7.2 24.2 %copy-start.4 = (bf16[8,32,384]{2,1,0:T(8,128)(2,1)S(1)}, bf16[8,32,384]{2,1,0:T(8,128)(2,1)}, u32[]{:S(2)}) copy-start(bf16[8,32,384]{2,1,0:T(8,128)(2,1)} %refs_13_.1) | copy-start | bytes 589828
  7.2 48.9 %all-gather.3.cloned.1.call-start = ((), (), s32[]{:S(2)}) async-start(), calls=%async_computation | async-start | bytes 1966080 | tf_op jit(solution)/shard_map/all_gather | solution.py:232
  9.3 11.5 %collective-permute-start.1 = (bf16[96,384]{1,0:T(8,128)(2,1)S(1)}, bf16[96,384]{1,0:T(8,128)(2,1)S(1)}, u32[]{:S(2)}, u32[]{:S(2)}) collective-permute-start(bf16[96,384]{1,0:T(8,128)(2,1)S(1)} %copy-done.15), channel_id=1, source_target_pairs={{0,0},{64,64},{4,128},{68,192},{128,4},{192,68},{132,132},{196,196... | collective-permute-start | bytes 221192 | tf_op jit(solution)/shard_map/ppermute | solution.py:233
  15.7 8.3 %collective-permute-start.2 = (bf16[96,384]{1,0:T(8,128)(2,1)S(1)}, bf16[96,384]{1,0:T(8,128)(2,1)S(1)}, u32[]{:S(2)}, u32[]{:S(2)}) collective-permute-start(bf16[96,384]{1,0:T(8,128)(2,1)S(1)} %copy-done.15), channel_id=1, source_target_pairs={{64,0},{4,64},{68,128},{0,192},{192,4},{132,68},{196,132},{128,196... | collective-permute-start | bytes 221192 | tf_op jit(solution)/shard_map/ppermute | solution.py:233
  15.8 8.2 %collective-permute-start.3 = (bf16[96,384]{1,0:T(8,128)(2,1)S(1)}, bf16[96,384]{1,0:T(8,128)(2,1)S(1)}, u32[]{:S(2)}, u32[]{:S(2)}) collective-permute-start(bf16[96,384]{1,0:T(8,128)(2,1)S(1)} %copy-done.15), channel_id=1, source_target_pairs={{4,0},{68,64},{0,128},{64,192},{132,4},{196,68},{128,132},{192,196... | collective-permute-start | bytes 221192 | tf_op jit(solution)/shard_map/ppermute | solution.py:233
  18.2 6.6 %collective-permute-start.4 = (bf16[96,384]{1,0:T(8,128)(2,1)S(1)}, bf16[96,384]{1,0:T(8,128)(2,1)S(1)}, u32[]{:S(2)}, u32[]{:S(2)}) collective-permute-start(bf16[96,384]{1,0:T(8,128)(2,1)S(1)} %copy-done.15), channel_id=1, source_target_pairs={{68,0},{0,64},{64,128},{4,192},{196,4},{128,68},{192,132},{132,196... | collective-permute-start | bytes 221192 | tf_op jit(solution)/shard_map/ppermute | solution.py:233
  24.9 13.6 %collective-permute-start.6 = (bf16[4,96,384]{2,1,0:T(8,128)(2,1)S(1)}, bf16[4,96,384]{2,1,0:T(8,128)(2,1)S(1)}, u32[]{:S(2)}, u32[]{:S(2)}) collective-permute-start(bf16[4,96,384]{2,1,0:T(8,128)(2,1)S(1)} %pad_maximum_fusion.3.refs_5_), channel_id=1, source_target_pairs={{32,0},{48,16},{0,32},{16,48},{33,1},{49,17},{1,33},{17,49},{34,2}... | collective-permute-start | bytes 884744 | tf_op jit(solution)/shard_map/ppermute | solution.py:208
  28.1 12.7 %collective-permute-start.7 = (bf16[4,96,384]{2,1,0:T(8,128)(2,1)S(1)}, bf16[4,96,384]{2,1,0:T(8,128)(2,1)S(1)}, u32[]{:S(2)}, u32[]{:S(2)}) collective-permute-start(bf16[4,96,384]{2,1,0:T(8,128)(2,1)S(1)} %pad_maximum_fusion.3.refs_5_), channel_id=1, source_target_pairs={{48,0},{0,16},{16,32},{32,48},{49,1},{1,17},{17,33},{33,49},{50,2}... | collective-permute-start | bytes 884744 | tf_op jit(solution)/shard_map/ppermute | solution.py:208
  28.8 12.4 %collective-permute-start.5 = (bf16[4,96,384]{2,1,0:T(8,128)(2,1)S(1)}, bf16[4,96,384]{2,1,0:T(8,128)(2,1)S(1)}, u32[]{:S(2)}, u32[]{:S(2)}) collective-permute-start(bf16[4,96,384]{2,1,0:T(8,128)(2,1)S(1)} %pad_maximum_fusion.3.refs_5_), channel_id=1, source_target_pairs={{16,0},{32,16},{48,32},{0,48},{17,1},{33,17},{49,33},{1,49},{18,2}... | collective-permute-start | bytes 884744 | tf_op jit(solution)/shard_map/ppermute | solution.py:208
  32.2 23.9 %collective-permute-start = (bf16[17,32,384]{2,1,0:T(8,128)(2,1)}, bf16[17,32,384]{2,1,0:T(8,128)(2,1)S(1)}, u32[]{:S(2)}, u32[]{:S(2)}) collective-permute-start(bf16[17,32,384]{2,1,0:T(8,128)(2,1)} %pad_maximum_fusion.1), channel_id=1, source_target_pairs={{4,0},{0,4},{5,1},{1,5},{6,2},{2,6},{7,3},{3,7},{12,8},{8,12},{13,... | collective-permute-start | bytes 1253384 | tf_op jit(solution)/shard_map/ppermute | solution.py:208
  38.4 3.0 %collective-permute-start.8 = (bf16[4,96,384]{2,1,0:T(8,128)(2,1)S(1)}, bf16[4,96,384]{2,1,0:T(8,128)(2,1)S(1)}, u32[]{:S(2)}, u32[]{:S(2)}) collective-permute-start(bf16[4,96,384]{2,1,0:T(8,128)(2,1)S(1)} %pad_maximum_fusion.3.refs_5_), channel_id=1, source_target_pairs={{8,0},{0,8},{9,1},{1,9},{10,2},{2,10},{11,3},{3,11},{12,4},{4,12},... | collective-permute-start | bytes 884744 | tf_op jit(solution)/shard_map/ppermute | solution.py:208
  38.5 17.7 %collective-permute-start.10 = (bf16[4,96,384]{2,1,0:T(8,128)(2,1)S(1)}, bf16[4,96,384]{2,1,0:T(8,128)(2,1)S(1)}, u32[]{:S(2)}, u32[]{:S(2)}) collective-permute-start(bf16[4,96,384]{2,1,0:T(8,128)(2,1)S(1)} %collective-permute-done.6.refs_7_), channel_id=1, source_target_pairs={{8,0},{0,8},{9,1},{1,9},{10,2},{2,10},{11,3},{3,11},{12,4},{4,12},... | collective-permute-start | bytes 884744 | tf_op jit(solution)/shard_map/ppermute | solution.py:208
  40.9 15.3 %collective-permute-start.11 = (bf16[4,96,384]{2,1,0:T(8,128)(2,1)S(1)}, bf16[4,96,384]{2,1,0:T(8,128)(2,1)S(1)}, u32[]{:S(2)}, u32[]{:S(2)}) collective-permute-start(bf16[4,96,384]{2,1,0:T(8,128)(2,1)S(1)} %collective-permute-done.7.refs_8_), channel_id=1, source_target_pairs={{8,0},{0,8},{9,1},{1,9},{10,2},{2,10},{11,3},{3,11},{12,4},{4,12},... | collective-permute-start | bytes 884744 | tf_op jit(solution)/shard_map/ppermute | solution.py:208
  41.2 14.9 %collective-permute-start.9 = (bf16[4,96,384]{2,1,0:T(8,128)(2,1)S(1)}, bf16[4,96,384]{2,1,0:T(8,128)(2,1)S(1)}, u32[]{:S(2)}, u32[]{:S(2)}) collective-permute-start(bf16[4,96,384]{2,1,0:T(8,128)(2,1)S(1)} %collective-permute-done.5.refs_6_), channel_id=1, source_target_pairs={{8,0},{0,8},{9,1},{1,9},{10,2},{2,10},{11,3},{3,11},{12,4},{4,12},... | collective-permute-start | bytes 884744 | tf_op jit(solution)/shard_map/ppermute | solution.py:208
  56.2 1.4 copy-start
  57.6 0.9 copy-start.11
  58.5 19.0 %copy-start.1 = (bf16[64,32,384]{2,1,0:T(8,128)(2,1)S(1)}, bf16[64,32,384]{2,1,0:T(8,128)(2,1)}, u32[]{:S(2)}) copy-start(bf16[64,32,384]{2,1,0:T(8,128)(2,1)} %all-gather.3.cloned.1.call-done) | copy-start | bytes 4718596
  68.3 4.7 %collective-permute-start.15 = (f32[8,1920]{1,0:T(8,128)S(1)}, f32[8,1920]{1,0:T(8,128)S(1)}, u32[]{:S(2)}, u32[]{:S(2)}) collective-permute-start(f32[8,1920]{1,0:T(8,128)S(1)} %get-tuple-element.35.refs_7_.refs_11_), channel_id=1, source_target_pairs={{1,0},{2,1},{3,2},{0,3},{5,4},{6,5},{7,6},{4,7},{9,8},{10,9},{11,1... | collective-permute-start | bytes 184328 | tf_op jit(solution)/shard_map/ppermute | solution.py:208
  71.1 5.7 %collective-permute-start.16 = (f32[8,1920]{1,0:T(8,128)S(1)}, f32[8,1920]{1,0:T(8,128)S(1)}, u32[]{:S(2)}, u32[]{:S(2)}) collective-permute-start(f32[8,1920]{1,0:T(8,128)S(1)} %get-tuple-element.35.refs_7_.refs_11_), channel_id=1, source_target_pairs={{2,0},{3,1},{0,2},{1,3},{6,4},{7,5},{4,6},{5,7},{10,8},{11,9},{8,1... | collective-permute-start | bytes 184328 | tf_op jit(solution)/shard_map/ppermute | solution.py:208
  71.9 5.6 %collective-permute-start.17 = (f32[8,1920]{1,0:T(8,128)S(1)}, f32[8,1920]{1,0:T(8,128)S(1)}, u32[]{:S(2)}, u32[]{:S(2)}) collective-permute-start(f32[8,1920]{1,0:T(8,128)S(1)} %get-tuple-element.35.refs_7_.refs_11_), channel_id=1, source_target_pairs={{3,0},{0,1},{1,2},{2,3},{7,4},{4,5},{5,6},{6,7},{11,8},{8,9},{9,10... | collective-permute-start | bytes 184328 | tf_op jit(solution)/shard_map/ppermute | solution.py:208
  93.0 6.4 %copy-start.5 = (f32[2,8,32,384]{3,2,1,0:T(8,128)}, f32[2,8,32,384]{3,2,1,0:T(8,128)S(1)}, u32[]{:S(2)}) copy-start(f32[2,8,32,384]{3,2,1,0:T(8,128)S(1)} %get-tuple-element.46) | copy-start | bytes 2359300
  93.1 9.2 %collective-permute-start.18 = (bf16[4,2,96,384]{3,2,1,0:T(8,128)(2,1)S(1)}, bf16[4,2,96,384]{3,2,1,0:T(8,128)(2,1)S(1)}, u32[]{:S(2)}, u32[]{:S(2)}) collective-permute-start(bf16[4,2,96,384]{3,2,1,0:T(8,128)(2,1)S(1)} %get-tuple-element.38), channel_id=1, source_target_pairs={{8,0},{0,8},{9,1},{1,9},{10,2},{2,10},{11,3},{3,11},{12,4},{4,12},... | collective-permute-start | bytes 1769480 | tf_op jit(solution)/shard_map/ppermute | solution.py:208
  99.4 4.9 %collective-permute-start.12 = (f32[8,1536]{1,0:T(8,128)S(1)}, f32[8,1536]{1,0:T(8,128)S(1)}, u32[]{:S(2)}, u32[]{:S(2)}) collective-permute-start(f32[8,1536]{1,0:T(8,128)S(1)} %get-tuple-element.34.refs_7_), channel_id=1, source_target_pairs={{1,0},{2,1},{3,2},{0,3},{5,4},{6,5},{7,6},{4,7},{9,8},{10,9},{11,1... | collective-permute-start | bytes 147464 | tf_op jit(solution)/shard_map/ppermute | solution.py:208
  100.1 5.7 %collective-permute-start.13 = (f32[8,1536]{1,0:T(8,128)S(1)}, f32[8,1536]{1,0:T(8,128)S(1)}, u32[]{:S(2)}, u32[]{:S(2)}) collective-permute-start(f32[8,1536]{1,0:T(8,128)S(1)} %get-tuple-element.34.refs_7_), channel_id=1, source_target_pairs={{2,0},{3,1},{0,2},{1,3},{6,4},{7,5},{4,6},{5,7},{10,8},{11,9},{8,1... | collective-permute-start | bytes 147464 | tf_op jit(solution)/shard_map/ppermute | solution.py:208
  101.1 5.5 %collective-permute-start.14 = (f32[8,1536]{1,0:T(8,128)S(1)}, f32[8,1536]{1,0:T(8,128)S(1)}, u32[]{:S(2)}, u32[]{:S(2)}) collective-permute-start(f32[8,1536]{1,0:T(8,128)S(1)} %get-tuple-element.34.refs_7_), channel_id=1, source_target_pairs={{3,0},{0,1},{1,2},{2,3},{7,4},{4,5},{5,6},{6,7},{11,8},{8,9},{9,10... | collective-permute-start | bytes 147464 | tf_op jit(solution)/shard_map/ppermute | solution.py:208
  106.6 21.9 %copy-start.6 = (f32[2,8,32,384]{3,2,1,0:T(8,128)S(1)}, f32[2,8,32,384]{3,2,1,0:T(8,128)}, u32[]{:S(2)}) copy-start(f32[2,8,32,384]{3,2,1,0:T(8,128)} %copy-done.5) | copy-start | bytes 2359300
  122.9 0.7 copy-start.7
  123.7 0.7 copy-start.9
  124.4 0.8 copy-start.12
  125.2 3.4 %collective-permute-start.19 = (bf16[4,2,96,384]{3,2,1,0:T(8,128)(2,1)}, bf16[4,2,96,384]{3,2,1,0:T(8,128)(2,1)S(1)}, u32[]{:S(2)}, u32[]{:S(2)}) collective-permute-start(bf16[4,2,96,384]{3,2,1,0:T(8,128)(2,1)} %get-tuple-element.44), channel_id=1, source_target_pairs={{8,0},{0,8},{9,1},{1,9},{10,2},{2,10},{11,3},{3,11},{12,4},{4,12},... | collective-permute-start | bytes 1769480 | tf_op jit(solution)/shard_map/ppermute | solution.py:208
  125.2 11.2 %collective-permute-start.24 = (bf16[2,96,384]{2,1,0:T(8,128)(2,1)}, bf16[2,96,384]{2,1,0:T(8,128)(2,1)S(1)}, u32[]{:S(2)}, u32[]{:S(2)}) collective-permute-start(bf16[2,96,384]{2,1,0:T(8,128)(2,1)} %get-tuple-element.52), channel_id=1, source_target_pairs={{0,16},{16,32},{32,48},{48,0},{1,17},{17,33},{33,49},{49,1},{2,18}... | collective-permute-start | bytes 442376 | tf_op jit(solution)/shard_map/ppermute | solution.py:212
  125.2 11.2 %collective-permute-start.25 = (bf16[2,96,384]{2,1,0:T(8,128)(2,1)}, bf16[2,96,384]{2,1,0:T(8,128)(2,1)S(1)}, u32[]{:S(2)}, u32[]{:S(2)}) collective-permute-start(bf16[2,96,384]{2,1,0:T(8,128)(2,1)} %get-tuple-element.53), channel_id=1, source_target_pairs={{0,32},{16,48},{32,0},{48,16},{1,33},{17,49},{33,1},{49,17},{2,34}... | collective-permute-start | bytes 442376 | tf_op jit(solution)/shard_map/ppermute | solution.py:212
  127.0 10.4 %collective-permute-start.26 = (bf16[2,96,384]{2,1,0:T(8,128)(2,1)S(1)}, bf16[2,96,384]{2,1,0:T(8,128)(2,1)S(1)}, u32[]{:S(2)}, u32[]{:S(2)}) collective-permute-start(bf16[2,96,384]{2,1,0:T(8,128)(2,1)S(1)} %get-tuple-element.54), channel_id=1, source_target_pairs={{0,48},{16,0},{32,16},{48,32},{1,49},{17,1},{33,17},{49,33},{2,50}... | collective-permute-start | bytes 442376 | tf_op jit(solution)/shard_map/ppermute | solution.py:212
  128.7 9.7 %copy-start.13 = (bf16[16,32,384]{2,1,0:T(8,128)(2,1)S(1)}, bf16[16,32,384]{2,1,0:T(8,128)(2,1)}, u32[]{:S(2)}) copy-start(bf16[16,32,384]{2,1,0:T(8,128)(2,1)} %copy-done.12) | copy-start | bytes 1179652
  128.8 14.2 %collective-permute-start.27 = (bf16[2,96,384]{2,1,0:T(8,128)(2,1)S(1)}, bf16[2,96,384]{2,1,0:T(8,128)(2,1)S(1)}, u32[]{:S(2)}, u32[]{:S(2)}) collective-permute-start(bf16[2,96,384]{2,1,0:T(8,128)(2,1)S(1)} %get-tuple-element.55), channel_id=1, source_target_pairs={{0,16},{16,32},{32,48},{48,0},{1,17},{17,33},{33,49},{49,1},{2,18}... | collective-permute-start | bytes 442376 | tf_op jit(solution)/shard_map/ppermute | solution.py:212
  130.0 15.6 %collective-permute-start.28 = (bf16[2,96,384]{2,1,0:T(8,128)(2,1)S(1)}, bf16[2,96,384]{2,1,0:T(8,128)(2,1)S(1)}, u32[]{:S(2)}, u32[]{:S(2)}) collective-permute-start(bf16[2,96,384]{2,1,0:T(8,128)(2,1)S(1)} %get-tuple-element.56), channel_id=1, source_target_pairs={{0,32},{16,48},{32,0},{48,16},{1,33},{17,49},{33,1},{49,17},{2,34}... | collective-permute-start | bytes 442376 | tf_op jit(solution)/shard_map/ppermute | solution.py:212
  136.4 9.8 %collective-permute-start.29 = (bf16[2,96,384]{2,1,0:T(8,128)(2,1)S(1)}, bf16[2,96,384]{2,1,0:T(8,128)(2,1)S(1)}, u32[]{:S(2)}, u32[]{:S(2)}) collective-permute-start(bf16[2,96,384]{2,1,0:T(8,128)(2,1)S(1)} %get-tuple-element.57), channel_id=1, source_target_pairs={{0,48},{16,0},{32,16},{48,32},{1,49},{17,1},{33,17},{49,33},{2,50}... | collective-permute-start | bytes 442376 | tf_op jit(solution)/shard_map/ppermute | solution.py:212
  138.4 26.4 %collective-permute-start.23 = (bf16[16,32,384]{2,1,0:T(8,128)(2,1)S(1)}, bf16[16,32,384]{2,1,0:T(8,128)(2,1)S(1)}, u32[]{:S(2)}, u32[]{:S(2)}) collective-permute-start(bf16[16,32,384]{2,1,0:T(8,128)(2,1)S(1)} %copy-done.13), channel_id=1, source_target_pairs={{4,0},{0,4},{5,1},{1,5},{6,2},{2,6},{7,3},{3,7},{12,8},{8,12},{13,... | collective-permute-start | bytes 1179656 | tf_op jit(solution)/shard_map/ppermute | solution.py:208
  142.3 9.1 %collective-permute-start.20 = (bf16[8,32,384]{2,1,0:T(8,128)(2,1)S(1)}, bf16[8,32,384]{2,1,0:T(8,128)(2,1)S(1)}, u32[]{:S(2)}, u32[]{:S(2)}) collective-permute-start(bf16[8,32,384]{2,1,0:T(8,128)(2,1)S(1)} %get-tuple-element.62), channel_id=1, source_target_pairs={{0,1},{1,2},{2,3},{3,0},{4,5},{5,6},{6,7},{7,4},{8,9},{9,10},{10,1... | collective-permute-start | bytes 589832 | tf_op jit(solution)/shard_map/ppermute | solution.py:212
  143.0 10.1 %collective-permute-start.21 = (bf16[8,32,384]{2,1,0:T(8,128)(2,1)S(1)}, bf16[8,32,384]{2,1,0:T(8,128)(2,1)S(1)}, u32[]{:S(2)}, u32[]{:S(2)}) collective-permute-start(bf16[8,32,384]{2,1,0:T(8,128)(2,1)S(1)} %get-tuple-element.64), channel_id=1, source_target_pairs={{0,2},{1,3},{2,0},{3,1},{4,6},{5,7},{6,4},{7,5},{8,10},{9,11},{10,... | collective-permute-start | bytes 589832 | tf_op jit(solution)/shard_map/ppermute | solution.py:212
  145.6 8.0 %collective-permute-start.22 = (bf16[8,32,384]{2,1,0:T(8,128)(2,1)S(1)}, bf16[8,32,384]{2,1,0:T(8,128)(2,1)S(1)}, u32[]{:S(2)}, u32[]{:S(2)}) collective-permute-start(bf16[8,32,384]{2,1,0:T(8,128)(2,1)S(1)} %get-tuple-element.63), channel_id=1, source_target_pairs={{0,3},{1,0},{2,1},{3,2},{4,7},{5,4},{6,5},{7,6},{8,11},{9,8},{10,9... | collective-permute-start | bytes 589832 | tf_op jit(solution)/shard_map/ppermute | solution.py:212
  146.4 17.7 %collective-permute-start.30 = (bf16[96,384]{1,0:T(8,128)(2,1)S(1)}, bf16[96,384]{1,0:T(8,128)(2,1)S(1)}, u32[]{:S(2)}, u32[]{:S(2)}) collective-permute-start(bf16[96,384]{1,0:T(8,128)(2,1)S(1)} %get-tuple-element.73), channel_id=1, source_target_pairs={{0,0},{64,64},{128,4},{192,68},{4,128},{68,192},{132,132},{196,196... | collective-permute-start | bytes 221192 | tf_op jit(solution)/shard_map/ppermute | solution.py:313
  151.4 12.7 %collective-permute-start.31 = (bf16[96,384]{1,0:T(8,128)(2,1)S(1)}, bf16[96,384]{1,0:T(8,128)(2,1)S(1)}, u32[]{:S(2)}, u32[]{:S(2)}) collective-permute-start(bf16[96,384]{1,0:T(8,128)(2,1)S(1)} %get-tuple-element.76), channel_id=1, source_target_pairs={{0,64},{64,4},{128,68},{192,0},{4,192},{68,132},{132,196},{196,128... | collective-permute-start | bytes 221192 | tf_op jit(solution)/shard_map/ppermute | solution.py:313
  153.1 11.0 %collective-permute-start.32 = (bf16[96,384]{1,0:T(8,128)(2,1)S(1)}, bf16[96,384]{1,0:T(8,128)(2,1)S(1)}, u32[]{:S(2)}, u32[]{:S(2)}) collective-permute-start(bf16[96,384]{1,0:T(8,128)(2,1)S(1)} %get-tuple-element.75), channel_id=1, source_target_pairs={{0,4},{64,68},{128,0},{192,64},{4,132},{68,196},{132,128},{196,192... | collective-permute-start | bytes 221192 | tf_op jit(solution)/shard_map/ppermute | solution.py:313
  153.7 11.2 %copy-start.8 = (f32[8,32,384]{2,1,0:T(8,128)S(1)}, f32[8,32,384]{2,1,0:T(8,128)}, u32[]{:S(2)}) copy-start(f32[8,32,384]{2,1,0:T(8,128)} %copy-done.7) | copy-start | bytes 1179652
  153.7 11.2 %copy-start.10 = (f32[8,32,384]{2,1,0:T(8,128)S(1)}, f32[8,32,384]{2,1,0:T(8,128)}, u32[]{:S(2)}) copy-start(f32[8,32,384]{2,1,0:T(8,128)} %copy-done.9) | copy-start | bytes 1179652
  153.7 10.4 %collective-permute-start.33 = (bf16[96,384]{1,0:T(8,128)(2,1)S(1)}, bf16[96,384]{1,0:T(8,128)(2,1)S(1)}, u32[]{:S(2)}, u32[]{:S(2)}) collective-permute-start(bf16[96,384]{1,0:T(8,128)(2,1)S(1)} %get-tuple-element.74), channel_id=1, source_target_pairs={{0,68},{64,0},{128,64},{192,4},{4,196},{68,128},{132,192},{196,132... | collective-permute-start | bytes 221192 | tf_op jit(solution)/shard_map/ppermute | solution.py:313
Sparse Core Ops, SparseCore 0:
  9.9 31.2 all-gather.2

commit v3 on v1

--- a/solution.py
+++ b/solution.py
@@ -33,10 +33,10 @@
     return out
 
 
-def put_keys(refs, masks, place, scale):
-    rows, head, width = refs[0].shape
-    for slot, (ref, mask) in enumerate(zip(refs, masks)):
-        offset = jnp.where(mask[...] == 0.0, MASKED, 0.0)
+def put_keys(keys, masks, place, scale):
+    rows, head, width = keys[0].shape
+    for slot, (ref, mask) in enumerate(zip(keys, masks)):
+        offset = jnp.where(mask == 0.0, MASKED, 0.0)
         extra = rows_of((-1.0, -1.0, -1.0, offset), head, width)
 
         def prepare(i, carry):
@@ -48,13 +48,13 @@
         lax.fori_loop(0, rows, prepare, 0)
 
 
-def put_values(refs, place):
-    rows, head, width = refs[0].shape
+def put_values(values, away, place):
+    rows, head, width = values.shape
     extra = rows_of((-1.0, -1.0, -1.0), 128 - head, width)
-    for slot, ref in enumerate(refs):
+    for slot, (ref, base) in enumerate(((values, 0), (away, rows))):
 
         def prepare(i, carry):
-            whole = jnp.concatenate((ref[i].astype(F32), extra), axis=0)
+            whole = jnp.concatenate((ref[base + i].astype(F32), extra), axis=0)
             place[i, slot * width : (slot + 1) * width, :] = whole.T.astype(BF16)
             return carry
 
@@ -78,14 +78,14 @@
 
 def stats_kernel(scale, at, *refs):
     q = refs[0:4]
-    keys, masks = refs[4:6], refs[6:8]
-    grad, outs = refs[8:10]
-    pieces = (refs[10:14], refs[14:18])
-    stat, bias_t = refs[18:20]
-    bias_n, bias_f, key_t = refs[20:]
-    rows, head, width = q[0].shape
+    keys, away, mask, grad, outs = refs[4:9]
+    pieces = (refs[9:13], refs[13:17])
+    stat, bias_t = refs[17:19]
+    bias_n, bias_f, key_t = refs[19:]
+    rows, head, width = keys.shape
     total = X * width
-    put_keys(keys, masks, key_t, scale * LOG2E)
+    masks = (mask[...], away[2 * rows, 0:1, :].astype(F32))
+    put_keys((keys, away), masks, key_t, scale * LOG2E)
     for yd, zd, other, slot, first in bias_pieces(at):
         bias_n[slot, pl.ds(first, 96), :] = pieces[other][yd][zd]
     for slot in range(2):
@@ -126,18 +126,17 @@
 
 
 def main_kernel(scale, at, *refs):
-    q, g = refs[0:4], refs[4:8]
-    keys, values, masks = refs[8:10], refs[10:12], refs[12:14]
-    stats = refs[14:18]
-    bias_t = refs[18]
-    dq = refs[19:23]
-    dk_own, dv_own, dkv_away = refs[23:26]
-    bias_own, bias_away = refs[26:30], refs[30:34]
-    bias_f, acc, turned, key_t, value_t, lse, delta = refs[34:]
-    rows, head, width = q[0].shape
+    q, (own_grad, keys, values, away, mask) = refs[0:4], refs[4:9]
+    stats = refs[9:13]
+    bias_t = refs[13]
+    dq = refs[14:18]
+    dk_own, dv_own, dkv_away, bias_own, bias_away = refs[18:23]
+    bias_f, acc, turned, key_t, value_t, lse, delta = refs[23:]
+    rows, head, width = keys.shape
     total = X * width
-    put_keys(keys, masks, key_t, scale * LOG2E)
-    put_values(values, value_t)
+    masks = (mask[...], away[2 * rows, 0:1, :].astype(F32))
+    put_keys((keys, away), masks, key_t, scale * LOG2E)
+    put_values(values, away, value_t)
     for d in range(X):
         cols = slice(d * width, (d + 1) * width)
         there = [(d - e) % X for e in range(X)]
@@ -154,7 +153,8 @@
         dk_row, dv_row = None, None
         for d in range(X):
             cols = slice(d * width, (d + 1) * width)
-            query, gradient = q[d][i], g[d][i]
+            query = q[d][i]
+            gradient = own_grad[i] if d == 0 else q[d][rows + i]
             high, middle, low = split3(lse[pl.ds(i, 1), cols])
             extra = rows_of((high, middle, low, 1.0), 16, width).astype(BF16)
             query_all = jnp.concatenate((query, query, query, extra), axis=0)
@@ -168,8 +168,8 @@
             dk_part = dot(query, dscores_low, 1, 1)
             dv_row = dv_part if d == 0 else dv_row + dv_part
             dk_row = dk_part if d == 0 else dk_row + dk_part
-            dq_part = dot(keys[0][i], dscores_low[:width], 1, 0) + dot(
-                keys[1][i], dscores_low[width:], 1, 0
+            dq_part = dot(keys[i], dscores_low[:width], 1, 0) + dot(
+                away[i], dscores_low[width:], 1, 0
             )
             dq[d][i] = dq_part.astype(dq[d].dtype)
         dk_own[i], dv_own[i] = dk_row[:, :width], dv_row[:, :width]
@@ -184,21 +184,21 @@
             turned[slot, j : j + 128, :] = tile
     for yd, zd, other, slot, first in bias_pieces(at):
         place = bias_own if other == 0 else bias_away
-        place[yd][zd] = turned[slot, pl.ds(first, 96), :].astype(place[yd].dtype)
+        place[yd, zd] = turned[slot, pl.ds(first, 96), :].astype(place.dtype)
 
 
 VMEM = pl.BlockSpec(memory_space=pltpu.VMEM)
 SMEM = pl.BlockSpec(memory_space=pltpu.SMEM)
 
 
-def call(kernel, name, args, outs, scratch):
+def call(kernel, name, args, outs, scratch, mebibytes):
     return pl.pallas_call(
         kernel,
         in_specs=[SMEM] + [VMEM] * (len(args) - 1),
         out_specs=[VMEM] * len(outs),
         out_shape=[jax.ShapeDtypeStruct(shape, dtype) for shape, dtype in outs],
         scratch_shapes=[pltpu.VMEM(shape, dtype) for shape, dtype in scratch],
-        compiler_params=pltpu.CompilerParams(vmem_limit_bytes=52 * 2**20),
+        compiler_params=pltpu.CompilerParams(vmem_limit_bytes=mebibytes * 2**20),
         name=name,
     )(*args)
 
@@ -223,39 +223,46 @@
 def per_device(queries, keys, values, out_grad, outputs, bias, key_mask):
     rows, head, width = keys.shape
     scale = head ** (-0.5)
-    total = X * width
+    total, both = X * width, 2 * width
     z_axes = ("zlo", "zhi")
     at = jnp.stack([lax.axis_index(name) for name in FINE]).astype(jnp.int32)
     mask = key_mask.astype(F32)[None, :]
-
-    from_z = jnp.stack([lax.ppermute(bias, z_axes, z_pairs(d)) for d in range(ZLO)])
-    q = [queries] + [fetch(queries, "x", X, d) for d in range(1, X)]
-    away = [fetch(a, "zhi", ZHI, 1) for a in (keys, values, mask)]
+    after = lax.optimization_barrier
+
+    from_z = [lax.ppermute(bias, z_axes, z_pairs(d)) for d in range(ZLO)]
+    qg = jnp.concatenate([queries, out_grad], axis=0)
+    qg1 = fetch(qg, "x", X, 1)
+    from_z, qg1 = after((jnp.stack(from_z), qg1))
+    mask_rows = jnp.broadcast_to(key_mask.astype(BF16), (1, head, width))
+    kvm = jnp.concatenate([keys, values, mask_rows], axis=0)
+    kvm, qg, _ = after((kvm, qg, from_z))
     here = [from_z] + [fetch(from_z, "y", Y, d) for d in range(1, Y)]
+    away = fetch(kvm, "zhi", ZHI, 1)
+    qg3 = fetch(qg, "x", X, 3)
+    qg, here[1] = after((qg, here[1]))
+    qg2 = fetch(qg, "x", X, 2)
     there = [fetch(a, "core", CORE, 1) for a in here]
-    g = [out_grad] + [fetch(out_grad, "x", X, d) for d in range(1, X)]
-
-    both = 2 * width
+    q = [queries, qg1, qg2, qg3]
+
     stat, bias_t = call(
         lambda *refs: stats_kernel(scale, *refs),
         "softmax_statistics",
-        [at, *q, keys, away[0], mask, away[2], out_grad, outputs, *here, *there],
+        [at, *q, keys, away, mask, out_grad, outputs, *here, *there],
         [((rows, 2 * total + width), F32), ((both, total), BF16)],
         [((2, total, width), BF16), ((both, total), F32), ((rows, both, 128), BF16)],
+        24,
     )
     stats = [stat] + [fetch(stat, "x", X, d) for d in range(1, X)]
 
-    block, piece = (rows, head, width), (ZLO, 96, width)
+    block, pieces = (rows, head, width), (Y, ZLO, 96, width)
     results = call(
         lambda *refs: main_kernel(scale, *refs),
         "attention_gradients",
-        [at, *q, *g, keys, away[0], values, away[1], mask, away[2], *stats, bias_t],
+        [at, *q, out_grad, keys, values, away, mask, *stats, bias_t],
         [(block, F32)]
         + [(block, BF16)] * 3
         + [(block, F32)] * 2
-        + [((2 * rows, head, width), BF16)]
-        + [(piece, F32)] * 4
-        + [(piece, BF16)] * 4,
+        + [((2 * rows, head, width), BF16), (pieces, F32), (pieces, BF16)],
         [
             ((both, total), F32),
             ((both, total), F32),
@@ -265,28 +272,31 @@
             ((rows, total), F32),
             ((rows, total), F32),
         ],
+        40,
     )
-    dq, (dk, dv, dkv_away) = results[0:4], results[4:7]
-    bias_own, bias_away = results[7:11], results[11:15]
-
-    near = [
-        own + fetch(other, "core", CORE, 1).astype(F32)
-        for own, other in zip(bias_own, bias_away)
-    ]
+    dq, (dk, dv, dkv_away, bias_own, bias_away) = results[0:4], results[4:9]
+
+    near = bias_own + fetch(bias_away, "core", CORE, 1).astype(F32)
+    arrived = fetch(dkv_away, "zhi", ZHI, 1)
+    sent = [near[d].astype(BF16) for d in range(1, Y)]
+    sent, dq = after((sent, dq))
+    far = [deliver(sent[d - 1], "y", Y, d) for d in range(1, Y)]
+    dq1 = deliver(dq[1], "x", X, 1)
     along_y = near[0]
-    for d in range(1, Y):
-        along_y = along_y + deliver(near[d].astype(BF16), "y", Y, d).astype(F32)
-    low = along_y.astype(BF16)
+    for part in far:
+        along_y = along_y + part.astype(F32)
+    low, arrived = after((along_y.astype(BF16), arrived))
+    dq1, dq = after((dq1, dq))
     bias_grad = None
     for d in range(ZLO):
         pairs = [(worker, owner) for owner, worker in z_pairs(d)]
         part = lax.ppermute(low[d], z_axes, pairs).astype(F32)
         bias_grad = part if bias_grad is None else bias_grad + part
 
-    query_sum = dq[0]
-    for d in range(1, X):
+    query_sum = dq[0] + dq1.astype(F32)
+    for d in (3, 2):
         query_sum = query_sum + deliver(dq[d], "x", X, d).astype(F32)
-    arrived = fetch(dkv_away, "zhi", ZHI, 1).astype(F32)
+    arrived = arrived.astype(F32)
     query_grad = (scale * query_sum).astype(BF16)
     key_grad = (scale * (dk + arrived[:rows])).astype(BF16)
     value_grad = (dv + arrived[rows:]).astype(BF16)

time: 168 us -> 162 us (0.964)
  Pallas kernels: 48.9 us -> 44.5 us
  starting transfers between devices: 66.6 us -> 63.8 us
    ppermute x24 -> x16, starting transfers between devices: 38 us -> 29.1 us  [fetch(): lax.ppermute(x, axis, [((n + distance) % size, n) for n in range(size)])]
    ppermute x24 -> x16, waiting for transfers between devices: 25.7 us -> 30.8 us  [fetch(): lax.ppermute(x, axis, [((n + distance) % size, n) for n in range(size)])]
    ppermute x4, starting transfers between devices: 9.37 us -> 14.1 us  [per_device(): part = lax.ppermute(low[d], z_axes, pairs).astype(F32)]
    pallas_call x2, Pallas kernels: 48.9 us -> 44.5 us  [call(): pl.pallas_call(kernel, in_specs=[SMEM] + [VMEM] * (len(args) - 1), out_sp...]
    ppermute x4, waiting for transfers between devices: 6.5 us -> 3.42 us  [per_device(): part = lax.ppermute(low[d], z_axes, pairs).astype(F32)]
    unnamed x40 -> x11, local copies, waits for them, and re-layouts: 5.05 us -> 2.63 us
    convert_element_type x5 -> x2, other arithmetic: 2.64 us -> 0.24 us  [the longest x1 0.17 us: per_device(): low, arrived = after((along_y.astype(BF16), arrived))]
    concatenate x0 -> x1, other arithmetic: none -> 1.83 us  [per_device(): kvm = jnp.concatenate([keys, values, mask_rows], axis=0)]
  transfers between devices with their start and end apart: 38 -> 30, of which waited for: 11 -> 14; matrix products, arithmetic and copies ran while one was open for 3% -> 3% of each run, Pallas kernels for 8% -> 0%
where the time goes in v3:
time: 162 us; the launch traced here: 160 us
  starting transfers between devices  63.8 us (39%)
  Pallas kernels  44.5 us (27%)
  waiting for transfers between devices  40.6 us (25%)
  other arithmetic  5.62 us (3%)
  local copies, waits for them, and re-layouts  4.47 us (3%)
    pallas_call x2, Pallas kernels, call(): pl.pallas_call(kernel, in_specs=[SMEM] + [VMEM] * (len(args) - 1), out_sp...  44.5 us
    ppermute x16, waiting for transfers between devices, fetch(): lax.ppermute(x, axis, [((n + distance) % size, n) for n in range(size)])  30.8 us
    ppermute x16, starting transfers between devices, fetch(): lax.ppermute(x, axis, [((n + distance) % size, n) for n in range(size)])  29.1 us
    ppermute x4, starting transfers between devices, per_device(): part = lax.ppermute(low[d], z_axes, pairs).astype(F32)  14.1 us
    ppermute x4, starting transfers between devices, per_device(): from_z = [lax.ppermute(bias, z_axes, z_pairs(d)) for d in range(ZLO)]  10.6 us
    ppermute x6, starting transfers between devices, deliver(): lax.ppermute(x, axis, [(n, (n + distance) % size) for n in range(size)])  10.1 us
    ppermute x4, waiting for transfers between devices, per_device(): from_z = [lax.ppermute(bias, z_axes, z_pairs(d)) for d in range(ZLO)]  4.7 us
    ppermute x4, waiting for transfers between devices, per_device(): part = lax.ppermute(low[d], z_axes, pairs).astype(F32)  3.42 us
  transfers between devices with their start and end apart: 30, of which 14 were waited for; matrix products, arithmetic and copies ran while one was open for 3% of the time, Pallas kernels for 0%

profile of v3, /device:TPU:64, one launch (start us, length us, event | category | flops | bytes accessed | tf_op | source)
XLA Modules:
  0.0 159.8 jit_solution(1396052495393880662)
XLA Ops:
  0.6 0.0 copy-start.1
  0.7 0.0 copy-start.2
  0.7 1.7 %constant_dynamic-update-slice_fusion.1 = bf16[16,32,384]{2,1,0:T(8,128)(2,1)} fusion(bf16[8,32,384]{2,1,0:T(8,128)(2,1)} %refs_1_.3), kind=kLoop, calls=%fused_computation.23 | loop fusion | bytes 393216
  2.4 1.6 %constant_dynamic-update-slice_fusion = bf16[16,32,384]{2,1,0:T(8,128)(2,1)} fusion(bf16[16,32,384]{2,1,0:T(8,128)(2,1)} %constant_dynamic-update-slice_fusion.1, bf16[8,32,384]{2,1,0:T(8,128)(2,1)} %refs_5_.3), kind=kLoop, calls=%fused_computation.22 | loop fusion | bytes 393216 | tf_op jit(solution)/shard_map/concatenate | solution.py:233
  4.0 2.8 %collective-permute-start.4 = (bf16[16,32,384]{2,1,0:T(8,128)(2,1)}, bf16[16,32,384]{2,1,0:T(8,128)(2,1)S(1)}, u32[]{:S(2)}, u32[]{:S(2)}) collective-permute-start(bf16[16,32,384]{2,1,0:T(8,128)(2,1)} %constant_dynamic-update-slice_fusion), channel_id=1, source_target_pairs={{1,0},{2,1},{3,2},{0,3},{5,4},{6,5},{7,6},{4,7},{9,8},{10,9},{11,1... | collective-permute-start | bytes 1179656 | tf_op jit(solution)/shard_map/ppermute | solution.py:207
  6.7 4.9 %collective-permute-start.1 = (bf16[96,384]{1,0:T(8,128)(2,1)}, bf16[96,384]{1,0:T(8,128)(2,1)S(1)}, u32[]{:S(2)}, u32[]{:S(2)}) collective-permute-start(bf16[96,384]{1,0:T(8,128)(2,1)} %param.12), channel_id=1, source_target_pairs={{64,0},{4,64},{68,128},{0,192},{192,4},{132,68},{196,132},{128,196... | collective-permute-start | bytes 221192 | tf_op jit(solution)/shard_map/ppermute | solution.py:232
  11.7 1.9 %collective-permute-start = (bf16[96,384]{1,0:T(8,128)(2,1)}, bf16[96,384]{1,0:T(8,128)(2,1)S(1)}, u32[]{:S(2)}, u32[]{:S(2)}) collective-permute-start(bf16[96,384]{1,0:T(8,128)(2,1)} %param.12), channel_id=1, source_target_pairs={{0,0},{64,64},{4,128},{68,192},{128,4},{192,68},{132,132},{196,196... | collective-permute-start | bytes 221192 | tf_op jit(solution)/shard_map/ppermute | solution.py:232
  13.6 3.7 %collective-permute-start.3 = (bf16[96,384]{1,0:T(8,128)(2,1)}, bf16[96,384]{1,0:T(8,128)(2,1)S(1)}, u32[]{:S(2)}, u32[]{:S(2)}) collective-permute-start(bf16[96,384]{1,0:T(8,128)(2,1)} %param.12), channel_id=1, source_target_pairs={{68,0},{0,64},{64,128},{4,192},{196,4},{128,68},{192,132},{132,196... | collective-permute-start | bytes 221192 | tf_op jit(solution)/shard_map/ppermute | solution.py:232
  17.3 0.0 collective-permute-start.2
  17.3 0.8 fusion.8
  18.1 0.0 collective-permute-done.1
  18.1 3.4 %collective-permute-done = bf16[96,384]{1,0:T(8,128)(2,1)S(1)} collective-permute-done((bf16[96,384]{1,0:T(8,128)(2,1)}, bf16[96,384]{1,0:T(8,128)(2,1)S(1)}, u32[]{:S(2)}, u32[]{:S(2)}) %collective-permute-start) | collective-permute-done | bytes 73760 | tf_op jit(solution)/shard_map/ppermute | solution.py:232
  21.5 0.0 collective-permute-done.3
  21.5 1.3 collective-permute-done.2
  22.9 0.0 collective-permute-done.4.refs_2_
  22.9 3.1 %collective-permute-start.5 = (bf16[4,96,384]{2,1,0:T(8,128)(2,1)S(1)}, bf16[4,96,384]{2,1,0:T(8,128)(2,1)S(1)}, u32[]{:S(2)}, u32[]{:S(2)}) collective-permute-start(bf16[4,96,384]{2,1,0:T(8,128)(2,1)S(1)} %pad_maximum_fusion.1.refs_10_), channel_id=1, source_target_pairs={{16,0},{32,16},{48,32},{0,48},{17,1},{33,17},{49,33},{1,49},{18,2}... | collective-permute-start | bytes 884744 | tf_op jit(solution)/shard_map/ppermute | solution.py:207
  26.0 1.8 %pad_maximum_fusion = bf16[17,32,384]{2,1,0:T(8,128)(2,1)} fusion(bf16[1,32,384]{2,1,0:T(8,128)(2,1)S(1)} %broadcast_in_dim.6, bf16[8,32,384]{2,1,0:T(8,128)(2,1)} %refs_7_.1, bf16[8,32,384]{2,1,0:T(8,128)(2,1)} %refs_6_.1), kind=kLoop, calls=%fused_computation.6 | loop fusion | flops 417792 | bytes 835584 | tf_op jit(solution)/shard_map/concatenate | solution.py:237
  27.8 0.0 collective-permute-start.11
  27.8 0.0 collective-permute-start.10
  27.8 2.2 %collective-permute-start.9 = (bf16[4,96,384]{2,1,0:T(8,128)(2,1)S(1)}, bf16[4,96,384]{2,1,0:T(8,128)(2,1)}, u32[]{:S(2)}, u32[]{:S(2)}) collective-permute-start(bf16[4,96,384]{2,1,0:T(8,128)(2,1)S(1)} %pad_maximum_fusion.1.refs_10_), channel_id=1, source_target_pairs={{32,0},{48,16},{0,32},{16,48},{33,1},{49,17},{1,33},{17,49},{34,2}... | collective-permute-start | bytes 884744 | tf_op jit(solution)/shard_map/ppermute | solution.py:207
  30.0 0.2 collective-permute-done.5.refs_11_
  30.2 4.9 %collective-permute-start.8 = (bf16[17,32,384]{2,1,0:T(8,128)(2,1)}, bf16[17,32,384]{2,1,0:T(8,128)(2,1)S(1)}, u32[]{:S(2)}, u32[]{:S(2)}) collective-permute-start(bf16[17,32,384]{2,1,0:T(8,128)(2,1)} %pad_maximum_fusion), channel_id=1, source_target_pairs={{4,0},{0,4},{5,1},{1,5},{6,2},{2,6},{7,3},{3,7},{12,8},{8,12},{13,... | collective-permute-start | bytes 1253384 | tf_op jit(solution)/shard_map/ppermute | solution.py:207
  35.1 0.0 collective-permute-done.11.refs_14_
  35.1 1.3 collective-permute-start.6
  36.5 8.3 %collective-permute-done.10.refs_13_ = bf16[4,96,384]{2,1,0:T(8,128)(2,1)S(1)} collective-permute-done((bf16[4,96,384]{2,1,0:T(8,128)(2,1)S(1)}, bf16[4,96,384]{2,1,0:T(8,128)(2,1)S(1)}, u32[]{:S(2)}, u32[]{:S(2)}) %collective-permute-start.10) | collective-permute-done | bytes 294944 | tf_op jit(solution)/shard_map/ppermute | solution.py:207
  44.7 0.0 collective-permute-start.14
  44.8 0.5 collective-permute-start.13
  45.3 0.1 collective-permute-start.12
  45.4 0.1 stack.38.refs_0_
  45.4 2.2 %collective-permute-done.8.refs_6_.refs_8_ = bf16[17,32,384]{2,1,0:T(8,128)(2,1)S(1)} collective-permute-done((bf16[17,32,384]{2,1,0:T(8,128)(2,1)}, bf16[17,32,384]{2,1,0:T(8,128)(2,1)S(1)}, u32[]{:S(2)}, u32[]{:S(2)}) %collective-permute-start.8) | collective-permute-done | bytes 417824 | tf_op jit(solution)/shard_map/ppermute | solution.py:207
  47.7 0.0 copy-start.4
  47.7 0.9 copy-done.4
  48.6 13.2 %softmax_statistics.1 = (f32[8,3456]{1,0:T(8,128)S(1)}, bf16[768,1536]{1,0:T(8,128)(2,1)S(1)}) custom-call(s32[5]{0:T(128)S(1)} %stack.38.refs_0_, bf16[8,32,384]{2,1,0:T(8,128)(2,1)S(1)} %copy-done, bf16[16,32,384]{2,1,0:T(8,128)(2,1)S(1)} %collective-permute-done.4.refs_2_, bf16[16,32,384]{2,1,0:T(8,128)(2,1)S(1)} %collective-permute-done.6.refs_3_, ...), custom_call_target="tpu_custom_call" | custom-call | tf_op jit(solution)/shard_map/softmax_statistics/pallas_call | solution.py:195
  61.8 1.0 collective-permute-start.17
  62.8 3.9 %collective-permute-start.16 = (f32[8,3456]{1,0:T(8,128)S(1)}, f32[8,3456]{1,0:T(8,128)S(1)}, u32[]{:S(2)}, u32[]{:S(2)}) collective-permute-start(f32[8,3456]{1,0:T(8,128)S(1)} %get-tuple-element.40.refs_10_), channel_id=1, source_target_pairs={{2,0},{3,1},{0,2},{1,3},{6,4},{7,5},{4,6},{5,7},{10,8},{11,9},{8,1... | collective-permute-start | bytes 331784 | tf_op jit(solution)/shard_map/ppermute | solution.py:207
  66.8 0.2 collective-permute-start.15
  67.0 1.3 collective-permute-done.17.refs_13_
  68.3 3.5 %collective-permute-done.16.refs_12_ = f32[8,3456]{1,0:T(8,128)S(1)} collective-permute-done((f32[8,3456]{1,0:T(8,128)S(1)}, f32[8,3456]{1,0:T(8,128)S(1)}, u32[]{:S(2)}, u32[]{:S(2)}) %collective-permute-start.16) | collective-permute-done | bytes 110624 | tf_op jit(solution)/shard_map/ppermute | solution.py:207
  71.9 31.3 %attention_gradients.1 = (f32[8,32,384]{2,1,0:T(8,128)S(1)}, bf16[8,32,384]{2,1,0:T(8,128)(2,1)S(1)}, bf16[8,32,384]{2,1,0:T(8,128)(2,1)S(1)}, bf16[8,32,384]{2,...) custom-call(s32[5]{0:T(128)S(1)} %stack.38.refs_0_, ...), custom_call_target="tpu_custom_call" | custom-call | tf_op jit(solution)/shard_map/attention_gradients/pallas_call | solution.py:195
  103.2 0.1 collective-permute-start.18
  103.3 2.8 %collective-permute-done.18 = bf16[4,4,96,384]{3,2,1,0:T(8,128)(2,1)S(1)} collective-permute-done((bf16[4,4,96,384]{3,2,1,0:T(8,128)(2,1)S(1)}, bf16[4,4,96,384]{3,2,1,0:T(8,128)(2,1)S(1)}, u32[]{:S(2)}, u32[]{:S(2)}) %collective-permute-start.18) | collective-permute-done | bytes 1179680 | tf_op jit(solution)/shard_map/ppermute | solution.py:207
  106.1 0.4 fusion.7
  106.5 0.1 slice_bitcast_fusion.1
  106.6 1.6 %collective-permute-start.22 = (bf16[4,96,384]{2,1,0:T(8,128)(2,1)S(1)}, bf16[4,96,384]{2,1,0:T(8,128)(2,1)S(1)}, u32[]{:S(2)}, u32[]{:S(2)}) collective-permute-start(bf16[4,96,384]{2,1,0:T(8,128)(2,1)S(1)} %get-tuple-element.57), channel_id=1, source_target_pairs={{0,16},{16,32},{32,48},{48,0},{1,17},{17,33},{33,49},{49,1},{2,18}... | collective-permute-start | bytes 884744 | tf_op jit(solution)/shard_map/ppermute | solution.py:211
  108.3 0.9 collective-permute-start.23
  109.2 1.9 %collective-permute-start.24 = (bf16[4,96,384]{2,1,0:T(8,128)(2,1)S(1)}, bf16[4,96,384]{2,1,0:T(8,128)(2,1)S(1)}, u32[]{:S(2)}, u32[]{:S(2)}) collective-permute-start(bf16[4,96,384]{2,1,0:T(8,128)(2,1)S(1)} %get-tuple-element.59), channel_id=1, source_target_pairs={{0,48},{16,0},{32,16},{48,32},{1,49},{17,1},{33,17},{49,33},{2,50}... | collective-permute-start | bytes 884744 | tf_op jit(solution)/shard_map/ppermute | solution.py:211
  111.0 0.2 collective-permute-start.19
  111.3 8.9 %collective-permute-start.25 = (bf16[16,32,384]{2,1,0:T(8,128)(2,1)S(1)}, bf16[16,32,384]{2,1,0:T(8,128)(2,1)S(1)}, u32[]{:S(2)}, u32[]{:S(2)}) collective-permute-start(bf16[16,32,384]{2,1,0:T(8,128)(2,1)S(1)} %get-tuple-element.60), channel_id=1, source_target_pairs={{4,0},{0,4},{5,1},{1,5},{6,2},{2,6},{7,3},{3,7},{12,8},{8,12},{13,... | collective-permute-start | bytes 1179656 | tf_op jit(solution)/shard_map/ppermute | solution.py:207
  120.2 2.4 %collective-permute-start.20 = (bf16[8,32,384]{2,1,0:T(8,128)(2,1)S(1)}, bf16[8,32,384]{2,1,0:T(8,128)(2,1)S(1)}, u32[]{:S(2)}, u32[]{:S(2)}) collective-permute-start(bf16[8,32,384]{2,1,0:T(8,128)(2,1)S(1)} %get-tuple-element.54), channel_id=1, source_target_pairs={{0,3},{1,0},{2,1},{3,2},{4,7},{5,4},{6,5},{7,6},{8,11},{9,8},{10,9... | collective-permute-start | bytes 589832 | tf_op jit(solution)/shard_map/ppermute | solution.py:211
  122.6 0.7 collective-permute-done.22
  123.3 0.6 collective-permute-done.24
  123.9 0.2 fusion.3
  124.1 12.4 %collective-permute-done.25 = bf16[16,32,384]{2,1,0:T(8,128)(2,1)S(1)} collective-permute-done((bf16[16,32,384]{2,1,0:T(8,128)(2,1)S(1)}, bf16[16,32,384]{2,1,0:T(8,128)(2,1)S(1)}, u32[]{:S(2)}, u32[]{:S(2)}) %collective-permute-start.25) | collective-permute-done | bytes 393248 | tf_op jit(solution)/shard_map/ppermute | solution.py:207
  136.5 6.3 %collective-permute-start.26 = (bf16[96,384]{1,0:T(8,128)(2,1)S(1)}, bf16[96,384]{1,0:T(8,128)(2,1)S(1)}, u32[]{:S(2)}, u32[]{:S(2)}) collective-permute-start(bf16[96,384]{1,0:T(8,128)(2,1)S(1)} %get-tuple-element.71), channel_id=1, source_target_pairs={{0,0},{64,64},{128,4},{192,68},{4,128},{68,192},{132,132},{196,196... | collective-permute-start | bytes 221192 | tf_op jit(solution)/shard_map/ppermute | solution.py:293
  142.8 0.1 collective-permute-start.29
  142.9 7.7 %collective-permute-start.28 = (bf16[96,384]{1,0:T(8,128)(2,1)S(1)}, bf16[96,384]{1,0:T(8,128)(2,1)S(1)}, u32[]{:S(2)}, u32[]{:S(2)}) collective-permute-start(bf16[96,384]{1,0:T(8,128)(2,1)S(1)} %get-tuple-element.73), channel_id=1, source_target_pairs={{0,4},{64,68},{128,0},{192,64},{4,132},{68,196},{132,128},{196,192... | collective-permute-start | bytes 221192 | tf_op jit(solution)/shard_map/ppermute | solution.py:293
  150.6 0.1 convert_element_type.80
  150.7 0.8 fusion.4
  151.5 3.0 %collective-permute-start.21 = (bf16[8,32,384]{2,1,0:T(8,128)(2,1)S(1)}, bf16[8,32,384]{2,1,0:T(8,128)(2,1)S(1)}, u32[]{:S(2)}, u32[]{:S(2)}) collective-permute-start(bf16[8,32,384]{2,1,0:T(8,128)(2,1)S(1)} %get-tuple-element.55), channel_id=1, source_target_pairs={{0,2},{1,3},{2,0},{3,1},{4,6},{5,7},{6,4},{7,5},{8,10},{9,11},{10,... | collective-permute-start | bytes 589832 | tf_op jit(solution)/shard_map/ppermute | solution.py:211
  154.5 1.5 collective-permute-done.29
  156.1 1.9 %collective-permute-done.27 = bf16[96,384]{1,0:T(8,128)(2,1)S(1)} collective-permute-done((bf16[96,384]{1,0:T(8,128)(2,1)S(1)}, bf16[96,384]{1,0:T(8,128)(2,1)S(1)}, u32[]{:S(2)}, u32[]{:S(2)}) %collective-permute-start.27) | collective-permute-done | bytes 73760 | tf_op jit(solution)/shard_map/ppermute | solution.py:293
  158.0 0.7 convert_add_fusion.1
  158.7 0.4 collective-permute-done.21
  159.0 0.8 multiply_convert_fusion
  (24 shorter events, 0.1 us)
Async XLA Ops:
  0.6 47.0 %copy-start = (bf16[8,32,384]{2,1,0:T(8,128)(2,1)S(1)}, bf16[8,32,384]{2,1,0:T(8,128)(2,1)}, u32[]{:S(2)}) copy-start(bf16[8,32,384]{2,1,0:T(8,128)(2,1)} %refs_1_.3) | copy-start | bytes 589828
  0.6 47.0 %copy-start.1 = (bf16[8,32,384]{2,1,0:T(8,128)(2,1)S(1)}, bf16[8,32,384]{2,1,0:T(8,128)(2,1)}, u32[]{:S(2)}) copy-start(bf16[8,32,384]{2,1,0:T(8,128)(2,1)} %refs_5_.3) | copy-start | bytes 589828
  0.7 47.0 %copy-start.2 = (bf16[8,32,384]{2,1,0:T(8,128)(2,1)S(1)}, bf16[8,32,384]{2,1,0:T(8,128)(2,1)}, u32[]{:S(2)}) copy-start(bf16[8,32,384]{2,1,0:T(8,128)(2,1)} %refs_6_.1) | copy-start | bytes 589828
  4.0 18.9 %collective-permute-start.4 = (bf16[16,32,384]{2,1,0:T(8,128)(2,1)}, bf16[16,32,384]{2,1,0:T(8,128)(2,1)S(1)}, u32[]{:S(2)}, u32[]{:S(2)}) collective-permute-start(bf16[16,32,384]{2,1,0:T(8,128)(2,1)} %constant_dynamic-update-slice_fusion), channel_id=1, source_target_pairs={{1,0},{2,1},{3,2},{0,3},{5,4},{6,5},{7,6},{4,7},{9,8},{10,9},{11,1... | collective-permute-start | bytes 1179656 | tf_op jit(solution)/shard_map/ppermute | solution.py:207
  6.7 11.4 %collective-permute-start.1 = (bf16[96,384]{1,0:T(8,128)(2,1)}, bf16[96,384]{1,0:T(8,128)(2,1)S(1)}, u32[]{:S(2)}, u32[]{:S(2)}) collective-permute-start(bf16[96,384]{1,0:T(8,128)(2,1)} %param.12), channel_id=1, source_target_pairs={{64,0},{4,64},{68,128},{0,192},{192,4},{132,68},{196,132},{128,196... | collective-permute-start | bytes 221192 | tf_op jit(solution)/shard_map/ppermute | solution.py:232
  11.7 9.8 %collective-permute-start = (bf16[96,384]{1,0:T(8,128)(2,1)}, bf16[96,384]{1,0:T(8,128)(2,1)S(1)}, u32[]{:S(2)}, u32[]{:S(2)}) collective-permute-start(bf16[96,384]{1,0:T(8,128)(2,1)} %param.12), channel_id=1, source_target_pairs={{0,0},{64,64},{4,128},{68,192},{128,4},{192,68},{132,132},{196,196... | collective-permute-start | bytes 221192 | tf_op jit(solution)/shard_map/ppermute | solution.py:232
  13.6 7.9 %collective-permute-start.3 = (bf16[96,384]{1,0:T(8,128)(2,1)}, bf16[96,384]{1,0:T(8,128)(2,1)S(1)}, u32[]{:S(2)}, u32[]{:S(2)}) collective-permute-start(bf16[96,384]{1,0:T(8,128)(2,1)} %param.12), channel_id=1, source_target_pairs={{68,0},{0,64},{64,128},{4,192},{196,4},{128,68},{192,132},{132,196... | collective-permute-start | bytes 221192 | tf_op jit(solution)/shard_map/ppermute | solution.py:232
  17.3 5.5 %collective-permute-start.2 = (bf16[96,384]{1,0:T(8,128)(2,1)}, bf16[96,384]{1,0:T(8,128)(2,1)S(1)}, u32[]{:S(2)}, u32[]{:S(2)}) collective-permute-start(bf16[96,384]{1,0:T(8,128)(2,1)} %param.12), channel_id=1, source_target_pairs={{4,0},{68,64},{0,128},{64,192},{132,4},{196,68},{128,132},{192,196... | collective-permute-start | bytes 221192 | tf_op jit(solution)/shard_map/ppermute | solution.py:232
  22.9 7.4 %collective-permute-start.5 = (bf16[4,96,384]{2,1,0:T(8,128)(2,1)S(1)}, bf16[4,96,384]{2,1,0:T(8,128)(2,1)S(1)}, u32[]{:S(2)}, u32[]{:S(2)}) collective-permute-start(bf16[4,96,384]{2,1,0:T(8,128)(2,1)S(1)} %pad_maximum_fusion.1.refs_10_), channel_id=1, source_target_pairs={{16,0},{32,16},{48,32},{0,48},{17,1},{33,17},{49,33},{1,49},{18,2}... | collective-permute-start | bytes 884744 | tf_op jit(solution)/shard_map/ppermute | solution.py:207
  27.8 17.5 %collective-permute-start.7 = (bf16[16,32,384]{2,1,0:T(8,128)(2,1)}, bf16[16,32,384]{2,1,0:T(8,128)(2,1)S(1)}, u32[]{:S(2)}, u32[]{:S(2)}) collective-permute-start(bf16[16,32,384]{2,1,0:T(8,128)(2,1)} %constant_dynamic-update-slice_fusion), channel_id=1, source_target_pairs={{3,0},{0,1},{1,2},{2,3},{7,4},{4,5},{5,6},{6,7},{11,8},{8,9},{9,10... | collective-permute-start | bytes 1179656 | tf_op jit(solution)/shard_map/ppermute | solution.py:207
  27.8 7.4 %collective-permute-start.11 = (bf16[4,96,384]{2,1,0:T(8,128)(2,1)S(1)}, bf16[4,96,384]{2,1,0:T(8,128)(2,1)S(1)}, u32[]{:S(2)}, u32[]{:S(2)}) collective-permute-start(bf16[4,96,384]{2,1,0:T(8,128)(2,1)S(1)} %pad_maximum_fusion.1.refs_10_), channel_id=1, source_target_pairs={{8,0},{0,8},{9,1},{1,9},{10,2},{2,10},{11,3},{3,11},{12,4},{4,12},... | collective-permute-start | bytes 884744 | tf_op jit(solution)/shard_map/ppermute | solution.py:207
  27.8 17.0 %collective-permute-start.10 = (bf16[4,96,384]{2,1,0:T(8,128)(2,1)S(1)}, bf16[4,96,384]{2,1,0:T(8,128)(2,1)S(1)}, u32[]{:S(2)}, u32[]{:S(2)}) collective-permute-start(bf16[4,96,384]{2,1,0:T(8,128)(2,1)S(1)} %pad_maximum_fusion.1.refs_10_), channel_id=1, source_target_pairs={{48,0},{0,16},{16,32},{32,48},{49,1},{1,17},{17,33},{33,49},{50,2}... | collective-permute-start | bytes 884744 | tf_op jit(solution)/shard_map/ppermute | solution.py:207
  27.8 16.9 %collective-permute-start.9 = (bf16[4,96,384]{2,1,0:T(8,128)(2,1)S(1)}, bf16[4,96,384]{2,1,0:T(8,128)(2,1)}, u32[]{:S(2)}, u32[]{:S(2)}) collective-permute-start(bf16[4,96,384]{2,1,0:T(8,128)(2,1)S(1)} %pad_maximum_fusion.1.refs_10_), channel_id=1, source_target_pairs={{32,0},{48,16},{0,32},{16,48},{33,1},{49,17},{1,33},{17,49},{34,2}... | collective-permute-start | bytes 884744 | tf_op jit(solution)/shard_map/ppermute | solution.py:207
  30.2 17.4 %collective-permute-start.8 = (bf16[17,32,384]{2,1,0:T(8,128)(2,1)}, bf16[17,32,384]{2,1,0:T(8,128)(2,1)S(1)}, u32[]{:S(2)}, u32[]{:S(2)}) collective-permute-start(bf16[17,32,384]{2,1,0:T(8,128)(2,1)} %pad_maximum_fusion), channel_id=1, source_target_pairs={{4,0},{0,4},{5,1},{1,5},{6,2},{2,6},{7,3},{3,7},{12,8},{8,12},{13,... | collective-permute-start | bytes 1253384 | tf_op jit(solution)/shard_map/ppermute | solution.py:207
  35.1 12.5 %collective-permute-start.6 = (bf16[16,32,384]{2,1,0:T(8,128)(2,1)}, bf16[16,32,384]{2,1,0:T(8,128)(2,1)S(1)}, u32[]{:S(2)}, u32[]{:S(2)}) collective-permute-start(bf16[16,32,384]{2,1,0:T(8,128)(2,1)} %constant_dynamic-update-slice_fusion), channel_id=1, source_target_pairs={{2,0},{3,1},{0,2},{1,3},{6,4},{7,5},{4,6},{5,7},{10,8},{11,9},{8,1... | collective-permute-start | bytes 1179656 | tf_op jit(solution)/shard_map/ppermute | solution.py:207
  44.7 2.9 %collective-permute-start.14 = (bf16[4,96,384]{2,1,0:T(8,128)(2,1)S(1)}, bf16[4,96,384]{2,1,0:T(8,128)(2,1)}, u32[]{:S(2)}, u32[]{:S(2)}) collective-permute-start(bf16[4,96,384]{2,1,0:T(8,128)(2,1)S(1)} %collective-permute-done.10.refs_13_), channel_id=1, source_target_pairs={{8,0},{0,8},{9,1},{1,9},{10,2},{2,10},{11,3},{3,11},{12,4},{4,12},... | collective-permute-start | bytes 884744 | tf_op jit(solution)/shard_map/ppermute | solution.py:207
  44.8 2.9 %collective-permute-start.13 = (bf16[4,96,384]{2,1,0:T(8,128)(2,1)}, bf16[4,96,384]{2,1,0:T(8,128)(2,1)}, u32[]{:S(2)}, u32[]{:S(2)}) collective-permute-start(bf16[4,96,384]{2,1,0:T(8,128)(2,1)} %collective-permute-done.9.refs_12_), channel_id=1, source_target_pairs={{8,0},{0,8},{9,1},{1,9},{10,2},{2,10},{11,3},{3,11},{12,4},{4,12},... | collective-permute-start | bytes 884744 | tf_op jit(solution)/shard_map/ppermute | solution.py:207
  45.3 2.4 %collective-permute-start.12 = (bf16[4,96,384]{2,1,0:T(8,128)(2,1)S(1)}, bf16[4,96,384]{2,1,0:T(8,128)(2,1)}, u32[]{:S(2)}, u32[]{:S(2)}) collective-permute-start(bf16[4,96,384]{2,1,0:T(8,128)(2,1)S(1)} %collective-permute-done.5.refs_11_), channel_id=1, source_target_pairs={{8,0},{0,8},{9,1},{1,9},{10,2},{2,10},{11,3},{3,11},{12,4},{4,12},... | collective-permute-start | bytes 884744 | tf_op jit(solution)/shard_map/ppermute | solution.py:207
  45.4 26.4 %copy-start.3 = (bf16[8,32,384]{2,1,0:T(8,128)(2,1)S(1)}, bf16[8,32,384]{2,1,0:T(8,128)(2,1)}, u32[]{:S(2)}) copy-start(bf16[8,32,384]{2,1,0:T(8,128)(2,1)} %refs_7_.1) | copy-start | bytes 589828
  47.7 0.9 copy-start.4
  61.8 6.5 %collective-permute-start.17 = (f32[8,3456]{1,0:T(8,128)S(1)}, f32[8,3456]{1,0:T(8,128)S(1)}, u32[]{:S(2)}, u32[]{:S(2)}) collective-permute-start(f32[8,3456]{1,0:T(8,128)S(1)} %get-tuple-element.40.refs_10_), channel_id=1, source_target_pairs={{3,0},{0,1},{1,2},{2,3},{7,4},{4,5},{5,6},{6,7},{11,8},{8,9},{9,10... | collective-permute-start | bytes 331784 | tf_op jit(solution)/shard_map/ppermute | solution.py:207
  62.8 9.0 %collective-permute-start.16 = (f32[8,3456]{1,0:T(8,128)S(1)}, f32[8,3456]{1,0:T(8,128)S(1)}, u32[]{:S(2)}, u32[]{:S(2)}) collective-permute-start(f32[8,3456]{1,0:T(8,128)S(1)} %get-tuple-element.40.refs_10_), channel_id=1, source_target_pairs={{2,0},{3,1},{0,2},{1,3},{6,4},{7,5},{4,6},{5,7},{10,8},{11,9},{8,1... | collective-permute-start | bytes 331784 | tf_op jit(solution)/shard_map/ppermute | solution.py:207
  66.8 5.1 %collective-permute-start.15 = (f32[8,3456]{1,0:T(8,128)S(1)}, f32[8,3456]{1,0:T(8,128)S(1)}, u32[]{:S(2)}, u32[]{:S(2)}) collective-permute-start(f32[8,3456]{1,0:T(8,128)S(1)} %get-tuple-element.40.refs_10_), channel_id=1, source_target_pairs={{1,0},{2,1},{3,2},{0,3},{5,4},{6,5},{7,6},{4,7},{9,8},{10,9},{11,1... | collective-permute-start | bytes 331784 | tf_op jit(solution)/shard_map/ppermute | solution.py:207
  103.2 2.9 %collective-permute-start.18 = (bf16[4,4,96,384]{3,2,1,0:T(8,128)(2,1)S(1)}, bf16[4,4,96,384]{3,2,1,0:T(8,128)(2,1)S(1)}, u32[]{:S(2)}, u32[]{:S(2)}) collective-permute-start(bf16[4,4,96,384]{3,2,1,0:T(8,128)(2,1)S(1)} %get-tuple-element.43), channel_id=1, source_target_pairs={{8,0},{0,8},{9,1},{1,9},{10,2},{2,10},{11,3},{3,11},{12,4},{4,12},... | collective-permute-start | bytes 3538952 | tf_op jit(solution)/shard_map/ppermute | solution.py:207
  106.6 16.7 %collective-permute-start.22 = (bf16[4,96,384]{2,1,0:T(8,128)(2,1)S(1)}, bf16[4,96,384]{2,1,0:T(8,128)(2,1)S(1)}, u32[]{:S(2)}, u32[]{:S(2)}) collective-permute-start(bf16[4,96,384]{2,1,0:T(8,128)(2,1)S(1)} %get-tuple-element.57), channel_id=1, source_target_pairs={{0,16},{16,32},{32,48},{48,0},{1,17},{17,33},{33,49},{49,1},{2,18}... | collective-permute-start | bytes 884744 | tf_op jit(solution)/shard_map/ppermute | solution.py:211
  108.3 15.0 %collective-permute-start.23 = (bf16[4,96,384]{2,1,0:T(8,128)(2,1)S(1)}, bf16[4,96,384]{2,1,0:T(8,128)(2,1)S(1)}, u32[]{:S(2)}, u32[]{:S(2)}) collective-permute-start(bf16[4,96,384]{2,1,0:T(8,128)(2,1)S(1)} %get-tuple-element.58), channel_id=1, source_target_pairs={{0,32},{16,48},{32,0},{48,16},{1,33},{17,49},{33,1},{49,17},{2,34}... | collective-permute-start | bytes 884744 | tf_op jit(solution)/shard_map/ppermute | solution.py:211
  109.2 14.8 %collective-permute-start.24 = (bf16[4,96,384]{2,1,0:T(8,128)(2,1)S(1)}, bf16[4,96,384]{2,1,0:T(8,128)(2,1)S(1)}, u32[]{:S(2)}, u32[]{:S(2)}) collective-permute-start(bf16[4,96,384]{2,1,0:T(8,128)(2,1)S(1)} %get-tuple-element.59), channel_id=1, source_target_pairs={{0,48},{16,0},{32,16},{48,32},{1,49},{17,1},{33,17},{49,33},{2,50}... | collective-permute-start | bytes 884744 | tf_op jit(solution)/shard_map/ppermute | solution.py:211
  111.0 9.1 %collective-permute-start.19 = (bf16[8,32,384]{2,1,0:T(8,128)(2,1)S(1)}, bf16[8,32,384]{2,1,0:T(8,128)(2,1)S(1)}, u32[]{:S(2)}, u32[]{:S(2)}) collective-permute-start(bf16[8,32,384]{2,1,0:T(8,128)(2,1)S(1)} %get-tuple-element.48), channel_id=1, source_target_pairs={{0,1},{1,2},{2,3},{3,0},{4,5},{5,6},{6,7},{7,4},{8,9},{9,10},{10,1... | collective-permute-start | bytes 589832 | tf_op jit(solution)/shard_map/ppermute | solution.py:211
  111.3 25.2 %collective-permute-start.25 = (bf16[16,32,384]{2,1,0:T(8,128)(2,1)S(1)}, bf16[16,32,384]{2,1,0:T(8,128)(2,1)S(1)}, u32[]{:S(2)}, u32[]{:S(2)}) collective-permute-start(bf16[16,32,384]{2,1,0:T(8,128)(2,1)S(1)} %get-tuple-element.60), channel_id=1, source_target_pairs={{4,0},{0,4},{5,1},{1,5},{6,2},{2,6},{7,3},{3,7},{12,8},{8,12},{13,... | collective-permute-start | bytes 1179656 | tf_op jit(solution)/shard_map/ppermute | solution.py:207
  120.2 38.5 %collective-permute-start.20 = (bf16[8,32,384]{2,1,0:T(8,128)(2,1)S(1)}, bf16[8,32,384]{2,1,0:T(8,128)(2,1)S(1)}, u32[]{:S(2)}, u32[]{:S(2)}) collective-permute-start(bf16[8,32,384]{2,1,0:T(8,128)(2,1)S(1)} %get-tuple-element.54), channel_id=1, source_target_pairs={{0,3},{1,0},{2,1},{3,2},{4,7},{5,4},{6,5},{7,6},{8,11},{9,8},{10,9... | collective-permute-start | bytes 589832 | tf_op jit(solution)/shard_map/ppermute | solution.py:211
  136.5 15.0 %collective-permute-start.26 = (bf16[96,384]{1,0:T(8,128)(2,1)S(1)}, bf16[96,384]{1,0:T(8,128)(2,1)S(1)}, u32[]{:S(2)}, u32[]{:S(2)}) collective-permute-start(bf16[96,384]{1,0:T(8,128)(2,1)S(1)} %get-tuple-element.71), channel_id=1, source_target_pairs={{0,0},{64,64},{128,4},{192,68},{4,128},{68,192},{132,132},{196,196... | collective-permute-start | bytes 221192 | tf_op jit(solution)/shard_map/ppermute | solution.py:293
  142.8 13.2 %collective-permute-start.29 = (bf16[96,384]{1,0:T(8,128)(2,1)S(1)}, bf16[96,384]{1,0:T(8,128)(2,1)S(1)}, u32[]{:S(2)}, u32[]{:S(2)}) collective-permute-start(bf16[96,384]{1,0:T(8,128)(2,1)S(1)} %get-tuple-element.72), channel_id=1, source_target_pairs={{0,68},{64,0},{128,64},{192,4},{4,196},{68,128},{132,192},{196,132... | collective-permute-start | bytes 221192 | tf_op jit(solution)/shard_map/ppermute | solution.py:293
  142.9 13.2 %collective-permute-start.28 = (bf16[96,384]{1,0:T(8,128)(2,1)S(1)}, bf16[96,384]{1,0:T(8,128)(2,1)S(1)}, u32[]{:S(2)}, u32[]{:S(2)}) collective-permute-start(bf16[96,384]{1,0:T(8,128)(2,1)S(1)} %get-tuple-element.73), channel_id=1, source_target_pairs={{0,4},{64,68},{128,0},{192,64},{4,132},{68,196},{132,128},{196,192... | collective-permute-start | bytes 221192 | tf_op jit(solution)/shard_map/ppermute | solution.py:293
  150.6 7.4 %collective-permute-start.27 = (bf16[96,384]{1,0:T(8,128)(2,1)S(1)}, bf16[96,384]{1,0:T(8,128)(2,1)S(1)}, u32[]{:S(2)}, u32[]{:S(2)}) collective-permute-start(bf16[96,384]{1,0:T(8,128)(2,1)S(1)} %get-tuple-element.74), channel_id=1, source_target_pairs={{0,64},{64,4},{128,68},{192,0},{4,192},{68,132},{132,196},{196,128... | collective-permute-start | bytes 221192 | tf_op jit(solution)/shard_map/ppermute | solution.py:293
  151.5 7.5 %collective-permute-start.21 = (bf16[8,32,384]{2,1,0:T(8,128)(2,1)S(1)}, bf16[8,32,384]{2,1,0:T(8,128)(2,1)S(1)}, u32[]{:S(2)}, u32[]{:S(2)}) collective-permute-start(bf16[8,32,384]{2,1,0:T(8,128)(2,1)S(1)} %get-tuple-element.55), channel_id=1, source_target_pairs={{0,2},{1,3},{2,0},{3,1},{4,6},{5,7},{6,4},{7,5},{8,10},{9,11},{10,... | collective-permute-start | bytes 589832 | tf_op jit(solution)/shard_map/ppermute | solution.py:211

commit v4 on v3

--- a/solution.py
+++ b/solution.py
@@ -33,14 +33,14 @@
     return out
 
 
-def put_keys(keys, masks, place, scale):
-    rows, head, width = keys[0].shape
+def put_keys(keys, masks, place, scale, start=0):
+    rows, head, width = place.shape[0], *keys[0].shape[1:]
     for slot, (ref, mask) in enumerate(zip(keys, masks)):
         offset = jnp.where(mask == 0.0, MASKED, 0.0)
         extra = rows_of((-1.0, -1.0, -1.0, offset), head, width)
 
         def prepare(i, carry):
-            parts = split3(ref[i].astype(F32) * scale)
+            parts = split3(ref[start + i].astype(F32) * scale)
             whole = jnp.concatenate(parts + (extra,), axis=0)
             place[i, slot * width : (slot + 1) * width, :] = whole.T.astype(BF16)
             return carry
@@ -48,13 +48,13 @@
         lax.fori_loop(0, rows, prepare, 0)
 
 
-def put_values(values, away, place):
-    rows, head, width = values.shape
+def put_values(values, place, start):
+    rows, head, width = place.shape[0], *values[0].shape[1:]
     extra = rows_of((-1.0, -1.0, -1.0), 128 - head, width)
-    for slot, (ref, base) in enumerate(((values, 0), (away, rows))):
+    for slot, ref in enumerate(values):
 
         def prepare(i, carry):
-            whole = jnp.concatenate((ref[base + i].astype(F32), extra), axis=0)
+            whole = jnp.concatenate((ref[start + i].astype(F32), extra), axis=0)
             place[i, slot * width : (slot + 1) * width, :] = whole.T.astype(BF16)
             return carry
 
@@ -84,7 +84,7 @@
     bias_n, bias_f, key_t = refs[19:]
     rows, head, width = keys.shape
     total = X * width
-    masks = (mask[...], away[2 * rows, 0:1, :].astype(F32))
+    masks = (mask[...], away[rows, 0:1, :].astype(F32))
     put_keys((keys, away), masks, key_t, scale * LOG2E)
     for yd, zd, other, slot, first in bias_pieces(at):
         bias_n[slot, pl.ds(first, 96), :] = pieces[other][yd][zd]
@@ -116,52 +116,57 @@
                     top = new
             most = jnp.max(top, axis=0, keepdims=True)
             summed = jnp.sum(total_sum * jnp.exp2(top - most), axis=0, keepdims=True)
-            stat[pl.ds(i, 1), cols] = most
-            stat[pl.ds(i, 1), total + d * width : total + (d + 1) * width] = summed
+            stat[pl.ds(i, 1), cols] = most + jnp.log(summed) * LOG2E
         product = grad[i].astype(F32) * outs[i].astype(F32)
-        stat[pl.ds(i, 1), 2 * total :] = jnp.sum(product, axis=0, keepdims=True)
+        stat[pl.ds(i, 1), total:] = jnp.sum(product, axis=0, keepdims=True)
         return carry
 
     lax.fori_loop(0, rows, row_step, 0)
 
 
-def main_kernel(scale, at, *refs):
-    q, (own_grad, keys, values, away, mask) = refs[0:4], refs[4:9]
-    stats = refs[9:13]
-    bias_t = refs[13]
-    dq = refs[14:18]
-    dk_own, dv_own, dkv_away, bias_own, bias_away = refs[18:23]
-    bias_f, acc, turned, key_t, value_t, lse, delta = refs[23:]
+def main_kernel(scale, start, at, *refs):
+    q, g = refs[0:4], refs[4:8]
+    keys, values, away, away_values, mask = refs[8:13]
+    stats = refs[13:17]
+    bias_t = refs[17]
+    refs = refs[18:]
+    if start == 0:
+        dq, (dk_own, dv_own, dkv_away, acc), scratch = refs[0:4], refs[4:8], refs[8:]
+    else:
+        acc_before, dq, refs = refs[0], refs[1:5], refs[5:]
+        (dk_own, dv_own, dkv_away, bias_own, bias_away), scratch = refs[0:5], refs[5:]
+        acc, turned = scratch[5:]
+    bias_f, key_t, value_t, lse, delta = scratch[:5]
     rows, head, width = keys.shape
+    count = key_t.shape[0]
     total = X * width
-    masks = (mask[...], away[2 * rows, 0:1, :].astype(F32))
-    put_keys((keys, away), masks, key_t, scale * LOG2E)
-    put_values(values, away, value_t)
+    masks = (mask[...], away[rows, 0:1, :].astype(F32))
+    put_keys((keys, away), masks, key_t, scale * LOG2E, start)
+    put_values((values, away_values), value_t, start)
     for d in range(X):
         cols = slice(d * width, (d + 1) * width)
         there = [(d - e) % X for e in range(X)]
-        tops = [stats[e][:, n * width : (n + 1) * width] for e, n in enumerate(there)]
-        sums = [stats[e][:, total + n * width : total + (n + 1) * width] for e, n in enumerate(there)]
-        top = jnp.maximum(jnp.maximum(tops[0], tops[1]), jnp.maximum(tops[2], tops[3]))
-        summed = sum(s * jnp.exp2(t - top) for s, t in zip(sums, tops))
+        parts = [stats[e][:, n * width : (n + 1) * width] for e, n in enumerate(there)]
+        top = jnp.maximum(jnp.maximum(parts[0], parts[1]), jnp.maximum(parts[2], parts[3]))
+        summed = sum(jnp.exp2(part - top) for part in parts)
         lse[:, cols] = top + jnp.log(summed) * LOG2E
-        delta[:, cols] = stats[d][:, 2 * total :]
+        delta[:, cols] = stats[d][:, total:]
     bias_f[...] = bias_t[...].astype(F32) * LOG2E
-    acc[...] = jnp.zeros_like(acc)
-
-    def row_step(i, carry):
+    acc[...] = jnp.zeros_like(acc) if start == 0 else acc_before[...]
+
+    def row_step(n, carry):
+        i = start + n
         dk_row, dv_row = None, None
         for d in range(X):
             cols = slice(d * width, (d + 1) * width)
-            query = q[d][i]
-            gradient = own_grad[i] if d == 0 else q[d][rows + i]
+            query, gradient = q[d][i], g[d][i]
             high, middle, low = split3(lse[pl.ds(i, 1), cols])
             extra = rows_of((high, middle, low, 1.0), 16, width).astype(BF16)
             query_all = jnp.concatenate((query, query, query, extra), axis=0)
             extra = rows_of(split3(delta[pl.ds(i, 1), cols]), 16, width).astype(BF16)
             gradient_all = jnp.concatenate((gradient, extra), axis=0)
-            probs = jnp.exp2(dot(key_t[i, :, :112], query_all, 1, 0) + bias_f[:, cols])
-            dscores = probs * dot(value_t[i, :, :48], gradient_all, 1, 0)
+            probs = jnp.exp2(dot(key_t[n, :, :112], query_all, 1, 0) + bias_f[:, cols])
+            dscores = probs * dot(value_t[n, :, :48], gradient_all, 1, 0)
             acc[:, cols] += dscores
             probs_low, dscores_low = probs.astype(BF16), dscores.astype(BF16)
             dv_part = dot(gradient, probs_low, 1, 1)
@@ -171,13 +176,15 @@
             dq_part = dot(keys[i], dscores_low[:width], 1, 0) + dot(
                 away[i], dscores_low[width:], 1, 0
             )
-            dq[d][i] = dq_part.astype(dq[d].dtype)
-        dk_own[i], dv_own[i] = dk_row[:, :width], dv_row[:, :width]
-        dkv_away[i] = dk_row[:, width:].astype(BF16)
-        dkv_away[rows + i] = dv_row[:, width:].astype(BF16)
+            dq[d][n] = dq_part.astype(dq[d].dtype)
+        dk_own[n], dv_own[n] = dk_row[:, :width], dv_row[:, :width]
+        dkv_away[n] = dk_row[:, width:].astype(BF16)
+        dkv_away[count + n] = dv_row[:, width:].astype(BF16)
         return carry
 
-    lax.fori_loop(0, rows, row_step, 0)
+    lax.fori_loop(0, count, row_step, 0)
+    if start == 0:
+        return
     for slot in range(2):
         for j in range(0, total, 128):
             tile = acc[slot * width : (slot + 1) * width, j : j + 128].T
@@ -230,77 +237,97 @@
     after = lax.optimization_barrier
 
     from_z = [lax.ppermute(bias, z_axes, z_pairs(d)) for d in range(ZLO)]
-    qg = jnp.concatenate([queries, out_grad], axis=0)
-    qg1 = fetch(qg, "x", X, 1)
-    from_z, qg1 = after((jnp.stack(from_z), qg1))
+    q1 = fetch(queries, "x", X, 1)
+    from_z, q1 = after((jnp.stack(from_z), q1))
     mask_rows = jnp.broadcast_to(key_mask.astype(BF16), (1, head, width))
-    kvm = jnp.concatenate([keys, values, mask_rows], axis=0)
-    kvm, qg, _ = after((kvm, qg, from_z))
+    km = jnp.concatenate([keys, mask_rows], axis=0)
+    km, source, _ = after((km, queries, from_z))
     here = [from_z] + [fetch(from_z, "y", Y, d) for d in range(1, Y)]
-    away = fetch(kvm, "zhi", ZHI, 1)
-    qg3 = fetch(qg, "x", X, 3)
-    qg, here[1] = after((qg, here[1]))
-    qg2 = fetch(qg, "x", X, 2)
+    away = fetch(km, "zhi", ZHI, 1)
+    q3 = fetch(source, "x", X, 3)
+    source, here[1] = after((source, here[1]))
+    q2 = fetch(source, "x", X, 2)
     there = [fetch(a, "core", CORE, 1) for a in here]
-    q = [queries, qg1, qg2, qg3]
+    grad, worth, here[1], here[2], here[3] = after((out_grad, values, *here[1:]))
+    g = [fetch(grad, "x", X, d) for d in range(1, X)]
+    away_values = fetch(worth, "zhi", ZHI, 1)
+    q = [queries, q1, q2, q3]
 
     stat, bias_t = call(
         lambda *refs: stats_kernel(scale, *refs),
         "softmax_statistics",
         [at, *q, keys, away, mask, out_grad, outputs, *here, *there],
-        [((rows, 2 * total + width), F32), ((both, total), BF16)],
+        [((rows, total + width), F32), ((both, total), BF16)],
         [((2, total, width), BF16), ((both, total), F32), ((rows, both, 128), BF16)],
         24,
     )
+    stat, g, away_values = after((stat, g, away_values))
+    g = [out_grad] + g
     stats = [stat] + [fetch(stat, "x", X, d) for d in range(1, X)]
 
-    block, pieces = (rows, head, width), (Y, ZLO, 96, width)
+    few = rows // 2
+    block, pieces = (few, head, width), (Y, ZLO, 96, width)
+    outs = [(block, F32)] + [(block, BF16)] * 3 + [(block, F32)] * 2
+    outs = outs + [((2 * few, head, width), BF16)]
+    scratch = [
+        ((both, total), F32),
+        ((few, both, 128), BF16),
+        ((few, both, 128), BF16),
+        ((rows, total), F32),
+        ((rows, total), F32),
+    ]
+    common = [at, *q, *g, keys, values, away, away_values, mask, *stats, bias_t]
     results = call(
-        lambda *refs: main_kernel(scale, *refs),
-        "attention_gradients",
-        [at, *q, out_grad, keys, values, away, mask, *stats, bias_t],
-        [(block, F32)]
-        + [(block, BF16)] * 3
-        + [(block, F32)] * 2
-        + [((2 * rows, head, width), BF16), (pieces, F32), (pieces, BF16)],
-        [
-            ((both, total), F32),
-            ((both, total), F32),
-            ((2, total, width), F32),
-            ((rows, both, 128), BF16),
-            ((rows, both, 128), BF16),
-            ((rows, total), F32),
-            ((rows, total), F32),
-        ],
+        lambda *refs: main_kernel(scale, 0, *refs),
+        "attention_gradients_low",
+        common,
+        outs + [((both, total), F32)],
+        scratch,
+        36,
+    )
+
+    def send(results):
+        dq, (dk, dv, dkv_away) = results[0:4], results[4:7]
+        arrived = fetch(dkv_away, "zhi", ZHI, 1)
+        return dq[0], [dq[d] for d in range(1, X)], dk, dv, arrived
+
+    def finish(query, others, dk, dv, arrived):
+        for part in others:
+            query = query + part.astype(F32)
+        arrived = arrived.astype(F32)
+        return scale * query, scale * (dk + arrived[:few]), dv + arrived[few:]
+
+    query0, dq0, dk0, dv0, arrived0 = send(results)
+    dq0 = [deliver(dq0[d - 1], "x", X, d) for d in range(1, X)]
+    results = call(
+        lambda *refs: main_kernel(scale, few, *refs),
+        "attention_gradients_high",
+        common + [results[7]],
+        outs + [(pieces, F32), (pieces, BF16)],
+        scratch + [((both, total), F32), ((2, total, width), F32)],
         40,
     )
-    dq, (dk, dv, dkv_away, bias_own, bias_away) = results[0:4], results[4:9]
-
+    bias_own, bias_away, dq0, arrived0 = after((results[7], results[8], dq0, arrived0))
+    query1, dq1, dk1, dv1, arrived1 = send(results)
     near = bias_own + fetch(bias_away, "core", CORE, 1).astype(F32)
-    arrived = fetch(dkv_away, "zhi", ZHI, 1)
     sent = [near[d].astype(BF16) for d in range(1, Y)]
-    sent, dq = after((sent, dq))
     far = [deliver(sent[d - 1], "y", Y, d) for d in range(1, Y)]
-    dq1 = deliver(dq[1], "x", X, 1)
+    far[0], dq1 = after((far[0], dq1))
+    dq1 = [deliver(dq1[d - 1], "x", X, d) for d in range(1, X)]
     along_y = near[0]
     for part in far:
         along_y = along_y + part.astype(F32)
-    low, arrived = after((along_y.astype(BF16), arrived))
-    dq1, dq = after((dq1, dq))
+    low, arrived1 = after((along_y.astype(BF16), arrived1))
     bias_grad = None
     for d in range(ZLO):
         pairs = [(worker, owner) for owner, worker in z_pairs(d)]
         part = lax.ppermute(low[d], z_axes, pairs).astype(F32)
         bias_grad = part if bias_grad is None else bias_grad + part
 
-    query_sum = dq[0] + dq1.astype(F32)
-    for d in (3, 2):
-        query_sum = query_sum + deliver(dq[d], "x", X, d).astype(F32)
-    arrived = arrived.astype(F32)
-    query_grad = (scale * query_sum).astype(BF16)
-    key_grad = (scale * (dk + arrived[:rows])).astype(BF16)
-    value_grad = (dv + arrived[rows:]).astype(BF16)
-    return query_grad, key_grad, value_grad, bias_grad
+    first = finish(query0, dq0, dk0, dv0, arrived0)
+    second = finish(query1, dq1, dk1, dv1, arrived1)
+    joined = [jnp.concatenate(pair, axis=0).astype(BF16) for pair in zip(first, second)]
+    return *joined, bias_grad
 
 
 def solution(mesh):

time: 162 us -> 164 us (1.012)
  waiting for transfers between devices: 40.6 us -> 33.3 us
  starting transfers between devices: 63.8 us -> 68.6 us
  local copies, waits for them, and re-layouts: 4.47 us -> 8.95 us
    ppermute x16 -> x21, waiting for transfers between devices: 30.8 us -> 10.9 us  [fetch(): lax.ppermute(x, axis, [((n + distance) % size, n) for n in range(size)])]
    ppermute x6 -> x9, waiting for transfers between devices: 1.64 us -> 13.3 us  [deliver(): lax.ppermute(x, axis, [(n, (n + distance) % size) for n in range(size)])]
    unnamed x11 -> x28, local copies, waits for them, and re-layouts: 2.63 us -> 8.74 us
    ppermute x6 -> x9, starting transfers between devices: 10.1 us -> 14.7 us  [deliver(): lax.ppermute(x, axis, [(n, (n + distance) % size) for n in range(size)])]
    ppermute x16 -> x21, starting transfers between devices: 29.1 us -> 32.9 us  [fetch(): lax.ppermute(x, axis, [((n + distance) % size, n) for n in range(size)])]
    ppermute x4, starting transfers between devices: 14.1 us -> 10.5 us  [per_device(): part = lax.ppermute(low[d], z_axes, pairs).astype(F32)]
    convert_element_type x4 -> x3, other arithmetic: 1.87 us -> 0.2 us  [the longest x1 0.14 us: per_device(): low, arrived1 = after((along_y.astype(BF16), arrived1))]
    pallas_call x2 -> x3, Pallas kernels: 44.5 us -> 45.7 us  [call(): pl.pallas_call(kernel, in_specs=[SMEM] + [VMEM] * (len(args) - 1), out_sp...]
  transfers between devices with their start and end apart: 30 -> 38, of which waited for: 14 -> 13; matrix products, arithmetic and copies ran while one was open for 3% -> 3% of each run, Pallas kernels for 0% -> 19%
where the time goes in v4:
time: 164 us; the launch traced here: 162 us
  starting transfers between devices  68.6 us (42%)
  Pallas kernels  45.7 us (28%)
  waiting for transfers between devices  33.3 us (20%)
  local copies, waits for them, and re-layouts  8.95 us (5%)
  other arithmetic  4.78 us (3%)
    pallas_call x3, Pallas kernels, call(): pl.pallas_call(kernel, in_specs=[SMEM] + [VMEM] * (len(args) - 1), out_sp...  45.7 us
    ppermute x21, starting transfers between devices, fetch(): lax.ppermute(x, axis, [((n + distance) % size, n) for n in range(size)])  32.9 us
    ppermute x9, starting transfers between devices, deliver(): lax.ppermute(x, axis, [(n, (n + distance) % size) for n in range(size)])  14.7 us
    ppermute x9, waiting for transfers between devices, deliver(): lax.ppermute(x, axis, [(n, (n + distance) % size) for n in range(size)])  13.3 us
    ppermute x21, waiting for transfers between devices, fetch(): lax.ppermute(x, axis, [((n + distance) % size, n) for n in range(size)])  10.9 us
    ppermute x4, starting transfers between devices, per_device(): from_z = [lax.ppermute(bias, z_axes, z_pairs(d)) for d in range(ZLO)]  10.6 us
    ppermute x4, starting transfers between devices, per_device(): part = lax.ppermute(low[d], z_axes, pairs).astype(F32)  10.5 us
    unnamed x28, local copies, waits for them, and re-layouts  8.74 us
  transfers between devices with their start and end apart: 38, of which 13 were waited for; matrix products, arithmetic and copies ran while one was open for 3% of the time, Pallas kernels for 19%

profile of v4, /device:TPU:64, one launch (start us, length us, event | category | flops | bytes accessed | tf_op | source)
XLA Modules:
  0.0 162.3 jit_solution(11433492778204097125)
XLA Ops:
  0.6 2.8 %collective-permute-start.4 = (bf16[8,32,384]{2,1,0:T(8,128)(2,1)}, bf16[8,32,384]{2,1,0:T(8,128)(2,1)S(1)}, u32[]{:S(2)}, u32[]{:S(2)}) collective-permute-start(bf16[8,32,384]{2,1,0:T(8,128)(2,1)} %refs_1_.5), channel_id=1, source_target_pairs={{1,0},{2,1},{3,2},{0,3},{5,4},{6,5},{7,6},{4,7},{9,8},{10,9},{11,1... | collective-permute-start | bytes 589832 | tf_op jit(solution)/shard_map/ppermute | solution.py:214
  3.5 4.9 %collective-permute-start.1 = (bf16[96,384]{1,0:T(8,128)(2,1)}, bf16[96,384]{1,0:T(8,128)(2,1)S(1)}, u32[]{:S(2)}, u32[]{:S(2)}) collective-permute-start(bf16[96,384]{1,0:T(8,128)(2,1)} %param.12), channel_id=1, source_target_pairs={{64,0},{4,64},{68,128},{0,192},{192,4},{132,68},{196,132},{128,196... | collective-permute-start | bytes 221192 | tf_op jit(solution)/shard_map/ppermute | solution.py:239
  8.4 1.9 %collective-permute-start = (bf16[96,384]{1,0:T(8,128)(2,1)}, bf16[96,384]{1,0:T(8,128)(2,1)S(1)}, u32[]{:S(2)}, u32[]{:S(2)}) collective-permute-start(bf16[96,384]{1,0:T(8,128)(2,1)} %param.12), channel_id=1, source_target_pairs={{0,0},{64,64},{4,128},{68,192},{128,4},{192,68},{132,132},{196,196... | collective-permute-start | bytes 221192 | tf_op jit(solution)/shard_map/ppermute | solution.py:239
  10.3 3.7 %collective-permute-start.3 = (bf16[96,384]{1,0:T(8,128)(2,1)}, bf16[96,384]{1,0:T(8,128)(2,1)S(1)}, u32[]{:S(2)}, u32[]{:S(2)}) collective-permute-start(bf16[96,384]{1,0:T(8,128)(2,1)} %param.12), channel_id=1, source_target_pairs={{68,0},{0,64},{64,128},{4,192},{196,4},{128,68},{192,132},{132,196... | collective-permute-start | bytes 221192 | tf_op jit(solution)/shard_map/ppermute | solution.py:239
  14.1 4.2 %collective-permute-done = bf16[96,384]{1,0:T(8,128)(2,1)S(1)} collective-permute-done((bf16[96,384]{1,0:T(8,128)(2,1)}, bf16[96,384]{1,0:T(8,128)(2,1)S(1)}, u32[]{:S(2)}, u32[]{:S(2)}) %collective-permute-start) | collective-permute-done | bytes 73760 | tf_op jit(solution)/shard_map/ppermute | solution.py:239
  18.3 1.3 collective-permute-done.2
  19.6 1.7 %collective-permute-start.10 = (bf16[4,96,384]{2,1,0:T(8,128)(2,1)S(1)}, bf16[4,96,384]{2,1,0:T(8,128)(2,1)S(1)}, u32[]{:S(2)}, u32[]{:S(2)}) collective-permute-start(bf16[4,96,384]{2,1,0:T(8,128)(2,1)S(1)} %pad_maximum_fusion.refs_10_), channel_id=1, source_target_pairs={{48,0},{0,16},{16,32},{32,48},{49,1},{1,17},{17,33},{33,49},{50,2}... | collective-permute-start | bytes 884744 | tf_op jit(solution)/shard_map/ppermute | solution.py:214
  21.3 2.9 %collective-permute-start.9 = (bf16[4,96,384]{2,1,0:T(8,128)(2,1)S(1)}, bf16[4,96,384]{2,1,0:T(8,128)(2,1)S(1)}, u32[]{:S(2)}, u32[]{:S(2)}) collective-permute-start(bf16[4,96,384]{2,1,0:T(8,128)(2,1)S(1)} %pad_maximum_fusion.refs_10_), channel_id=1, source_target_pairs={{32,0},{48,16},{0,32},{16,48},{33,1},{49,17},{1,33},{17,49},{34,2}... | collective-permute-start | bytes 884744 | tf_op jit(solution)/shard_map/ppermute | solution.py:214
  24.2 1.3 collective-permute-start.5
  25.5 0.8 fusion.11
  26.3 1.0 pad_maximum_fusion.1
  27.2 0.1 collective-permute-start.7
  27.3 4.3 %collective-permute-start.8 = (bf16[9,32,384]{2,1,0:T(8,128)(2,1)S(1)}, bf16[9,32,384]{2,1,0:T(8,128)(2,1)S(1)}, u32[]{:S(2)}, u32[]{:S(2)}) collective-permute-start(bf16[9,32,384]{2,1,0:T(8,128)(2,1)S(1)} %pad_maximum_fusion.1), channel_id=1, source_target_pairs={{4,0},{0,4},{5,1},{1,5},{6,2},{2,6},{7,3},{3,7},{12,8},{8,12},{13,... | collective-permute-start | bytes 663560 | tf_op jit(solution)/shard_map/ppermute | solution.py:214
  31.6 3.6 %collective-permute-done.9.refs_12_ = bf16[4,96,384]{2,1,0:T(8,128)(2,1)S(1)} collective-permute-done((bf16[4,96,384]{2,1,0:T(8,128)(2,1)S(1)}, bf16[4,96,384]{2,1,0:T(8,128)(2,1)S(1)}, u32[]{:S(2)}, u32[]{:S(2)}) %collective-permute-start.9) | collective-permute-done | bytes 294944 | tf_op jit(solution)/shard_map/ppermute | solution.py:214
  35.2 0.5 collective-permute-start.13
  35.8 0.8 collective-permute-start.6
  36.6 1.6 collective-permute-done.8.refs_6_.refs_11_
  38.2 0.7 copy-done.7
  38.9 3.4 %collective-permute-start.18 = (bf16[8,32,384]{2,1,0:T(8,128)(2,1)}, bf16[8,32,384]{2,1,0:T(8,128)(2,1)S(1)}, u32[]{:S(2)}, u32[]{:S(2)}) collective-permute-start(bf16[8,32,384]{2,1,0:T(8,128)(2,1)} %refs_10_.3), channel_id=1, source_target_pairs={{4,0},{0,4},{5,1},{1,5},{6,2},{2,6},{7,3},{3,7},{12,8},{8,12},{13,... | collective-permute-start | bytes 589832 | tf_op jit(solution)/shard_map/ppermute | solution.py:214
  42.3 2.0 %collective-permute-done.6.refs_3_ = bf16[8,32,384]{2,1,0:T(8,128)(2,1)S(1)} collective-permute-done((bf16[8,32,384]{2,1,0:T(8,128)(2,1)}, bf16[8,32,384]{2,1,0:T(8,128)(2,1)S(1)}, u32[]{:S(2)}, u32[]{:S(2)}) %collective-permute-start.6) | collective-permute-done | bytes 196640 | tf_op jit(solution)/shard_map/ppermute | solution.py:214
  44.4 0.7 copy-done.9
  45.1 2.5 %collective-permute-start.16 = (bf16[8,32,384]{2,1,0:T(8,128)(2,1)}, bf16[8,32,384]{2,1,0:T(8,128)(2,1)S(1)}, u32[]{:S(2)}, u32[]{:S(2)}) collective-permute-start(bf16[8,32,384]{2,1,0:T(8,128)(2,1)} %refs_5_.5), channel_id=1, source_target_pairs={{2,0},{3,1},{0,2},{1,3},{6,4},{7,5},{4,6},{5,7},{10,8},{11,9},{8,1... | collective-permute-start | bytes 589832 | tf_op jit(solution)/shard_map/ppermute | solution.py:214
  47.6 0.7 copy-done.11
  48.3 0.9 collective-permute-start.15
  49.3 0.9 copy-done
  50.2 0.9 copy-done.2
  51.2 0.9 copy-done.4
  52.1 1.0 copy-done.8
  53.1 1.0 copy-done.10
  54.0 1.0 copy-done.12
  55.0 0.9 copy-done.13
  55.9 13.3 %softmax_statistics.1 = (f32[8,1920]{1,0:T(8,128)S(1)}, bf16[768,1536]{1,0:T(8,128)(2,1)S(1)}) custom-call(s32[5]{0:T(128)S(1)} %stack.38.refs_0_, bf16[8,32,384]{2,1,0:T(8,128)(2,1)S(1)} %copy-done.2, bf16[8,32,384]{2,1,0:T(8,128)(2,1)S(1)} %collective-permute-done.4.refs_2_, bf16[8,32,384]{2,1,0:T(8,128)(2,1)S(1)} %collective-permute-done.6.refs_3_, ...), custom_call_target="tpu_custom_call" | custom-call | tf_op jit(solution)/shard_map/softmax_statistics/pallas_call | solution.py:202
  69.2 1.2 collective-permute-start.21
  70.4 1.7 %collective-permute-start.20 = (f32[8,1920]{1,0:T(8,128)S(1)}, f32[8,1920]{1,0:T(8,128)S(1)}, u32[]{:S(2)}, u32[]{:S(2)}) collective-permute-start(f32[8,1920]{1,0:T(8,128)S(1)} %get-tuple-element.67.refs_14_), channel_id=1, source_target_pairs={{2,0},{3,1},{0,2},{1,3},{6,4},{7,5},{4,6},{5,7},{10,8},{11,9},{8,1... | collective-permute-start | bytes 184328 | tf_op jit(solution)/shard_map/ppermute | solution.py:214
  72.1 2.5 %collective-permute-start.19 = (f32[8,1920]{1,0:T(8,128)S(1)}, f32[8,1920]{1,0:T(8,128)S(1)}, u32[]{:S(2)}, u32[]{:S(2)}) collective-permute-start(f32[8,1920]{1,0:T(8,128)S(1)} %get-tuple-element.67.refs_14_), channel_id=1, source_target_pairs={{1,0},{2,1},{3,2},{0,3},{5,4},{6,5},{7,6},{4,7},{9,8},{10,9},{11,1... | collective-permute-start | bytes 184328 | tf_op jit(solution)/shard_map/ppermute | solution.py:214
  74.7 0.5 collective-permute-done.21.refs_17_
  75.2 1.0 collective-permute-done.20.refs_16_
  76.2 0.4 collective-permute-done.19.refs_15_
  76.5 15.5 %attention_gradients_low.1 = (f32[4,32,384]{2,1,0:T(8,128)S(1)}, bf16[4,32,384]{2,1,0:T(8,128)(2,1)S(1)}, bf16[4,32,384]{2,1,0:T(8,128)(2,1)S(1)}, bf16[4,32,384...) custom-call(s32[5]{0:T(128)S(1)} %stack.38.refs_0_, ...), custom_call_target="tpu_custom_call" | custom-call | tf_op jit(solution)/shard_map/attention_gradients_low/pallas_call | solution.py:202
  92.0 5.0 %collective-permute-start.25 = (bf16[8,32,384]{2,1,0:T(8,128)(2,1)S(1)}, bf16[8,32,384]{2,1,0:T(8,128)(2,1)S(1)}, u32[]{:S(2)}, u32[]{:S(2)}) collective-permute-start(bf16[8,32,384]{2,1,0:T(8,128)(2,1)S(1)} %get-tuple-element.76), channel_id=1, source_target_pairs={{4,0},{0,4},{5,1},{1,5},{6,2},{2,6},{7,3},{3,7},{12,8},{8,12},{13,... | collective-permute-start | bytes 589832 | tf_op jit(solution)/shard_map/ppermute | solution.py:214
  97.0 1.8 %collective-permute-start.22 = (bf16[4,32,384]{2,1,0:T(8,128)(2,1)S(1)}, bf16[4,32,384]{2,1,0:T(8,128)(2,1)S(1)}, u32[]{:S(2)}, u32[]{:S(2)}) collective-permute-start(bf16[4,32,384]{2,1,0:T(8,128)(2,1)S(1)} %get-tuple-element.73), channel_id=1, source_target_pairs={{0,1},{1,2},{2,3},{3,0},{4,5},{5,6},{6,7},{7,4},{8,9},{9,10},{10,1... | collective-permute-start | bytes 294920 | tf_op jit(solution)/shard_map/ppermute | solution.py:218
  98.7 3.3 %collective-permute-start.23 = (bf16[4,32,384]{2,1,0:T(8,128)(2,1)S(1)}, bf16[4,32,384]{2,1,0:T(8,128)(2,1)S(1)}, u32[]{:S(2)}, u32[]{:S(2)}) collective-permute-start(bf16[4,32,384]{2,1,0:T(8,128)(2,1)S(1)} %get-tuple-element.74), channel_id=1, source_target_pairs={{0,2},{1,3},{2,0},{3,1},{4,6},{5,7},{6,4},{7,5},{8,10},{9,11},{10,... | collective-permute-start | bytes 294920 | tf_op jit(solution)/shard_map/ppermute | solution.py:218
  102.1 17.0 %attention_gradients_high.1 = (f32[4,32,384]{2,1,0:T(8,128)S(1)}, bf16[4,32,384]{2,1,0:T(8,128)(2,1)S(1)}, bf16[4,32,384]{2,1,0:T(8,128)(2,1)S(1)}, bf16[4,32,38...) custom-call(s32[5]{0:T(128)S(1)} %stack.38.refs_0_, ...), custom_call_target="tpu_custom_call" | custom-call | tf_op jit(solution)/shard_map/attention_gradients_high/pallas_call | solution.py:202
  119.1 0.1 collective-permute-start.26
  119.2 1.1 collective-permute-start.33
  120.3 1.7 %collective-permute-done.26 = bf16[4,4,96,384]{3,2,1,0:T(8,128)(2,1)S(1)} collective-permute-done((bf16[4,4,96,384]{3,2,1,0:T(8,128)(2,1)S(1)}, bf16[4,4,96,384]{3,2,1,0:T(8,128)(2,1)S(1)}, u32[]{:S(2)}, u32[]{:S(2)}) %collective-permute-start.26) | collective-permute-done | bytes 1179680 | tf_op jit(solution)/shard_map/ppermute | solution.py:214
  122.0 0.4 fusion.10
  122.4 0.1 slice_bitcast_fusion.2
  122.5 2.7 %collective-permute-start.31 = (bf16[4,96,384]{2,1,0:T(8,128)(2,1)S(1)}, bf16[4,96,384]{2,1,0:T(8,128)(2,1)S(1)}, u32[]{:S(2)}, u32[]{:S(2)}) collective-permute-start(bf16[4,96,384]{2,1,0:T(8,128)(2,1)S(1)} %get-tuple-element.100), channel_id=1, source_target_pairs={{0,32},{16,48},{32,0},{48,16},{1,33},{17,49},{33,1},{49,17},{2,34}... | collective-permute-start | bytes 884744 | tf_op jit(solution)/shard_map/ppermute | solution.py:218
  125.2 1.3 collective-permute-start.32
  126.6 0.7 collective-permute-start.27
  127.4 12.1 %collective-permute-done.27 = bf16[4,96,384]{2,1,0:T(8,128)(2,1)S(1)} collective-permute-done((bf16[4,96,384]{2,1,0:T(8,128)(2,1)S(1)}, bf16[4,96,384]{2,1,0:T(8,128)(2,1)S(1)}, u32[]{:S(2)}, u32[]{:S(2)}) %collective-permute-start.27) | collective-permute-done | bytes 294944 | tf_op jit(solution)/shard_map/ppermute | solution.py:218
  139.5 0.1 fusion.3
  139.7 2.0 %collective-permute-start.28 = (bf16[4,32,384]{2,1,0:T(8,128)(2,1)S(1)}, bf16[4,32,384]{2,1,0:T(8,128)(2,1)S(1)}, u32[]{:S(2)}, u32[]{:S(2)}) collective-permute-start(bf16[4,32,384]{2,1,0:T(8,128)(2,1)S(1)} %get-tuple-element.86), channel_id=1, source_target_pairs={{0,1},{1,2},{2,3},{3,0},{4,5},{5,6},{6,7},{7,4},{8,9},{9,10},{10,1... | collective-permute-start | bytes 294920 | tf_op jit(solution)/shard_map/ppermute | solution.py:218
  141.8 4.6 %collective-permute-start.34 = (bf16[96,384]{1,0:T(8,128)(2,1)S(1)}, bf16[96,384]{1,0:T(8,128)(2,1)S(1)}, u32[]{:S(2)}, u32[]{:S(2)}) collective-permute-start(bf16[96,384]{1,0:T(8,128)(2,1)S(1)} %get-tuple-element.107), channel_id=1, source_target_pairs={{0,0},{64,64},{128,4},{192,68},{4,128},{68,192},{132,132},{196,196... | collective-permute-start | bytes 221192 | tf_op jit(solution)/shard_map/ppermute | solution.py:324
  146.5 5.8 %collective-permute-start.36 = (bf16[96,384]{1,0:T(8,128)(2,1)S(1)}, bf16[96,384]{1,0:T(8,128)(2,1)S(1)}, u32[]{:S(2)}, u32[]{:S(2)}) collective-permute-start(bf16[96,384]{1,0:T(8,128)(2,1)S(1)} %get-tuple-element.109), channel_id=1, source_target_pairs={{0,4},{64,68},{128,0},{192,64},{4,132},{68,196},{132,128},{196,192... | collective-permute-start | bytes 221192 | tf_op jit(solution)/shard_map/ppermute | solution.py:324
  152.3 0.8 pad_maximum_fusion.3
  153.1 0.4 collective-permute-start.29
  153.5 3.4 %collective-permute-done.37 = bf16[96,384]{1,0:T(8,128)(2,1)S(1)} collective-permute-done((bf16[96,384]{1,0:T(8,128)(2,1)S(1)}, bf16[96,384]{1,0:T(8,128)(2,1)S(1)}, u32[]{:S(2)}, u32[]{:S(2)}) %collective-permute-start.37) | collective-permute-done | bytes 73760 | tf_op jit(solution)/shard_map/ppermute | solution.py:324
  156.9 2.5 %collective-permute-start.30 = (bf16[4,32,384]{2,1,0:T(8,128)(2,1)S(1)}, bf16[4,32,384]{2,1,0:T(8,128)(2,1)S(1)}, u32[]{:S(2)}, u32[]{:S(2)}) collective-permute-start(bf16[4,32,384]{2,1,0:T(8,128)(2,1)S(1)} %get-tuple-element.88), channel_id=1, source_target_pairs={{0,3},{1,0},{2,1},{3,2},{4,7},{5,4},{6,5},{7,6},{8,11},{9,8},{10,9... | collective-permute-start | bytes 294920 | tf_op jit(solution)/shard_map/ppermute | solution.py:218
  159.4 0.3 collective-permute-done.35
  159.6 0.7 convert_add_fusion.1
  160.3 1.2 collective-permute-done.30
  161.6 0.7 pad_maximum_fusion.2
  (62 shorter events, 0.7 us)
Async XLA Ops:
  0.6 19.0 %collective-permute-start.4 = (bf16[8,32,384]{2,1,0:T(8,128)(2,1)}, bf16[8,32,384]{2,1,0:T(8,128)(2,1)S(1)}, u32[]{:S(2)}, u32[]{:S(2)}) collective-permute-start(bf16[8,32,384]{2,1,0:T(8,128)(2,1)} %refs_1_.5), channel_id=1, source_target_pairs={{1,0},{2,1},{3,2},{0,3},{5,4},{6,5},{7,6},{4,7},{9,8},{10,9},{11,1... | collective-permute-start | bytes 589832 | tf_op jit(solution)/shard_map/ppermute | solution.py:214
  3.5 10.6 %collective-permute-start.1 = (bf16[96,384]{1,0:T(8,128)(2,1)}, bf16[96,384]{1,0:T(8,128)(2,1)S(1)}, u32[]{:S(2)}, u32[]{:S(2)}) collective-permute-start(bf16[96,384]{1,0:T(8,128)(2,1)} %param.12), channel_id=1, source_target_pairs={{64,0},{4,64},{68,128},{0,192},{192,4},{132,68},{196,132},{128,196... | collective-permute-start | bytes 221192 | tf_op jit(solution)/shard_map/ppermute | solution.py:239
  8.4 9.8 %collective-permute-start = (bf16[96,384]{1,0:T(8,128)(2,1)}, bf16[96,384]{1,0:T(8,128)(2,1)S(1)}, u32[]{:S(2)}, u32[]{:S(2)}) collective-permute-start(bf16[96,384]{1,0:T(8,128)(2,1)} %param.12), channel_id=1, source_target_pairs={{0,0},{64,64},{4,128},{68,192},{128,4},{192,68},{132,132},{196,196... | collective-permute-start | bytes 221192 | tf_op jit(solution)/shard_map/ppermute | solution.py:239
  10.3 7.9 %collective-permute-start.3 = (bf16[96,384]{1,0:T(8,128)(2,1)}, bf16[96,384]{1,0:T(8,128)(2,1)S(1)}, u32[]{:S(2)}, u32[]{:S(2)}) collective-permute-start(bf16[96,384]{1,0:T(8,128)(2,1)} %param.12), channel_id=1, source_target_pairs={{68,0},{0,64},{64,128},{4,192},{196,4},{128,68},{192,132},{132,196... | collective-permute-start | bytes 221192 | tf_op jit(solution)/shard_map/ppermute | solution.py:239
  14.1 5.5 %collective-permute-start.2 = (bf16[96,384]{1,0:T(8,128)(2,1)}, bf16[96,384]{1,0:T(8,128)(2,1)S(1)}, u32[]{:S(2)}, u32[]{:S(2)}) collective-permute-start(bf16[96,384]{1,0:T(8,128)(2,1)} %param.12), channel_id=1, source_target_pairs={{4,0},{68,64},{0,128},{64,192},{132,4},{196,68},{128,132},{192,196... | collective-permute-start | bytes 221192 | tf_op jit(solution)/shard_map/ppermute | solution.py:239
  19.5 57.0 %copy-start.5 = (bf16[8,32,384]{2,1,0:T(8,128)(2,1)S(1)}, bf16[8,32,384]{2,1,0:T(8,128)(2,1)}, u32[]{:S(2)}) copy-start(bf16[8,32,384]{2,1,0:T(8,128)(2,1)} %refs_5_.5) | copy-start | bytes 589828
  19.5 57.0 %copy-start.6 = (bf16[8,32,384]{2,1,0:T(8,128)(2,1)S(1)}, bf16[8,32,384]{2,1,0:T(8,128)(2,1)}, u32[]{:S(2)}) copy-start(bf16[8,32,384]{2,1,0:T(8,128)(2,1)} %refs_10_.3) | copy-start | bytes 589828
  19.6 57.0 %copy-start.1 = (bf16[8,32,384]{2,1,0:T(8,128)(2,1)S(1)}, bf16[8,32,384]{2,1,0:T(8,128)(2,1)}, u32[]{:S(2)}) copy-start(bf16[8,32,384]{2,1,0:T(8,128)(2,1)} %refs_9_.5) | copy-start | bytes 589828
  19.6 56.9 %copy-start.3 = (bf16[8,32,384]{2,1,0:T(8,128)(2,1)S(1)}, bf16[8,32,384]{2,1,0:T(8,128)(2,1)}, u32[]{:S(2)}) copy-start(bf16[8,32,384]{2,1,0:T(8,128)(2,1)} %refs_1_.5) | copy-start | bytes 589828
  19.6 12.0 %collective-permute-start.10 = (bf16[4,96,384]{2,1,0:T(8,128)(2,1)S(1)}, bf16[4,96,384]{2,1,0:T(8,128)(2,1)S(1)}, u32[]{:S(2)}, u32[]{:S(2)}) collective-permute-start(bf16[4,96,384]{2,1,0:T(8,128)(2,1)S(1)} %pad_maximum_fusion.refs_10_), channel_id=1, source_target_pairs={{48,0},{0,16},{16,32},{32,48},{49,1},{1,17},{17,33},{33,49},{50,2}... | collective-permute-start | bytes 884744 | tf_op jit(solution)/shard_map/ppermute | solution.py:214
  21.3 14.0 %collective-permute-start.9 = (bf16[4,96,384]{2,1,0:T(8,128)(2,1)S(1)}, bf16[4,96,384]{2,1,0:T(8,128)(2,1)S(1)}, u32[]{:S(2)}, u32[]{:S(2)}) collective-permute-start(bf16[4,96,384]{2,1,0:T(8,128)(2,1)S(1)} %pad_maximum_fusion.refs_10_), channel_id=1, source_target_pairs={{32,0},{48,16},{0,32},{16,48},{33,1},{49,17},{1,33},{17,49},{34,2}... | collective-permute-start | bytes 884744 | tf_op jit(solution)/shard_map/ppermute | solution.py:214
  24.2 11.1 %collective-permute-start.5 = (bf16[4,96,384]{2,1,0:T(8,128)(2,1)S(1)}, bf16[4,96,384]{2,1,0:T(8,128)(2,1)}, u32[]{:S(2)}, u32[]{:S(2)}) collective-permute-start(bf16[4,96,384]{2,1,0:T(8,128)(2,1)S(1)} %pad_maximum_fusion.refs_10_), channel_id=1, source_target_pairs={{16,0},{32,16},{48,32},{0,48},{17,1},{33,17},{49,33},{1,49},{18,2}... | collective-permute-start | bytes 884744 | tf_op jit(solution)/shard_map/ppermute | solution.py:214
  27.2 8.5 %collective-permute-start.7 = (bf16[8,32,384]{2,1,0:T(8,128)(2,1)}, bf16[8,32,384]{2,1,0:T(8,128)(2,1)S(1)}, u32[]{:S(2)}, u32[]{:S(2)}) collective-permute-start(bf16[8,32,384]{2,1,0:T(8,128)(2,1)} %refs_1_.5), channel_id=1, source_target_pairs={{3,0},{0,1},{1,2},{2,3},{7,4},{4,5},{5,6},{6,7},{11,8},{8,9},{9,10... | collective-permute-start | bytes 589832 | tf_op jit(solution)/shard_map/ppermute | solution.py:214
  27.3 10.8 %collective-permute-start.8 = (bf16[9,32,384]{2,1,0:T(8,128)(2,1)S(1)}, bf16[9,32,384]{2,1,0:T(8,128)(2,1)S(1)}, u32[]{:S(2)}, u32[]{:S(2)}) collective-permute-start(bf16[9,32,384]{2,1,0:T(8,128)(2,1)S(1)} %pad_maximum_fusion.1), channel_id=1, source_target_pairs={{4,0},{0,4},{5,1},{1,5},{6,2},{2,6},{7,3},{3,7},{12,8},{8,12},{13,... | collective-permute-start | bytes 663560 | tf_op jit(solution)/shard_map/ppermute | solution.py:214
  31.6 6.5 %collective-permute-start.11 = (bf16[4,96,384]{2,1,0:T(8,128)(2,1)S(1)}, bf16[4,96,384]{2,1,0:T(8,128)(2,1)S(1)}, u32[]{:S(2)}, u32[]{:S(2)}) collective-permute-start(bf16[4,96,384]{2,1,0:T(8,128)(2,1)S(1)} %pad_maximum_fusion.refs_10_), channel_id=1, source_target_pairs={{8,0},{0,8},{9,1},{1,9},{10,2},{2,10},{11,3},{3,11},{12,4},{4,12},... | collective-permute-start | bytes 884744 | tf_op jit(solution)/shard_map/ppermute | solution.py:214
  35.2 9.1 %collective-permute-start.14 = (bf16[4,96,384]{2,1,0:T(8,128)(2,1)S(1)}, bf16[4,96,384]{2,1,0:T(8,128)(2,1)S(1)}, u32[]{:S(2)}, u32[]{:S(2)}) collective-permute-start(bf16[4,96,384]{2,1,0:T(8,128)(2,1)S(1)} %collective-permute-done.10.refs_13_), channel_id=1, source_target_pairs={{8,0},{0,8},{9,1},{1,9},{10,2},{2,10},{11,3},{3,11},{12,4},{4,12},... | collective-permute-start | bytes 884744 | tf_op jit(solution)/shard_map/ppermute | solution.py:214
  35.2 12.4 %collective-permute-start.13 = (bf16[4,96,384]{2,1,0:T(8,128)(2,1)S(1)}, bf16[4,96,384]{2,1,0:T(8,128)(2,1)S(1)}, u32[]{:S(2)}, u32[]{:S(2)}) collective-permute-start(bf16[4,96,384]{2,1,0:T(8,128)(2,1)S(1)} %collective-permute-done.9.refs_12_), channel_id=1, source_target_pairs={{8,0},{0,8},{9,1},{1,9},{10,2},{2,10},{11,3},{3,11},{12,4},{4,12},... | collective-permute-start | bytes 884744 | tf_op jit(solution)/shard_map/ppermute | solution.py:214
  35.8 8.6 %collective-permute-start.6 = (bf16[8,32,384]{2,1,0:T(8,128)(2,1)}, bf16[8,32,384]{2,1,0:T(8,128)(2,1)S(1)}, u32[]{:S(2)}, u32[]{:S(2)}) collective-permute-start(bf16[8,32,384]{2,1,0:T(8,128)(2,1)} %refs_1_.5), channel_id=1, source_target_pairs={{2,0},{3,1},{0,2},{1,3},{6,4},{7,5},{4,6},{5,7},{10,8},{11,9},{8,1... | collective-permute-start | bytes 589832 | tf_op jit(solution)/shard_map/ppermute | solution.py:214
  38.2 11.2 %collective-permute-start.12 = (bf16[4,96,384]{2,1,0:T(8,128)(2,1)}, bf16[4,96,384]{2,1,0:T(8,128)(2,1)}, u32[]{:S(2)}, u32[]{:S(2)}) collective-permute-start(bf16[4,96,384]{2,1,0:T(8,128)(2,1)} %collective-permute-done.5.refs_11_), channel_id=1, source_target_pairs={{8,0},{0,8},{9,1},{1,9},{10,2},{2,10},{11,3},{3,11},{12,4},{4,12},... | collective-permute-start | bytes 884744 | tf_op jit(solution)/shard_map/ppermute | solution.py:214
  38.2 0.7 copy-start.7
  38.9 30.3 %collective-permute-start.18 = (bf16[8,32,384]{2,1,0:T(8,128)(2,1)}, bf16[8,32,384]{2,1,0:T(8,128)(2,1)S(1)}, u32[]{:S(2)}, u32[]{:S(2)}) collective-permute-start(bf16[8,32,384]{2,1,0:T(8,128)(2,1)} %refs_10_.3), channel_id=1, source_target_pairs={{4,0},{0,4},{5,1},{1,5},{6,2},{2,6},{7,3},{3,7},{12,8},{8,12},{13,... | collective-permute-start | bytes 589832 | tf_op jit(solution)/shard_map/ppermute | solution.py:214
  44.4 24.8 %collective-permute-start.17 = (bf16[8,32,384]{2,1,0:T(8,128)(2,1)}, bf16[8,32,384]{2,1,0:T(8,128)(2,1)S(1)}, u32[]{:S(2)}, u32[]{:S(2)}) collective-permute-start(bf16[8,32,384]{2,1,0:T(8,128)(2,1)} %refs_5_.5), channel_id=1, source_target_pairs={{3,0},{0,1},{1,2},{2,3},{7,4},{4,5},{5,6},{6,7},{11,8},{8,9},{9,10... | collective-permute-start | bytes 589832 | tf_op jit(solution)/shard_map/ppermute | solution.py:214
  44.4 0.7 copy-start.9
  45.1 24.1 %collective-permute-start.16 = (bf16[8,32,384]{2,1,0:T(8,128)(2,1)}, bf16[8,32,384]{2,1,0:T(8,128)(2,1)S(1)}, u32[]{:S(2)}, u32[]{:S(2)}) collective-permute-start(bf16[8,32,384]{2,1,0:T(8,128)(2,1)} %refs_5_.5), channel_id=1, source_target_pairs={{2,0},{3,1},{0,2},{1,3},{6,4},{7,5},{4,6},{5,7},{10,8},{11,9},{8,1... | collective-permute-start | bytes 589832 | tf_op jit(solution)/shard_map/ppermute | solution.py:214
  47.6 0.7 copy-start.11
  48.3 20.9 %collective-permute-start.15 = (bf16[8,32,384]{2,1,0:T(8,128)(2,1)}, bf16[8,32,384]{2,1,0:T(8,128)(2,1)S(1)}, u32[]{:S(2)}, u32[]{:S(2)}) collective-permute-start(bf16[8,32,384]{2,1,0:T(8,128)(2,1)} %refs_5_.5), channel_id=1, source_target_pairs={{1,0},{2,1},{3,2},{0,3},{5,4},{6,5},{7,6},{4,7},{9,8},{10,9},{11,1... | collective-permute-start | bytes 589832 | tf_op jit(solution)/shard_map/ppermute | solution.py:214
  49.3 0.9 copy-start
  50.2 0.9 copy-start.2
  51.2 0.9 copy-start.4
  52.1 1.0 copy-start.8
  53.1 1.0 copy-start.10
  54.0 1.0 copy-start.12
  55.0 0.9 copy-start.13
  69.2 6.0 %collective-permute-start.21 = (f32[8,1920]{1,0:T(8,128)S(1)}, f32[8,1920]{1,0:T(8,128)S(1)}, u32[]{:S(2)}, u32[]{:S(2)}) collective-permute-start(f32[8,1920]{1,0:T(8,128)S(1)} %get-tuple-element.67.refs_14_), channel_id=1, source_target_pairs={{3,0},{0,1},{1,2},{2,3},{7,4},{4,5},{5,6},{6,7},{11,8},{8,9},{9,10... | collective-permute-start | bytes 184328 | tf_op jit(solution)/shard_map/ppermute | solution.py:214
  70.4 5.7 %collective-permute-start.20 = (f32[8,1920]{1,0:T(8,128)S(1)}, f32[8,1920]{1,0:T(8,128)S(1)}, u32[]{:S(2)}, u32[]{:S(2)}) collective-permute-start(f32[8,1920]{1,0:T(8,128)S(1)} %get-tuple-element.67.refs_14_), channel_id=1, source_target_pairs={{2,0},{3,1},{0,2},{1,3},{6,4},{7,5},{4,6},{5,7},{10,8},{11,9},{8,1... | collective-permute-start | bytes 184328 | tf_op jit(solution)/shard_map/ppermute | solution.py:214
  72.1 4.4 %collective-permute-start.19 = (f32[8,1920]{1,0:T(8,128)S(1)}, f32[8,1920]{1,0:T(8,128)S(1)}, u32[]{:S(2)}, u32[]{:S(2)}) collective-permute-start(f32[8,1920]{1,0:T(8,128)S(1)} %get-tuple-element.67.refs_14_), channel_id=1, source_target_pairs={{1,0},{2,1},{3,2},{0,3},{5,4},{6,5},{7,6},{4,7},{9,8},{10,9},{11,1... | collective-permute-start | bytes 184328 | tf_op jit(solution)/shard_map/ppermute | solution.py:214
  92.0 27.1 %collective-permute-start.25 = (bf16[8,32,384]{2,1,0:T(8,128)(2,1)S(1)}, bf16[8,32,384]{2,1,0:T(8,128)(2,1)S(1)}, u32[]{:S(2)}, u32[]{:S(2)}) collective-permute-start(bf16[8,32,384]{2,1,0:T(8,128)(2,1)S(1)} %get-tuple-element.76), channel_id=1, source_target_pairs={{4,0},{0,4},{5,1},{1,5},{6,2},{2,6},{7,3},{3,7},{12,8},{8,12},{13,... | collective-permute-start | bytes 589832 | tf_op jit(solution)/shard_map/ppermute | solution.py:214
  97.0 22.1 %collective-permute-start.22 = (bf16[4,32,384]{2,1,0:T(8,128)(2,1)S(1)}, bf16[4,32,384]{2,1,0:T(8,128)(2,1)S(1)}, u32[]{:S(2)}, u32[]{:S(2)}) collective-permute-start(bf16[4,32,384]{2,1,0:T(8,128)(2,1)S(1)} %get-tuple-element.73), channel_id=1, source_target_pairs={{0,1},{1,2},{2,3},{3,0},{4,5},{5,6},{6,7},{7,4},{8,9},{9,10},{10,1... | collective-permute-start | bytes 294920 | tf_op jit(solution)/shard_map/ppermute | solution.py:218
  98.7 20.3 %collective-permute-start.23 = (bf16[4,32,384]{2,1,0:T(8,128)(2,1)S(1)}, bf16[4,32,384]{2,1,0:T(8,128)(2,1)S(1)}, u32[]{:S(2)}, u32[]{:S(2)}) collective-permute-start(bf16[4,32,384]{2,1,0:T(8,128)(2,1)S(1)} %get-tuple-element.74), channel_id=1, source_target_pairs={{0,2},{1,3},{2,0},{3,1},{4,6},{5,7},{6,4},{7,5},{8,10},{9,11},{10,... | collective-permute-start | bytes 294920 | tf_op jit(solution)/shard_map/ppermute | solution.py:218
  102.0 17.1 %collective-permute-start.24 = (bf16[4,32,384]{2,1,0:T(8,128)(2,1)S(1)}, bf16[4,32,384]{2,1,0:T(8,128)(2,1)S(1)}, u32[]{:S(2)}, u32[]{:S(2)}) collective-permute-start(bf16[4,32,384]{2,1,0:T(8,128)(2,1)S(1)} %get-tuple-element.75), channel_id=1, source_target_pairs={{0,3},{1,0},{2,1},{3,2},{4,7},{5,4},{6,5},{7,6},{8,11},{9,8},{10,9... | collective-permute-start | bytes 294920 | tf_op jit(solution)/shard_map/ppermute | solution.py:218
  119.1 2.9 %collective-permute-start.26 = (bf16[4,4,96,384]{3,2,1,0:T(8,128)(2,1)S(1)}, bf16[4,4,96,384]{3,2,1,0:T(8,128)(2,1)S(1)}, u32[]{:S(2)}, u32[]{:S(2)}) collective-permute-start(bf16[4,4,96,384]{3,2,1,0:T(8,128)(2,1)S(1)} %get-tuple-element.82), channel_id=1, source_target_pairs={{8,0},{0,8},{9,1},{1,9},{10,2},{2,10},{11,3},{3,11},{12,4},{4,12},... | collective-permute-start | bytes 3538952 | tf_op jit(solution)/shard_map/ppermute | solution.py:214
  119.2 20.4 %collective-permute-start.33 = (bf16[8,32,384]{2,1,0:T(8,128)(2,1)S(1)}, bf16[8,32,384]{2,1,0:T(8,128)(2,1)S(1)}, u32[]{:S(2)}, u32[]{:S(2)}) collective-permute-start(bf16[8,32,384]{2,1,0:T(8,128)(2,1)S(1)} %get-tuple-element.93), channel_id=1, source_target_pairs={{4,0},{0,4},{5,1},{1,5},{6,2},{2,6},{7,3},{3,7},{12,8},{8,12},{13,... | collective-permute-start | bytes 589832 | tf_op jit(solution)/shard_map/ppermute | solution.py:214
  122.5 17.0 %collective-permute-start.31 = (bf16[4,96,384]{2,1,0:T(8,128)(2,1)S(1)}, bf16[4,96,384]{2,1,0:T(8,128)(2,1)S(1)}, u32[]{:S(2)}, u32[]{:S(2)}) collective-permute-start(bf16[4,96,384]{2,1,0:T(8,128)(2,1)S(1)} %get-tuple-element.100), channel_id=1, source_target_pairs={{0,32},{16,48},{32,0},{48,16},{1,33},{17,49},{33,1},{49,17},{2,34}... | collective-permute-start | bytes 884744 | tf_op jit(solution)/shard_map/ppermute | solution.py:218
  125.2 14.3 %collective-permute-start.32 = (bf16[4,96,384]{2,1,0:T(8,128)(2,1)S(1)}, bf16[4,96,384]{2,1,0:T(8,128)(2,1)S(1)}, u32[]{:S(2)}, u32[]{:S(2)}) collective-permute-start(bf16[4,96,384]{2,1,0:T(8,128)(2,1)S(1)} %get-tuple-element.101), channel_id=1, source_target_pairs={{0,48},{16,0},{32,16},{48,32},{1,49},{17,1},{33,17},{49,33},{2,50}... | collective-permute-start | bytes 884744 | tf_op jit(solution)/shard_map/ppermute | solution.py:218
  126.6 12.9 %collective-permute-start.27 = (bf16[4,96,384]{2,1,0:T(8,128)(2,1)S(1)}, bf16[4,96,384]{2,1,0:T(8,128)(2,1)S(1)}, u32[]{:S(2)}, u32[]{:S(2)}) collective-permute-start(bf16[4,96,384]{2,1,0:T(8,128)(2,1)S(1)} %get-tuple-element.102), channel_id=1, source_target_pairs={{0,16},{16,32},{32,48},{48,0},{1,17},{17,33},{33,49},{49,1},{2,18}... | collective-permute-start | bytes 884744 | tf_op jit(solution)/shard_map/ppermute | solution.py:218
  139.7 20.7 %collective-permute-start.28 = (bf16[4,32,384]{2,1,0:T(8,128)(2,1)S(1)}, bf16[4,32,384]{2,1,0:T(8,128)(2,1)S(1)}, u32[]{:S(2)}, u32[]{:S(2)}) collective-permute-start(bf16[4,32,384]{2,1,0:T(8,128)(2,1)S(1)} %get-tuple-element.86), channel_id=1, source_target_pairs={{0,1},{1,2},{2,3},{3,0},{4,5},{5,6},{6,7},{7,4},{8,9},{9,10},{10,1... | collective-permute-start | bytes 294920 | tf_op jit(solution)/shard_map/ppermute | solution.py:218
  141.8 11.3 %collective-permute-start.34 = (bf16[96,384]{1,0:T(8,128)(2,1)S(1)}, bf16[96,384]{1,0:T(8,128)(2,1)S(1)}, u32[]{:S(2)}, u32[]{:S(2)}) collective-permute-start(bf16[96,384]{1,0:T(8,128)(2,1)S(1)} %get-tuple-element.107), channel_id=1, source_target_pairs={{0,0},{64,64},{128,4},{192,68},{4,128},{68,192},{132,132},{196,196... | collective-permute-start | bytes 221192 | tf_op jit(solution)/shard_map/ppermute | solution.py:324
  146.4 10.5 %collective-permute-start.37 = (bf16[96,384]{1,0:T(8,128)(2,1)S(1)}, bf16[96,384]{1,0:T(8,128)(2,1)S(1)}, u32[]{:S(2)}, u32[]{:S(2)}) collective-permute-start(bf16[96,384]{1,0:T(8,128)(2,1)S(1)} %get-tuple-element.108), channel_id=1, source_target_pairs={{0,68},{64,0},{128,64},{192,4},{4,196},{68,128},{132,192},{196,132... | collective-permute-start | bytes 221192 | tf_op jit(solution)/shard_map/ppermute | solution.py:324
  146.5 12.9 %collective-permute-start.36 = (bf16[96,384]{1,0:T(8,128)(2,1)S(1)}, bf16[96,384]{1,0:T(8,128)(2,1)S(1)}, u32[]{:S(2)}, u32[]{:S(2)}) collective-permute-start(bf16[96,384]{1,0:T(8,128)(2,1)S(1)} %get-tuple-element.109), channel_id=1, source_target_pairs={{0,4},{64,68},{128,0},{192,64},{4,132},{68,196},{132,128},{196,192... | collective-permute-start | bytes 221192 | tf_op jit(solution)/shard_map/ppermute | solution.py:324
  152.3 7.4 %collective-permute-start.35 = (bf16[96,384]{1,0:T(8,128)(2,1)S(1)}, bf16[96,384]{1,0:T(8,128)(2,1)S(1)}, u32[]{:S(2)}, u32[]{:S(2)}) collective-permute-start(bf16[96,384]{1,0:T(8,128)(2,1)S(1)} %get-tuple-element.110), channel_id=1, source_target_pairs={{0,64},{64,4},{128,68},{192,0},{4,192},{68,132},{132,196},{196,128... | collective-permute-start | bytes 221192 | tf_op jit(solution)/shard_map/ppermute | solution.py:324
  153.1 7.2 %collective-permute-start.29 = (bf16[4,32,384]{2,1,0:T(8,128)(2,1)S(1)}, bf16[4,32,384]{2,1,0:T(8,128)(2,1)S(1)}, u32[]{:S(2)}, u32[]{:S(2)}) collective-permute-start(bf16[4,32,384]{2,1,0:T(8,128)(2,1)S(1)} %get-tuple-element.87), channel_id=1, source_target_pairs={{0,2},{1,3},{2,0},{3,1},{4,6},{5,7},{6,4},{7,5},{8,10},{9,11},{10,... | collective-permute-start | bytes 294920 | tf_op jit(solution)/shard_map/ppermute | solution.py:218
  156.9 4.7 %collective-permute-start.30 = (bf16[4,32,384]{2,1,0:T(8,128)(2,1)S(1)}, bf16[4,32,384]{2,1,0:T(8,128)(2,1)S(1)}, u32[]{:S(2)}, u32[]{:S(2)}) collective-permute-start(bf16[4,32,384]{2,1,0:T(8,128)(2,1)S(1)} %get-tuple-element.88), channel_id=1, source_target_pairs={{0,3},{1,0},{2,1},{3,2},{4,7},{5,4},{6,5},{7,6},{8,11},{9,8},{10,9... | collective-permute-start | bytes 294920 | tf_op jit(solution)/shard_map/ppermute | solution.py:218

commit v5 on v3

--- a/solution.py
+++ b/solution.py
@@ -33,32 +33,42 @@
     return out
 
 
-def put_keys(keys, masks, place, scale):
-    rows, head, width = keys[0].shape
-    for slot, (ref, mask) in enumerate(zip(keys, masks)):
-        offset = jnp.where(mask == 0.0, MASKED, 0.0)
-        extra = rows_of((-1.0, -1.0, -1.0, offset), head, width)
-
-        def prepare(i, carry):
-            parts = split3(ref[i].astype(F32) * scale)
-            whole = jnp.concatenate(parts + (extra,), axis=0)
-            place[i, slot * width : (slot + 1) * width, :] = whole.T.astype(BF16)
-            return carry
-
-        lax.fori_loop(0, rows, prepare, 0)
-
-
-def put_values(values, away, place):
+def put_keys(keys, mask, place, first, scale):
+    rows, (_, head, width) = place.shape[0], keys.shape
+    extra = rows_of((-1.0, -1.0, -1.0, jnp.where(mask == 0.0, MASKED, 0.0)), head, width)
+
+    def prepare(i, carry):
+        parts = split3(keys[i].astype(F32) * scale)
+        whole = jnp.concatenate(parts + (extra,), axis=0)
+        place[i, first : first + width, :] = whole.T.astype(BF16)
+        return carry
+
+    lax.fori_loop(0, rows, prepare, 0)
+
+
+def put_values(values, place, first):
     rows, head, width = values.shape
     extra = rows_of((-1.0, -1.0, -1.0), 128 - head, width)
-    for slot, (ref, base) in enumerate(((values, 0), (away, rows))):
-
-        def prepare(i, carry):
-            whole = jnp.concatenate((ref[base + i].astype(F32), extra), axis=0)
-            place[i, slot * width : (slot + 1) * width, :] = whole.T.astype(BF16)
-            return carry
-
-        lax.fori_loop(0, rows, prepare, 0)
+
+    def prepare(i, carry):
+        whole = jnp.concatenate((values[i].astype(F32), extra), axis=0)
+        place[i, first : first + width, :] = whole.T.astype(BF16)
+        return carry
+
+    lax.fori_loop(0, rows, prepare, 0)
+
+
+def prepare_kernel(scale, q, grad, outs, keys, values, mask, *made):
+    qg, km, v, g, key_own, value_own, delta = made
+    rows, head, width = keys.shape
+    put_keys(keys, mask[...], key_own, 0, scale * LOG2E)
+    put_values(values, value_own, 0)
+    qg[:rows], qg[rows:], g[...] = q[...], grad[...], grad[...]
+    km[:rows], v[...] = keys[...], values[...]
+    km[rows] = jnp.broadcast_to(mask[...], (head, width)).astype(BF16)
+    for i in range(rows):
+        product = grad[i].astype(F32) * outs[i].astype(F32)
+        delta[i : i + 1, :] = jnp.sum(product, axis=0, keepdims=True)
 
 
 def bias_pieces(at):
@@ -66,7 +76,7 @@
     for yd in range(Y):
         row = lax.rem(y + yd, Y)
         for zd in range(ZLO):
-            piece = lax.rem(zlo + zd, ZLO)
+            piece = lax.bitwise_xor(zlo, zd)
             half, part = lax.div(piece, 2), lax.rem(piece, 2)
             slot = lax.rem(half + zhi, 2)
             chunk = lax.rem(part * 2 + lax.div(row, 2) - x + X, X)
@@ -77,15 +87,15 @@
 
 
 def stats_kernel(scale, at, *refs):
-    q = refs[0:4]
-    keys, away, mask, grad, outs = refs[4:9]
-    pieces = (refs[9:13], refs[13:17])
-    stat, bias_t = refs[17:19]
-    bias_n, bias_f, key_t = refs[19:]
-    rows, head, width = keys.shape
+    q, (away, key_own, delta) = refs[0:4], refs[4:7]
+    pieces = (refs[7:11], refs[11:15])
+    stat, bias_t, key_t = refs[15:18]
+    bias_n, bias_f = refs[18:]
+    rows, width, _ = key_own.shape
     total = X * width
-    masks = (mask[...], away[2 * rows, 0:1, :].astype(F32))
-    put_keys((keys, away), masks, key_t, scale * LOG2E)
+    put_keys(away, away[rows, 0:1, :].astype(F32), key_t, width, scale * LOG2E)
+    key_t[:, :width, :] = key_own[...]
+    stat[:, total:] = delta[...]
     for yd, zd, other, slot, first in bias_pieces(at):
         bias_n[slot, pl.ds(first, 96), :] = pieces[other][yd][zd]
     for slot in range(2):
@@ -116,36 +126,31 @@
                     top = new
             most = jnp.max(top, axis=0, keepdims=True)
             summed = jnp.sum(total_sum * jnp.exp2(top - most), axis=0, keepdims=True)
-            stat[pl.ds(i, 1), cols] = most
-            stat[pl.ds(i, 1), total + d * width : total + (d + 1) * width] = summed
-        product = grad[i].astype(F32) * outs[i].astype(F32)
-        stat[pl.ds(i, 1), 2 * total :] = jnp.sum(product, axis=0, keepdims=True)
+            stat[pl.ds(i, 1), cols] = most + jnp.log(summed) * LOG2E
         return carry
 
     lax.fori_loop(0, rows, row_step, 0)
 
 
-def main_kernel(scale, at, *refs):
-    q, (own_grad, keys, values, away, mask) = refs[0:4], refs[4:9]
-    stats = refs[9:13]
-    bias_t = refs[13]
-    dq = refs[14:18]
-    dk_own, dv_own, dkv_away, bias_own, bias_away = refs[18:23]
-    bias_f, acc, turned, key_t, value_t, lse, delta = refs[23:]
-    rows, head, width = keys.shape
+def main_kernel(at, *refs):
+    q, (g2, keys, away, away_values, key_t, value_own) = refs[0:4], refs[4:10]
+    stats = refs[10:14]
+    bias_t = refs[14]
+    dq = refs[15:19]
+    dk_own, dv_own, dkv_away, bias_own, bias_away = refs[19:24]
+    bias_f, acc, turned, value_t, lse, delta = refs[24:]
+    rows, head, width = away_values.shape
     total = X * width
-    masks = (mask[...], away[2 * rows, 0:1, :].astype(F32))
-    put_keys((keys, away), masks, key_t, scale * LOG2E)
-    put_values(values, away, value_t)
+    put_values(away_values, value_t, width)
+    value_t[:, :width, :] = value_own[...]
     for d in range(X):
         cols = slice(d * width, (d + 1) * width)
         there = [(d - e) % X for e in range(X)]
-        tops = [stats[e][:, n * width : (n + 1) * width] for e, n in enumerate(there)]
-        sums = [stats[e][:, total + n * width : total + (n + 1) * width] for e, n in enumerate(there)]
-        top = jnp.maximum(jnp.maximum(tops[0], tops[1]), jnp.maximum(tops[2], tops[3]))
-        summed = sum(s * jnp.exp2(t - top) for s, t in zip(sums, tops))
+        parts = [stats[e][:, n * width : (n + 1) * width] for e, n in enumerate(there)]
+        top = jnp.maximum(jnp.maximum(parts[0], parts[1]), jnp.maximum(parts[2], parts[3]))
+        summed = sum(jnp.exp2(part - top) for part in parts)
         lse[:, cols] = top + jnp.log(summed) * LOG2E
-        delta[:, cols] = stats[d][:, 2 * total :]
+        delta[:, cols] = stats[d][:, total:]
     bias_f[...] = bias_t[...].astype(F32) * LOG2E
     acc[...] = jnp.zeros_like(acc)
 
@@ -154,7 +159,7 @@
         for d in range(X):
             cols = slice(d * width, (d + 1) * width)
             query = q[d][i]
-            gradient = own_grad[i] if d == 0 else q[d][rows + i]
+            gradient = g2[i] if d == 2 else q[d][rows + i]
             high, middle, low = split3(lse[pl.ds(i, 1), cols])
             extra = rows_of((high, middle, low, 1.0), 16, width).astype(BF16)
             query_all = jnp.concatenate((query, query, query, extra), axis=0)
@@ -191,10 +196,10 @@
 SMEM = pl.BlockSpec(memory_space=pltpu.SMEM)
 
 
-def call(kernel, name, args, outs, scratch, mebibytes):
+def call(kernel, name, args, outs, scratch, mebibytes, places=1):
     return pl.pallas_call(
         kernel,
-        in_specs=[SMEM] + [VMEM] * (len(args) - 1),
+        in_specs=[SMEM] * places + [VMEM] * (len(args) - places),
         out_specs=[VMEM] * len(outs),
         out_shape=[jax.ShapeDtypeStruct(shape, dtype) for shape, dtype in outs],
         scratch_shapes=[pltpu.VMEM(shape, dtype) for shape, dtype in scratch],
@@ -215,7 +220,7 @@
     pairs = []
     for group in range(ZHI):
         for place in range(ZLO):
-            half, part = divmod((place + distance) % ZLO, 2)
+            half, part = divmod(place ^ distance, 2)
             pairs.append(((2 * group + part) * ZHI + half, place * ZHI + group))
     return pairs
 
@@ -230,35 +235,48 @@
     after = lax.optimization_barrier
 
     from_z = [lax.ppermute(bias, z_axes, z_pairs(d)) for d in range(ZLO)]
-    qg = jnp.concatenate([queries, out_grad], axis=0)
-    qg1 = fetch(qg, "x", X, 1)
-    from_z, qg1 = after((jnp.stack(from_z), qg1))
-    mask_rows = jnp.broadcast_to(key_mask.astype(BF16), (1, head, width))
-    kvm = jnp.concatenate([keys, values, mask_rows], axis=0)
-    kvm, qg, _ = after((kvm, qg, from_z))
+    q2 = fetch(queries, "x", X, 2)
+    block, turned = (rows, head, width), (rows, width, 128)
+    made = call(
+        lambda *refs: prepare_kernel(scale, *refs),
+        "prepare",
+        [queries, out_grad, outputs, keys, values, mask],
+        [((2 * rows, head, width), BF16), ((rows + 1, head, width), BF16)]
+        + [(block, BF16), (block, BF16), (turned, BF16), (turned, BF16)]
+        + [((rows, width), F32)],
+        [],
+        16,
+        0,
+    )
+    from_z, q2, made = after((from_z, q2, made))
+    qg, km, own_values, own_grad, key_own, value_own, delta = made
+    from_z = jnp.stack(from_z)
     here = [from_z] + [fetch(from_z, "y", Y, d) for d in range(1, Y)]
-    away = fetch(kvm, "zhi", ZHI, 1)
-    qg3 = fetch(qg, "x", X, 3)
-    qg, here[1] = after((qg, here[1]))
-    qg2 = fetch(qg, "x", X, 2)
+    qg1, qg3 = fetch(qg, "x", X, 1), fetch(qg, "x", X, 3)
+    qg1, km = after((qg1, km))
+    away = fetch(km, "zhi", ZHI, 1)
     there = [fetch(a, "core", CORE, 1) for a in here]
-    q = [queries, qg1, qg2, qg3]
-
-    stat, bias_t = call(
+    away, own_values, own_grad = after((away, own_values, own_grad))
+    away_values = fetch(own_values, "zhi", ZHI, 1)
+    g2 = fetch(own_grad, "x", X, 2)
+    q = [qg, qg1, q2, qg3]
+
+    stat, bias_t, key_t = call(
         lambda *refs: stats_kernel(scale, *refs),
         "softmax_statistics",
-        [at, *q, keys, away, mask, out_grad, outputs, *here, *there],
-        [((rows, 2 * total + width), F32), ((both, total), BF16)],
-        [((2, total, width), BF16), ((both, total), F32), ((rows, both, 128), BF16)],
+        [at, *q, away, key_own, delta, *here, *there],
+        [((rows, total + width), F32), ((both, total), BF16), ((rows, both, 128), BF16)],
+        [((2, total, width), BF16), ((both, total), F32)],
         24,
     )
+    stat, away_values, g2 = after((stat, away_values, g2))
     stats = [stat] + [fetch(stat, "x", X, d) for d in range(1, X)]
 
-    block, pieces = (rows, head, width), (Y, ZLO, 96, width)
+    pieces = (Y, ZLO, 96, width)
     results = call(
-        lambda *refs: main_kernel(scale, *refs),
+        main_kernel,
         "attention_gradients",
-        [at, *q, out_grad, keys, values, away, mask, *stats, bias_t],
+        [at, *q, g2, km, away, away_values, key_t, value_own, *stats, bias_t],
         [(block, F32)]
         + [(block, BF16)] * 3
         + [(block, F32)] * 2
@@ -268,7 +286,6 @@
             ((both, total), F32),
             ((2, total, width), F32),
             ((rows, both, 128), BF16),
-            ((rows, both, 128), BF16),
             ((rows, total), F32),
             ((rows, total), F32),
         ],
@@ -278,23 +295,23 @@
 
     near = bias_own + fetch(bias_away, "core", CORE, 1).astype(F32)
     arrived = fetch(dkv_away, "zhi", ZHI, 1)
-    sent = [near[d].astype(BF16) for d in range(1, Y)]
-    sent, dq = after((sent, dq))
+    sent, first = after(([near[d].astype(BF16) for d in range(1, Y)], dq[1]))
     far = [deliver(sent[d - 1], "y", Y, d) for d in range(1, Y)]
-    dq1 = deliver(dq[1], "x", X, 1)
+    first = deliver(first, "x", X, 1)
+    far[0], arrived, first, dq = after((far[0], arrived, first, dq))
     along_y = near[0]
     for part in far:
         along_y = along_y + part.astype(F32)
-    low, arrived = after((along_y.astype(BF16), arrived))
-    dq1, dq = after((dq1, dq))
+    across = [(n, n ^ 2) for n in range(ZLO)]
+    kept = along_y[:2] + lax.ppermute(along_y[2:].astype(BF16), "zlo", across).astype(F32)
     bias_grad = None
-    for d in range(ZLO):
+    for d in range(2):
         pairs = [(worker, owner) for owner, worker in z_pairs(d)]
-        part = lax.ppermute(low[d], z_axes, pairs).astype(F32)
+        part = lax.ppermute(kept[d].astype(BF16), z_axes, pairs).astype(F32)
         bias_grad = part if bias_grad is None else bias_grad + part
 
-    query_sum = dq[0] + dq1.astype(F32)
-    for d in (3, 2):
+    query_sum = dq[0] + first.astype(F32)
+    for d in range(2, X):
         query_sum = query_sum + deliver(dq[d], "x", X, d).astype(F32)
     arrived = arrived.astype(F32)
     query_grad = (scale * query_sum).astype(BF16)

time: 162 us -> 150 us (0.926)
  waiting for transfers between devices: 40.6 us -> 32.1 us
  starting transfers between devices: 63.8 us -> 61.6 us
  local copies, waits for them, and re-layouts: 4.47 us -> 6.52 us
  other arithmetic: 5.62 us -> 3.7 us
    ppermute x16 -> x18, waiting for transfers between devices: 30.8 us -> 19.9 us  [fetch(): lax.ppermute(x, axis, [((n + distance) % size, n) for n in range(size)])]
    ppermute x4 -> x3, waiting for transfers between devices: 3.42 us -> 9.1 us  [the longest x2 6.54 us: per_device(): part = lax.ppermute(kept[d].astype(BF16), z_axes, pairs).astype(F32)]
    ppermute x4, waiting for transfers between devices: 4.7 us -> 0.01 us  [per_device(): from_z = [lax.ppermute(bias, z_axes, z_pairs(d)) for d in range(ZLO)]]
    unnamed x11 -> x18, local copies, waits for them, and re-layouts: 2.63 us -> 6.3 us
    ppermute x16 -> x18, starting transfers between devices: 29.1 us -> 25.7 us  [fetch(): lax.ppermute(x, axis, [((n + distance) % size, n) for n in range(size)])]
    concatenate x1 -> x0, other arithmetic: 1.83 us -> none  [per_device(): kvm = jnp.concatenate([keys, values, mask_rows], axis=0)]
    concatenate x1 -> x0, local copies, waits for them, and re-layouts: 1.63 us -> none  [per_device(): qg = jnp.concatenate([queries, out_grad], axis=0)]
    ppermute x4 -> x3, starting transfers between devices: 14.1 us -> 14.5 us  [the longest x1 8.44 us: per_device(): lax.ppermute(along_y[2:].astype(BF16), 'zlo', across).astype(F32)]
  transfers between devices with their start and end apart: 30 -> 31, of which waited for: 14 -> 13; matrix products, arithmetic and copies ran while one was open for 3% -> 2% of each run, Pallas kernels for 0% -> 10%
where the time goes in v5:
time: 150 us; the launch traced here: 149 us
  starting transfers between devices  61.6 us (41%)
  Pallas kernels  44.6 us (30%)
  waiting for transfers between devices  32.1 us (21%)
  local copies, waits for them, and re-layouts  6.52 us (4%)
  other arithmetic  3.7 us (2%)
    pallas_call x3, Pallas kernels, call(): pl.pallas_call(kernel, in_specs=[SMEM] * places + [VMEM] * (len(args) - p...  44.6 us
    ppermute x18, starting transfers between devices, fetch(): lax.ppermute(x, axis, [((n + distance) % size, n) for n in range(size)])  25.7 us
    ppermute x18, waiting for transfers between devices, fetch(): lax.ppermute(x, axis, [((n + distance) % size, n) for n in range(size)])  19.9 us
    ppermute x4, starting transfers between devices, per_device(): from_z = [lax.ppermute(bias, z_axes, z_pairs(d)) for d in range(ZLO)]  12.1 us
    ppermute x6, starting transfers between devices, deliver(): lax.ppermute(x, axis, [(n, (n + distance) % size) for n in range(size)])  9.29 us
    ppermute x1, starting transfers between devices, per_device(): lax.ppermute(along_y[2:].astype(BF16), 'zlo', across).astype(F32)  8.44 us
    ppermute x2, waiting for transfers between devices, per_device(): part = lax.ppermute(kept[d].astype(BF16), z_axes, pairs).astype(F32)  6.54 us
    unnamed x18, local copies, waits for them, and re-layouts  6.3 us
  transfers between devices with their start and end apart: 31, of which 13 were waited for; matrix products, arithmetic and copies ran while one was open for 2% of the time, Pallas kernels for 10%

profile of v5, /device:TPU:64, one launch (start us, length us, event | category | flops | bytes accessed | tf_op | source)
XLA Modules:
  0.0 149.3 jit_solution(10189727722317030229)
XLA Ops:
  0.6 3.1 %collective-permute-start.4 = (bf16[8,32,384]{2,1,0:T(8,128)(2,1)}, bf16[8,32,384]{2,1,0:T(8,128)(2,1)S(1)}, u32[]{:S(2)}, u32[]{:S(2)}) collective-permute-start(bf16[8,32,384]{2,1,0:T(8,128)(2,1)} %refs_0_.1), channel_id=1, source_target_pairs={{2,0},{3,1},{0,2},{1,3},{6,4},{7,5},{4,6},{5,7},{10,8},{11,9},{8,1... | collective-permute-start | bytes 589832 | tf_op jit(solution)/shard_map/ppermute | solution.py:212
  3.7 4.9 %collective-permute-start.1 = (bf16[96,384]{1,0:T(8,128)(2,1)}, bf16[96,384]{1,0:T(8,128)(2,1)S(1)}, u32[]{:S(2)}, u32[]{:S(2)}) collective-permute-start(bf16[96,384]{1,0:T(8,128)(2,1)} %param.12), channel_id=1, source_target_pairs={{64,0},{0,64},{68,128},{4,192},{192,4},{128,68},{196,132},{132,196... | collective-permute-start | bytes 221192 | tf_op jit(solution)/shard_map/ppermute | solution.py:237
  8.7 1.9 %collective-permute-start = (bf16[96,384]{1,0:T(8,128)(2,1)}, bf16[96,384]{1,0:T(8,128)(2,1)S(1)}, u32[]{:S(2)}, u32[]{:S(2)}) collective-permute-start(bf16[96,384]{1,0:T(8,128)(2,1)} %param.12), channel_id=1, source_target_pairs={{0,0},{64,64},{4,128},{68,192},{128,4},{192,68},{132,132},{196,196... | collective-permute-start | bytes 221192 | tf_op jit(solution)/shard_map/ppermute | solution.py:237
  10.6 0.6 collective-permute-start.3
  11.2 4.6 %collective-permute-start.2 = (bf16[96,384]{1,0:T(8,128)(2,1)}, bf16[96,384]{1,0:T(8,128)(2,1)S(1)}, u32[]{:S(2)}, u32[]{:S(2)}) collective-permute-start(bf16[96,384]{1,0:T(8,128)(2,1)} %param.12), channel_id=1, source_target_pairs={{4,0},{68,64},{0,128},{64,192},{132,4},{196,68},{128,132},{192,196... | collective-permute-start | bytes 221192 | tf_op jit(solution)/shard_map/ppermute | solution.py:237
  15.8 0.7 convert_element_type.66
  16.5 0.9 copy-done.4
  17.4 0.9 copy-done.5
  18.3 0.9 copy-done.6
  19.3 0.9 copy-done.7
  20.2 0.9 copy-done.8
  21.1 2.5 %prepare.1 = (bf16[16,32,384]{2,1,0:T(8,128)(2,1)S(1)}, bf16[9,32,384]{2,1,0:T(8,128)(2,1)S(1)}, bf16[8,32,384]{2,1,0:T(8,128)(2,1)}, bf16[8,32,384]{2,1,0:T(8,1...) custom-call(bf16[8,32,384]{2,1,0:T(8,128)(2,1)S(1)} %copy-done.8, ...), custom_call_target="tpu_custom_call" | custom-call | tf_op jit(solution)/shard_map/prepare/pallas_call | solution.py:200
  23.6 0.0 collective-permute-done.1
  23.6 0.0 collective-permute-done
  23.7 0.0 collective-permute-done.4.refs_3_.refs_2_
  23.7 1.2 collective-permute-start.5
  24.9 1.7 %collective-permute-start.10 = (bf16[4,96,384]{2,1,0:T(8,128)(2,1)S(1)}, bf16[4,96,384]{2,1,0:T(8,128)(2,1)}, u32[]{:S(2)}, u32[]{:S(2)}) collective-permute-start(bf16[4,96,384]{2,1,0:T(8,128)(2,1)S(1)} %pad_maximum_fusion.refs_8_), channel_id=1, source_target_pairs={{48,0},{0,16},{16,32},{32,48},{49,1},{1,17},{17,33},{33,49},{50,2}... | collective-permute-start | bytes 884744 | tf_op jit(solution)/shard_map/ppermute | solution.py:212
  26.6 2.9 %collective-permute-start.9 = (bf16[4,96,384]{2,1,0:T(8,128)(2,1)S(1)}, bf16[4,96,384]{2,1,0:T(8,128)(2,1)}, u32[]{:S(2)}, u32[]{:S(2)}) collective-permute-start(bf16[4,96,384]{2,1,0:T(8,128)(2,1)S(1)} %pad_maximum_fusion.refs_8_), channel_id=1, source_target_pairs={{32,0},{48,16},{0,32},{16,48},{33,1},{49,17},{1,33},{17,49},{34,2}... | collective-permute-start | bytes 884744 | tf_op jit(solution)/shard_map/ppermute | solution.py:212
  29.5 1.3 collective-permute-start.8
  30.9 0.9 collective-permute-start.6
  31.7 1.5 collective-permute-done.5.refs_2_.refs_1_
  33.2 1.7 %collective-permute-start.7 = (bf16[9,32,384]{2,1,0:T(8,128)(2,1)S(1)}, bf16[9,32,384]{2,1,0:T(8,128)(2,1)S(1)}, u32[]{:S(2)}, u32[]{:S(2)}) collective-permute-start(bf16[9,32,384]{2,1,0:T(8,128)(2,1)S(1)} %get-tuple-element.64.refs_5_), channel_id=1, source_target_pairs={{4,0},{0,4},{5,1},{1,5},{6,2},{2,6},{7,3},{3,7},{12,8},{8,12},{13,... | collective-permute-start | bytes 663560 | tf_op jit(solution)/shard_map/ppermute | solution.py:212
  34.9 0.2 collective-permute-done.10.refs_11_
  35.2 5.8 %collective-permute-done.9.refs_10_ = bf16[4,96,384]{2,1,0:T(8,128)(2,1)} collective-permute-done((bf16[4,96,384]{2,1,0:T(8,128)(2,1)S(1)}, bf16[4,96,384]{2,1,0:T(8,128)(2,1)}, u32[]{:S(2)}, u32[]{:S(2)}) %collective-permute-start.9) | collective-permute-done | bytes 294944 | tf_op jit(solution)/shard_map/ppermute | solution.py:212
  41.0 0.5 collective-permute-start.13
  41.5 3.5 %collective-permute-done.7.refs_5_.refs_6_ = bf16[9,32,384]{2,1,0:T(8,128)(2,1)S(1)} collective-permute-done((bf16[9,32,384]{2,1,0:T(8,128)(2,1)S(1)}, bf16[9,32,384]{2,1,0:T(8,128)(2,1)S(1)}, u32[]{:S(2)}, u32[]{:S(2)}) %collective-permute-start.7) | collective-permute-done | bytes 221216 | tf_op jit(solution)/shard_map/ppermute | solution.py:212
  45.0 0.7 copy-done
  45.7 3.8 %collective-permute-start.15 = (bf16[8,32,384]{2,1,0:T(8,128)(2,1)}, bf16[8,32,384]{2,1,0:T(8,128)(2,1)}, u32[]{:S(2)}, u32[]{:S(2)}) collective-permute-start(bf16[8,32,384]{2,1,0:T(8,128)(2,1)} %get-tuple-element.75), channel_id=1, source_target_pairs={{4,0},{0,4},{5,1},{1,5},{6,2},{2,6},{7,3},{3,7},{12,8},{8,12},{13,... | collective-permute-start | bytes 589832 | tf_op jit(solution)/shard_map/ppermute | solution.py:212
  49.4 0.8 collective-permute-start.16
  50.3 0.1 stack.38.refs_0_.at
  50.4 1.0 copy-done.1
  51.3 12.9 %softmax_statistics.1 = (f32[8,1920]{1,0:T(8,128)S(1)}, bf16[768,1536]{1,0:T(8,128)(2,1)S(1)}, bf16[8,768,128]{2,1,0:T(8,128)(2,1)S(1)}) custom-call(s32[5]{0:T(128)S(1)} %stack.38.refs_0_.at, bf16[16,32,384]{2,1,0:T(8,128)(2,1)S(1)} %get-tuple-element.60.refs_1_.refs_0_, bf16[16,32,384]{2,1,0:T(8,128)(2,1)S(1)} %collective-permute-done.5.refs_2_.refs_1_, ...), custom_call_target="tpu_custom_call" | custom-call | tf_op jit(solution)/shard_map/softmax_statistics/pallas_call | solution.py:200
  64.2 2.5 %collective-permute-start.19 = (f32[8,1920]{1,0:T(8,128)S(1)}, f32[8,1920]{1,0:T(8,128)S(1)}, u32[]{:S(2)}, u32[]{:S(2)}) collective-permute-start(f32[8,1920]{1,0:T(8,128)S(1)} %get-tuple-element.81.refs_10_), channel_id=1, source_target_pairs={{3,0},{0,1},{1,2},{2,3},{7,4},{4,5},{5,6},{6,7},{11,8},{8,9},{9,10... | collective-permute-start | bytes 184328 | tf_op jit(solution)/shard_map/ppermute | solution.py:212
  66.7 1.5 %collective-permute-start.18 = (f32[8,1920]{1,0:T(8,128)S(1)}, f32[8,1920]{1,0:T(8,128)S(1)}, u32[]{:S(2)}, u32[]{:S(2)}) collective-permute-start(f32[8,1920]{1,0:T(8,128)S(1)} %get-tuple-element.81.refs_10_), channel_id=1, source_target_pairs={{2,0},{3,1},{0,2},{1,3},{6,4},{7,5},{4,6},{5,7},{10,8},{11,9},{8,1... | collective-permute-start | bytes 184328 | tf_op jit(solution)/shard_map/ppermute | solution.py:212
  68.2 1.4 collective-permute-start.17
  69.6 0.1 collective-permute-done.19.refs_13_
  69.7 2.7 %collective-permute-done.18.refs_12_ = f32[8,1920]{1,0:T(8,128)S(1)} collective-permute-done((f32[8,1920]{1,0:T(8,128)S(1)}, f32[8,1920]{1,0:T(8,128)S(1)}, u32[]{:S(2)}, u32[]{:S(2)}) %collective-permute-start.18) | collective-permute-done | bytes 61472 | tf_op jit(solution)/shard_map/ppermute | solution.py:212
  72.4 0.0 collective-permute-done.17.refs_11_
  72.4 29.2 %attention_gradients.1 = (f32[8,32,384]{2,1,0:T(8,128)S(1)}, bf16[8,32,384]{2,1,0:T(8,128)(2,1)S(1)}, bf16[8,32,384]{2,1,0:T(8,128)(2,1)S(1)}, bf16[8,32,384]{2,...) custom-call(s32[5]{0:T(128)S(1)} %stack.38.refs_0_.at, ...), custom_call_target="tpu_custom_call" | custom-call | tf_op jit(solution)/shard_map/attention_gradients/pallas_call | solution.py:200
  101.7 0.1 collective-permute-start.20
  101.8 2.3 %collective-permute-start.22 = (bf16[16,32,384]{2,1,0:T(8,128)(2,1)S(1)}, bf16[16,32,384]{2,1,0:T(8,128)(2,1)S(1)}, u32[]{:S(2)}, u32[]{:S(2)}) collective-permute-start(bf16[16,32,384]{2,1,0:T(8,128)(2,1)S(1)} %get-tuple-element.87), channel_id=1, source_target_pairs={{4,0},{0,4},{5,1},{1,5},{6,2},{2,6},{7,3},{3,7},{12,8},{8,12},{13,... | collective-permute-start | bytes 1179656 | tf_op jit(solution)/shard_map/ppermute | solution.py:212
  104.0 0.6 collective-permute-done.20
  104.6 0.4 fusion.7
  105.0 0.1 slice_bitcast_fusion.1
  105.1 1.7 %collective-permute-start.21 = (bf16[4,96,384]{2,1,0:T(8,128)(2,1)S(1)}, bf16[4,96,384]{2,1,0:T(8,128)(2,1)S(1)}, u32[]{:S(2)}, u32[]{:S(2)}) collective-permute-start(bf16[4,96,384]{2,1,0:T(8,128)(2,1)S(1)} %get-tuple-element.86), channel_id=1, source_target_pairs={{0,16},{16,32},{32,48},{48,0},{1,17},{17,33},{33,49},{49,1},{2,18}... | collective-permute-start | bytes 884744 | tf_op jit(solution)/shard_map/ppermute | solution.py:216
  106.7 2.9 %collective-permute-start.26 = (bf16[4,96,384]{2,1,0:T(8,128)(2,1)S(1)}, bf16[4,96,384]{2,1,0:T(8,128)(2,1)S(1)}, u32[]{:S(2)}, u32[]{:S(2)}) collective-permute-start(bf16[4,96,384]{2,1,0:T(8,128)(2,1)S(1)} %get-tuple-element.100), channel_id=1, source_target_pairs={{0,32},{16,48},{32,0},{48,16},{1,33},{17,49},{33,1},{49,17},{2,34}... | collective-permute-start | bytes 884744 | tf_op jit(solution)/shard_map/ppermute | solution.py:216
  109.6 1.3 collective-permute-start.27
  111.0 0.8 collective-permute-start.23
  111.8 5.5 %collective-permute-done.22 = bf16[16,32,384]{2,1,0:T(8,128)(2,1)S(1)} collective-permute-done((bf16[16,32,384]{2,1,0:T(8,128)(2,1)S(1)}, bf16[16,32,384]{2,1,0:T(8,128)(2,1)S(1)}, u32[]{:S(2)}, u32[]{:S(2)}) %collective-permute-start.22) | collective-permute-done | bytes 393248 | tf_op jit(solution)/shard_map/ppermute | solution.py:212
  117.3 1.0 collective-permute-done.23
  118.3 1.0 collective-permute-start.24
  119.3 1.5 %collective-permute-start.25 = (bf16[8,32,384]{2,1,0:T(8,128)(2,1)S(1)}, bf16[8,32,384]{2,1,0:T(8,128)(2,1)S(1)}, u32[]{:S(2)}, u32[]{:S(2)}) collective-permute-start(bf16[8,32,384]{2,1,0:T(8,128)(2,1)S(1)} %get-tuple-element.95), channel_id=1, source_target_pairs={{0,3},{1,0},{2,1},{3,2},{4,7},{5,4},{6,5},{7,6},{8,11},{9,8},{10,9... | collective-permute-start | bytes 589832 | tf_op jit(solution)/shard_map/ppermute | solution.py:216
  120.9 2.1 %collective-permute-done.26 = bf16[4,96,384]{2,1,0:T(8,128)(2,1)S(1)} collective-permute-done((bf16[4,96,384]{2,1,0:T(8,128)(2,1)S(1)}, bf16[4,96,384]{2,1,0:T(8,128)(2,1)S(1)}, u32[]{:S(2)}, u32[]{:S(2)}) %collective-permute-start.26) | collective-permute-done | bytes 294944 | tf_op jit(solution)/shard_map/ppermute | solution.py:216
  123.0 0.1 fusion.2
  123.2 8.4 %collective-permute-start.28 = (bf16[2,96,384]{2,1,0:T(8,128)(2,1)S(1)}, bf16[2,96,384]{2,1,0:T(8,128)(2,1)S(1)}, u32[]{:S(2)}, u32[]{:S(2)}) collective-permute-start(bf16[2,96,384]{2,1,0:T(8,128)(2,1)S(1)} %slice.80), channel_id=1, source_target_pairs={{0,128},{64,192},{128,0},{192,64},{1,129},{65,193},{129,1},{193,65... | collective-permute-start | bytes 442376 | tf_op jit(solution)/shard_map/ppermute | solution.py:306
  131.6 0.1 convert_element_type.75
  131.7 0.9 fusion.3
  132.6 2.6 %collective-permute-done.28 = bf16[2,96,384]{2,1,0:T(8,128)(2,1)S(1)} collective-permute-done((bf16[2,96,384]{2,1,0:T(8,128)(2,1)S(1)}, bf16[2,96,384]{2,1,0:T(8,128)(2,1)S(1)}, u32[]{:S(2)}, u32[]{:S(2)}) %collective-permute-start.28) | collective-permute-done | bytes 147488 | tf_op jit(solution)/shard_map/ppermute | solution.py:306
  135.2 6.0 %collective-permute-start.29 = (bf16[96,384]{1,0:T(8,128)(2,1)S(1)}, bf16[96,384]{1,0:T(8,128)(2,1)S(1)}, u32[]{:S(2)}, u32[]{:S(2)}) collective-permute-start(bf16[96,384]{1,0:T(8,128)(2,1)S(1)} %get-tuple-element.109), channel_id=1, source_target_pairs={{0,0},{64,64},{128,4},{192,68},{4,128},{68,192},{132,132},{196,196... | collective-permute-start | bytes 221192 | tf_op jit(solution)/shard_map/ppermute | solution.py:310
  141.2 0.1 collective-permute-start.30
  141.3 0.8 multiply_convert_fusion
  142.1 1.8 %collective-permute-done.29 = bf16[96,384]{1,0:T(8,128)(2,1)S(1)} collective-permute-done((bf16[96,384]{1,0:T(8,128)(2,1)S(1)}, bf16[96,384]{1,0:T(8,128)(2,1)S(1)}, u32[]{:S(2)}, u32[]{:S(2)}) %collective-permute-start.29) | collective-permute-done | bytes 73760 | tf_op jit(solution)/shard_map/ppermute | solution.py:310
  143.9 4.8 %collective-permute-done.30 = bf16[96,384]{1,0:T(8,128)(2,1)S(1)} collective-permute-done((bf16[96,384]{1,0:T(8,128)(2,1)S(1)}, bf16[96,384]{1,0:T(8,128)(2,1)S(1)}, u32[]{:S(2)}, u32[]{:S(2)}) %collective-permute-start.30) | collective-permute-done | bytes 73760 | tf_op jit(solution)/shard_map/ppermute | solution.py:310
  148.6 0.7 convert_add_fusion.1
  (33 shorter events, 0.2 us)
Async XLA Ops:
  0.6 23.0 %collective-permute-start.4 = (bf16[8,32,384]{2,1,0:T(8,128)(2,1)}, bf16[8,32,384]{2,1,0:T(8,128)(2,1)S(1)}, u32[]{:S(2)}, u32[]{:S(2)}) collective-permute-start(bf16[8,32,384]{2,1,0:T(8,128)(2,1)} %refs_0_.1), channel_id=1, source_target_pairs={{2,0},{3,1},{0,2},{1,3},{6,4},{7,5},{4,6},{5,7},{10,8},{11,9},{8,1... | collective-permute-start | bytes 589832 | tf_op jit(solution)/shard_map/ppermute | solution.py:212
  3.7 19.9 %collective-permute-start.1 = (bf16[96,384]{1,0:T(8,128)(2,1)}, bf16[96,384]{1,0:T(8,128)(2,1)S(1)}, u32[]{:S(2)}, u32[]{:S(2)}) collective-permute-start(bf16[96,384]{1,0:T(8,128)(2,1)} %param.12), channel_id=1, source_target_pairs={{64,0},{0,64},{68,128},{4,192},{192,4},{128,68},{196,132},{132,196... | collective-permute-start | bytes 221192 | tf_op jit(solution)/shard_map/ppermute | solution.py:237
  8.7 15.0 %collective-permute-start = (bf16[96,384]{1,0:T(8,128)(2,1)}, bf16[96,384]{1,0:T(8,128)(2,1)S(1)}, u32[]{:S(2)}, u32[]{:S(2)}) collective-permute-start(bf16[96,384]{1,0:T(8,128)(2,1)} %param.12), channel_id=1, source_target_pairs={{0,0},{64,64},{4,128},{68,192},{128,4},{192,68},{132,132},{196,196... | collective-permute-start | bytes 221192 | tf_op jit(solution)/shard_map/ppermute | solution.py:237
  10.6 13.1 %collective-permute-start.3 = (bf16[96,384]{1,0:T(8,128)(2,1)}, bf16[96,384]{1,0:T(8,128)(2,1)S(1)}, u32[]{:S(2)}, u32[]{:S(2)}) collective-permute-start(bf16[96,384]{1,0:T(8,128)(2,1)} %param.12), channel_id=1, source_target_pairs={{68,0},{4,64},{64,128},{0,192},{196,4},{132,68},{192,132},{128,196... | collective-permute-start | bytes 221192 | tf_op jit(solution)/shard_map/ppermute | solution.py:237
  11.2 12.4 %collective-permute-start.2 = (bf16[96,384]{1,0:T(8,128)(2,1)}, bf16[96,384]{1,0:T(8,128)(2,1)S(1)}, u32[]{:S(2)}, u32[]{:S(2)}) collective-permute-start(bf16[96,384]{1,0:T(8,128)(2,1)} %param.12), channel_id=1, source_target_pairs={{4,0},{68,64},{0,128},{64,192},{132,4},{196,68},{128,132},{192,196... | collective-permute-start | bytes 221192 | tf_op jit(solution)/shard_map/ppermute | solution.py:237
  16.5 0.9 copy-start.4
  17.4 0.9 copy-start.5
  18.3 0.9 copy-start.6
  19.3 0.9 copy-start.7
  20.2 0.9 copy-start.8
  23.6 25.8 %copy-start.2 = (bf16[9,32,384]{2,1,0:T(8,128)(2,1)}, bf16[9,32,384]{2,1,0:T(8,128)(2,1)S(1)}, u32[]{:S(2)}) copy-start(bf16[9,32,384]{2,1,0:T(8,128)(2,1)S(1)} %get-tuple-element.64.refs_5_) | copy-start | bytes 663556
  23.7 9.5 %collective-permute-start.5 = (bf16[16,32,384]{2,1,0:T(8,128)(2,1)S(1)}, bf16[16,32,384]{2,1,0:T(8,128)(2,1)S(1)}, u32[]{:S(2)}, u32[]{:S(2)}) collective-permute-start(bf16[16,32,384]{2,1,0:T(8,128)(2,1)S(1)} %get-tuple-element.60.refs_1_.refs_0_), channel_id=1, source_target_pairs={{1,0},{2,1},{3,2},{0,3},{5,4},{6,5},{7,6},{4,7},{9,8},{10,9},{11,1... | collective-permute-start | bytes 1179656 | tf_op jit(solution)/shard_map/ppermute | solution.py:212
  24.9 10.2 %collective-permute-start.10 = (bf16[4,96,384]{2,1,0:T(8,128)(2,1)S(1)}, bf16[4,96,384]{2,1,0:T(8,128)(2,1)}, u32[]{:S(2)}, u32[]{:S(2)}) collective-permute-start(bf16[4,96,384]{2,1,0:T(8,128)(2,1)S(1)} %pad_maximum_fusion.refs_8_), channel_id=1, source_target_pairs={{48,0},{0,16},{16,32},{32,48},{49,1},{1,17},{17,33},{33,49},{50,2}... | collective-permute-start | bytes 884744 | tf_op jit(solution)/shard_map/ppermute | solution.py:212
  26.6 14.4 %collective-permute-start.9 = (bf16[4,96,384]{2,1,0:T(8,128)(2,1)S(1)}, bf16[4,96,384]{2,1,0:T(8,128)(2,1)}, u32[]{:S(2)}, u32[]{:S(2)}) collective-permute-start(bf16[4,96,384]{2,1,0:T(8,128)(2,1)S(1)} %pad_maximum_fusion.refs_8_), channel_id=1, source_target_pairs={{32,0},{48,16},{0,32},{16,48},{33,1},{49,17},{1,33},{17,49},{34,2}... | collective-permute-start | bytes 884744 | tf_op jit(solution)/shard_map/ppermute | solution.py:212
  29.5 11.5 %collective-permute-start.8 = (bf16[4,96,384]{2,1,0:T(8,128)(2,1)S(1)}, bf16[4,96,384]{2,1,0:T(8,128)(2,1)}, u32[]{:S(2)}, u32[]{:S(2)}) collective-permute-start(bf16[4,96,384]{2,1,0:T(8,128)(2,1)S(1)} %pad_maximum_fusion.refs_8_), channel_id=1, source_target_pairs={{16,0},{32,16},{48,32},{0,48},{17,1},{33,17},{49,33},{1,49},{18,2}... | collective-permute-start | bytes 884744 | tf_op jit(solution)/shard_map/ppermute | solution.py:212
  30.9 18.6 %collective-permute-start.6 = (bf16[16,32,384]{2,1,0:T(8,128)(2,1)S(1)}, bf16[16,32,384]{2,1,0:T(8,128)(2,1)S(1)}, u32[]{:S(2)}, u32[]{:S(2)}) collective-permute-start(bf16[16,32,384]{2,1,0:T(8,128)(2,1)S(1)} %get-tuple-element.60.refs_1_.refs_0_), channel_id=1, source_target_pairs={{3,0},{0,1},{1,2},{2,3},{7,4},{4,5},{5,6},{6,7},{11,8},{8,9},{9,10... | collective-permute-start | bytes 1179656 | tf_op jit(solution)/shard_map/ppermute | solution.py:212
  33.2 11.8 %collective-permute-start.7 = (bf16[9,32,384]{2,1,0:T(8,128)(2,1)S(1)}, bf16[9,32,384]{2,1,0:T(8,128)(2,1)S(1)}, u32[]{:S(2)}, u32[]{:S(2)}) collective-permute-start(bf16[9,32,384]{2,1,0:T(8,128)(2,1)S(1)} %get-tuple-element.64.refs_5_), channel_id=1, source_target_pairs={{4,0},{0,4},{5,1},{1,5},{6,2},{2,6},{7,3},{3,7},{12,8},{8,12},{13,... | collective-permute-start | bytes 663560 | tf_op jit(solution)/shard_map/ppermute | solution.py:212
  35.2 9.8 %collective-permute-start.11 = (bf16[4,96,384]{2,1,0:T(8,128)(2,1)S(1)}, bf16[4,96,384]{2,1,0:T(8,128)(2,1)S(1)}, u32[]{:S(2)}, u32[]{:S(2)}) collective-permute-start(bf16[4,96,384]{2,1,0:T(8,128)(2,1)S(1)} %pad_maximum_fusion.refs_8_), channel_id=1, source_target_pairs={{8,0},{0,8},{9,1},{1,9},{10,2},{2,10},{11,3},{3,11},{12,4},{4,12},... | collective-permute-start | bytes 884744 | tf_op jit(solution)/shard_map/ppermute | solution.py:212
  41.0 9.4 %collective-permute-start.14 = (bf16[4,96,384]{2,1,0:T(8,128)(2,1)}, bf16[4,96,384]{2,1,0:T(8,128)(2,1)}, u32[]{:S(2)}, u32[]{:S(2)}) collective-permute-start(bf16[4,96,384]{2,1,0:T(8,128)(2,1)} %collective-permute-done.10.refs_11_), channel_id=1, source_target_pairs={{8,0},{0,8},{9,1},{1,9},{10,2},{2,10},{11,3},{3,11},{12,4},{4,12},... | collective-permute-start | bytes 884744 | tf_op jit(solution)/shard_map/ppermute | solution.py:212
  41.0 9.4 %collective-permute-start.13 = (bf16[4,96,384]{2,1,0:T(8,128)(2,1)}, bf16[4,96,384]{2,1,0:T(8,128)(2,1)}, u32[]{:S(2)}, u32[]{:S(2)}) collective-permute-start(bf16[4,96,384]{2,1,0:T(8,128)(2,1)} %collective-permute-done.9.refs_10_), channel_id=1, source_target_pairs={{8,0},{0,8},{9,1},{1,9},{10,2},{2,10},{11,3},{3,11},{12,4},{4,12},... | collective-permute-start | bytes 884744 | tf_op jit(solution)/shard_map/ppermute | solution.py:212
  45.0 5.4 %collective-permute-start.12 = (bf16[4,96,384]{2,1,0:T(8,128)(2,1)}, bf16[4,96,384]{2,1,0:T(8,128)(2,1)}, u32[]{:S(2)}, u32[]{:S(2)}) collective-permute-start(bf16[4,96,384]{2,1,0:T(8,128)(2,1)} %collective-permute-done.8.refs_9_), channel_id=1, source_target_pairs={{8,0},{0,8},{9,1},{1,9},{10,2},{2,10},{11,3},{3,11},{12,4},{4,12},... | collective-permute-start | bytes 884744 | tf_op jit(solution)/shard_map/ppermute | solution.py:212
  45.0 0.7 copy-start
  45.7 18.5 %collective-permute-start.15 = (bf16[8,32,384]{2,1,0:T(8,128)(2,1)}, bf16[8,32,384]{2,1,0:T(8,128)(2,1)}, u32[]{:S(2)}, u32[]{:S(2)}) collective-permute-start(bf16[8,32,384]{2,1,0:T(8,128)(2,1)} %get-tuple-element.75), channel_id=1, source_target_pairs={{4,0},{0,4},{5,1},{1,5},{6,2},{2,6},{7,3},{3,7},{12,8},{8,12},{13,... | collective-permute-start | bytes 589832 | tf_op jit(solution)/shard_map/ppermute | solution.py:212
  49.4 14.7 %collective-permute-start.16 = (bf16[8,32,384]{2,1,0:T(8,128)(2,1)}, bf16[8,32,384]{2,1,0:T(8,128)(2,1)}, u32[]{:S(2)}, u32[]{:S(2)}) collective-permute-start(bf16[8,32,384]{2,1,0:T(8,128)(2,1)} %get-tuple-element.76), channel_id=1, source_target_pairs={{2,0},{3,1},{0,2},{1,3},{6,4},{7,5},{4,6},{5,7},{10,8},{11,9},{8,1... | collective-permute-start | bytes 589832 | tf_op jit(solution)/shard_map/ppermute | solution.py:212
  50.4 1.0 copy-start.1
  51.3 21.1 %copy-start.3 = (bf16[9,32,384]{2,1,0:T(8,128)(2,1)S(1)}, bf16[9,32,384]{2,1,0:T(8,128)(2,1)}, u32[]{:S(2)}) copy-start(bf16[9,32,384]{2,1,0:T(8,128)(2,1)} %copy-done.2) | copy-start | bytes 663556
  64.2 5.5 %collective-permute-start.19 = (f32[8,1920]{1,0:T(8,128)S(1)}, f32[8,1920]{1,0:T(8,128)S(1)}, u32[]{:S(2)}, u32[]{:S(2)}) collective-permute-start(f32[8,1920]{1,0:T(8,128)S(1)} %get-tuple-element.81.refs_10_), channel_id=1, source_target_pairs={{3,0},{0,1},{1,2},{2,3},{7,4},{4,5},{5,6},{6,7},{11,8},{8,9},{9,10... | collective-permute-start | bytes 184328 | tf_op jit(solution)/shard_map/ppermute | solution.py:212
  66.7 5.7 %collective-permute-start.18 = (f32[8,1920]{1,0:T(8,128)S(1)}, f32[8,1920]{1,0:T(8,128)S(1)}, u32[]{:S(2)}, u32[]{:S(2)}) collective-permute-start(f32[8,1920]{1,0:T(8,128)S(1)} %get-tuple-element.81.refs_10_), channel_id=1, source_target_pairs={{2,0},{3,1},{0,2},{1,3},{6,4},{7,5},{4,6},{5,7},{10,8},{11,9},{8,1... | collective-permute-start | bytes 184328 | tf_op jit(solution)/shard_map/ppermute | solution.py:212
  68.2 4.2 %collective-permute-start.17 = (f32[8,1920]{1,0:T(8,128)S(1)}, f32[8,1920]{1,0:T(8,128)S(1)}, u32[]{:S(2)}, u32[]{:S(2)}) collective-permute-start(f32[8,1920]{1,0:T(8,128)S(1)} %get-tuple-element.81.refs_10_), channel_id=1, source_target_pairs={{1,0},{2,1},{3,2},{0,3},{5,4},{6,5},{7,6},{4,7},{9,8},{10,9},{11,1... | collective-permute-start | bytes 184328 | tf_op jit(solution)/shard_map/ppermute | solution.py:212
  101.7 2.9 %collective-permute-start.20 = (bf16[4,4,96,384]{3,2,1,0:T(8,128)(2,1)S(1)}, bf16[4,4,96,384]{3,2,1,0:T(8,128)(2,1)S(1)}, u32[]{:S(2)}, u32[]{:S(2)}) collective-permute-start(bf16[4,4,96,384]{3,2,1,0:T(8,128)(2,1)S(1)} %get-tuple-element.84), channel_id=1, source_target_pairs={{8,0},{0,8},{9,1},{1,9},{10,2},{2,10},{11,3},{3,11},{12,4},{4,12},... | collective-permute-start | bytes 3538952 | tf_op jit(solution)/shard_map/ppermute | solution.py:212
  101.8 15.6 %collective-permute-start.22 = (bf16[16,32,384]{2,1,0:T(8,128)(2,1)S(1)}, bf16[16,32,384]{2,1,0:T(8,128)(2,1)S(1)}, u32[]{:S(2)}, u32[]{:S(2)}) collective-permute-start(bf16[16,32,384]{2,1,0:T(8,128)(2,1)S(1)} %get-tuple-element.87), channel_id=1, source_target_pairs={{4,0},{0,4},{5,1},{1,5},{6,2},{2,6},{7,3},{3,7},{12,8},{8,12},{13,... | collective-permute-start | bytes 1179656 | tf_op jit(solution)/shard_map/ppermute | solution.py:212
  105.1 13.2 %collective-permute-start.21 = (bf16[4,96,384]{2,1,0:T(8,128)(2,1)S(1)}, bf16[4,96,384]{2,1,0:T(8,128)(2,1)S(1)}, u32[]{:S(2)}, u32[]{:S(2)}) collective-permute-start(bf16[4,96,384]{2,1,0:T(8,128)(2,1)S(1)} %get-tuple-element.86), channel_id=1, source_target_pairs={{0,16},{16,32},{32,48},{48,0},{1,17},{17,33},{33,49},{49,1},{2,18}... | collective-permute-start | bytes 884744 | tf_op jit(solution)/shard_map/ppermute | solution.py:216
  106.7 16.2 %collective-permute-start.26 = (bf16[4,96,384]{2,1,0:T(8,128)(2,1)S(1)}, bf16[4,96,384]{2,1,0:T(8,128)(2,1)S(1)}, u32[]{:S(2)}, u32[]{:S(2)}) collective-permute-start(bf16[4,96,384]{2,1,0:T(8,128)(2,1)S(1)} %get-tuple-element.100), channel_id=1, source_target_pairs={{0,32},{16,48},{32,0},{48,16},{1,33},{17,49},{33,1},{49,17},{2,34}... | collective-permute-start | bytes 884744 | tf_op jit(solution)/shard_map/ppermute | solution.py:216
  109.6 13.3 %collective-permute-start.27 = (bf16[4,96,384]{2,1,0:T(8,128)(2,1)S(1)}, bf16[4,96,384]{2,1,0:T(8,128)(2,1)S(1)}, u32[]{:S(2)}, u32[]{:S(2)}) collective-permute-start(bf16[4,96,384]{2,1,0:T(8,128)(2,1)S(1)} %get-tuple-element.101), channel_id=1, source_target_pairs={{0,48},{16,0},{32,16},{48,32},{1,49},{17,1},{33,17},{49,33},{2,50}... | collective-permute-start | bytes 884744 | tf_op jit(solution)/shard_map/ppermute | solution.py:216
  111.0 7.3 %collective-permute-start.23 = (bf16[8,32,384]{2,1,0:T(8,128)(2,1)S(1)}, bf16[8,32,384]{2,1,0:T(8,128)(2,1)S(1)}, u32[]{:S(2)}, u32[]{:S(2)}) collective-permute-start(bf16[8,32,384]{2,1,0:T(8,128)(2,1)S(1)} %get-tuple-element.88), channel_id=1, source_target_pairs={{0,1},{1,2},{2,3},{3,0},{4,5},{5,6},{6,7},{7,4},{8,9},{9,10},{10,1... | collective-permute-start | bytes 589832 | tf_op jit(solution)/shard_map/ppermute | solution.py:216
  118.3 23.0 %collective-permute-start.24 = (bf16[8,32,384]{2,1,0:T(8,128)(2,1)S(1)}, bf16[8,32,384]{2,1,0:T(8,128)(2,1)S(1)}, u32[]{:S(2)}, u32[]{:S(2)}) collective-permute-start(bf16[8,32,384]{2,1,0:T(8,128)(2,1)S(1)} %get-tuple-element.94), channel_id=1, source_target_pairs={{0,2},{1,3},{2,0},{3,1},{4,6},{5,7},{6,4},{7,5},{8,10},{9,11},{10,... | collective-permute-start | bytes 589832 | tf_op jit(solution)/shard_map/ppermute | solution.py:216
  119.3 22.0 %collective-permute-start.25 = (bf16[8,32,384]{2,1,0:T(8,128)(2,1)S(1)}, bf16[8,32,384]{2,1,0:T(8,128)(2,1)S(1)}, u32[]{:S(2)}, u32[]{:S(2)}) collective-permute-start(bf16[8,32,384]{2,1,0:T(8,128)(2,1)S(1)} %get-tuple-element.95), channel_id=1, source_target_pairs={{0,3},{1,0},{2,1},{3,2},{4,7},{5,4},{6,5},{7,6},{8,11},{9,8},{10,9... | collective-permute-start | bytes 589832 | tf_op jit(solution)/shard_map/ppermute | solution.py:216
  123.2 12.0 %collective-permute-start.28 = (bf16[2,96,384]{2,1,0:T(8,128)(2,1)S(1)}, bf16[2,96,384]{2,1,0:T(8,128)(2,1)S(1)}, u32[]{:S(2)}, u32[]{:S(2)}) collective-permute-start(bf16[2,96,384]{2,1,0:T(8,128)(2,1)S(1)} %slice.80), channel_id=1, source_target_pairs={{0,128},{64,192},{128,0},{192,64},{1,129},{65,193},{129,1},{193,65... | collective-permute-start | bytes 442376 | tf_op jit(solution)/shard_map/ppermute | solution.py:306
  135.2 8.7 %collective-permute-start.29 = (bf16[96,384]{1,0:T(8,128)(2,1)S(1)}, bf16[96,384]{1,0:T(8,128)(2,1)S(1)}, u32[]{:S(2)}, u32[]{:S(2)}) collective-permute-start(bf16[96,384]{1,0:T(8,128)(2,1)S(1)} %get-tuple-element.109), channel_id=1, source_target_pairs={{0,0},{64,64},{128,4},{192,68},{4,128},{68,192},{132,132},{196,196... | collective-permute-start | bytes 221192 | tf_op jit(solution)/shard_map/ppermute | solution.py:310
  141.2 7.4 %collective-permute-start.30 = (bf16[96,384]{1,0:T(8,128)(2,1)S(1)}, bf16[96,384]{1,0:T(8,128)(2,1)S(1)}, u32[]{:S(2)}, u32[]{:S(2)}) collective-permute-start(bf16[96,384]{1,0:T(8,128)(2,1)S(1)} %get-tuple-element.110), channel_id=1, source_target_pairs={{0,64},{64,0},{128,68},{192,4},{4,192},{68,128},{132,196},{196,132... | collective-permute-start | bytes 221192 | tf_op jit(solution)/shard_map/ppermute | solution.py:310

commit v6 on v5

--- a/solution.py
+++ b/solution.py
@@ -11,6 +11,7 @@
 ZLO, Y, CORE, ZHI, X = 4, 4, 2, 2, 4
 LOG2E = math.log2(math.e)
 MASKED = -8192.0
+ORDER = (0, 2, 1, 3)
 BF16, F32 = jnp.bfloat16, jnp.float32
 
 
@@ -59,13 +60,13 @@
 
 
 def prepare_kernel(scale, q, grad, outs, keys, values, mask, *made):
-    qg, km, v, g, key_own, value_own, delta = made
+    qg, kvm, g, key_own, value_own, delta = made
     rows, head, width = keys.shape
     put_keys(keys, mask[...], key_own, 0, scale * LOG2E)
     put_values(values, value_own, 0)
     qg[:rows], qg[rows:], g[...] = q[...], grad[...], grad[...]
-    km[:rows], v[...] = keys[...], values[...]
-    km[rows] = jnp.broadcast_to(mask[...], (head, width)).astype(BF16)
+    kvm[:rows], kvm[rows : 2 * rows] = keys[...], values[...]
+    kvm[2 * rows] = jnp.broadcast_to(mask[...], (head, width)).astype(BF16)
     for i in range(rows):
         product = grad[i].astype(F32) * outs[i].astype(F32)
         delta[i : i + 1, :] = jnp.sum(product, axis=0, keepdims=True)
@@ -93,7 +94,7 @@
     bias_n, bias_f = refs[18:]
     rows, width, _ = key_own.shape
     total = X * width
-    put_keys(away, away[rows, 0:1, :].astype(F32), key_t, width, scale * LOG2E)
+    put_keys(away, away[2 * rows, 0:1, :].astype(F32), key_t, width, scale * LOG2E)
     key_t[:, :width, :] = key_own[...]
     stat[:, total:] = delta[...]
     for yd, zd, other, slot, first in bias_pieces(at):
@@ -111,9 +112,9 @@
             augmented = jnp.concatenate((query, query, query, ones), axis=0)
             cols = slice(d * width, (d + 1) * width)
             top, total_sum = None, None
-            for k in range(0, 2 * width, 128):
-                scores = dot(key_t[i, k : k + 128, :112], augmented, 1, 0)
-                scores = (scores + bias_f[k : k + 128, cols]).reshape(16, 8, width)
+            for k in range(0, 2 * width, 64):
+                scores = dot(key_t[i, k : k + 64, :112], augmented, 1, 0)
+                scores = (scores + bias_f[k : k + 64, cols]).reshape(8, 8, width)
                 here = jnp.max(scores, axis=0)
                 if top is None:
                     top = here
@@ -129,19 +130,19 @@
             stat[pl.ds(i, 1), cols] = most + jnp.log(summed) * LOG2E
         return carry
 
-    lax.fori_loop(0, rows, row_step, 0)
+    lax.fori_loop(0, rows, row_step, 0, unroll=2)
 
 
 def main_kernel(at, *refs):
-    q, (g2, keys, away, away_values, key_t, value_own) = refs[0:4], refs[4:10]
-    stats = refs[10:14]
-    bias_t = refs[14]
-    dq = refs[15:19]
-    dk_own, dv_own, dkv_away, bias_own, bias_away = refs[19:24]
-    bias_f, acc, turned, value_t, lse, delta = refs[24:]
-    rows, head, width = away_values.shape
+    q, (g2, keys, away, key_t, value_own) = refs[0:4], refs[4:9]
+    stats = refs[9:13]
+    bias_t = refs[13]
+    dq = refs[14:18]
+    dk_own, dv_own, dkv_away, bias_own, bias_away = refs[18:23]
+    bias_f, acc, turned, value_t, lse, delta = refs[23:]
+    rows, head, width = g2.shape
     total = X * width
-    put_values(away_values, value_t, width)
+    put_values(away.at[rows : 2 * rows], value_t, width)
     value_t[:, :width, :] = value_own[...]
     for d in range(X):
         cols = slice(d * width, (d + 1) * width)
@@ -156,6 +157,7 @@
 
     def row_step(i, carry):
         dk_row, dv_row = None, None
+        both_keys = jnp.concatenate((keys[i], away[i]), axis=1)
         for d in range(X):
             cols = slice(d * width, (d + 1) * width)
             query = q[d][i]
@@ -173,23 +175,20 @@
             dk_part = dot(query, dscores_low, 1, 1)
             dv_row = dv_part if d == 0 else dv_row + dv_part
             dk_row = dk_part if d == 0 else dk_row + dk_part
-            dq_part = dot(keys[i], dscores_low[:width], 1, 0) + dot(
-                away[i], dscores_low[width:], 1, 0
-            )
-            dq[d][i] = dq_part.astype(dq[d].dtype)
+            dq[d][i] = dot(both_keys, dscores_low, 1, 0).astype(dq[d].dtype)
         dk_own[i], dv_own[i] = dk_row[:, :width], dv_row[:, :width]
         dkv_away[i] = dk_row[:, width:].astype(BF16)
         dkv_away[rows + i] = dv_row[:, width:].astype(BF16)
         return carry
 
-    lax.fori_loop(0, rows, row_step, 0)
+    lax.fori_loop(0, rows, row_step, 0, unroll=2)
     for slot in range(2):
         for j in range(0, total, 128):
             tile = acc[slot * width : (slot + 1) * width, j : j + 128].T
             turned[slot, j : j + 128, :] = tile
     for yd, zd, other, slot, first in bias_pieces(at):
         place = bias_own if other == 0 else bias_away
-        place[yd, zd] = turned[slot, pl.ds(first, 96), :].astype(place.dtype)
+        place[yd, ORDER[zd]] = turned[slot, pl.ds(first, 96), :].astype(place.dtype)
 
 
 VMEM = pl.BlockSpec(memory_space=pltpu.VMEM)
@@ -241,23 +240,23 @@
         lambda *refs: prepare_kernel(scale, *refs),
         "prepare",
         [queries, out_grad, outputs, keys, values, mask],
-        [((2 * rows, head, width), BF16), ((rows + 1, head, width), BF16)]
-        + [(block, BF16), (block, BF16), (turned, BF16), (turned, BF16)]
-        + [((rows, width), F32)],
+        [((2 * rows, head, width), BF16), ((2 * rows + 1, head, width), BF16)]
+        + [(block, BF16), (turned, BF16), (turned, BF16), ((rows, width), F32)],
         [],
-        16,
+        8,
         0,
     )
     from_z, q2, made = after((from_z, q2, made))
-    qg, km, own_values, own_grad, key_own, value_own, delta = made
+    qg, kvm, own_grad, key_own, value_own, delta = made
     from_z = jnp.stack(from_z)
-    here = [from_z] + [fetch(from_z, "y", Y, d) for d in range(1, Y)]
+    before, behind = fetch(from_z, "y", Y, 1), fetch(from_z, "y", Y, 3)
     qg1, qg3 = fetch(qg, "x", X, 1), fetch(qg, "x", X, 3)
-    qg1, km = after((qg1, km))
-    away = fetch(km, "zhi", ZHI, 1)
+    away = fetch(kvm, "zhi", ZHI, 1)
+    before, qg3, source = after((before, qg3, from_z))
+    here = [from_z, before, fetch(source, "y", Y, 2), behind]
+    here[2], away = after((here[2], away))
     there = [fetch(a, "core", CORE, 1) for a in here]
-    away, own_values, own_grad = after((away, own_values, own_grad))
-    away_values = fetch(own_values, "zhi", ZHI, 1)
+    qg1, own_grad = after((qg1, own_grad))
     g2 = fetch(own_grad, "x", X, 2)
     q = [qg, qg1, q2, qg3]
 
@@ -267,16 +266,16 @@
         [at, *q, away, key_own, delta, *here, *there],
         [((rows, total + width), F32), ((both, total), BF16), ((rows, both, 128), BF16)],
         [((2, total, width), BF16), ((both, total), F32)],
-        24,
+        14,
     )
-    stat, away_values, g2 = after((stat, away_values, g2))
+    stat, g2 = after((stat, g2))
     stats = [stat] + [fetch(stat, "x", X, d) for d in range(1, X)]
 
     pieces = (Y, ZLO, 96, width)
     results = call(
         main_kernel,
         "attention_gradients",
-        [at, *q, g2, km, away, away_values, key_t, value_own, *stats, bias_t],
+        [at, *q, g2, kvm, away, key_t, value_own, *stats, bias_t],
         [(block, F32)]
         + [(block, BF16)] * 3
         + [(block, F32)] * 2
@@ -289,7 +288,7 @@
             ((rows, total), F32),
             ((rows, total), F32),
         ],
-        40,
+        30,
     )
     dq, (dk, dv, dkv_away, bias_own, bias_away) = results[0:4], results[4:9]
 
@@ -298,15 +297,16 @@
     sent, first = after(([near[d].astype(BF16) for d in range(1, Y)], dq[1]))
     far = [deliver(sent[d - 1], "y", Y, d) for d in range(1, Y)]
     first = deliver(first, "x", X, 1)
-    far[0], arrived, first, dq = after((far[0], arrived, first, dq))
+    far[0], arrived, first = after((far[0], arrived, first))
     along_y = near[0]
     for part in far:
         along_y = along_y + part.astype(F32)
-    across = [(n, n ^ 2) for n in range(ZLO)]
+    along_y, dq = after((along_y, dq))
+    across = [(n, n ^ 1) for n in range(ZLO)]
     kept = along_y[:2] + lax.ppermute(along_y[2:].astype(BF16), "zlo", across).astype(F32)
     bias_grad = None
     for d in range(2):
-        pairs = [(worker, owner) for owner, worker in z_pairs(d)]
+        pairs = [(worker, owner) for owner, worker in z_pairs(2 * d)]
         part = lax.ppermute(kept[d].astype(BF16), z_axes, pairs).astype(F32)
         bias_grad = part if bias_grad is None else bias_grad + part
 

time: 150 us -> 141 us (0.940)
  starting transfers between devices: 61.6 us -> 51 us
  waiting for transfers between devices: 32.1 us -> 37.2 us
  Pallas kernels: 44.6 us -> 41.1 us
    ppermute x6, waiting for transfers between devices: 3.09 us -> 7.93 us  [deliver(): lax.ppermute(x, axis, [(n, (n + distance) % size) for n in range(size)])]
    ppermute x18 -> x17, waiting for transfers between devices: 19.9 us -> 23.6 us  [fetch(): lax.ppermute(x, axis, [((n + distance) % size, n) for n in range(size)])]
    pallas_call x3, Pallas kernels: 44.6 us -> 41.1 us  [call(): pl.pallas_call(kernel, in_specs=[SMEM] * places + [VMEM] * (len(args) - p...]
    ppermute x18 -> x17, starting transfers between devices: 25.7 us -> 22.3 us  [fetch(): lax.ppermute(x, axis, [((n + distance) % size, n) for n in range(size)])]
    ppermute x1, starting transfers between devices: 8.44 us -> 5.45 us  [per_device(): lax.ppermute(along_y[2:].astype(BF16), 'zlo', across).astype(F32)]
    ppermute x1, waiting for transfers between devices: 2.56 us -> 0.01 us  [per_device(): lax.ppermute(along_y[2:].astype(BF16), 'zlo', across).astype(F32)]
    ppermute x6, starting transfers between devices: 9.29 us -> 6.76 us  [deliver(): lax.ppermute(x, axis, [(n, (n + distance) % size) for n in range(size)])]
    ppermute x2, starting transfers between devices: 6.07 us -> 4.49 us  [per_device(): part = lax.ppermute(kept[d].astype(BF16), z_axes, pairs).astype(F32)]
  transfers between devices with their start and end apart: 31 -> 30, of which waited for: 13 -> 14; matrix products, arithmetic and copies ran while one was open for 2% -> 2% of each run, Pallas kernels for 10% -> 10%
where the time goes in v6:
time: 141 us
  starting transfers between devices  51 us (36%)
  Pallas kernels  41.1 us (29%)
  waiting for transfers between devices  37.2 us (26%)
  local copies, waits for them, and re-layouts  7.2 us (5%)
  other arithmetic  3.69 us (3%)
    pallas_call x3, Pallas kernels, call(): pl.pallas_call(kernel, in_specs=[SMEM] * places + [VMEM] * (len(args) - p...  41.1 us
    ppermute x17, waiting for transfers between devices, fetch(): lax.ppermute(x, axis, [((n + distance) % size, n) for n in range(size)])  23.6 us
    ppermute x17, starting transfers between devices, fetch(): lax.ppermute(x, axis, [((n + distance) % size, n) for n in range(size)])  22.3 us
    ppermute x4, starting transfers between devices, per_device(): from_z = [lax.ppermute(bias, z_axes, z_pairs(d)) for d in range(ZLO)]  12.1 us
    ppermute x6, waiting for transfers between devices, deliver(): lax.ppermute(x, axis, [(n, (n + distance) % size) for n in range(size)])  7.93 us
    unnamed x20, local copies, waits for them, and re-layouts  6.98 us
    ppermute x6, starting transfers between devices, deliver(): lax.ppermute(x, axis, [(n, (n + distance) % size) for n in range(size)])  6.76 us
    ppermute x2, waiting for transfers between devices, per_device(): part = lax.ppermute(kept[d].astype(BF16), z_axes, pairs).astype(F32)  5.58 us
  transfers between devices with their start and end apart: 30, of which 14 were waited for; matrix products, arithmetic and copies ran while one was open for 2% of the time, Pallas kernels for 10%

profile of v6, /device:TPU:64, one launch (start us, length us, event | category | flops | bytes accessed | tf_op | source)
XLA Modules:
  0.0 141.0 jit_solution(13355129202102545043)
XLA Ops:
  0.6 3.1 %collective-permute-start.4 = (bf16[8,32,384]{2,1,0:T(8,128)(2,1)}, bf16[8,32,384]{2,1,0:T(8,128)(2,1)S(1)}, u32[]{:S(2)}, u32[]{:S(2)}) collective-permute-start(bf16[8,32,384]{2,1,0:T(8,128)(2,1)} %refs_0_.1), channel_id=1, source_target_pairs={{2,0},{3,1},{0,2},{1,3},{6,4},{7,5},{4,6},{5,7},{10,8},{11,9},{8,1... | collective-permute-start | bytes 589832 | tf_op jit(solution)/shard_map/ppermute | solution.py:211
  3.7 4.9 %collective-permute-start.1 = (bf16[96,384]{1,0:T(8,128)(2,1)}, bf16[96,384]{1,0:T(8,128)(2,1)S(1)}, u32[]{:S(2)}, u32[]{:S(2)}) collective-permute-start(bf16[96,384]{1,0:T(8,128)(2,1)} %param.12), channel_id=1, source_target_pairs={{64,0},{0,64},{68,128},{4,192},{192,4},{128,68},{196,132},{132,196... | collective-permute-start | bytes 221192 | tf_op jit(solution)/shard_map/ppermute | solution.py:236
  8.7 1.9 %collective-permute-start = (bf16[96,384]{1,0:T(8,128)(2,1)}, bf16[96,384]{1,0:T(8,128)(2,1)S(1)}, u32[]{:S(2)}, u32[]{:S(2)}) collective-permute-start(bf16[96,384]{1,0:T(8,128)(2,1)} %param.12), channel_id=1, source_target_pairs={{0,0},{64,64},{4,128},{68,192},{128,4},{192,68},{132,132},{196,196... | collective-permute-start | bytes 221192 | tf_op jit(solution)/shard_map/ppermute | solution.py:236
  10.6 0.6 collective-permute-start.3
  11.2 4.6 %collective-permute-start.2 = (bf16[96,384]{1,0:T(8,128)(2,1)}, bf16[96,384]{1,0:T(8,128)(2,1)S(1)}, u32[]{:S(2)}, u32[]{:S(2)}) collective-permute-start(bf16[96,384]{1,0:T(8,128)(2,1)} %param.12), channel_id=1, source_target_pairs={{4,0},{68,64},{0,128},{64,192},{132,4},{196,68},{128,132},{192,196... | collective-permute-start | bytes 221192 | tf_op jit(solution)/shard_map/ppermute | solution.py:236
  15.8 0.7 convert_element_type.66
  16.5 0.9 copy-done.5
  17.4 0.9 copy-done.6
  18.3 0.9 copy-done.7
  19.3 0.9 copy-done.8
  20.2 0.9 copy-done.9
  21.1 2.5 %prepare.1 = (bf16[16,32,384]{2,1,0:T(8,128)(2,1)S(1)}, bf16[17,32,384]{2,1,0:T(8,128)(2,1)S(1)}, bf16[8,32,384]{2,1,0:T(8,128)(2,1)}, bf16[8,384,128]{2,1,0:T(8...) custom-call(bf16[8,32,384]{2,1,0:T(8,128)(2,1)S(1)} %copy-done.9, ...), custom_call_target="tpu_custom_call" | custom-call | tf_op jit(solution)/shard_map/prepare/pallas_call | solution.py:199
  23.6 0.0 collective-permute-done.2
  23.6 0.0 collective-permute-done.4.refs_3_.refs_2_
  23.6 0.0 copy-start
  23.6 0.7 copy-done
  24.3 0.6 collective-permute-start.7
  24.9 3.1 %collective-permute-start.6 = (bf16[4,96,384]{2,1,0:T(8,128)(2,1)S(1)}, bf16[4,96,384]{2,1,0:T(8,128)(2,1)}, u32[]{:S(2)}, u32[]{:S(2)}) collective-permute-start(bf16[4,96,384]{2,1,0:T(8,128)(2,1)S(1)} %pad_maximum_fusion.refs_8_), channel_id=1, source_target_pairs={{16,0},{32,16},{48,32},{0,48},{17,1},{33,17},{49,33},{1,49},{18,2}... | collective-permute-start | bytes 884744 | tf_op jit(solution)/shard_map/ppermute | solution.py:211
  28.0 1.5 %collective-permute-start.9 = (bf16[17,32,384]{2,1,0:T(8,128)(2,1)S(1)}, bf16[17,32,384]{2,1,0:T(8,128)(2,1)S(1)}, u32[]{:S(2)}, u32[]{:S(2)}) collective-permute-start(bf16[17,32,384]{2,1,0:T(8,128)(2,1)S(1)} %get-tuple-element.69.refs_5_), channel_id=1, source_target_pairs={{4,0},{0,4},{5,1},{1,5},{6,2},{2,6},{7,3},{3,7},{12,8},{8,12},{13,... | collective-permute-start | bytes 1253384 | tf_op jit(solution)/shard_map/ppermute | solution.py:211
  29.5 0.7 copy-done.3
  30.3 0.0 collective-permute-start.10
  30.3 2.3 %collective-permute-done.6.refs_9_ = bf16[4,96,384]{2,1,0:T(8,128)(2,1)} collective-permute-done((bf16[4,96,384]{2,1,0:T(8,128)(2,1)S(1)}, bf16[4,96,384]{2,1,0:T(8,128)(2,1)}, u32[]{:S(2)}, u32[]{:S(2)}) %collective-permute-start.6) | collective-permute-done | bytes 294944 | tf_op jit(solution)/shard_map/ppermute | solution.py:211
  32.6 2.3 %collective-permute-done.7.refs_4_.refs_3_ = bf16[16,32,384]{2,1,0:T(8,128)(2,1)S(1)} collective-permute-done((bf16[16,32,384]{2,1,0:T(8,128)(2,1)S(1)}, bf16[16,32,384]{2,1,0:T(8,128)(2,1)S(1)}, u32[]{:S(2)}, u32[]{:S(2)}) %collective-permute-start.7) | collective-permute-done | bytes 393248 | tf_op jit(solution)/shard_map/ppermute | solution.py:211
  35.0 3.2 %collective-permute-start.8 = (bf16[4,96,384]{2,1,0:T(8,128)(2,1)S(1)}, bf16[4,96,384]{2,1,0:T(8,128)(2,1)}, u32[]{:S(2)}, u32[]{:S(2)}) collective-permute-start(bf16[4,96,384]{2,1,0:T(8,128)(2,1)S(1)} %pad_maximum_fusion.refs_8_), channel_id=1, source_target_pairs={{32,0},{48,16},{0,32},{16,48},{33,1},{49,17},{1,33},{17,49},{34,2}... | collective-permute-start | bytes 884744 | tf_op jit(solution)/shard_map/ppermute | solution.py:211
  38.2 6.5 %collective-permute-done.10.refs_11_ = bf16[4,96,384]{2,1,0:T(8,128)(2,1)} collective-permute-done((bf16[4,96,384]{2,1,0:T(8,128)(2,1)S(1)}, bf16[4,96,384]{2,1,0:T(8,128)(2,1)}, u32[]{:S(2)}, u32[]{:S(2)}) %collective-permute-start.10) | collective-permute-done | bytes 294944 | tf_op jit(solution)/shard_map/ppermute | solution.py:211
  44.7 1.1 collective-permute-done.9.refs_5_.refs_6_
  45.8 0.5 collective-permute-start.13
  46.3 0.1 collective-permute-done.5.refs_2_.refs_1_
  46.4 1.9 %collective-permute-start.15 = (bf16[8,32,384]{2,1,0:T(8,128)(2,1)}, bf16[8,32,384]{2,1,0:T(8,128)(2,1)}, u32[]{:S(2)}, u32[]{:S(2)}) collective-permute-start(bf16[8,32,384]{2,1,0:T(8,128)(2,1)} %get-tuple-element.76), channel_id=1, source_target_pairs={{2,0},{3,1},{0,2},{1,3},{6,4},{7,5},{4,6},{5,7},{10,8},{11,9},{8,1... | collective-permute-start | bytes 589832 | tf_op jit(solution)/shard_map/ppermute | solution.py:211
  48.3 0.1 stack.38.refs_0_.at
  48.4 0.0 copy-start.1
  48.4 0.9 copy-done.1
  49.4 11.8 %softmax_statistics.1 = (f32[8,1920]{1,0:T(8,128)S(1)}, bf16[768,1536]{1,0:T(8,128)(2,1)S(1)}, bf16[8,768,128]{2,1,0:T(8,128)(2,1)S(1)}) custom-call(s32[5]{0:T(128)S(1)} %stack.38.refs_0_.at, bf16[16,32,384]{2,1,0:T(8,128)(2,1)S(1)} %get-tuple-element.59.refs_1_.refs_0_, bf16[16,32,384]{2,1,0:T(8,128)(2,1)S(1)} %collective-permute-done.5.refs_2_.refs_1_, ...), custom_call_target="tpu_custom_call" | custom-call | tf_op jit(solution)/shard_map/softmax_statistics/pallas_call | solution.py:199
  61.1 1.6 %collective-permute-start.18 = (f32[8,1920]{1,0:T(8,128)S(1)}, f32[8,1920]{1,0:T(8,128)S(1)}, u32[]{:S(2)}, u32[]{:S(2)}) collective-permute-start(f32[8,1920]{1,0:T(8,128)S(1)} %get-tuple-element.80.refs_9_), channel_id=1, source_target_pairs={{3,0},{0,1},{1,2},{2,3},{7,4},{4,5},{5,6},{6,7},{11,8},{8,9},{9,10... | collective-permute-start | bytes 184328 | tf_op jit(solution)/shard_map/ppermute | solution.py:211
  62.7 2.3 %collective-permute-start.17 = (f32[8,1920]{1,0:T(8,128)S(1)}, f32[8,1920]{1,0:T(8,128)S(1)}, u32[]{:S(2)}, u32[]{:S(2)}) collective-permute-start(f32[8,1920]{1,0:T(8,128)S(1)} %get-tuple-element.80.refs_9_), channel_id=1, source_target_pairs={{2,0},{3,1},{0,2},{1,3},{6,4},{7,5},{4,6},{5,7},{10,8},{11,9},{8,1... | collective-permute-start | bytes 184328 | tf_op jit(solution)/shard_map/ppermute | solution.py:211
  65.0 0.5 collective-permute-start.16
  65.6 1.3 collective-permute-done.18.refs_12_
  66.8 1.7 %collective-permute-done.17.refs_11_ = f32[8,1920]{1,0:T(8,128)S(1)} collective-permute-done((f32[8,1920]{1,0:T(8,128)S(1)}, f32[8,1920]{1,0:T(8,128)S(1)}, u32[]{:S(2)}, u32[]{:S(2)}) %collective-permute-start.17) | collective-permute-done | bytes 61472 | tf_op jit(solution)/shard_map/ppermute | solution.py:211
  68.5 0.8 collective-permute-done.16.refs_10_
  69.2 26.9 %attention_gradients.1 = (f32[8,32,384]{2,1,0:T(8,128)S(1)}, bf16[8,32,384]{2,1,0:T(8,128)(2,1)S(1)}, bf16[8,32,384]{2,1,0:T(8,128)(2,1)S(1)}, bf16[8,32,384]{2,...) custom-call(s32[5]{0:T(128)S(1)} %stack.38.refs_0_.at, ...), custom_call_target="tpu_custom_call" | custom-call | tf_op jit(solution)/shard_map/attention_gradients/pallas_call | solution.py:199
  96.1 0.1 collective-permute-start.19
  96.2 3.9 %collective-permute-start.21 = (bf16[16,32,384]{2,1,0:T(8,128)(2,1)S(1)}, bf16[16,32,384]{2,1,0:T(8,128)(2,1)S(1)}, u32[]{:S(2)}, u32[]{:S(2)}) collective-permute-start(bf16[16,32,384]{2,1,0:T(8,128)(2,1)S(1)} %get-tuple-element.86), channel_id=1, source_target_pairs={{4,0},{0,4},{5,1},{1,5},{6,2},{2,6},{7,3},{3,7},{12,8},{8,12},{13,... | collective-permute-start | bytes 1179656 | tf_op jit(solution)/shard_map/ppermute | solution.py:211
  100.1 0.4 fusion.6
  100.5 0.1 slice_bitcast_fusion.1
  100.6 0.1 collective-permute-start.20
  100.7 2.2 %collective-permute-start.23 = (bf16[4,96,384]{2,1,0:T(8,128)(2,1)S(1)}, bf16[4,96,384]{2,1,0:T(8,128)(2,1)S(1)}, u32[]{:S(2)}, u32[]{:S(2)}) collective-permute-start(bf16[4,96,384]{2,1,0:T(8,128)(2,1)S(1)} %get-tuple-element.89), channel_id=1, source_target_pairs={{0,32},{16,48},{32,0},{48,16},{1,33},{17,49},{33,1},{49,17},{2,34}... | collective-permute-start | bytes 884744 | tf_op jit(solution)/shard_map/ppermute | solution.py:215
  102.9 1.1 collective-permute-start.24
  103.9 0.4 collective-permute-start.22
  104.3 7.5 %collective-permute-done.21 = bf16[16,32,384]{2,1,0:T(8,128)(2,1)S(1)} collective-permute-done((bf16[16,32,384]{2,1,0:T(8,128)(2,1)S(1)}, bf16[16,32,384]{2,1,0:T(8,128)(2,1)S(1)}, u32[]{:S(2)}, u32[]{:S(2)}) %collective-permute-start.21) | collective-permute-done | bytes 393248 | tf_op jit(solution)/shard_map/ppermute | solution.py:211
  111.8 5.4 %collective-permute-done.20 = bf16[4,96,384]{2,1,0:T(8,128)(2,1)S(1)} collective-permute-done((bf16[4,96,384]{2,1,0:T(8,128)(2,1)S(1)}, bf16[4,96,384]{2,1,0:T(8,128)(2,1)S(1)}, u32[]{:S(2)}, u32[]{:S(2)}) %collective-permute-start.20) | collective-permute-done | bytes 294944 | tf_op jit(solution)/shard_map/ppermute | solution.py:215
  117.2 0.6 collective-permute-done.24
  117.9 0.1 fusion.2
  118.0 5.4 %collective-permute-start.27 = (bf16[2,96,384]{2,1,0:T(8,128)(2,1)S(1)}, bf16[2,96,384]{2,1,0:T(8,128)(2,1)S(1)}, u32[]{:S(2)}, u32[]{:S(2)}) collective-permute-start(bf16[2,96,384]{2,1,0:T(8,128)(2,1)S(1)} %slice.77), channel_id=1, source_target_pairs={{0,64},{64,0},{128,192},{192,128},{1,65},{65,1},{129,193},{193,129... | collective-permute-start | bytes 442376 | tf_op jit(solution)/shard_map/ppermute | solution.py:306
  123.5 1.5 %collective-permute-start.25 = (bf16[8,32,384]{2,1,0:T(8,128)(2,1)S(1)}, bf16[8,32,384]{2,1,0:T(8,128)(2,1)S(1)}, u32[]{:S(2)}, u32[]{:S(2)}) collective-permute-start(bf16[8,32,384]{2,1,0:T(8,128)(2,1)S(1)} %get-tuple-element.96), channel_id=1, source_target_pairs={{0,2},{1,3},{2,0},{3,1},{4,6},{5,7},{6,4},{7,5},{8,10},{9,11},{10,... | collective-permute-start | bytes 589832 | tf_op jit(solution)/shard_map/ppermute | solution.py:215
  125.0 1.5 %collective-permute-start.26 = (bf16[8,32,384]{2,1,0:T(8,128)(2,1)S(1)}, bf16[8,32,384]{2,1,0:T(8,128)(2,1)S(1)}, u32[]{:S(2)}, u32[]{:S(2)}) collective-permute-start(bf16[8,32,384]{2,1,0:T(8,128)(2,1)S(1)} %get-tuple-element.97), channel_id=1, source_target_pairs={{0,3},{1,0},{2,1},{3,2},{4,7},{5,4},{6,5},{7,6},{8,11},{9,8},{10,9... | collective-permute-start | bytes 589832 | tf_op jit(solution)/shard_map/ppermute | solution.py:215
  126.5 0.1 convert_element_type.78
  126.6 0.9 fusion.3
  127.5 4.4 %collective-permute-start.28 = (bf16[96,384]{1,0:T(8,128)(2,1)S(1)}, bf16[96,384]{1,0:T(8,128)(2,1)S(1)}, u32[]{:S(2)}, u32[]{:S(2)}) collective-permute-start(bf16[96,384]{1,0:T(8,128)(2,1)S(1)} %get-tuple-element.109), channel_id=1, source_target_pairs={{0,0},{64,64},{128,4},{192,68},{4,128},{68,192},{132,132},{196,196... | collective-permute-start | bytes 221192 | tf_op jit(solution)/shard_map/ppermute | solution.py:310
  132.0 0.1 collective-permute-start.29
  132.1 1.9 %collective-permute-done.26 = bf16[8,32,384]{2,1,0:T(8,128)(2,1)S(1)} collective-permute-done((bf16[8,32,384]{2,1,0:T(8,128)(2,1)S(1)}, bf16[8,32,384]{2,1,0:T(8,128)(2,1)S(1)}, u32[]{:S(2)}, u32[]{:S(2)}) %collective-permute-start.26) | collective-permute-done | bytes 196640 | tf_op jit(solution)/shard_map/ppermute | solution.py:215
  133.9 0.8 multiply_convert_fusion
  134.7 2.0 %collective-permute-done.28 = bf16[96,384]{1,0:T(8,128)(2,1)S(1)} collective-permute-done((bf16[96,384]{1,0:T(8,128)(2,1)S(1)}, bf16[96,384]{1,0:T(8,128)(2,1)S(1)}, u32[]{:S(2)}, u32[]{:S(2)}) %collective-permute-start.28) | collective-permute-done | bytes 73760 | tf_op jit(solution)/shard_map/ppermute | solution.py:310
  136.7 3.6 %collective-permute-done.29 = bf16[96,384]{1,0:T(8,128)(2,1)S(1)} collective-permute-done((bf16[96,384]{1,0:T(8,128)(2,1)S(1)}, bf16[96,384]{1,0:T(8,128)(2,1)S(1)}, u32[]{:S(2)}, u32[]{:S(2)}) %collective-permute-start.29) | collective-permute-done | bytes 73760 | tf_op jit(solution)/shard_map/ppermute | solution.py:310
  140.3 0.7 convert_add_fusion.1
  (33 shorter events, 0.2 us)
Async XLA Ops:
  0.6 23.0 %collective-permute-start.4 = (bf16[8,32,384]{2,1,0:T(8,128)(2,1)}, bf16[8,32,384]{2,1,0:T(8,128)(2,1)S(1)}, u32[]{:S(2)}, u32[]{:S(2)}) collective-permute-start(bf16[8,32,384]{2,1,0:T(8,128)(2,1)} %refs_0_.1), channel_id=1, source_target_pairs={{2,0},{3,1},{0,2},{1,3},{6,4},{7,5},{4,6},{5,7},{10,8},{11,9},{8,1... | collective-permute-start | bytes 589832 | tf_op jit(solution)/shard_map/ppermute | solution.py:211
  3.7 19.8 %collective-permute-start.1 = (bf16[96,384]{1,0:T(8,128)(2,1)}, bf16[96,384]{1,0:T(8,128)(2,1)S(1)}, u32[]{:S(2)}, u32[]{:S(2)}) collective-permute-start(bf16[96,384]{1,0:T(8,128)(2,1)} %param.12), channel_id=1, source_target_pairs={{64,0},{0,64},{68,128},{4,192},{192,4},{128,68},{196,132},{132,196... | collective-permute-start | bytes 221192 | tf_op jit(solution)/shard_map/ppermute | solution.py:236
  8.7 14.9 %collective-permute-start = (bf16[96,384]{1,0:T(8,128)(2,1)}, bf16[96,384]{1,0:T(8,128)(2,1)S(1)}, u32[]{:S(2)}, u32[]{:S(2)}) collective-permute-start(bf16[96,384]{1,0:T(8,128)(2,1)} %param.12), channel_id=1, source_target_pairs={{0,0},{64,64},{4,128},{68,192},{128,4},{192,68},{132,132},{196,196... | collective-permute-start | bytes 221192 | tf_op jit(solution)/shard_map/ppermute | solution.py:236
  10.6 13.0 %collective-permute-start.3 = (bf16[96,384]{1,0:T(8,128)(2,1)}, bf16[96,384]{1,0:T(8,128)(2,1)S(1)}, u32[]{:S(2)}, u32[]{:S(2)}) collective-permute-start(bf16[96,384]{1,0:T(8,128)(2,1)} %param.12), channel_id=1, source_target_pairs={{68,0},{4,64},{64,128},{0,192},{196,4},{132,68},{192,132},{128,196... | collective-permute-start | bytes 221192 | tf_op jit(solution)/shard_map/ppermute | solution.py:236
  11.2 12.4 %collective-permute-start.2 = (bf16[96,384]{1,0:T(8,128)(2,1)}, bf16[96,384]{1,0:T(8,128)(2,1)S(1)}, u32[]{:S(2)}, u32[]{:S(2)}) collective-permute-start(bf16[96,384]{1,0:T(8,128)(2,1)} %param.12), channel_id=1, source_target_pairs={{4,0},{68,64},{0,128},{64,192},{132,4},{196,68},{128,132},{192,196... | collective-permute-start | bytes 221192 | tf_op jit(solution)/shard_map/ppermute | solution.py:236
  16.5 0.9 copy-start.5
  17.4 0.9 copy-start.6
  18.3 0.9 copy-start.7
  19.3 0.9 copy-start.8
  20.2 0.9 copy-start.9
  23.6 0.7 copy-start
  24.3 10.7 %collective-permute-start.7 = (bf16[16,32,384]{2,1,0:T(8,128)(2,1)S(1)}, bf16[16,32,384]{2,1,0:T(8,128)(2,1)S(1)}, u32[]{:S(2)}, u32[]{:S(2)}) collective-permute-start(bf16[16,32,384]{2,1,0:T(8,128)(2,1)S(1)} %get-tuple-element.59.refs_1_.refs_0_), channel_id=1, source_target_pairs={{3,0},{0,1},{1,2},{2,3},{7,4},{4,5},{5,6},{6,7},{11,8},{8,9},{9,10... | collective-permute-start | bytes 1179656 | tf_op jit(solution)/shard_map/ppermute | solution.py:211
  24.9 7.7 %collective-permute-start.6 = (bf16[4,96,384]{2,1,0:T(8,128)(2,1)S(1)}, bf16[4,96,384]{2,1,0:T(8,128)(2,1)}, u32[]{:S(2)}, u32[]{:S(2)}) collective-permute-start(bf16[4,96,384]{2,1,0:T(8,128)(2,1)S(1)} %pad_maximum_fusion.refs_8_), channel_id=1, source_target_pairs={{16,0},{32,16},{48,32},{0,48},{17,1},{33,17},{49,33},{1,49},{18,2}... | collective-permute-start | bytes 884744 | tf_op jit(solution)/shard_map/ppermute | solution.py:211
  28.0 17.8 %collective-permute-start.9 = (bf16[17,32,384]{2,1,0:T(8,128)(2,1)S(1)}, bf16[17,32,384]{2,1,0:T(8,128)(2,1)S(1)}, u32[]{:S(2)}, u32[]{:S(2)}) collective-permute-start(bf16[17,32,384]{2,1,0:T(8,128)(2,1)S(1)} %get-tuple-element.69.refs_5_), channel_id=1, source_target_pairs={{4,0},{0,4},{5,1},{1,5},{6,2},{2,6},{7,3},{3,7},{12,8},{8,12},{13,... | collective-permute-start | bytes 1253384 | tf_op jit(solution)/shard_map/ppermute | solution.py:211
  29.5 0.7 copy-start.3
  30.3 14.4 %collective-permute-start.10 = (bf16[4,96,384]{2,1,0:T(8,128)(2,1)S(1)}, bf16[4,96,384]{2,1,0:T(8,128)(2,1)}, u32[]{:S(2)}, u32[]{:S(2)}) collective-permute-start(bf16[4,96,384]{2,1,0:T(8,128)(2,1)S(1)} %pad_maximum_fusion.refs_8_), channel_id=1, source_target_pairs={{48,0},{0,16},{16,32},{32,48},{49,1},{1,17},{17,33},{33,49},{50,2}... | collective-permute-start | bytes 884744 | tf_op jit(solution)/shard_map/ppermute | solution.py:211
  35.0 10.8 %collective-permute-start.8 = (bf16[4,96,384]{2,1,0:T(8,128)(2,1)S(1)}, bf16[4,96,384]{2,1,0:T(8,128)(2,1)}, u32[]{:S(2)}, u32[]{:S(2)}) collective-permute-start(bf16[4,96,384]{2,1,0:T(8,128)(2,1)S(1)} %pad_maximum_fusion.refs_8_), channel_id=1, source_target_pairs={{32,0},{48,16},{0,32},{16,48},{33,1},{49,17},{1,33},{17,49},{34,2}... | collective-permute-start | bytes 884744 | tf_op jit(solution)/shard_map/ppermute | solution.py:211
  38.2 8.2 %collective-permute-start.5 = (bf16[16,32,384]{2,1,0:T(8,128)(2,1)S(1)}, bf16[16,32,384]{2,1,0:T(8,128)(2,1)S(1)}, u32[]{:S(2)}, u32[]{:S(2)}) collective-permute-start(bf16[16,32,384]{2,1,0:T(8,128)(2,1)S(1)} %get-tuple-element.59.refs_1_.refs_0_), channel_id=1, source_target_pairs={{1,0},{2,1},{3,2},{0,3},{5,4},{6,5},{7,6},{4,7},{9,8},{10,9},{11,1... | collective-permute-start | bytes 1179656 | tf_op jit(solution)/shard_map/ppermute | solution.py:211
  38.2 10.2 %collective-permute-start.11 = (bf16[4,96,384]{2,1,0:T(8,128)(2,1)S(1)}, bf16[4,96,384]{2,1,0:T(8,128)(2,1)}, u32[]{:S(2)}, u32[]{:S(2)}) collective-permute-start(bf16[4,96,384]{2,1,0:T(8,128)(2,1)S(1)} %pad_maximum_fusion.refs_8_), channel_id=1, source_target_pairs={{8,0},{0,8},{9,1},{1,9},{10,2},{2,10},{11,3},{3,11},{12,4},{4,12},... | collective-permute-start | bytes 884744 | tf_op jit(solution)/shard_map/ppermute | solution.py:211
  44.6 3.8 %collective-permute-start.14 = (bf16[4,96,384]{2,1,0:T(8,128)(2,1)}, bf16[4,96,384]{2,1,0:T(8,128)(2,1)}, u32[]{:S(2)}, u32[]{:S(2)}) collective-permute-start(bf16[4,96,384]{2,1,0:T(8,128)(2,1)} %collective-permute-done.10.refs_11_), channel_id=1, source_target_pairs={{8,0},{0,8},{9,1},{1,9},{10,2},{2,10},{11,3},{3,11},{12,4},{4,12},... | collective-permute-start | bytes 884744 | tf_op jit(solution)/shard_map/ppermute | solution.py:211
  45.8 2.6 %collective-permute-start.12 = (bf16[4,96,384]{2,1,0:T(8,128)(2,1)}, bf16[4,96,384]{2,1,0:T(8,128)(2,1)}, u32[]{:S(2)}, u32[]{:S(2)}) collective-permute-start(bf16[4,96,384]{2,1,0:T(8,128)(2,1)} %collective-permute-done.6.refs_9_), channel_id=1, source_target_pairs={{8,0},{0,8},{9,1},{1,9},{10,2},{2,10},{11,3},{3,11},{12,4},{4,12},... | collective-permute-start | bytes 884744 | tf_op jit(solution)/shard_map/ppermute | solution.py:211
  45.8 2.6 %collective-permute-start.13 = (bf16[4,96,384]{2,1,0:T(8,128)(2,1)}, bf16[4,96,384]{2,1,0:T(8,128)(2,1)}, u32[]{:S(2)}, u32[]{:S(2)}) collective-permute-start(bf16[4,96,384]{2,1,0:T(8,128)(2,1)} %collective-permute-done.8.refs_10_), channel_id=1, source_target_pairs={{8,0},{0,8},{9,1},{1,9},{10,2},{2,10},{11,3},{3,11},{12,4},{4,12},... | collective-permute-start | bytes 884744 | tf_op jit(solution)/shard_map/ppermute | solution.py:211
  46.4 14.7 %collective-permute-start.15 = (bf16[8,32,384]{2,1,0:T(8,128)(2,1)}, bf16[8,32,384]{2,1,0:T(8,128)(2,1)}, u32[]{:S(2)}, u32[]{:S(2)}) collective-permute-start(bf16[8,32,384]{2,1,0:T(8,128)(2,1)} %get-tuple-element.76), channel_id=1, source_target_pairs={{2,0},{3,1},{0,2},{1,3},{6,4},{7,5},{4,6},{5,7},{10,8},{11,9},{8,1... | collective-permute-start | bytes 589832 | tf_op jit(solution)/shard_map/ppermute | solution.py:211
  48.4 0.9 copy-start.1
  49.4 19.9 %copy-start.2 = (bf16[8,32,384]{2,1,0:T(8,128)(2,1)S(1)}, bf16[8,32,384]{2,1,0:T(8,128)(2,1)}, u32[]{:S(2)}) copy-start(bf16[8,32,384]{2,1,0:T(8,128)(2,1)} %copy-done) | copy-start | bytes 589828
  49.4 19.9 %copy-start.4 = (bf16[17,32,384]{2,1,0:T(8,128)(2,1)S(1)}, bf16[17,32,384]{2,1,0:T(8,128)(2,1)}, u32[]{:S(2)}) copy-start(bf16[17,32,384]{2,1,0:T(8,128)(2,1)} %copy-done.3) | copy-start | bytes 1253380
  61.1 5.7 %collective-permute-start.18 = (f32[8,1920]{1,0:T(8,128)S(1)}, f32[8,1920]{1,0:T(8,128)S(1)}, u32[]{:S(2)}, u32[]{:S(2)}) collective-permute-start(f32[8,1920]{1,0:T(8,128)S(1)} %get-tuple-element.80.refs_9_), channel_id=1, source_target_pairs={{3,0},{0,1},{1,2},{2,3},{7,4},{4,5},{5,6},{6,7},{11,8},{8,9},{9,10... | collective-permute-start | bytes 184328 | tf_op jit(solution)/shard_map/ppermute | solution.py:211
  62.7 5.8 %collective-permute-start.17 = (f32[8,1920]{1,0:T(8,128)S(1)}, f32[8,1920]{1,0:T(8,128)S(1)}, u32[]{:S(2)}, u32[]{:S(2)}) collective-permute-start(f32[8,1920]{1,0:T(8,128)S(1)} %get-tuple-element.80.refs_9_), channel_id=1, source_target_pairs={{2,0},{3,1},{0,2},{1,3},{6,4},{7,5},{4,6},{5,7},{10,8},{11,9},{8,1... | collective-permute-start | bytes 184328 | tf_op jit(solution)/shard_map/ppermute | solution.py:211
  65.0 4.2 %collective-permute-start.16 = (f32[8,1920]{1,0:T(8,128)S(1)}, f32[8,1920]{1,0:T(8,128)S(1)}, u32[]{:S(2)}, u32[]{:S(2)}) collective-permute-start(f32[8,1920]{1,0:T(8,128)S(1)} %get-tuple-element.80.refs_9_), channel_id=1, source_target_pairs={{1,0},{2,1},{3,2},{0,3},{5,4},{6,5},{7,6},{4,7},{9,8},{10,9},{11,1... | collective-permute-start | bytes 184328 | tf_op jit(solution)/shard_map/ppermute | solution.py:211
  96.1 4.0 %collective-permute-start.19 = (bf16[4,4,96,384]{3,2,1,0:T(8,128)(2,1)S(1)}, bf16[4,4,96,384]{3,2,1,0:T(8,128)(2,1)S(1)}, u32[]{:S(2)}, u32[]{:S(2)}) collective-permute-start(bf16[4,4,96,384]{3,2,1,0:T(8,128)(2,1)S(1)} %get-tuple-element.83), channel_id=1, source_target_pairs={{8,0},{0,8},{9,1},{1,9},{10,2},{2,10},{11,3},{3,11},{12,4},{4,12},... | collective-permute-start | bytes 3538952 | tf_op jit(solution)/shard_map/ppermute | solution.py:211
  96.2 15.6 %collective-permute-start.21 = (bf16[16,32,384]{2,1,0:T(8,128)(2,1)S(1)}, bf16[16,32,384]{2,1,0:T(8,128)(2,1)S(1)}, u32[]{:S(2)}, u32[]{:S(2)}) collective-permute-start(bf16[16,32,384]{2,1,0:T(8,128)(2,1)S(1)} %get-tuple-element.86), channel_id=1, source_target_pairs={{4,0},{0,4},{5,1},{1,5},{6,2},{2,6},{7,3},{3,7},{12,8},{8,12},{13,... | collective-permute-start | bytes 1179656 | tf_op jit(solution)/shard_map/ppermute | solution.py:211
  100.6 16.7 %collective-permute-start.20 = (bf16[4,96,384]{2,1,0:T(8,128)(2,1)S(1)}, bf16[4,96,384]{2,1,0:T(8,128)(2,1)S(1)}, u32[]{:S(2)}, u32[]{:S(2)}) collective-permute-start(bf16[4,96,384]{2,1,0:T(8,128)(2,1)S(1)} %get-tuple-element.85), channel_id=1, source_target_pairs={{0,16},{16,32},{32,48},{48,0},{1,17},{17,33},{33,49},{49,1},{2,18}... | collective-permute-start | bytes 884744 | tf_op jit(solution)/shard_map/ppermute | solution.py:215
  100.7 16.6 %collective-permute-start.23 = (bf16[4,96,384]{2,1,0:T(8,128)(2,1)S(1)}, bf16[4,96,384]{2,1,0:T(8,128)(2,1)S(1)}, u32[]{:S(2)}, u32[]{:S(2)}) collective-permute-start(bf16[4,96,384]{2,1,0:T(8,128)(2,1)S(1)} %get-tuple-element.89), channel_id=1, source_target_pairs={{0,32},{16,48},{32,0},{48,16},{1,33},{17,49},{33,1},{49,17},{2,34}... | collective-permute-start | bytes 884744 | tf_op jit(solution)/shard_map/ppermute | solution.py:215
  102.9 15.0 %collective-permute-start.24 = (bf16[4,96,384]{2,1,0:T(8,128)(2,1)S(1)}, bf16[4,96,384]{2,1,0:T(8,128)(2,1)S(1)}, u32[]{:S(2)}, u32[]{:S(2)}) collective-permute-start(bf16[4,96,384]{2,1,0:T(8,128)(2,1)S(1)} %get-tuple-element.90), channel_id=1, source_target_pairs={{0,48},{16,0},{32,16},{48,32},{1,49},{17,1},{33,17},{49,33},{2,50}... | collective-permute-start | bytes 884744 | tf_op jit(solution)/shard_map/ppermute | solution.py:215
  103.9 7.9 %collective-permute-start.22 = (bf16[8,32,384]{2,1,0:T(8,128)(2,1)S(1)}, bf16[8,32,384]{2,1,0:T(8,128)(2,1)S(1)}, u32[]{:S(2)}, u32[]{:S(2)}) collective-permute-start(bf16[8,32,384]{2,1,0:T(8,128)(2,1)S(1)} %get-tuple-element.87), channel_id=1, source_target_pairs={{0,1},{1,2},{2,3},{3,0},{4,5},{5,6},{6,7},{7,4},{8,9},{9,10},{10,1... | collective-permute-start | bytes 589832 | tf_op jit(solution)/shard_map/ppermute | solution.py:215
  118.0 9.4 %collective-permute-start.27 = (bf16[2,96,384]{2,1,0:T(8,128)(2,1)S(1)}, bf16[2,96,384]{2,1,0:T(8,128)(2,1)S(1)}, u32[]{:S(2)}, u32[]{:S(2)}) collective-permute-start(bf16[2,96,384]{2,1,0:T(8,128)(2,1)S(1)} %slice.77), channel_id=1, source_target_pairs={{0,64},{64,0},{128,192},{192,128},{1,65},{65,1},{129,193},{193,129... | collective-permute-start | bytes 442376 | tf_op jit(solution)/shard_map/ppermute | solution.py:306
  123.5 8.6 %collective-permute-start.25 = (bf16[8,32,384]{2,1,0:T(8,128)(2,1)S(1)}, bf16[8,32,384]{2,1,0:T(8,128)(2,1)S(1)}, u32[]{:S(2)}, u32[]{:S(2)}) collective-permute-start(bf16[8,32,384]{2,1,0:T(8,128)(2,1)S(1)} %get-tuple-element.96), channel_id=1, source_target_pairs={{0,2},{1,3},{2,0},{3,1},{4,6},{5,7},{6,4},{7,5},{8,10},{9,11},{10,... | collective-permute-start | bytes 589832 | tf_op jit(solution)/shard_map/ppermute | solution.py:215
  125.0 8.9 %collective-permute-start.26 = (bf16[8,32,384]{2,1,0:T(8,128)(2,1)S(1)}, bf16[8,32,384]{2,1,0:T(8,128)(2,1)S(1)}, u32[]{:S(2)}, u32[]{:S(2)}) collective-permute-start(bf16[8,32,384]{2,1,0:T(8,128)(2,1)S(1)} %get-tuple-element.97), channel_id=1, source_target_pairs={{0,3},{1,0},{2,1},{3,2},{4,7},{5,4},{6,5},{7,6},{8,11},{9,8},{10,9... | collective-permute-start | bytes 589832 | tf_op jit(solution)/shard_map/ppermute | solution.py:215
  127.5 9.1 %collective-permute-start.28 = (bf16[96,384]{1,0:T(8,128)(2,1)S(1)}, bf16[96,384]{1,0:T(8,128)(2,1)S(1)}, u32[]{:S(2)}, u32[]{:S(2)}) collective-permute-start(bf16[96,384]{1,0:T(8,128)(2,1)S(1)} %get-tuple-element.109), channel_id=1, source_target_pairs={{0,0},{64,64},{128,4},{192,68},{4,128},{68,192},{132,132},{196,196... | collective-permute-start | bytes 221192 | tf_op jit(solution)/shard_map/ppermute | solution.py:310
  132.0 8.3 %collective-permute-start.29 = (bf16[96,384]{1,0:T(8,128)(2,1)S(1)}, bf16[96,384]{1,0:T(8,128)(2,1)S(1)}, u32[]{:S(2)}, u32[]{:S(2)}) collective-permute-start(bf16[96,384]{1,0:T(8,128)(2,1)S(1)} %get-tuple-element.110), channel_id=1, source_target_pairs={{0,4},{64,68},{128,0},{192,64},{4,132},{68,196},{132,128},{196,192... | collective-permute-start | bytes 221192 | tf_op jit(solution)/shard_map/ppermute | solution.py:310

commit v7 on v6

--- a/solution.py
+++ b/solution.py
@@ -59,16 +59,21 @@
     lax.fori_loop(0, rows, prepare, 0)
 
 
-def prepare_kernel(scale, q, grad, outs, keys, values, mask, *made):
-    qg, kvm, g, key_own, value_own, delta = made
+def join_kernel(q, grad, keys, values, mask, *made):
+    qg, kvm, g = made
     rows, head, width = keys.shape
-    put_keys(keys, mask[...], key_own, 0, scale * LOG2E)
-    put_values(values, value_own, 0)
     qg[:rows], qg[rows:], g[...] = q[...], grad[...], grad[...]
     kvm[:rows], kvm[rows : 2 * rows] = keys[...], values[...]
-    kvm[2 * rows] = jnp.broadcast_to(mask[...], (head, width)).astype(BF16)
+    kvm[2 * rows] = jnp.broadcast_to(mask[...], (head, width)).astype(F32).astype(BF16)
+
+
+def prepare_kernel(scale, qg, kvm, outs, *made):
+    key_own, value_own, delta = made
+    rows, head, width = outs.shape
+    put_keys(kvm, kvm[2 * rows, 0:1, :].astype(F32), key_own, 0, scale * LOG2E)
+    put_values(kvm.at[rows : 2 * rows], value_own, 0)
     for i in range(rows):
-        product = grad[i].astype(F32) * outs[i].astype(F32)
+        product = qg[rows + i].astype(F32) * outs[i].astype(F32)
         delta[i : i + 1, :] = jnp.sum(product, axis=0, keepdims=True)
 
 
@@ -230,31 +235,39 @@
     total, both = X * width, 2 * width
     z_axes = ("zlo", "zhi")
     at = jnp.stack([lax.axis_index(name) for name in FINE]).astype(jnp.int32)
-    mask = key_mask.astype(F32)[None, :]
     after = lax.optimization_barrier
 
     from_z = [lax.ppermute(bias, z_axes, z_pairs(d)) for d in range(ZLO)]
     q2 = fetch(queries, "x", X, 2)
     block, turned = (rows, head, width), (rows, width, 128)
     made = call(
+        join_kernel,
+        "join",
+        [queries, out_grad, keys, values, key_mask[None, :]],
+        [((2 * rows, head, width), BF16), ((2 * rows + 1, head, width), BF16), (block, BF16)],
+        [],
+        6,
+        0,
+    )
+    from_z, q2, made = after((from_z, q2, made))
+    qg, kvm, own_grad = made
+    made = call(
         lambda *refs: prepare_kernel(scale, *refs),
         "prepare",
-        [queries, out_grad, outputs, keys, values, mask],
-        [((2 * rows, head, width), BF16), ((2 * rows + 1, head, width), BF16)]
-        + [(block, BF16), (turned, BF16), (turned, BF16), ((rows, width), F32)],
+        [qg, kvm, outputs],
+        [(turned, BF16), (turned, BF16), ((rows, width), F32)],
         [],
         8,
         0,
     )
-    from_z, q2, made = after((from_z, q2, made))
-    qg, kvm, own_grad, key_own, value_own, delta = made
     from_z = jnp.stack(from_z)
     before, behind = fetch(from_z, "y", Y, 1), fetch(from_z, "y", Y, 3)
     qg1, qg3 = fetch(qg, "x", X, 1), fetch(qg, "x", X, 3)
     away = fetch(kvm, "zhi", ZHI, 1)
     before, qg3, source = after((before, qg3, from_z))
     here = [from_z, before, fetch(source, "y", Y, 2), behind]
-    here[2], away = after((here[2], away))
+    key_own, value_own, delta = made
+    here[2], away, delta = after((here[2], away, delta))
     there = [fetch(a, "core", CORE, 1) for a in here]
     qg1, own_grad = after((qg1, own_grad))
     g2 = fetch(own_grad, "x", X, 2)

time: 141 us -> 139 us (0.986)
  waiting for transfers between devices: 37.2 us -> 31.9 us
  starting transfers between devices: 51 us -> 54.4 us
    ppermute x17, waiting for transfers between devices: 23.6 us -> 19.1 us  [fetch(): lax.ppermute(x, axis, [((n + distance) % size, n) for n in range(size)])]
    ppermute x1, starting transfers between devices: 5.45 us -> 8.09 us  [per_device(): lax.ppermute(along_y[2:].astype(BF16), 'zlo', across).astype(F32)]
    pallas_call x3 -> x4, Pallas kernels: 41.1 us -> 40.5 us  [call(): pl.pallas_call(kernel, in_specs=[SMEM] * places + [VMEM] * (len(args) - p...]
    unnamed x20 -> x14, local copies, waits for them, and re-layouts: 6.98 us -> 6.66 us
where the time goes in v7:
time: 139 us; the launch traced here: 138 us
  starting transfers between devices  54.4 us (39%)
  Pallas kernels  40.5 us (29%)
  waiting for transfers between devices  31.9 us (23%)
  local copies, waits for them, and re-layouts  7.55 us (5%)
  other arithmetic  3.01 us (2%)
    pallas_call x4, Pallas kernels, call(): pl.pallas_call(kernel, in_specs=[SMEM] * places + [VMEM] * (len(args) - p...  40.5 us
    ppermute x17, starting transfers between devices, fetch(): lax.ppermute(x, axis, [((n + distance) % size, n) for n in range(size)])  23.3 us
    ppermute x17, waiting for transfers between devices, fetch(): lax.ppermute(x, axis, [((n + distance) % size, n) for n in range(size)])  19.1 us
    ppermute x4, starting transfers between devices, per_device(): from_z = [lax.ppermute(bias, z_axes, z_pairs(d)) for d in range(ZLO)]  12.1 us
    ppermute x1, starting transfers between devices, per_device(): lax.ppermute(along_y[2:].astype(BF16), 'zlo', across).astype(F32)  8.09 us
    ppermute x6, waiting for transfers between devices, deliver(): lax.ppermute(x, axis, [(n, (n + distance) % size) for n in range(size)])  7.93 us
    ppermute x6, starting transfers between devices, deliver(): lax.ppermute(x, axis, [(n, (n + distance) % size) for n in range(size)])  7.26 us
    unnamed x14, local copies, waits for them, and re-layouts  6.66 us
  transfers between devices with their start and end apart: 30, of which 14 were waited for; matrix products, arithmetic and copies ran while one was open for 2% of the time, Pallas kernels for 10%

profile of v7, /device:TPU:64, one launch (start us, length us, event | category | flops | bytes accessed | tf_op | source)
XLA Modules:
  0.0 138.2 jit_solution(18051002495504308585)
XLA Ops:
  0.6 3.1 %collective-permute-start.4 = (bf16[8,32,384]{2,1,0:T(8,128)(2,1)}, bf16[8,32,384]{2,1,0:T(8,128)(2,1)S(1)}, u32[]{:S(2)}, u32[]{:S(2)}) collective-permute-start(bf16[8,32,384]{2,1,0:T(8,128)(2,1)} %q.1), channel_id=1, source_target_pairs={{2,0},{3,1},{0,2},{1,3},{6,4},{7,5},{4,6},{5,7},{10,8},{11,9},{8,1... | collective-permute-start | bytes 589832 | tf_op jit(solution)/shard_map/ppermute | solution.py:216
  3.7 4.9 %collective-permute-start.1 = (bf16[96,384]{1,0:T(8,128)(2,1)}, bf16[96,384]{1,0:T(8,128)(2,1)S(1)}, u32[]{:S(2)}, u32[]{:S(2)}) collective-permute-start(bf16[96,384]{1,0:T(8,128)(2,1)} %param.12), channel_id=1, source_target_pairs={{64,0},{0,64},{68,128},{4,192},{192,4},{128,68},{196,132},{132,196... | collective-permute-start | bytes 221192 | tf_op jit(solution)/shard_map/ppermute | solution.py:240
  8.7 1.9 %collective-permute-start = (bf16[96,384]{1,0:T(8,128)(2,1)}, bf16[96,384]{1,0:T(8,128)(2,1)S(1)}, u32[]{:S(2)}, u32[]{:S(2)}) collective-permute-start(bf16[96,384]{1,0:T(8,128)(2,1)} %param.12), channel_id=1, source_target_pairs={{0,0},{64,64},{4,128},{68,192},{128,4},{192,68},{132,132},{196,196... | collective-permute-start | bytes 221192 | tf_op jit(solution)/shard_map/ppermute | solution.py:240
  10.6 0.6 collective-permute-start.3
  11.2 4.6 %collective-permute-start.2 = (bf16[96,384]{1,0:T(8,128)(2,1)}, bf16[96,384]{1,0:T(8,128)(2,1)S(1)}, u32[]{:S(2)}, u32[]{:S(2)}) collective-permute-start(bf16[96,384]{1,0:T(8,128)(2,1)} %param.12), channel_id=1, source_target_pairs={{4,0},{68,64},{0,128},{64,192},{132,4},{196,68},{128,132},{192,196... | collective-permute-start | bytes 221192 | tf_op jit(solution)/shard_map/ppermute | solution.py:240
  15.8 0.7 broadcast_in_dim.3.mask
  16.5 0.9 copy-done.2
  17.4 0.9 copy-done.3
  18.3 0.9 copy-done.4
  19.3 0.9 copy-done.5
  20.2 0.8 join.1
  21.0 0.0 collective-permute-done.1
  21.0 0.0 collective-permute-done
  21.0 0.0 collective-permute-done.2
  21.0 0.7 collective-permute-start.7
  21.7 3.1 %collective-permute-start.6 = (bf16[4,96,384]{2,1,0:T(8,128)(2,1)S(1)}, bf16[4,96,384]{2,1,0:T(8,128)(2,1)}, u32[]{:S(2)}, u32[]{:S(2)}) collective-permute-start(bf16[4,96,384]{2,1,0:T(8,128)(2,1)S(1)} %pad_maximum_fusion.refs_8_), channel_id=1, source_target_pairs={{16,0},{32,16},{48,32},{0,48},{17,1},{33,17},{49,33},{1,49},{18,2}... | collective-permute-start | bytes 884744 | tf_op jit(solution)/shard_map/ppermute | solution.py:216
  24.8 4.0 %collective-permute-start.9 = (bf16[17,32,384]{2,1,0:T(8,128)(2,1)S(1)}, bf16[17,32,384]{2,1,0:T(8,128)(2,1)S(1)}, u32[]{:S(2)}, u32[]{:S(2)}) collective-permute-start(bf16[17,32,384]{2,1,0:T(8,128)(2,1)S(1)} %get-tuple-element.64.refs_1_.refs_5_), channel_id=1, source_target_pairs={{4,0},{0,4},{5,1},{1,5},{6,2},{2,6},{7,3},{3,7},{12,8},{8,12},{13,... | collective-permute-start | bytes 1253384 | tf_op jit(solution)/shard_map/ppermute | solution.py:216
  28.8 0.0 collective-permute-start.10
  28.8 0.5 collective-permute-done.6.refs_9_
  29.4 2.3 %collective-permute-done.7.refs_4_.refs_3_ = bf16[16,32,384]{2,1,0:T(8,128)(2,1)S(1)} collective-permute-done((bf16[16,32,384]{2,1,0:T(8,128)(2,1)S(1)}, bf16[16,32,384]{2,1,0:T(8,128)(2,1)S(1)}, u32[]{:S(2)}, u32[]{:S(2)}) %collective-permute-start.7) | collective-permute-done | bytes 393248 | tf_op jit(solution)/shard_map/ppermute | solution.py:216
  31.7 3.2 %collective-permute-start.8 = (bf16[4,96,384]{2,1,0:T(8,128)(2,1)S(1)}, bf16[4,96,384]{2,1,0:T(8,128)(2,1)}, u32[]{:S(2)}, u32[]{:S(2)}) collective-permute-start(bf16[4,96,384]{2,1,0:T(8,128)(2,1)S(1)} %pad_maximum_fusion.refs_8_), channel_id=1, source_target_pairs={{32,0},{48,16},{0,32},{16,48},{33,1},{49,17},{1,33},{17,49},{34,2}... | collective-permute-start | bytes 884744 | tf_op jit(solution)/shard_map/ppermute | solution.py:216
  34.9 0.9 copy-done.6
  35.9 1.8 %prepare.1 = (bf16[8,384,128]{2,1,0:T(8,128)(2,1)S(1)}, bf16[8,384,128]{2,1,0:T(8,128)(2,1)S(1)}, f32[8,384]{1,0:T(8,128)S(1)}) custom-call(bf16[16,32,384]{2,1,0:T(8,128)(2,1)S(1)} %get-tuple-element.54.refs_0_.refs_1_, bf16[17,32,384]{2,1,0:T(8,128)(2,1)S(1)} %get-tuple-element.64.refs_1_.refs_5_, bf16[8,32,384]{2,1,0:T(8,128)(2,1)S(1)} %copy-done.6), custom_call_target="tpu_custom_call" | custom-call | tf_op jit(solution)/shard_map/prepare/pallas_call | solution.py:204
  37.6 0.9 copy-done
  38.5 4.5 %collective-permute-done.10.refs_11_ = bf16[4,96,384]{2,1,0:T(8,128)(2,1)} collective-permute-done((bf16[4,96,384]{2,1,0:T(8,128)(2,1)S(1)}, bf16[4,96,384]{2,1,0:T(8,128)(2,1)}, u32[]{:S(2)}, u32[]{:S(2)}) %collective-permute-start.10) | collective-permute-done | bytes 294944 | tf_op jit(solution)/shard_map/ppermute | solution.py:216
  43.1 0.5 collective-permute-start.12
  43.6 0.1 collective-permute-start.13
  43.7 1.0 collective-permute-start.15
  44.6 0.1 stack.38.refs_0_.at
  44.7 0.3 collective-permute-done.14.refs_15_
  45.0 0.4 collective-permute-done.12.refs_13_
  45.4 0.4 collective-permute-done.13.refs_14_
  45.8 1.1 copy-done.1
  46.9 11.5 %softmax_statistics.1 = (f32[8,1920]{1,0:T(8,128)S(1)}, bf16[768,1536]{1,0:T(8,128)(2,1)S(1)}, bf16[8,768,128]{2,1,0:T(8,128)(2,1)S(1)}) custom-call(s32[5]{0:T(128)S(1)} %stack.38.refs_0_.at, bf16[16,32,384]{2,1,0:T(8,128)(2,1)S(1)} %get-tuple-element.54.refs_0_.refs_1_, bf16[16,32,384]{2,1,0:T(8,128)(2,1)S(1)} %collective-permute-done.5.refs_2_.refs_1_, ...), custom_call_target="tpu_custom_call" | custom-call | tf_op jit(solution)/shard_map/softmax_statistics/pallas_call | solution.py:204
  58.5 0.5 collective-permute-start.18
  59.0 2.5 %collective-permute-start.17 = (f32[8,1920]{1,0:T(8,128)S(1)}, f32[8,1920]{1,0:T(8,128)S(1)}, u32[]{:S(2)}, u32[]{:S(2)}) collective-permute-start(f32[8,1920]{1,0:T(8,128)S(1)} %get-tuple-element.76.refs_9_), channel_id=1, source_target_pairs={{2,0},{3,1},{0,2},{1,3},{6,4},{7,5},{4,6},{5,7},{10,8},{11,9},{8,1... | collective-permute-start | bytes 184328 | tf_op jit(solution)/shard_map/ppermute | solution.py:216
  61.5 1.4 %collective-permute-start.16 = (f32[8,1920]{1,0:T(8,128)S(1)}, f32[8,1920]{1,0:T(8,128)S(1)}, u32[]{:S(2)}, u32[]{:S(2)}) collective-permute-start(f32[8,1920]{1,0:T(8,128)S(1)} %get-tuple-element.76.refs_9_), channel_id=1, source_target_pairs={{1,0},{2,1},{3,2},{0,3},{5,4},{6,5},{7,6},{4,7},{9,8},{10,9},{11,1... | collective-permute-start | bytes 184328 | tf_op jit(solution)/shard_map/ppermute | solution.py:216
  62.9 2.3 %collective-permute-done.18.refs_12_ = f32[8,1920]{1,0:T(8,128)S(1)} collective-permute-done((f32[8,1920]{1,0:T(8,128)S(1)}, f32[8,1920]{1,0:T(8,128)S(1)}, u32[]{:S(2)}, u32[]{:S(2)}) %collective-permute-start.18) | collective-permute-done | bytes 61472 | tf_op jit(solution)/shard_map/ppermute | solution.py:216
  65.2 0.6 collective-permute-done.16.refs_10_
  65.7 26.4 %attention_gradients.1 = (f32[8,32,384]{2,1,0:T(8,128)S(1)}, bf16[8,32,384]{2,1,0:T(8,128)(2,1)S(1)}, bf16[8,32,384]{2,1,0:T(8,128)(2,1)S(1)}, bf16[8,32,384]{2,...) custom-call(s32[5]{0:T(128)S(1)} %stack.38.refs_0_.at, ...), custom_call_target="tpu_custom_call" | custom-call | tf_op jit(solution)/shard_map/attention_gradients/pallas_call | solution.py:204
  92.1 0.1 collective-permute-start.19
  92.2 3.1 %collective-permute-start.21 = (bf16[16,32,384]{2,1,0:T(8,128)(2,1)S(1)}, bf16[16,32,384]{2,1,0:T(8,128)(2,1)S(1)}, u32[]{:S(2)}, u32[]{:S(2)}) collective-permute-start(bf16[16,32,384]{2,1,0:T(8,128)(2,1)S(1)} %get-tuple-element.82), channel_id=1, source_target_pairs={{4,0},{0,4},{5,1},{1,5},{6,2},{2,6},{7,3},{3,7},{12,8},{8,12},{13,... | collective-permute-start | bytes 1179656 | tf_op jit(solution)/shard_map/ppermute | solution.py:216
  95.4 0.4 fusion.6
  95.7 0.1 slice_bitcast_fusion.1
  95.8 0.2 collective-permute-start.20
  96.0 0.9 collective-permute-start.23
  96.9 2.3 %collective-permute-start.24 = (bf16[4,96,384]{2,1,0:T(8,128)(2,1)S(1)}, bf16[4,96,384]{2,1,0:T(8,128)(2,1)S(1)}, u32[]{:S(2)}, u32[]{:S(2)}) collective-permute-start(bf16[4,96,384]{2,1,0:T(8,128)(2,1)S(1)} %get-tuple-element.86), channel_id=1, source_target_pairs={{0,48},{16,0},{32,16},{48,32},{1,49},{17,1},{33,17},{49,33},{2,50}... | collective-permute-start | bytes 884744 | tf_op jit(solution)/shard_map/ppermute | solution.py:220
  99.2 0.9 collective-permute-start.22
  100.1 7.8 %collective-permute-done.21 = bf16[16,32,384]{2,1,0:T(8,128)(2,1)S(1)} collective-permute-done((bf16[16,32,384]{2,1,0:T(8,128)(2,1)S(1)}, bf16[16,32,384]{2,1,0:T(8,128)(2,1)S(1)}, u32[]{:S(2)}, u32[]{:S(2)}) %collective-permute-start.21) | collective-permute-done | bytes 393248 | tf_op jit(solution)/shard_map/ppermute | solution.py:216
  107.8 4.7 %collective-permute-done.20 = bf16[4,96,384]{2,1,0:T(8,128)(2,1)S(1)} collective-permute-done((bf16[4,96,384]{2,1,0:T(8,128)(2,1)S(1)}, bf16[4,96,384]{2,1,0:T(8,128)(2,1)S(1)}, u32[]{:S(2)}, u32[]{:S(2)}) %collective-permute-start.20) | collective-permute-done | bytes 294944 | tf_op jit(solution)/shard_map/ppermute | solution.py:220
  112.5 0.6 collective-permute-done.24
  113.1 0.1 fusion.2
  113.3 8.1 %collective-permute-start.27 = (bf16[2,96,384]{2,1,0:T(8,128)(2,1)S(1)}, bf16[2,96,384]{2,1,0:T(8,128)(2,1)S(1)}, u32[]{:S(2)}, u32[]{:S(2)}) collective-permute-start(bf16[2,96,384]{2,1,0:T(8,128)(2,1)S(1)} %slice.77), channel_id=1, source_target_pairs={{0,64},{64,0},{128,192},{192,128},{1,65},{65,1},{129,193},{193,129... | collective-permute-start | bytes 442376 | tf_op jit(solution)/shard_map/ppermute | solution.py:319
  121.4 1.5 %collective-permute-start.25 = (bf16[8,32,384]{2,1,0:T(8,128)(2,1)S(1)}, bf16[8,32,384]{2,1,0:T(8,128)(2,1)S(1)}, u32[]{:S(2)}, u32[]{:S(2)}) collective-permute-start(bf16[8,32,384]{2,1,0:T(8,128)(2,1)S(1)} %get-tuple-element.92), channel_id=1, source_target_pairs={{0,2},{1,3},{2,0},{3,1},{4,6},{5,7},{6,4},{7,5},{8,10},{9,11},{10,... | collective-permute-start | bytes 589832 | tf_op jit(solution)/shard_map/ppermute | solution.py:220
  122.9 1.5 %collective-permute-start.26 = (bf16[8,32,384]{2,1,0:T(8,128)(2,1)S(1)}, bf16[8,32,384]{2,1,0:T(8,128)(2,1)S(1)}, u32[]{:S(2)}, u32[]{:S(2)}) collective-permute-start(bf16[8,32,384]{2,1,0:T(8,128)(2,1)S(1)} %get-tuple-element.93), channel_id=1, source_target_pairs={{0,3},{1,0},{2,1},{3,2},{4,7},{5,4},{6,5},{7,6},{8,11},{9,8},{10,9... | collective-permute-start | bytes 589832 | tf_op jit(solution)/shard_map/ppermute | solution.py:220
  124.4 0.1 convert_element_type.74
  124.5 0.9 fusion.3
  125.5 3.7 %collective-permute-start.28 = (bf16[96,384]{1,0:T(8,128)(2,1)S(1)}, bf16[96,384]{1,0:T(8,128)(2,1)S(1)}, u32[]{:S(2)}, u32[]{:S(2)}) collective-permute-start(bf16[96,384]{1,0:T(8,128)(2,1)S(1)} %get-tuple-element.105), channel_id=1, source_target_pairs={{0,0},{64,64},{128,4},{192,68},{4,128},{68,192},{132,132},{196,196... | collective-permute-start | bytes 221192 | tf_op jit(solution)/shard_map/ppermute | solution.py:323
  129.1 0.1 collective-permute-start.29
  129.2 2.6 %collective-permute-done.26 = bf16[8,32,384]{2,1,0:T(8,128)(2,1)S(1)} collective-permute-done((bf16[8,32,384]{2,1,0:T(8,128)(2,1)S(1)}, bf16[8,32,384]{2,1,0:T(8,128)(2,1)S(1)}, u32[]{:S(2)}, u32[]{:S(2)}) %collective-permute-start.26) | collective-permute-done | bytes 196640 | tf_op jit(solution)/shard_map/ppermute | solution.py:220
  131.9 0.8 multiply_convert_fusion
  132.7 2.7 %collective-permute-done.28 = bf16[96,384]{1,0:T(8,128)(2,1)S(1)} collective-permute-done((bf16[96,384]{1,0:T(8,128)(2,1)S(1)}, bf16[96,384]{1,0:T(8,128)(2,1)S(1)}, u32[]{:S(2)}, u32[]{:S(2)}) %collective-permute-start.28) | collective-permute-done | bytes 73760 | tf_op jit(solution)/shard_map/ppermute | solution.py:323
  135.4 2.1 %collective-permute-done.29 = bf16[96,384]{1,0:T(8,128)(2,1)S(1)} collective-permute-done((bf16[96,384]{1,0:T(8,128)(2,1)S(1)}, bf16[96,384]{1,0:T(8,128)(2,1)S(1)}, u32[]{:S(2)}, u32[]{:S(2)}) %collective-permute-start.29) | collective-permute-done | bytes 73760 | tf_op jit(solution)/shard_map/ppermute | solution.py:323
  137.5 0.7 convert_add_fusion.1
  (27 shorter events, 0.2 us)
Async XLA Ops:
  0.6 20.4 %collective-permute-start.4 = (bf16[8,32,384]{2,1,0:T(8,128)(2,1)}, bf16[8,32,384]{2,1,0:T(8,128)(2,1)S(1)}, u32[]{:S(2)}, u32[]{:S(2)}) collective-permute-start(bf16[8,32,384]{2,1,0:T(8,128)(2,1)} %q.1), channel_id=1, source_target_pairs={{2,0},{3,1},{0,2},{1,3},{6,4},{7,5},{4,6},{5,7},{10,8},{11,9},{8,1... | collective-permute-start | bytes 589832 | tf_op jit(solution)/shard_map/ppermute | solution.py:216
  3.7 17.2 %collective-permute-start.1 = (bf16[96,384]{1,0:T(8,128)(2,1)}, bf16[96,384]{1,0:T(8,128)(2,1)S(1)}, u32[]{:S(2)}, u32[]{:S(2)}) collective-permute-start(bf16[96,384]{1,0:T(8,128)(2,1)} %param.12), channel_id=1, source_target_pairs={{64,0},{0,64},{68,128},{4,192},{192,4},{128,68},{196,132},{132,196... | collective-permute-start | bytes 221192 | tf_op jit(solution)/shard_map/ppermute | solution.py:240
  8.7 12.3 %collective-permute-start = (bf16[96,384]{1,0:T(8,128)(2,1)}, bf16[96,384]{1,0:T(8,128)(2,1)S(1)}, u32[]{:S(2)}, u32[]{:S(2)}) collective-permute-start(bf16[96,384]{1,0:T(8,128)(2,1)} %param.12), channel_id=1, source_target_pairs={{0,0},{64,64},{4,128},{68,192},{128,4},{192,68},{132,132},{196,196... | collective-permute-start | bytes 221192 | tf_op jit(solution)/shard_map/ppermute | solution.py:240
  10.6 10.4 %collective-permute-start.3 = (bf16[96,384]{1,0:T(8,128)(2,1)}, bf16[96,384]{1,0:T(8,128)(2,1)S(1)}, u32[]{:S(2)}, u32[]{:S(2)}) collective-permute-start(bf16[96,384]{1,0:T(8,128)(2,1)} %param.12), channel_id=1, source_target_pairs={{68,0},{4,64},{64,128},{0,192},{196,4},{132,68},{192,132},{128,196... | collective-permute-start | bytes 221192 | tf_op jit(solution)/shard_map/ppermute | solution.py:240
  11.2 9.7 %collective-permute-start.2 = (bf16[96,384]{1,0:T(8,128)(2,1)}, bf16[96,384]{1,0:T(8,128)(2,1)S(1)}, u32[]{:S(2)}, u32[]{:S(2)}) collective-permute-start(bf16[96,384]{1,0:T(8,128)(2,1)} %param.12), channel_id=1, source_target_pairs={{4,0},{68,64},{0,128},{64,192},{132,4},{196,68},{128,132},{192,196... | collective-permute-start | bytes 221192 | tf_op jit(solution)/shard_map/ppermute | solution.py:240
  16.5 0.9 copy-start.2
  17.4 0.9 copy-start.3
  18.3 0.9 copy-start.4
  19.3 0.9 copy-start.5
  21.0 10.7 %collective-permute-start.7 = (bf16[16,32,384]{2,1,0:T(8,128)(2,1)S(1)}, bf16[16,32,384]{2,1,0:T(8,128)(2,1)S(1)}, u32[]{:S(2)}, u32[]{:S(2)}) collective-permute-start(bf16[16,32,384]{2,1,0:T(8,128)(2,1)S(1)} %get-tuple-element.54.refs_0_.refs_1_), channel_id=1, source_target_pairs={{3,0},{0,1},{1,2},{2,3},{7,4},{4,5},{5,6},{6,7},{11,8},{8,9},{9,10... | collective-permute-start | bytes 1179656 | tf_op jit(solution)/shard_map/ppermute | solution.py:216
  21.7 7.7 %collective-permute-start.6 = (bf16[4,96,384]{2,1,0:T(8,128)(2,1)S(1)}, bf16[4,96,384]{2,1,0:T(8,128)(2,1)}, u32[]{:S(2)}, u32[]{:S(2)}) collective-permute-start(bf16[4,96,384]{2,1,0:T(8,128)(2,1)S(1)} %pad_maximum_fusion.refs_8_), channel_id=1, source_target_pairs={{16,0},{32,16},{48,32},{0,48},{17,1},{33,17},{49,33},{1,49},{18,2}... | collective-permute-start | bytes 884744 | tf_op jit(solution)/shard_map/ppermute | solution.py:216
  24.8 18.2 %collective-permute-start.9 = (bf16[17,32,384]{2,1,0:T(8,128)(2,1)S(1)}, bf16[17,32,384]{2,1,0:T(8,128)(2,1)S(1)}, u32[]{:S(2)}, u32[]{:S(2)}) collective-permute-start(bf16[17,32,384]{2,1,0:T(8,128)(2,1)S(1)} %get-tuple-element.64.refs_1_.refs_5_), channel_id=1, source_target_pairs={{4,0},{0,4},{5,1},{1,5},{6,2},{2,6},{7,3},{3,7},{12,8},{8,12},{13,... | collective-permute-start | bytes 1253384 | tf_op jit(solution)/shard_map/ppermute | solution.py:216
  28.8 14.2 %collective-permute-start.10 = (bf16[4,96,384]{2,1,0:T(8,128)(2,1)S(1)}, bf16[4,96,384]{2,1,0:T(8,128)(2,1)}, u32[]{:S(2)}, u32[]{:S(2)}) collective-permute-start(bf16[4,96,384]{2,1,0:T(8,128)(2,1)S(1)} %pad_maximum_fusion.refs_8_), channel_id=1, source_target_pairs={{48,0},{0,16},{16,32},{32,48},{49,1},{1,17},{17,33},{33,49},{50,2}... | collective-permute-start | bytes 884744 | tf_op jit(solution)/shard_map/ppermute | solution.py:216
  31.7 11.8 %collective-permute-start.8 = (bf16[4,96,384]{2,1,0:T(8,128)(2,1)S(1)}, bf16[4,96,384]{2,1,0:T(8,128)(2,1)}, u32[]{:S(2)}, u32[]{:S(2)}) collective-permute-start(bf16[4,96,384]{2,1,0:T(8,128)(2,1)S(1)} %pad_maximum_fusion.refs_8_), channel_id=1, source_target_pairs={{32,0},{48,16},{0,32},{16,48},{33,1},{49,17},{1,33},{17,49},{34,2}... | collective-permute-start | bytes 884744 | tf_op jit(solution)/shard_map/ppermute | solution.py:216
  34.9 8.7 %collective-permute-start.5 = (bf16[16,32,384]{2,1,0:T(8,128)(2,1)S(1)}, bf16[16,32,384]{2,1,0:T(8,128)(2,1)S(1)}, u32[]{:S(2)}, u32[]{:S(2)}) collective-permute-start(bf16[16,32,384]{2,1,0:T(8,128)(2,1)S(1)} %get-tuple-element.54.refs_0_.refs_1_), channel_id=1, source_target_pairs={{1,0},{2,1},{3,2},{0,3},{5,4},{6,5},{7,6},{4,7},{9,8},{10,9},{11,1... | collective-permute-start | bytes 1179656 | tf_op jit(solution)/shard_map/ppermute | solution.py:216
  34.9 9.8 %collective-permute-start.11 = (bf16[4,96,384]{2,1,0:T(8,128)(2,1)S(1)}, bf16[4,96,384]{2,1,0:T(8,128)(2,1)}, u32[]{:S(2)}, u32[]{:S(2)}) collective-permute-start(bf16[4,96,384]{2,1,0:T(8,128)(2,1)S(1)} %pad_maximum_fusion.refs_8_), channel_id=1, source_target_pairs={{8,0},{0,8},{9,1},{1,9},{10,2},{2,10},{11,3},{3,11},{12,4},{4,12},... | collective-permute-start | bytes 884744 | tf_op jit(solution)/shard_map/ppermute | solution.py:216
  34.9 0.9 copy-start.6
  37.6 0.9 copy-start
  43.0 1.9 %collective-permute-start.14 = (bf16[4,96,384]{2,1,0:T(8,128)(2,1)}, bf16[4,96,384]{2,1,0:T(8,128)(2,1)}, u32[]{:S(2)}, u32[]{:S(2)}) collective-permute-start(bf16[4,96,384]{2,1,0:T(8,128)(2,1)} %collective-permute-done.10.refs_11_), channel_id=1, source_target_pairs={{8,0},{0,8},{9,1},{1,9},{10,2},{2,10},{11,3},{3,11},{12,4},{4,12},... | collective-permute-start | bytes 884744 | tf_op jit(solution)/shard_map/ppermute | solution.py:216
  43.1 2.3 %collective-permute-start.12 = (bf16[4,96,384]{2,1,0:T(8,128)(2,1)}, bf16[4,96,384]{2,1,0:T(8,128)(2,1)}, u32[]{:S(2)}, u32[]{:S(2)}) collective-permute-start(bf16[4,96,384]{2,1,0:T(8,128)(2,1)} %collective-permute-done.6.refs_9_), channel_id=1, source_target_pairs={{8,0},{0,8},{9,1},{1,9},{10,2},{2,10},{11,3},{3,11},{12,4},{4,12},... | collective-permute-start | bytes 884744 | tf_op jit(solution)/shard_map/ppermute | solution.py:216
  43.6 2.3 %collective-permute-start.13 = (bf16[4,96,384]{2,1,0:T(8,128)(2,1)}, bf16[4,96,384]{2,1,0:T(8,128)(2,1)}, u32[]{:S(2)}, u32[]{:S(2)}) collective-permute-start(bf16[4,96,384]{2,1,0:T(8,128)(2,1)} %collective-permute-done.8.refs_10_), channel_id=1, source_target_pairs={{8,0},{0,8},{9,1},{1,9},{10,2},{2,10},{11,3},{3,11},{12,4},{4,12},... | collective-permute-start | bytes 884744 | tf_op jit(solution)/shard_map/ppermute | solution.py:216
  43.7 14.8 %collective-permute-start.15 = (bf16[8,32,384]{2,1,0:T(8,128)(2,1)}, bf16[8,32,384]{2,1,0:T(8,128)(2,1)S(1)}, u32[]{:S(2)}, u32[]{:S(2)}) collective-permute-start(bf16[8,32,384]{2,1,0:T(8,128)(2,1)} %get-tuple-element.72), channel_id=1, source_target_pairs={{2,0},{3,1},{0,2},{1,3},{6,4},{7,5},{4,6},{5,7},{10,8},{11,9},{8,1... | collective-permute-start | bytes 589832 | tf_op jit(solution)/shard_map/ppermute | solution.py:216
  45.8 1.1 copy-start.1
  58.5 6.7 %collective-permute-start.18 = (f32[8,1920]{1,0:T(8,128)S(1)}, f32[8,1920]{1,0:T(8,128)S(1)}, u32[]{:S(2)}, u32[]{:S(2)}) collective-permute-start(f32[8,1920]{1,0:T(8,128)S(1)} %get-tuple-element.76.refs_9_), channel_id=1, source_target_pairs={{3,0},{0,1},{1,2},{2,3},{7,4},{4,5},{5,6},{6,7},{11,8},{8,9},{9,10... | collective-permute-start | bytes 184328 | tf_op jit(solution)/shard_map/ppermute | solution.py:216
  59.0 6.2 %collective-permute-start.17 = (f32[8,1920]{1,0:T(8,128)S(1)}, f32[8,1920]{1,0:T(8,128)S(1)}, u32[]{:S(2)}, u32[]{:S(2)}) collective-permute-start(f32[8,1920]{1,0:T(8,128)S(1)} %get-tuple-element.76.refs_9_), channel_id=1, source_target_pairs={{2,0},{3,1},{0,2},{1,3},{6,4},{7,5},{4,6},{5,7},{10,8},{11,9},{8,1... | collective-permute-start | bytes 184328 | tf_op jit(solution)/shard_map/ppermute | solution.py:216
  61.5 4.3 %collective-permute-start.16 = (f32[8,1920]{1,0:T(8,128)S(1)}, f32[8,1920]{1,0:T(8,128)S(1)}, u32[]{:S(2)}, u32[]{:S(2)}) collective-permute-start(f32[8,1920]{1,0:T(8,128)S(1)} %get-tuple-element.76.refs_9_), channel_id=1, source_target_pairs={{1,0},{2,1},{3,2},{0,3},{5,4},{6,5},{7,6},{4,7},{9,8},{10,9},{11,1... | collective-permute-start | bytes 184328 | tf_op jit(solution)/shard_map/ppermute | solution.py:216
  92.1 3.2 %collective-permute-start.19 = (bf16[4,4,96,384]{3,2,1,0:T(8,128)(2,1)S(1)}, bf16[4,4,96,384]{3,2,1,0:T(8,128)(2,1)S(1)}, u32[]{:S(2)}, u32[]{:S(2)}) collective-permute-start(bf16[4,4,96,384]{3,2,1,0:T(8,128)(2,1)S(1)} %get-tuple-element.79), channel_id=1, source_target_pairs={{8,0},{0,8},{9,1},{1,9},{10,2},{2,10},{11,3},{3,11},{12,4},{4,12},... | collective-permute-start | bytes 3538952 | tf_op jit(solution)/shard_map/ppermute | solution.py:216
  92.2 15.6 %collective-permute-start.21 = (bf16[16,32,384]{2,1,0:T(8,128)(2,1)S(1)}, bf16[16,32,384]{2,1,0:T(8,128)(2,1)S(1)}, u32[]{:S(2)}, u32[]{:S(2)}) collective-permute-start(bf16[16,32,384]{2,1,0:T(8,128)(2,1)S(1)} %get-tuple-element.82), channel_id=1, source_target_pairs={{4,0},{0,4},{5,1},{1,5},{6,2},{2,6},{7,3},{3,7},{12,8},{8,12},{13,... | collective-permute-start | bytes 1179656 | tf_op jit(solution)/shard_map/ppermute | solution.py:216
  95.8 16.7 %collective-permute-start.20 = (bf16[4,96,384]{2,1,0:T(8,128)(2,1)S(1)}, bf16[4,96,384]{2,1,0:T(8,128)(2,1)S(1)}, u32[]{:S(2)}, u32[]{:S(2)}) collective-permute-start(bf16[4,96,384]{2,1,0:T(8,128)(2,1)S(1)} %get-tuple-element.81), channel_id=1, source_target_pairs={{0,16},{16,32},{32,48},{48,0},{1,17},{17,33},{33,49},{49,1},{2,18}... | collective-permute-start | bytes 884744 | tf_op jit(solution)/shard_map/ppermute | solution.py:220
  96.0 16.5 %collective-permute-start.23 = (bf16[4,96,384]{2,1,0:T(8,128)(2,1)S(1)}, bf16[4,96,384]{2,1,0:T(8,128)(2,1)S(1)}, u32[]{:S(2)}, u32[]{:S(2)}) collective-permute-start(bf16[4,96,384]{2,1,0:T(8,128)(2,1)S(1)} %get-tuple-element.85), channel_id=1, source_target_pairs={{0,32},{16,48},{32,0},{48,16},{1,33},{17,49},{33,1},{49,17},{2,34}... | collective-permute-start | bytes 884744 | tf_op jit(solution)/shard_map/ppermute | solution.py:220
  96.9 16.3 %collective-permute-start.24 = (bf16[4,96,384]{2,1,0:T(8,128)(2,1)S(1)}, bf16[4,96,384]{2,1,0:T(8,128)(2,1)S(1)}, u32[]{:S(2)}, u32[]{:S(2)}) collective-permute-start(bf16[4,96,384]{2,1,0:T(8,128)(2,1)S(1)} %get-tuple-element.86), channel_id=1, source_target_pairs={{0,48},{16,0},{32,16},{48,32},{1,49},{17,1},{33,17},{49,33},{2,50}... | collective-permute-start | bytes 884744 | tf_op jit(solution)/shard_map/ppermute | solution.py:220
  99.2 8.7 %collective-permute-start.22 = (bf16[8,32,384]{2,1,0:T(8,128)(2,1)S(1)}, bf16[8,32,384]{2,1,0:T(8,128)(2,1)S(1)}, u32[]{:S(2)}, u32[]{:S(2)}) collective-permute-start(bf16[8,32,384]{2,1,0:T(8,128)(2,1)S(1)} %get-tuple-element.83), channel_id=1, source_target_pairs={{0,1},{1,2},{2,3},{3,0},{4,5},{5,6},{6,7},{7,4},{8,9},{9,10},{10,1... | collective-permute-start | bytes 589832 | tf_op jit(solution)/shard_map/ppermute | solution.py:220
  113.3 12.1 %collective-permute-start.27 = (bf16[2,96,384]{2,1,0:T(8,128)(2,1)S(1)}, bf16[2,96,384]{2,1,0:T(8,128)(2,1)S(1)}, u32[]{:S(2)}, u32[]{:S(2)}) collective-permute-start(bf16[2,96,384]{2,1,0:T(8,128)(2,1)S(1)} %slice.77), channel_id=1, source_target_pairs={{0,64},{64,0},{128,192},{192,128},{1,65},{65,1},{129,193},{193,129... | collective-permute-start | bytes 442376 | tf_op jit(solution)/shard_map/ppermute | solution.py:319
  121.4 7.8 %collective-permute-start.25 = (bf16[8,32,384]{2,1,0:T(8,128)(2,1)S(1)}, bf16[8,32,384]{2,1,0:T(8,128)(2,1)S(1)}, u32[]{:S(2)}, u32[]{:S(2)}) collective-permute-start(bf16[8,32,384]{2,1,0:T(8,128)(2,1)S(1)} %get-tuple-element.92), channel_id=1, source_target_pairs={{0,2},{1,3},{2,0},{3,1},{4,6},{5,7},{6,4},{7,5},{8,10},{9,11},{10,... | collective-permute-start | bytes 589832 | tf_op jit(solution)/shard_map/ppermute | solution.py:220
  122.9 9.0 %collective-permute-start.26 = (bf16[8,32,384]{2,1,0:T(8,128)(2,1)S(1)}, bf16[8,32,384]{2,1,0:T(8,128)(2,1)S(1)}, u32[]{:S(2)}, u32[]{:S(2)}) collective-permute-start(bf16[8,32,384]{2,1,0:T(8,128)(2,1)S(1)} %get-tuple-element.93), channel_id=1, source_target_pairs={{0,3},{1,0},{2,1},{3,2},{4,7},{5,4},{6,5},{7,6},{8,11},{9,8},{10,9... | collective-permute-start | bytes 589832 | tf_op jit(solution)/shard_map/ppermute | solution.py:220
  125.5 9.9 %collective-permute-start.28 = (bf16[96,384]{1,0:T(8,128)(2,1)S(1)}, bf16[96,384]{1,0:T(8,128)(2,1)S(1)}, u32[]{:S(2)}, u32[]{:S(2)}) collective-permute-start(bf16[96,384]{1,0:T(8,128)(2,1)S(1)} %get-tuple-element.105), channel_id=1, source_target_pairs={{0,0},{64,64},{128,4},{192,68},{4,128},{68,192},{132,132},{196,196... | collective-permute-start | bytes 221192 | tf_op jit(solution)/shard_map/ppermute | solution.py:323
  129.1 8.3 %collective-permute-start.29 = (bf16[96,384]{1,0:T(8,128)(2,1)S(1)}, bf16[96,384]{1,0:T(8,128)(2,1)S(1)}, u32[]{:S(2)}, u32[]{:S(2)}) collective-permute-start(bf16[96,384]{1,0:T(8,128)(2,1)S(1)} %get-tuple-element.106), channel_id=1, source_target_pairs={{0,4},{64,68},{128,0},{192,64},{4,132},{68,196},{132,128},{196,192... | collective-permute-start | bytes 221192 | tf_op jit(solution)/shard_map/ppermute | solution.py:323

commit v8 on v7

--- a/solution.py
+++ b/solution.py
@@ -67,10 +67,9 @@
     kvm[2 * rows] = jnp.broadcast_to(mask[...], (head, width)).astype(F32).astype(BF16)
 
 
-def prepare_kernel(scale, qg, kvm, outs, *made):
-    key_own, value_own, delta = made
+def prepare_kernel(qg, kvm, outs, *made):
+    value_own, delta = made
     rows, head, width = outs.shape
-    put_keys(kvm, kvm[2 * rows, 0:1, :].astype(F32), key_own, 0, scale * LOG2E)
     put_values(kvm.at[rows : 2 * rows], value_own, 0)
     for i in range(rows):
         product = qg[rows + i].astype(F32) * outs[i].astype(F32)
@@ -93,14 +92,14 @@
 
 
 def stats_kernel(scale, at, *refs):
-    q, (away, key_own, delta) = refs[0:4], refs[4:7]
+    q, (away, own, delta) = refs[0:4], refs[4:7]
     pieces = (refs[7:11], refs[11:15])
     stat, bias_t, key_t = refs[15:18]
     bias_n, bias_f = refs[18:]
-    rows, width, _ = key_own.shape
+    rows, width = delta.shape
     total = X * width
     put_keys(away, away[2 * rows, 0:1, :].astype(F32), key_t, width, scale * LOG2E)
-    key_t[:, :width, :] = key_own[...]
+    put_keys(own, own[2 * rows, 0:1, :].astype(F32), key_t, 0, scale * LOG2E)
     stat[:, total:] = delta[...]
     for yd, zd, other, slot, first in bias_pieces(at):
         bias_n[slot, pl.ds(first, 96), :] = pieces[other][yd][zd]
@@ -252,10 +251,10 @@
     from_z, q2, made = after((from_z, q2, made))
     qg, kvm, own_grad = made
     made = call(
-        lambda *refs: prepare_kernel(scale, *refs),
+        prepare_kernel,
         "prepare",
         [qg, kvm, outputs],
-        [(turned, BF16), (turned, BF16), ((rows, width), F32)],
+        [(turned, BF16), ((rows, width), F32)],
         [],
         8,
         0,
@@ -266,7 +265,7 @@
     away = fetch(kvm, "zhi", ZHI, 1)
     before, qg3, source = after((before, qg3, from_z))
     here = [from_z, before, fetch(source, "y", Y, 2), behind]
-    key_own, value_own, delta = made
+    value_own, delta = made
     here[2], away, delta = after((here[2], away, delta))
     there = [fetch(a, "core", CORE, 1) for a in here]
     qg1, own_grad = after((qg1, own_grad))
@@ -276,7 +275,7 @@
     stat, bias_t, key_t = call(
         lambda *refs: stats_kernel(scale, *refs),
         "softmax_statistics",
-        [at, *q, away, key_own, delta, *here, *there],
+        [at, *q, away, kvm, delta, *here, *there],
         [((rows, total + width), F32), ((both, total), BF16), ((rows, both, 128), BF16)],
         [((2, total, width), BF16), ((both, total), F32)],
         14,

time: 139 us -> 138 us (level)
  local copies, waits for them, and re-layouts: 7.55 us -> 5.53 us
  waiting for transfers between devices: 31.9 us -> 33.7 us
    unnamed x14 -> x10, local copies, waits for them, and re-layouts: 6.66 us -> 4.63 us
    ppermute x17, waiting for transfers between devices: 19.1 us -> 20.9 us  [fetch(): lax.ppermute(x, axis, [((n + distance) % size, n) for n in range(size)])]
where the time goes in v8:
time: 138 us
  starting transfers between devices  54.4 us (39%)
  Pallas kernels  40.5 us (29%)
  waiting for transfers between devices  33.7 us (24%)
  local copies, waits for them, and re-layouts  5.53 us (4%)
  other arithmetic  3.01 us (2%)
    pallas_call x4, Pallas kernels, call(): pl.pallas_call(kernel, in_specs=[SMEM] * places + [VMEM] * (len(args) - p...  40.5 us
    ppermute x17, starting transfers between devices, fetch(): lax.ppermute(x, axis, [((n + distance) % size, n) for n in range(size)])  23.3 us
    ppermute x17, waiting for transfers between devices, fetch(): lax.ppermute(x, axis, [((n + distance) % size, n) for n in range(size)])  20.9 us
    ppermute x4, starting transfers between devices, per_device(): from_z = [lax.ppermute(bias, z_axes, z_pairs(d)) for d in range(ZLO)]  12.1 us
    ppermute x1, starting transfers between devices, per_device(): lax.ppermute(along_y[2:].astype(BF16), 'zlo', across).astype(F32)  8.09 us
    ppermute x6, waiting for transfers between devices, deliver(): lax.ppermute(x, axis, [(n, (n + distance) % size) for n in range(size)])  7.89 us
    ppermute x6, starting transfers between devices, deliver(): lax.ppermute(x, axis, [(n, (n + distance) % size) for n in range(size)])  7.27 us
    ppermute x2, waiting for transfers between devices, per_device(): part = lax.ppermute(kept[d].astype(BF16), z_axes, pairs).astype(F32)  4.87 us
  transfers between devices with their start and end apart: 30, of which 14 were waited for; matrix products, arithmetic and copies ran while one was open for 2% of the time, Pallas kernels for 10%

profile of v8, /device:TPU:64, one launch (start us, length us, event | category | flops | bytes accessed | tf_op | source)
XLA Modules:
  0.0 137.9 jit_solution(15577620635806124979)
XLA Ops:
  0.6 3.1 %collective-permute-start.4 = (bf16[8,32,384]{2,1,0:T(8,128)(2,1)}, bf16[8,32,384]{2,1,0:T(8,128)(2,1)S(1)}, u32[]{:S(2)}, u32[]{:S(2)}) collective-permute-start(bf16[8,32,384]{2,1,0:T(8,128)(2,1)} %q.1), channel_id=1, source_target_pairs={{2,0},{3,1},{0,2},{1,3},{6,4},{7,5},{4,6},{5,7},{10,8},{11,9},{8,1... | collective-permute-start | bytes 589832 | tf_op jit(solution)/shard_map/ppermute | solution.py:215
  3.7 4.9 %collective-permute-start.1 = (bf16[96,384]{1,0:T(8,128)(2,1)}, bf16[96,384]{1,0:T(8,128)(2,1)S(1)}, u32[]{:S(2)}, u32[]{:S(2)}) collective-permute-start(bf16[96,384]{1,0:T(8,128)(2,1)} %param.12), channel_id=1, source_target_pairs={{64,0},{0,64},{68,128},{4,192},{192,4},{128,68},{196,132},{132,196... | collective-permute-start | bytes 221192 | tf_op jit(solution)/shard_map/ppermute | solution.py:239
  8.7 1.9 %collective-permute-start = (bf16[96,384]{1,0:T(8,128)(2,1)}, bf16[96,384]{1,0:T(8,128)(2,1)S(1)}, u32[]{:S(2)}, u32[]{:S(2)}) collective-permute-start(bf16[96,384]{1,0:T(8,128)(2,1)} %param.12), channel_id=1, source_target_pairs={{0,0},{64,64},{4,128},{68,192},{128,4},{192,68},{132,132},{196,196... | collective-permute-start | bytes 221192 | tf_op jit(solution)/shard_map/ppermute | solution.py:239
  10.6 0.6 collective-permute-start.3
  11.2 4.6 %collective-permute-start.2 = (bf16[96,384]{1,0:T(8,128)(2,1)}, bf16[96,384]{1,0:T(8,128)(2,1)S(1)}, u32[]{:S(2)}, u32[]{:S(2)}) collective-permute-start(bf16[96,384]{1,0:T(8,128)(2,1)} %param.12), channel_id=1, source_target_pairs={{4,0},{68,64},{0,128},{64,192},{132,4},{196,68},{128,132},{192,196... | collective-permute-start | bytes 221192 | tf_op jit(solution)/shard_map/ppermute | solution.py:239
  15.8 0.7 broadcast_in_dim.3.mask
  16.5 0.9 copy-done
  17.4 0.9 copy-done.1
  18.3 0.9 copy-done.2
  19.3 0.9 copy-done.3
  20.2 0.8 join.1
  21.0 0.0 collective-permute-done.2
  21.0 0.0 collective-permute-done.4.refs_3_.refs_2_
  21.0 0.7 collective-permute-start.7
  21.7 3.1 %collective-permute-start.6 = (bf16[4,96,384]{2,1,0:T(8,128)(2,1)S(1)}, bf16[4,96,384]{2,1,0:T(8,128)(2,1)}, u32[]{:S(2)}, u32[]{:S(2)}) collective-permute-start(bf16[4,96,384]{2,1,0:T(8,128)(2,1)S(1)} %pad_maximum_fusion.refs_8_), channel_id=1, source_target_pairs={{16,0},{32,16},{48,32},{0,48},{17,1},{33,17},{49,33},{1,49},{18,2}... | collective-permute-start | bytes 884744 | tf_op jit(solution)/shard_map/ppermute | solution.py:215
  24.8 4.0 %collective-permute-start.9 = (bf16[17,32,384]{2,1,0:T(8,128)(2,1)S(1)}, bf16[17,32,384]{2,1,0:T(8,128)(2,1)S(1)}, u32[]{:S(2)}, u32[]{:S(2)}) collective-permute-start(bf16[17,32,384]{2,1,0:T(8,128)(2,1)S(1)} %get-tuple-element.63.kvm.refs_6_.refs_5_), channel_id=1, source_target_pairs={{4,0},{0,4},{5,1},{1,5},{6,2},{2,6},{7,3},{3,7},{12,8},{8,12},{13,... | collective-permute-start | bytes 1253384 | tf_op jit(solution)/shard_map/ppermute | solution.py:215
  28.8 0.0 collective-permute-start.10
  28.8 0.5 collective-permute-done.6.refs_9_
  29.4 2.3 %collective-permute-done.7.refs_4_.refs_3_ = bf16[16,32,384]{2,1,0:T(8,128)(2,1)S(1)} collective-permute-done((bf16[16,32,384]{2,1,0:T(8,128)(2,1)S(1)}, bf16[16,32,384]{2,1,0:T(8,128)(2,1)S(1)}, u32[]{:S(2)}, u32[]{:S(2)}) %collective-permute-start.7) | collective-permute-done | bytes 393248 | tf_op jit(solution)/shard_map/ppermute | solution.py:215
  31.7 3.2 %collective-permute-start.8 = (bf16[4,96,384]{2,1,0:T(8,128)(2,1)S(1)}, bf16[4,96,384]{2,1,0:T(8,128)(2,1)}, u32[]{:S(2)}, u32[]{:S(2)}) collective-permute-start(bf16[4,96,384]{2,1,0:T(8,128)(2,1)S(1)} %pad_maximum_fusion.refs_8_), channel_id=1, source_target_pairs={{32,0},{48,16},{0,32},{16,48},{33,1},{49,17},{1,33},{17,49},{34,2}... | collective-permute-start | bytes 884744 | tf_op jit(solution)/shard_map/ppermute | solution.py:215
  34.9 0.0 collective-permute-start.5
  34.9 0.0 collective-permute-start.11
  34.9 0.9 copy-done.4
  35.9 0.9 prepare.1
  36.8 6.3 %collective-permute-done.10.refs_11_ = bf16[4,96,384]{2,1,0:T(8,128)(2,1)} collective-permute-done((bf16[4,96,384]{2,1,0:T(8,128)(2,1)S(1)}, bf16[4,96,384]{2,1,0:T(8,128)(2,1)}, u32[]{:S(2)}, u32[]{:S(2)}) %collective-permute-start.10) | collective-permute-done | bytes 294944 | tf_op jit(solution)/shard_map/ppermute | solution.py:215
  43.0 0.0 collective-permute-done.9.refs_5_.refs_6_
  43.1 0.5 collective-permute-start.12
  43.6 0.1 collective-permute-start.13
  43.7 1.0 collective-permute-start.15
  44.6 0.1 stack.38.refs_0_.at
  44.7 0.3 collective-permute-done.14.refs_15_
  45.0 0.4 collective-permute-done.12.refs_13_
  45.4 0.4 collective-permute-done.13.refs_14_
  45.8 12.4 %softmax_statistics.1 = (f32[8,1920]{1,0:T(8,128)S(1)}, bf16[768,1536]{1,0:T(8,128)(2,1)S(1)}, bf16[8,768,128]{2,1,0:T(8,128)(2,1)S(1)}) custom-call(s32[5]{0:T(128)S(1)} %stack.38.refs_0_.at, bf16[16,32,384]{2,1,0:T(8,128)(2,1)S(1)} %get-tuple-element.53.qg.refs_1_.refs_0_, bf16[16,32,384]{2,1,0:T(8,128)(2,1)S(1)} %collective-permute-done.5.refs_2_.refs_1_, ...), custom_call_target="tpu_custom_call" | custom-call | tf_op jit(solution)/shard_map/softmax_statistics/pallas_call | solution.py:203
  58.2 0.5 collective-permute-start.18
  58.7 2.5 %collective-permute-start.17 = (f32[8,1920]{1,0:T(8,128)S(1)}, f32[8,1920]{1,0:T(8,128)S(1)}, u32[]{:S(2)}, u32[]{:S(2)}) collective-permute-start(f32[8,1920]{1,0:T(8,128)S(1)} %get-tuple-element.74.refs_9_), channel_id=1, source_target_pairs={{2,0},{3,1},{0,2},{1,3},{6,4},{7,5},{4,6},{5,7},{10,8},{11,9},{8,1... | collective-permute-start | bytes 184328 | tf_op jit(solution)/shard_map/ppermute | solution.py:215
  61.2 1.4 %collective-permute-start.16 = (f32[8,1920]{1,0:T(8,128)S(1)}, f32[8,1920]{1,0:T(8,128)S(1)}, u32[]{:S(2)}, u32[]{:S(2)}) collective-permute-start(f32[8,1920]{1,0:T(8,128)S(1)} %get-tuple-element.74.refs_9_), channel_id=1, source_target_pairs={{1,0},{2,1},{3,2},{0,3},{5,4},{6,5},{7,6},{4,7},{9,8},{10,9},{11,1... | collective-permute-start | bytes 184328 | tf_op jit(solution)/shard_map/ppermute | solution.py:215
  62.6 2.3 %collective-permute-done.18.refs_12_ = f32[8,1920]{1,0:T(8,128)S(1)} collective-permute-done((f32[8,1920]{1,0:T(8,128)S(1)}, f32[8,1920]{1,0:T(8,128)S(1)}, u32[]{:S(2)}, u32[]{:S(2)}) %collective-permute-start.18) | collective-permute-done | bytes 61472 | tf_op jit(solution)/shard_map/ppermute | solution.py:215
  64.9 0.6 collective-permute-done.16.refs_10_
  65.5 26.4 %attention_gradients.1 = (f32[8,32,384]{2,1,0:T(8,128)S(1)}, bf16[8,32,384]{2,1,0:T(8,128)(2,1)S(1)}, bf16[8,32,384]{2,1,0:T(8,128)(2,1)S(1)}, bf16[8,32,384]{2,...) custom-call(s32[5]{0:T(128)S(1)} %stack.38.refs_0_.at, ...), custom_call_target="tpu_custom_call" | custom-call | tf_op jit(solution)/shard_map/attention_gradients/pallas_call | solution.py:203
  91.9 0.1 collective-permute-start.19
  92.0 3.1 %collective-permute-start.21 = (bf16[16,32,384]{2,1,0:T(8,128)(2,1)S(1)}, bf16[16,32,384]{2,1,0:T(8,128)(2,1)S(1)}, u32[]{:S(2)}, u32[]{:S(2)}) collective-permute-start(bf16[16,32,384]{2,1,0:T(8,128)(2,1)S(1)} %get-tuple-element.80), channel_id=1, source_target_pairs={{4,0},{0,4},{5,1},{1,5},{6,2},{2,6},{7,3},{3,7},{12,8},{8,12},{13,... | collective-permute-start | bytes 1179656 | tf_op jit(solution)/shard_map/ppermute | solution.py:215
  95.1 0.4 fusion.6
  95.5 0.1 slice_bitcast_fusion.1
  95.6 0.2 collective-permute-start.20
  95.8 0.8 collective-permute-start.23
  96.6 2.3 %collective-permute-start.24 = (bf16[4,96,384]{2,1,0:T(8,128)(2,1)S(1)}, bf16[4,96,384]{2,1,0:T(8,128)(2,1)S(1)}, u32[]{:S(2)}, u32[]{:S(2)}) collective-permute-start(bf16[4,96,384]{2,1,0:T(8,128)(2,1)S(1)} %get-tuple-element.84), channel_id=1, source_target_pairs={{0,48},{16,0},{32,16},{48,32},{1,49},{17,1},{33,17},{49,33},{2,50}... | collective-permute-start | bytes 884744 | tf_op jit(solution)/shard_map/ppermute | solution.py:219
  98.9 0.9 collective-permute-start.22
  99.8 7.8 %collective-permute-done.21 = bf16[16,32,384]{2,1,0:T(8,128)(2,1)S(1)} collective-permute-done((bf16[16,32,384]{2,1,0:T(8,128)(2,1)S(1)}, bf16[16,32,384]{2,1,0:T(8,128)(2,1)S(1)}, u32[]{:S(2)}, u32[]{:S(2)}) %collective-permute-start.21) | collective-permute-done | bytes 393248 | tf_op jit(solution)/shard_map/ppermute | solution.py:215
  107.6 4.7 %collective-permute-done.20 = bf16[4,96,384]{2,1,0:T(8,128)(2,1)S(1)} collective-permute-done((bf16[4,96,384]{2,1,0:T(8,128)(2,1)S(1)}, bf16[4,96,384]{2,1,0:T(8,128)(2,1)S(1)}, u32[]{:S(2)}, u32[]{:S(2)}) %collective-permute-start.20) | collective-permute-done | bytes 294944 | tf_op jit(solution)/shard_map/ppermute | solution.py:219
  112.2 0.6 collective-permute-done.24
  112.9 0.1 fusion.2
  113.0 8.1 %collective-permute-start.27 = (bf16[2,96,384]{2,1,0:T(8,128)(2,1)S(1)}, bf16[2,96,384]{2,1,0:T(8,128)(2,1)S(1)}, u32[]{:S(2)}, u32[]{:S(2)}) collective-permute-start(bf16[2,96,384]{2,1,0:T(8,128)(2,1)S(1)} %slice.77), channel_id=1, source_target_pairs={{0,64},{64,0},{128,192},{192,128},{1,65},{65,1},{129,193},{193,129... | collective-permute-start | bytes 442376 | tf_op jit(solution)/shard_map/ppermute | solution.py:318
  121.1 1.5 %collective-permute-start.25 = (bf16[8,32,384]{2,1,0:T(8,128)(2,1)S(1)}, bf16[8,32,384]{2,1,0:T(8,128)(2,1)S(1)}, u32[]{:S(2)}, u32[]{:S(2)}) collective-permute-start(bf16[8,32,384]{2,1,0:T(8,128)(2,1)S(1)} %get-tuple-element.90), channel_id=1, source_target_pairs={{0,2},{1,3},{2,0},{3,1},{4,6},{5,7},{6,4},{7,5},{8,10},{9,11},{10,... | collective-permute-start | bytes 589832 | tf_op jit(solution)/shard_map/ppermute | solution.py:219
  122.6 1.6 %collective-permute-start.26 = (bf16[8,32,384]{2,1,0:T(8,128)(2,1)S(1)}, bf16[8,32,384]{2,1,0:T(8,128)(2,1)S(1)}, u32[]{:S(2)}, u32[]{:S(2)}) collective-permute-start(bf16[8,32,384]{2,1,0:T(8,128)(2,1)S(1)} %get-tuple-element.91), channel_id=1, source_target_pairs={{0,3},{1,0},{2,1},{3,2},{4,7},{5,4},{6,5},{7,6},{8,11},{9,8},{10,9... | collective-permute-start | bytes 589832 | tf_op jit(solution)/shard_map/ppermute | solution.py:219
  124.2 0.1 convert_element_type.74
  124.3 0.9 fusion.3
  125.2 3.7 %collective-permute-start.28 = (bf16[96,384]{1,0:T(8,128)(2,1)S(1)}, bf16[96,384]{1,0:T(8,128)(2,1)S(1)}, u32[]{:S(2)}, u32[]{:S(2)}) collective-permute-start(bf16[96,384]{1,0:T(8,128)(2,1)S(1)} %get-tuple-element.103), channel_id=1, source_target_pairs={{0,0},{64,64},{128,4},{192,68},{4,128},{68,192},{132,132},{196,196... | collective-permute-start | bytes 221192 | tf_op jit(solution)/shard_map/ppermute | solution.py:322
  128.9 0.1 collective-permute-start.29
  129.0 2.6 %collective-permute-done.26 = bf16[8,32,384]{2,1,0:T(8,128)(2,1)S(1)} collective-permute-done((bf16[8,32,384]{2,1,0:T(8,128)(2,1)S(1)}, bf16[8,32,384]{2,1,0:T(8,128)(2,1)S(1)}, u32[]{:S(2)}, u32[]{:S(2)}) %collective-permute-start.26) | collective-permute-done | bytes 196640 | tf_op jit(solution)/shard_map/ppermute | solution.py:219
  131.6 0.8 multiply_convert_fusion
  132.3 2.8 %collective-permute-done.28 = bf16[96,384]{1,0:T(8,128)(2,1)S(1)} collective-permute-done((bf16[96,384]{1,0:T(8,128)(2,1)S(1)}, bf16[96,384]{1,0:T(8,128)(2,1)S(1)}, u32[]{:S(2)}, u32[]{:S(2)}) %collective-permute-start.28) | collective-permute-done | bytes 73760 | tf_op jit(solution)/shard_map/ppermute | solution.py:322
  135.1 2.1 %collective-permute-done.29 = bf16[96,384]{1,0:T(8,128)(2,1)S(1)} collective-permute-done((bf16[96,384]{1,0:T(8,128)(2,1)S(1)}, bf16[96,384]{1,0:T(8,128)(2,1)S(1)}, u32[]{:S(2)}, u32[]{:S(2)}) %collective-permute-start.29) | collective-permute-done | bytes 73760 | tf_op jit(solution)/shard_map/ppermute | solution.py:322
  137.2 0.7 convert_add_fusion.1
  (23 shorter events, 0.2 us)
Async XLA Ops:
  0.6 20.4 %collective-permute-start.4 = (bf16[8,32,384]{2,1,0:T(8,128)(2,1)}, bf16[8,32,384]{2,1,0:T(8,128)(2,1)S(1)}, u32[]{:S(2)}, u32[]{:S(2)}) collective-permute-start(bf16[8,32,384]{2,1,0:T(8,128)(2,1)} %q.1), channel_id=1, source_target_pairs={{2,0},{3,1},{0,2},{1,3},{6,4},{7,5},{4,6},{5,7},{10,8},{11,9},{8,1... | collective-permute-start | bytes 589832 | tf_op jit(solution)/shard_map/ppermute | solution.py:215
  3.7 17.2 %collective-permute-start.1 = (bf16[96,384]{1,0:T(8,128)(2,1)}, bf16[96,384]{1,0:T(8,128)(2,1)S(1)}, u32[]{:S(2)}, u32[]{:S(2)}) collective-permute-start(bf16[96,384]{1,0:T(8,128)(2,1)} %param.12), channel_id=1, source_target_pairs={{64,0},{0,64},{68,128},{4,192},{192,4},{128,68},{196,132},{132,196... | collective-permute-start | bytes 221192 | tf_op jit(solution)/shard_map/ppermute | solution.py:239
  8.7 12.3 %collective-permute-start = (bf16[96,384]{1,0:T(8,128)(2,1)}, bf16[96,384]{1,0:T(8,128)(2,1)S(1)}, u32[]{:S(2)}, u32[]{:S(2)}) collective-permute-start(bf16[96,384]{1,0:T(8,128)(2,1)} %param.12), channel_id=1, source_target_pairs={{0,0},{64,64},{4,128},{68,192},{128,4},{192,68},{132,132},{196,196... | collective-permute-start | bytes 221192 | tf_op jit(solution)/shard_map/ppermute | solution.py:239
  10.6 10.4 %collective-permute-start.3 = (bf16[96,384]{1,0:T(8,128)(2,1)}, bf16[96,384]{1,0:T(8,128)(2,1)S(1)}, u32[]{:S(2)}, u32[]{:S(2)}) collective-permute-start(bf16[96,384]{1,0:T(8,128)(2,1)} %param.12), channel_id=1, source_target_pairs={{68,0},{4,64},{64,128},{0,192},{196,4},{132,68},{192,132},{128,196... | collective-permute-start | bytes 221192 | tf_op jit(solution)/shard_map/ppermute | solution.py:239
  11.2 9.7 %collective-permute-start.2 = (bf16[96,384]{1,0:T(8,128)(2,1)}, bf16[96,384]{1,0:T(8,128)(2,1)S(1)}, u32[]{:S(2)}, u32[]{:S(2)}) collective-permute-start(bf16[96,384]{1,0:T(8,128)(2,1)} %param.12), channel_id=1, source_target_pairs={{4,0},{68,64},{0,128},{64,192},{132,4},{196,68},{128,132},{192,196... | collective-permute-start | bytes 221192 | tf_op jit(solution)/shard_map/ppermute | solution.py:239
  16.5 0.9 copy-start
  17.4 0.9 copy-start.1
  18.3 0.9 copy-start.2
  19.3 0.9 copy-start.3
  21.0 10.7 %collective-permute-start.7 = (bf16[16,32,384]{2,1,0:T(8,128)(2,1)S(1)}, bf16[16,32,384]{2,1,0:T(8,128)(2,1)S(1)}, u32[]{:S(2)}, u32[]{:S(2)}) collective-permute-start(bf16[16,32,384]{2,1,0:T(8,128)(2,1)S(1)} %get-tuple-element.53.qg.refs_1_.refs_0_), channel_id=1, source_target_pairs={{3,0},{0,1},{1,2},{2,3},{7,4},{4,5},{5,6},{6,7},{11,8},{8,9},{9,10... | collective-permute-start | bytes 1179656 | tf_op jit(solution)/shard_map/ppermute | solution.py:215
  21.7 7.7 %collective-permute-start.6 = (bf16[4,96,384]{2,1,0:T(8,128)(2,1)S(1)}, bf16[4,96,384]{2,1,0:T(8,128)(2,1)}, u32[]{:S(2)}, u32[]{:S(2)}) collective-permute-start(bf16[4,96,384]{2,1,0:T(8,128)(2,1)S(1)} %pad_maximum_fusion.refs_8_), channel_id=1, source_target_pairs={{16,0},{32,16},{48,32},{0,48},{17,1},{33,17},{49,33},{1,49},{18,2}... | collective-permute-start | bytes 884744 | tf_op jit(solution)/shard_map/ppermute | solution.py:215
  24.8 18.2 %collective-permute-start.9 = (bf16[17,32,384]{2,1,0:T(8,128)(2,1)S(1)}, bf16[17,32,384]{2,1,0:T(8,128)(2,1)S(1)}, u32[]{:S(2)}, u32[]{:S(2)}) collective-permute-start(bf16[17,32,384]{2,1,0:T(8,128)(2,1)S(1)} %get-tuple-element.63.kvm.refs_6_.refs_5_), channel_id=1, source_target_pairs={{4,0},{0,4},{5,1},{1,5},{6,2},{2,6},{7,3},{3,7},{12,8},{8,12},{13,... | collective-permute-start | bytes 1253384 | tf_op jit(solution)/shard_map/ppermute | solution.py:215
  28.8 14.2 %collective-permute-start.10 = (bf16[4,96,384]{2,1,0:T(8,128)(2,1)S(1)}, bf16[4,96,384]{2,1,0:T(8,128)(2,1)}, u32[]{:S(2)}, u32[]{:S(2)}) collective-permute-start(bf16[4,96,384]{2,1,0:T(8,128)(2,1)S(1)} %pad_maximum_fusion.refs_8_), channel_id=1, source_target_pairs={{48,0},{0,16},{16,32},{32,48},{49,1},{1,17},{17,33},{33,49},{50,2}... | collective-permute-start | bytes 884744 | tf_op jit(solution)/shard_map/ppermute | solution.py:215
  31.7 11.8 %collective-permute-start.8 = (bf16[4,96,384]{2,1,0:T(8,128)(2,1)S(1)}, bf16[4,96,384]{2,1,0:T(8,128)(2,1)}, u32[]{:S(2)}, u32[]{:S(2)}) collective-permute-start(bf16[4,96,384]{2,1,0:T(8,128)(2,1)S(1)} %pad_maximum_fusion.refs_8_), channel_id=1, source_target_pairs={{32,0},{48,16},{0,32},{16,48},{33,1},{49,17},{1,33},{17,49},{34,2}... | collective-permute-start | bytes 884744 | tf_op jit(solution)/shard_map/ppermute | solution.py:215
  34.9 8.7 %collective-permute-start.5 = (bf16[16,32,384]{2,1,0:T(8,128)(2,1)S(1)}, bf16[16,32,384]{2,1,0:T(8,128)(2,1)S(1)}, u32[]{:S(2)}, u32[]{:S(2)}) collective-permute-start(bf16[16,32,384]{2,1,0:T(8,128)(2,1)S(1)} %get-tuple-element.53.qg.refs_1_.refs_0_), channel_id=1, source_target_pairs={{1,0},{2,1},{3,2},{0,3},{5,4},{6,5},{7,6},{4,7},{9,8},{10,9},{11,1... | collective-permute-start | bytes 1179656 | tf_op jit(solution)/shard_map/ppermute | solution.py:215
  34.9 9.8 %collective-permute-start.11 = (bf16[4,96,384]{2,1,0:T(8,128)(2,1)S(1)}, bf16[4,96,384]{2,1,0:T(8,128)(2,1)}, u32[]{:S(2)}, u32[]{:S(2)}) collective-permute-start(bf16[4,96,384]{2,1,0:T(8,128)(2,1)S(1)} %pad_maximum_fusion.refs_8_), channel_id=1, source_target_pairs={{8,0},{0,8},{9,1},{1,9},{10,2},{2,10},{11,3},{3,11},{12,4},{4,12},... | collective-permute-start | bytes 884744 | tf_op jit(solution)/shard_map/ppermute | solution.py:215
  34.9 0.9 copy-start.4
  43.0 1.9 %collective-permute-start.14 = (bf16[4,96,384]{2,1,0:T(8,128)(2,1)}, bf16[4,96,384]{2,1,0:T(8,128)(2,1)}, u32[]{:S(2)}, u32[]{:S(2)}) collective-permute-start(bf16[4,96,384]{2,1,0:T(8,128)(2,1)} %collective-permute-done.10.refs_11_), channel_id=1, source_target_pairs={{8,0},{0,8},{9,1},{1,9},{10,2},{2,10},{11,3},{3,11},{12,4},{4,12},... | collective-permute-start | bytes 884744 | tf_op jit(solution)/shard_map/ppermute | solution.py:215
  43.1 2.3 %collective-permute-start.12 = (bf16[4,96,384]{2,1,0:T(8,128)(2,1)}, bf16[4,96,384]{2,1,0:T(8,128)(2,1)}, u32[]{:S(2)}, u32[]{:S(2)}) collective-permute-start(bf16[4,96,384]{2,1,0:T(8,128)(2,1)} %collective-permute-done.6.refs_9_), channel_id=1, source_target_pairs={{8,0},{0,8},{9,1},{1,9},{10,2},{2,10},{11,3},{3,11},{12,4},{4,12},... | collective-permute-start | bytes 884744 | tf_op jit(solution)/shard_map/ppermute | solution.py:215
  43.6 2.3 %collective-permute-start.13 = (bf16[4,96,384]{2,1,0:T(8,128)(2,1)}, bf16[4,96,384]{2,1,0:T(8,128)(2,1)}, u32[]{:S(2)}, u32[]{:S(2)}) collective-permute-start(bf16[4,96,384]{2,1,0:T(8,128)(2,1)} %collective-permute-done.8.refs_10_), channel_id=1, source_target_pairs={{8,0},{0,8},{9,1},{1,9},{10,2},{2,10},{11,3},{3,11},{12,4},{4,12},... | collective-permute-start | bytes 884744 | tf_op jit(solution)/shard_map/ppermute | solution.py:215
  43.7 14.6 %collective-permute-start.15 = (bf16[8,32,384]{2,1,0:T(8,128)(2,1)}, bf16[8,32,384]{2,1,0:T(8,128)(2,1)S(1)}, u32[]{:S(2)}, u32[]{:S(2)}) collective-permute-start(bf16[8,32,384]{2,1,0:T(8,128)(2,1)} %get-tuple-element.70), channel_id=1, source_target_pairs={{2,0},{3,1},{0,2},{1,3},{6,4},{7,5},{4,6},{5,7},{10,8},{11,9},{8,1... | collective-permute-start | bytes 589832 | tf_op jit(solution)/shard_map/ppermute | solution.py:215
  58.2 6.7 %collective-permute-start.18 = (f32[8,1920]{1,0:T(8,128)S(1)}, f32[8,1920]{1,0:T(8,128)S(1)}, u32[]{:S(2)}, u32[]{:S(2)}) collective-permute-start(f32[8,1920]{1,0:T(8,128)S(1)} %get-tuple-element.74.refs_9_), channel_id=1, source_target_pairs={{3,0},{0,1},{1,2},{2,3},{7,4},{4,5},{5,6},{6,7},{11,8},{8,9},{9,10... | collective-permute-start | bytes 184328 | tf_op jit(solution)/shard_map/ppermute | solution.py:215
  58.7 6.1 %collective-permute-start.17 = (f32[8,1920]{1,0:T(8,128)S(1)}, f32[8,1920]{1,0:T(8,128)S(1)}, u32[]{:S(2)}, u32[]{:S(2)}) collective-permute-start(f32[8,1920]{1,0:T(8,128)S(1)} %get-tuple-element.74.refs_9_), channel_id=1, source_target_pairs={{2,0},{3,1},{0,2},{1,3},{6,4},{7,5},{4,6},{5,7},{10,8},{11,9},{8,1... | collective-permute-start | bytes 184328 | tf_op jit(solution)/shard_map/ppermute | solution.py:215
  61.2 4.3 %collective-permute-start.16 = (f32[8,1920]{1,0:T(8,128)S(1)}, f32[8,1920]{1,0:T(8,128)S(1)}, u32[]{:S(2)}, u32[]{:S(2)}) collective-permute-start(f32[8,1920]{1,0:T(8,128)S(1)} %get-tuple-element.74.refs_9_), channel_id=1, source_target_pairs={{1,0},{2,1},{3,2},{0,3},{5,4},{6,5},{7,6},{4,7},{9,8},{10,9},{11,1... | collective-permute-start | bytes 184328 | tf_op jit(solution)/shard_map/ppermute | solution.py:215
  91.9 3.2 %collective-permute-start.19 = (bf16[4,4,96,384]{3,2,1,0:T(8,128)(2,1)S(1)}, bf16[4,4,96,384]{3,2,1,0:T(8,128)(2,1)S(1)}, u32[]{:S(2)}, u32[]{:S(2)}) collective-permute-start(bf16[4,4,96,384]{3,2,1,0:T(8,128)(2,1)S(1)} %get-tuple-element.77), channel_id=1, source_target_pairs={{8,0},{0,8},{9,1},{1,9},{10,2},{2,10},{11,3},{3,11},{12,4},{4,12},... | collective-permute-start | bytes 3538952 | tf_op jit(solution)/shard_map/ppermute | solution.py:215
  92.0 15.6 %collective-permute-start.21 = (bf16[16,32,384]{2,1,0:T(8,128)(2,1)S(1)}, bf16[16,32,384]{2,1,0:T(8,128)(2,1)S(1)}, u32[]{:S(2)}, u32[]{:S(2)}) collective-permute-start(bf16[16,32,384]{2,1,0:T(8,128)(2,1)S(1)} %get-tuple-element.80), channel_id=1, source_target_pairs={{4,0},{0,4},{5,1},{1,5},{6,2},{2,6},{7,3},{3,7},{12,8},{8,12},{13,... | collective-permute-start | bytes 1179656 | tf_op jit(solution)/shard_map/ppermute | solution.py:215
  95.6 16.7 %collective-permute-start.20 = (bf16[4,96,384]{2,1,0:T(8,128)(2,1)S(1)}, bf16[4,96,384]{2,1,0:T(8,128)(2,1)S(1)}, u32[]{:S(2)}, u32[]{:S(2)}) collective-permute-start(bf16[4,96,384]{2,1,0:T(8,128)(2,1)S(1)} %get-tuple-element.79), channel_id=1, source_target_pairs={{0,16},{16,32},{32,48},{48,0},{1,17},{17,33},{33,49},{49,1},{2,18}... | collective-permute-start | bytes 884744 | tf_op jit(solution)/shard_map/ppermute | solution.py:219
  95.8 16.5 %collective-permute-start.23 = (bf16[4,96,384]{2,1,0:T(8,128)(2,1)S(1)}, bf16[4,96,384]{2,1,0:T(8,128)(2,1)S(1)}, u32[]{:S(2)}, u32[]{:S(2)}) collective-permute-start(bf16[4,96,384]{2,1,0:T(8,128)(2,1)S(1)} %get-tuple-element.83), channel_id=1, source_target_pairs={{0,32},{16,48},{32,0},{48,16},{1,33},{17,49},{33,1},{49,17},{2,34}... | collective-permute-start | bytes 884744 | tf_op jit(solution)/shard_map/ppermute | solution.py:219
  96.6 16.3 %collective-permute-start.24 = (bf16[4,96,384]{2,1,0:T(8,128)(2,1)S(1)}, bf16[4,96,384]{2,1,0:T(8,128)(2,1)S(1)}, u32[]{:S(2)}, u32[]{:S(2)}) collective-permute-start(bf16[4,96,384]{2,1,0:T(8,128)(2,1)S(1)} %get-tuple-element.84), channel_id=1, source_target_pairs={{0,48},{16,0},{32,16},{48,32},{1,49},{17,1},{33,17},{49,33},{2,50}... | collective-permute-start | bytes 884744 | tf_op jit(solution)/shard_map/ppermute | solution.py:219
  98.9 8.7 %collective-permute-start.22 = (bf16[8,32,384]{2,1,0:T(8,128)(2,1)S(1)}, bf16[8,32,384]{2,1,0:T(8,128)(2,1)S(1)}, u32[]{:S(2)}, u32[]{:S(2)}) collective-permute-start(bf16[8,32,384]{2,1,0:T(8,128)(2,1)S(1)} %get-tuple-element.81), channel_id=1, source_target_pairs={{0,1},{1,2},{2,3},{3,0},{4,5},{5,6},{6,7},{7,4},{8,9},{9,10},{10,1... | collective-permute-start | bytes 589832 | tf_op jit(solution)/shard_map/ppermute | solution.py:219
  113.0 12.1 %collective-permute-start.27 = (bf16[2,96,384]{2,1,0:T(8,128)(2,1)S(1)}, bf16[2,96,384]{2,1,0:T(8,128)(2,1)S(1)}, u32[]{:S(2)}, u32[]{:S(2)}) collective-permute-start(bf16[2,96,384]{2,1,0:T(8,128)(2,1)S(1)} %slice.77), channel_id=1, source_target_pairs={{0,64},{64,0},{128,192},{192,128},{1,65},{65,1},{129,193},{193,129... | collective-permute-start | bytes 442376 | tf_op jit(solution)/shard_map/ppermute | solution.py:318
  121.1 7.8 %collective-permute-start.25 = (bf16[8,32,384]{2,1,0:T(8,128)(2,1)S(1)}, bf16[8,32,384]{2,1,0:T(8,128)(2,1)S(1)}, u32[]{:S(2)}, u32[]{:S(2)}) collective-permute-start(bf16[8,32,384]{2,1,0:T(8,128)(2,1)S(1)} %get-tuple-element.90), channel_id=1, source_target_pairs={{0,2},{1,3},{2,0},{3,1},{4,6},{5,7},{6,4},{7,5},{8,10},{9,11},{10,... | collective-permute-start | bytes 589832 | tf_op jit(solution)/shard_map/ppermute | solution.py:219
  122.6 8.9 %collective-permute-start.26 = (bf16[8,32,384]{2,1,0:T(8,128)(2,1)S(1)}, bf16[8,32,384]{2,1,0:T(8,128)(2,1)S(1)}, u32[]{:S(2)}, u32[]{:S(2)}) collective-permute-start(bf16[8,32,384]{2,1,0:T(8,128)(2,1)S(1)} %get-tuple-element.91), channel_id=1, source_target_pairs={{0,3},{1,0},{2,1},{3,2},{4,7},{5,4},{6,5},{7,6},{8,11},{9,8},{10,9... | collective-permute-start | bytes 589832 | tf_op jit(solution)/shard_map/ppermute | solution.py:219
  125.2 9.9 %collective-permute-start.28 = (bf16[96,384]{1,0:T(8,128)(2,1)S(1)}, bf16[96,384]{1,0:T(8,128)(2,1)S(1)}, u32[]{:S(2)}, u32[]{:S(2)}) collective-permute-start(bf16[96,384]{1,0:T(8,128)(2,1)S(1)} %get-tuple-element.103), channel_id=1, source_target_pairs={{0,0},{64,64},{128,4},{192,68},{4,128},{68,192},{132,132},{196,196... | collective-permute-start | bytes 221192 | tf_op jit(solution)/shard_map/ppermute | solution.py:322
  128.9 8.3 %collective-permute-start.29 = (bf16[96,384]{1,0:T(8,128)(2,1)S(1)}, bf16[96,384]{1,0:T(8,128)(2,1)S(1)}, u32[]{:S(2)}, u32[]{:S(2)}) collective-permute-start(bf16[96,384]{1,0:T(8,128)(2,1)S(1)} %get-tuple-element.104), channel_id=1, source_target_pairs={{0,4},{64,68},{128,0},{192,64},{4,132},{68,196},{132,128},{196,192... | collective-permute-start | bytes 221192 | tf_op jit(solution)/shard_map/ppermute | solution.py:322

commit v9 on v8

--- a/solution.py
+++ b/solution.py
@@ -134,7 +134,7 @@
             stat[pl.ds(i, 1), cols] = most + jnp.log(summed) * LOG2E
         return carry
 
-    lax.fori_loop(0, rows, row_step, 0, unroll=2)
+    lax.fori_loop(0, rows, row_step, 0, unroll=4)
 
 
 def main_kernel(at, *refs):

time: 138 us -> 138 us (level)
  no operation moved by 1% of the time
where the time goes in v9:
time: 138 us
  starting transfers between devices  54.5 us (39%)
  Pallas kernels  40.1 us (29%)
  waiting for transfers between devices  33.7 us (24%)
  local copies, waits for them, and re-layouts  5.53 us (4%)
  other arithmetic  3.01 us (2%)
    pallas_call x4, Pallas kernels, call(): pl.pallas_call(kernel, in_specs=[SMEM] * places + [VMEM] * (len(args) - p...  40.1 us
    ppermute x17, starting transfers between devices, fetch(): lax.ppermute(x, axis, [((n + distance) % size, n) for n in range(size)])  23.3 us
    ppermute x17, waiting for transfers between devices, fetch(): lax.ppermute(x, axis, [((n + distance) % size, n) for n in range(size)])  20.9 us
    ppermute x4, starting transfers between devices, per_device(): from_z = [lax.ppermute(bias, z_axes, z_pairs(d)) for d in range(ZLO)]  12.1 us
    ppermute x1, starting transfers between devices, per_device(): lax.ppermute(along_y[2:].astype(BF16), 'zlo', across).astype(F32)  8.13 us
    ppermute x6, waiting for transfers between devices, deliver(): lax.ppermute(x, axis, [(n, (n + distance) % size) for n in range(size)])  7.9 us
    ppermute x6, starting transfers between devices, deliver(): lax.ppermute(x, axis, [(n, (n + distance) % size) for n in range(size)])  7.27 us
    ppermute x2, waiting for transfers between devices, per_device(): part = lax.ppermute(kept[d].astype(BF16), z_axes, pairs).astype(F32)  4.86 us
  transfers between devices with their start and end apart: 30, of which 14 were waited for; matrix products, arithmetic and copies ran while one was open for 2% of the time, Pallas kernels for 10%

profile of v9, /device:TPU:64, one launch (start us, length us, event | category | flops | bytes accessed | tf_op | source)
XLA Modules:
  0.0 137.5 jit_solution(196162826757734255)
XLA Ops:
  0.6 3.1 %collective-permute-start.4 = (bf16[8,32,384]{2,1,0:T(8,128)(2,1)}, bf16[8,32,384]{2,1,0:T(8,128)(2,1)S(1)}, u32[]{:S(2)}, u32[]{:S(2)}) collective-permute-start(bf16[8,32,384]{2,1,0:T(8,128)(2,1)} %q.1), channel_id=1, source_target_pairs={{2,0},{3,1},{0,2},{1,3},{6,4},{7,5},{4,6},{5,7},{10,8},{11,9},{8,1... | collective-permute-start | bytes 589832 | tf_op jit(solution)/shard_map/ppermute | solution.py:215
  3.7 4.9 %collective-permute-start.1 = (bf16[96,384]{1,0:T(8,128)(2,1)}, bf16[96,384]{1,0:T(8,128)(2,1)S(1)}, u32[]{:S(2)}, u32[]{:S(2)}) collective-permute-start(bf16[96,384]{1,0:T(8,128)(2,1)} %param.12), channel_id=1, source_target_pairs={{64,0},{0,64},{68,128},{4,192},{192,4},{128,68},{196,132},{132,196... | collective-permute-start | bytes 221192 | tf_op jit(solution)/shard_map/ppermute | solution.py:239
  8.7 1.9 %collective-permute-start = (bf16[96,384]{1,0:T(8,128)(2,1)}, bf16[96,384]{1,0:T(8,128)(2,1)S(1)}, u32[]{:S(2)}, u32[]{:S(2)}) collective-permute-start(bf16[96,384]{1,0:T(8,128)(2,1)} %param.12), channel_id=1, source_target_pairs={{0,0},{64,64},{4,128},{68,192},{128,4},{192,68},{132,132},{196,196... | collective-permute-start | bytes 221192 | tf_op jit(solution)/shard_map/ppermute | solution.py:239
  10.6 0.6 collective-permute-start.3
  11.2 4.6 %collective-permute-start.2 = (bf16[96,384]{1,0:T(8,128)(2,1)}, bf16[96,384]{1,0:T(8,128)(2,1)S(1)}, u32[]{:S(2)}, u32[]{:S(2)}) collective-permute-start(bf16[96,384]{1,0:T(8,128)(2,1)} %param.12), channel_id=1, source_target_pairs={{4,0},{68,64},{0,128},{64,192},{132,4},{196,68},{128,132},{192,196... | collective-permute-start | bytes 221192 | tf_op jit(solution)/shard_map/ppermute | solution.py:239
  15.8 0.7 broadcast_in_dim.3.mask
  16.5 0.9 copy-done
  17.4 0.9 copy-done.1
  18.3 0.9 copy-done.2
  19.3 0.9 copy-done.3
  20.2 0.8 join.1
  21.0 0.0 collective-permute-done.1
  21.0 0.0 collective-permute-done.2
  21.0 0.7 collective-permute-start.7
  21.7 3.1 %collective-permute-start.6 = (bf16[4,96,384]{2,1,0:T(8,128)(2,1)S(1)}, bf16[4,96,384]{2,1,0:T(8,128)(2,1)}, u32[]{:S(2)}, u32[]{:S(2)}) collective-permute-start(bf16[4,96,384]{2,1,0:T(8,128)(2,1)S(1)} %pad_maximum_fusion.refs_8_), channel_id=1, source_target_pairs={{16,0},{32,16},{48,32},{0,48},{17,1},{33,17},{49,33},{1,49},{18,2}... | collective-permute-start | bytes 884744 | tf_op jit(solution)/shard_map/ppermute | solution.py:215
  24.8 4.0 %collective-permute-start.9 = (bf16[17,32,384]{2,1,0:T(8,128)(2,1)S(1)}, bf16[17,32,384]{2,1,0:T(8,128)(2,1)S(1)}, u32[]{:S(2)}, u32[]{:S(2)}) collective-permute-start(bf16[17,32,384]{2,1,0:T(8,128)(2,1)S(1)} %get-tuple-element.63.kvm.refs_6_.refs_5_), channel_id=1, source_target_pairs={{4,0},{0,4},{5,1},{1,5},{6,2},{2,6},{7,3},{3,7},{12,8},{8,12},{13,... | collective-permute-start | bytes 1253384 | tf_op jit(solution)/shard_map/ppermute | solution.py:215
  28.8 0.0 collective-permute-start.10
  28.8 0.5 collective-permute-done.6.refs_9_
  29.4 2.3 %collective-permute-done.7.refs_4_.refs_3_ = bf16[16,32,384]{2,1,0:T(8,128)(2,1)S(1)} collective-permute-done((bf16[16,32,384]{2,1,0:T(8,128)(2,1)S(1)}, bf16[16,32,384]{2,1,0:T(8,128)(2,1)S(1)}, u32[]{:S(2)}, u32[]{:S(2)}) %collective-permute-start.7) | collective-permute-done | bytes 393248 | tf_op jit(solution)/shard_map/ppermute | solution.py:215
  31.7 3.2 %collective-permute-start.8 = (bf16[4,96,384]{2,1,0:T(8,128)(2,1)S(1)}, bf16[4,96,384]{2,1,0:T(8,128)(2,1)}, u32[]{:S(2)}, u32[]{:S(2)}) collective-permute-start(bf16[4,96,384]{2,1,0:T(8,128)(2,1)S(1)} %pad_maximum_fusion.refs_8_), channel_id=1, source_target_pairs={{32,0},{48,16},{0,32},{16,48},{33,1},{49,17},{1,33},{17,49},{34,2}... | collective-permute-start | bytes 884744 | tf_op jit(solution)/shard_map/ppermute | solution.py:215
  34.9 0.0 collective-permute-start.5
  34.9 0.0 collective-permute-start.11
  34.9 0.9 copy-done.4
  35.9 0.9 prepare.1
  36.8 6.3 %collective-permute-done.10.refs_11_ = bf16[4,96,384]{2,1,0:T(8,128)(2,1)} collective-permute-done((bf16[4,96,384]{2,1,0:T(8,128)(2,1)S(1)}, bf16[4,96,384]{2,1,0:T(8,128)(2,1)}, u32[]{:S(2)}, u32[]{:S(2)}) %collective-permute-start.10) | collective-permute-done | bytes 294944 | tf_op jit(solution)/shard_map/ppermute | solution.py:215
  43.1 0.5 collective-permute-start.12
  43.6 0.1 collective-permute-start.13
  43.7 1.0 collective-permute-start.15
  44.6 0.1 stack.38.refs_0_.at
  44.7 0.3 collective-permute-done.14.refs_15_
  45.0 0.4 collective-permute-done.12.refs_13_
  45.4 0.4 collective-permute-done.13.refs_14_
  45.8 12.0 %softmax_statistics.1 = (f32[8,1920]{1,0:T(8,128)S(1)}, bf16[768,1536]{1,0:T(8,128)(2,1)S(1)}, bf16[8,768,128]{2,1,0:T(8,128)(2,1)S(1)}) custom-call(s32[5]{0:T(128)S(1)} %stack.38.refs_0_.at, bf16[16,32,384]{2,1,0:T(8,128)(2,1)S(1)} %get-tuple-element.53.qg.refs_1_.refs_0_, bf16[16,32,384]{2,1,0:T(8,128)(2,1)S(1)} %collective-permute-done.5.refs_2_.refs_1_, ...), custom_call_target="tpu_custom_call" | custom-call | tf_op jit(solution)/shard_map/softmax_statistics/pallas_call | solution.py:203
  57.8 0.5 collective-permute-start.18
  58.3 2.5 %collective-permute-start.17 = (f32[8,1920]{1,0:T(8,128)S(1)}, f32[8,1920]{1,0:T(8,128)S(1)}, u32[]{:S(2)}, u32[]{:S(2)}) collective-permute-start(f32[8,1920]{1,0:T(8,128)S(1)} %get-tuple-element.74.refs_9_), channel_id=1, source_target_pairs={{2,0},{3,1},{0,2},{1,3},{6,4},{7,5},{4,6},{5,7},{10,8},{11,9},{8,1... | collective-permute-start | bytes 184328 | tf_op jit(solution)/shard_map/ppermute | solution.py:215
  60.8 1.4 %collective-permute-start.16 = (f32[8,1920]{1,0:T(8,128)S(1)}, f32[8,1920]{1,0:T(8,128)S(1)}, u32[]{:S(2)}, u32[]{:S(2)}) collective-permute-start(f32[8,1920]{1,0:T(8,128)S(1)} %get-tuple-element.74.refs_9_), channel_id=1, source_target_pairs={{1,0},{2,1},{3,2},{0,3},{5,4},{6,5},{7,6},{4,7},{9,8},{10,9},{11,1... | collective-permute-start | bytes 184328 | tf_op jit(solution)/shard_map/ppermute | solution.py:215
  62.2 2.3 %collective-permute-done.18.refs_12_ = f32[8,1920]{1,0:T(8,128)S(1)} collective-permute-done((f32[8,1920]{1,0:T(8,128)S(1)}, f32[8,1920]{1,0:T(8,128)S(1)}, u32[]{:S(2)}, u32[]{:S(2)}) %collective-permute-start.18) | collective-permute-done | bytes 61472 | tf_op jit(solution)/shard_map/ppermute | solution.py:215
  64.5 0.6 collective-permute-done.16.refs_10_
  65.0 26.4 %attention_gradients.1 = (f32[8,32,384]{2,1,0:T(8,128)S(1)}, bf16[8,32,384]{2,1,0:T(8,128)(2,1)S(1)}, bf16[8,32,384]{2,1,0:T(8,128)(2,1)S(1)}, bf16[8,32,384]{2,...) custom-call(s32[5]{0:T(128)S(1)} %stack.38.refs_0_.at, ...), custom_call_target="tpu_custom_call" | custom-call | tf_op jit(solution)/shard_map/attention_gradients/pallas_call | solution.py:203
  91.5 0.1 collective-permute-start.19
  91.6 3.1 %collective-permute-start.21 = (bf16[16,32,384]{2,1,0:T(8,128)(2,1)S(1)}, bf16[16,32,384]{2,1,0:T(8,128)(2,1)S(1)}, u32[]{:S(2)}, u32[]{:S(2)}) collective-permute-start(bf16[16,32,384]{2,1,0:T(8,128)(2,1)S(1)} %get-tuple-element.80), channel_id=1, source_target_pairs={{4,0},{0,4},{5,1},{1,5},{6,2},{2,6},{7,3},{3,7},{12,8},{8,12},{13,... | collective-permute-start | bytes 1179656 | tf_op jit(solution)/shard_map/ppermute | solution.py:215
  94.7 0.0 collective-permute-done.19
  94.7 0.4 fusion.6
  95.1 0.1 slice_bitcast_fusion.1
  95.2 0.2 collective-permute-start.20
  95.3 0.9 collective-permute-start.23
  96.2 2.3 %collective-permute-start.24 = (bf16[4,96,384]{2,1,0:T(8,128)(2,1)S(1)}, bf16[4,96,384]{2,1,0:T(8,128)(2,1)S(1)}, u32[]{:S(2)}, u32[]{:S(2)}) collective-permute-start(bf16[4,96,384]{2,1,0:T(8,128)(2,1)S(1)} %get-tuple-element.84), channel_id=1, source_target_pairs={{0,48},{16,0},{32,16},{48,32},{1,49},{17,1},{33,17},{49,33},{2,50}... | collective-permute-start | bytes 884744 | tf_op jit(solution)/shard_map/ppermute | solution.py:219
  98.5 0.9 collective-permute-start.22
  99.4 7.8 %collective-permute-done.21 = bf16[16,32,384]{2,1,0:T(8,128)(2,1)S(1)} collective-permute-done((bf16[16,32,384]{2,1,0:T(8,128)(2,1)S(1)}, bf16[16,32,384]{2,1,0:T(8,128)(2,1)S(1)}, u32[]{:S(2)}, u32[]{:S(2)}) %collective-permute-start.21) | collective-permute-done | bytes 393248 | tf_op jit(solution)/shard_map/ppermute | solution.py:215
  107.2 4.7 %collective-permute-done.20 = bf16[4,96,384]{2,1,0:T(8,128)(2,1)S(1)} collective-permute-done((bf16[4,96,384]{2,1,0:T(8,128)(2,1)S(1)}, bf16[4,96,384]{2,1,0:T(8,128)(2,1)S(1)}, u32[]{:S(2)}, u32[]{:S(2)}) %collective-permute-start.20) | collective-permute-done | bytes 294944 | tf_op jit(solution)/shard_map/ppermute | solution.py:219
  111.8 0.6 collective-permute-done.24
  112.5 0.1 fusion.2
  112.6 8.1 %collective-permute-start.27 = (bf16[2,96,384]{2,1,0:T(8,128)(2,1)S(1)}, bf16[2,96,384]{2,1,0:T(8,128)(2,1)S(1)}, u32[]{:S(2)}, u32[]{:S(2)}) collective-permute-start(bf16[2,96,384]{2,1,0:T(8,128)(2,1)S(1)} %slice.77), channel_id=1, source_target_pairs={{0,64},{64,0},{128,192},{192,128},{1,65},{65,1},{129,193},{193,129... | collective-permute-start | bytes 442376 | tf_op jit(solution)/shard_map/ppermute | solution.py:318
  120.8 1.5 %collective-permute-start.25 = (bf16[8,32,384]{2,1,0:T(8,128)(2,1)S(1)}, bf16[8,32,384]{2,1,0:T(8,128)(2,1)S(1)}, u32[]{:S(2)}, u32[]{:S(2)}) collective-permute-start(bf16[8,32,384]{2,1,0:T(8,128)(2,1)S(1)} %get-tuple-element.90), channel_id=1, source_target_pairs={{0,2},{1,3},{2,0},{3,1},{4,6},{5,7},{6,4},{7,5},{8,10},{9,11},{10,... | collective-permute-start | bytes 589832 | tf_op jit(solution)/shard_map/ppermute | solution.py:219
  122.3 1.6 %collective-permute-start.26 = (bf16[8,32,384]{2,1,0:T(8,128)(2,1)S(1)}, bf16[8,32,384]{2,1,0:T(8,128)(2,1)S(1)}, u32[]{:S(2)}, u32[]{:S(2)}) collective-permute-start(bf16[8,32,384]{2,1,0:T(8,128)(2,1)S(1)} %get-tuple-element.91), channel_id=1, source_target_pairs={{0,3},{1,0},{2,1},{3,2},{4,7},{5,4},{6,5},{7,6},{8,11},{9,8},{10,9... | collective-permute-start | bytes 589832 | tf_op jit(solution)/shard_map/ppermute | solution.py:219
  123.8 0.1 convert_element_type.74
  123.9 0.9 fusion.3
  124.8 3.7 %collective-permute-start.28 = (bf16[96,384]{1,0:T(8,128)(2,1)S(1)}, bf16[96,384]{1,0:T(8,128)(2,1)S(1)}, u32[]{:S(2)}, u32[]{:S(2)}) collective-permute-start(bf16[96,384]{1,0:T(8,128)(2,1)S(1)} %get-tuple-element.103), channel_id=1, source_target_pairs={{0,0},{64,64},{128,4},{192,68},{4,128},{68,192},{132,132},{196,196... | collective-permute-start | bytes 221192 | tf_op jit(solution)/shard_map/ppermute | solution.py:322
  128.5 0.1 collective-permute-start.29
  128.6 2.6 %collective-permute-done.26 = bf16[8,32,384]{2,1,0:T(8,128)(2,1)S(1)} collective-permute-done((bf16[8,32,384]{2,1,0:T(8,128)(2,1)S(1)}, bf16[8,32,384]{2,1,0:T(8,128)(2,1)S(1)}, u32[]{:S(2)}, u32[]{:S(2)}) %collective-permute-start.26) | collective-permute-done | bytes 196640 | tf_op jit(solution)/shard_map/ppermute | solution.py:219
  131.2 0.8 multiply_convert_fusion
  132.0 2.8 %collective-permute-done.28 = bf16[96,384]{1,0:T(8,128)(2,1)S(1)} collective-permute-done((bf16[96,384]{1,0:T(8,128)(2,1)S(1)}, bf16[96,384]{1,0:T(8,128)(2,1)S(1)}, u32[]{:S(2)}, u32[]{:S(2)}) %collective-permute-start.28) | collective-permute-done | bytes 73760 | tf_op jit(solution)/shard_map/ppermute | solution.py:322
  134.8 2.1 %collective-permute-done.29 = bf16[96,384]{1,0:T(8,128)(2,1)S(1)} collective-permute-done((bf16[96,384]{1,0:T(8,128)(2,1)S(1)}, bf16[96,384]{1,0:T(8,128)(2,1)S(1)}, u32[]{:S(2)}, u32[]{:S(2)}) %collective-permute-start.29) | collective-permute-done | bytes 73760 | tf_op jit(solution)/shard_map/ppermute | solution.py:322
  136.8 0.7 convert_add_fusion.1
  (23 shorter events, 0.2 us)
Async XLA Ops:
  0.6 20.4 %collective-permute-start.4 = (bf16[8,32,384]{2,1,0:T(8,128)(2,1)}, bf16[8,32,384]{2,1,0:T(8,128)(2,1)S(1)}, u32[]{:S(2)}, u32[]{:S(2)}) collective-permute-start(bf16[8,32,384]{2,1,0:T(8,128)(2,1)} %q.1), channel_id=1, source_target_pairs={{2,0},{3,1},{0,2},{1,3},{6,4},{7,5},{4,6},{5,7},{10,8},{11,9},{8,1... | collective-permute-start | bytes 589832 | tf_op jit(solution)/shard_map/ppermute | solution.py:215
  3.7 17.2 %collective-permute-start.1 = (bf16[96,384]{1,0:T(8,128)(2,1)}, bf16[96,384]{1,0:T(8,128)(2,1)S(1)}, u32[]{:S(2)}, u32[]{:S(2)}) collective-permute-start(bf16[96,384]{1,0:T(8,128)(2,1)} %param.12), channel_id=1, source_target_pairs={{64,0},{0,64},{68,128},{4,192},{192,4},{128,68},{196,132},{132,196... | collective-permute-start | bytes 221192 | tf_op jit(solution)/shard_map/ppermute | solution.py:239
  8.7 12.3 %collective-permute-start = (bf16[96,384]{1,0:T(8,128)(2,1)}, bf16[96,384]{1,0:T(8,128)(2,1)S(1)}, u32[]{:S(2)}, u32[]{:S(2)}) collective-permute-start(bf16[96,384]{1,0:T(8,128)(2,1)} %param.12), channel_id=1, source_target_pairs={{0,0},{64,64},{4,128},{68,192},{128,4},{192,68},{132,132},{196,196... | collective-permute-start | bytes 221192 | tf_op jit(solution)/shard_map/ppermute | solution.py:239
  10.6 10.4 %collective-permute-start.3 = (bf16[96,384]{1,0:T(8,128)(2,1)}, bf16[96,384]{1,0:T(8,128)(2,1)S(1)}, u32[]{:S(2)}, u32[]{:S(2)}) collective-permute-start(bf16[96,384]{1,0:T(8,128)(2,1)} %param.12), channel_id=1, source_target_pairs={{68,0},{4,64},{64,128},{0,192},{196,4},{132,68},{192,132},{128,196... | collective-permute-start | bytes 221192 | tf_op jit(solution)/shard_map/ppermute | solution.py:239
  11.2 9.7 %collective-permute-start.2 = (bf16[96,384]{1,0:T(8,128)(2,1)}, bf16[96,384]{1,0:T(8,128)(2,1)S(1)}, u32[]{:S(2)}, u32[]{:S(2)}) collective-permute-start(bf16[96,384]{1,0:T(8,128)(2,1)} %param.12), channel_id=1, source_target_pairs={{4,0},{68,64},{0,128},{64,192},{132,4},{196,68},{128,132},{192,196... | collective-permute-start | bytes 221192 | tf_op jit(solution)/shard_map/ppermute | solution.py:239
  16.5 0.9 copy-start
  17.4 0.9 copy-start.1
  18.3 0.9 copy-start.2
  19.3 0.9 copy-start.3
  21.0 10.7 %collective-permute-start.7 = (bf16[16,32,384]{2,1,0:T(8,128)(2,1)S(1)}, bf16[16,32,384]{2,1,0:T(8,128)(2,1)S(1)}, u32[]{:S(2)}, u32[]{:S(2)}) collective-permute-start(bf16[16,32,384]{2,1,0:T(8,128)(2,1)S(1)} %get-tuple-element.53.qg.refs_1_.refs_0_), channel_id=1, source_target_pairs={{3,0},{0,1},{1,2},{2,3},{7,4},{4,5},{5,6},{6,7},{11,8},{8,9},{9,10... | collective-permute-start | bytes 1179656 | tf_op jit(solution)/shard_map/ppermute | solution.py:215
  21.7 7.7 %collective-permute-start.6 = (bf16[4,96,384]{2,1,0:T(8,128)(2,1)S(1)}, bf16[4,96,384]{2,1,0:T(8,128)(2,1)}, u32[]{:S(2)}, u32[]{:S(2)}) collective-permute-start(bf16[4,96,384]{2,1,0:T(8,128)(2,1)S(1)} %pad_maximum_fusion.refs_8_), channel_id=1, source_target_pairs={{16,0},{32,16},{48,32},{0,48},{17,1},{33,17},{49,33},{1,49},{18,2}... | collective-permute-start | bytes 884744 | tf_op jit(solution)/shard_map/ppermute | solution.py:215
  24.8 18.2 %collective-permute-start.9 = (bf16[17,32,384]{2,1,0:T(8,128)(2,1)S(1)}, bf16[17,32,384]{2,1,0:T(8,128)(2,1)S(1)}, u32[]{:S(2)}, u32[]{:S(2)}) collective-permute-start(bf16[17,32,384]{2,1,0:T(8,128)(2,1)S(1)} %get-tuple-element.63.kvm.refs_6_.refs_5_), channel_id=1, source_target_pairs={{4,0},{0,4},{5,1},{1,5},{6,2},{2,6},{7,3},{3,7},{12,8},{8,12},{13,... | collective-permute-start | bytes 1253384 | tf_op jit(solution)/shard_map/ppermute | solution.py:215
  28.8 14.2 %collective-permute-start.10 = (bf16[4,96,384]{2,1,0:T(8,128)(2,1)S(1)}, bf16[4,96,384]{2,1,0:T(8,128)(2,1)}, u32[]{:S(2)}, u32[]{:S(2)}) collective-permute-start(bf16[4,96,384]{2,1,0:T(8,128)(2,1)S(1)} %pad_maximum_fusion.refs_8_), channel_id=1, source_target_pairs={{48,0},{0,16},{16,32},{32,48},{49,1},{1,17},{17,33},{33,49},{50,2}... | collective-permute-start | bytes 884744 | tf_op jit(solution)/shard_map/ppermute | solution.py:215
  31.7 11.8 %collective-permute-start.8 = (bf16[4,96,384]{2,1,0:T(8,128)(2,1)S(1)}, bf16[4,96,384]{2,1,0:T(8,128)(2,1)}, u32[]{:S(2)}, u32[]{:S(2)}) collective-permute-start(bf16[4,96,384]{2,1,0:T(8,128)(2,1)S(1)} %pad_maximum_fusion.refs_8_), channel_id=1, source_target_pairs={{32,0},{48,16},{0,32},{16,48},{33,1},{49,17},{1,33},{17,49},{34,2}... | collective-permute-start | bytes 884744 | tf_op jit(solution)/shard_map/ppermute | solution.py:215
  34.9 8.7 %collective-permute-start.5 = (bf16[16,32,384]{2,1,0:T(8,128)(2,1)S(1)}, bf16[16,32,384]{2,1,0:T(8,128)(2,1)S(1)}, u32[]{:S(2)}, u32[]{:S(2)}) collective-permute-start(bf16[16,32,384]{2,1,0:T(8,128)(2,1)S(1)} %get-tuple-element.53.qg.refs_1_.refs_0_), channel_id=1, source_target_pairs={{1,0},{2,1},{3,2},{0,3},{5,4},{6,5},{7,6},{4,7},{9,8},{10,9},{11,1... | collective-permute-start | bytes 1179656 | tf_op jit(solution)/shard_map/ppermute | solution.py:215
  34.9 9.8 %collective-permute-start.11 = (bf16[4,96,384]{2,1,0:T(8,128)(2,1)S(1)}, bf16[4,96,384]{2,1,0:T(8,128)(2,1)}, u32[]{:S(2)}, u32[]{:S(2)}) collective-permute-start(bf16[4,96,384]{2,1,0:T(8,128)(2,1)S(1)} %pad_maximum_fusion.refs_8_), channel_id=1, source_target_pairs={{8,0},{0,8},{9,1},{1,9},{10,2},{2,10},{11,3},{3,11},{12,4},{4,12},... | collective-permute-start | bytes 884744 | tf_op jit(solution)/shard_map/ppermute | solution.py:215
  34.9 0.9 copy-start.4
  43.0 1.9 %collective-permute-start.14 = (bf16[4,96,384]{2,1,0:T(8,128)(2,1)}, bf16[4,96,384]{2,1,0:T(8,128)(2,1)}, u32[]{:S(2)}, u32[]{:S(2)}) collective-permute-start(bf16[4,96,384]{2,1,0:T(8,128)(2,1)} %collective-permute-done.10.refs_11_), channel_id=1, source_target_pairs={{8,0},{0,8},{9,1},{1,9},{10,2},{2,10},{11,3},{3,11},{12,4},{4,12},... | collective-permute-start | bytes 884744 | tf_op jit(solution)/shard_map/ppermute | solution.py:215
  43.1 2.3 %collective-permute-start.12 = (bf16[4,96,384]{2,1,0:T(8,128)(2,1)}, bf16[4,96,384]{2,1,0:T(8,128)(2,1)}, u32[]{:S(2)}, u32[]{:S(2)}) collective-permute-start(bf16[4,96,384]{2,1,0:T(8,128)(2,1)} %collective-permute-done.6.refs_9_), channel_id=1, source_target_pairs={{8,0},{0,8},{9,1},{1,9},{10,2},{2,10},{11,3},{3,11},{12,4},{4,12},... | collective-permute-start | bytes 884744 | tf_op jit(solution)/shard_map/ppermute | solution.py:215
  43.6 2.3 %collective-permute-start.13 = (bf16[4,96,384]{2,1,0:T(8,128)(2,1)}, bf16[4,96,384]{2,1,0:T(8,128)(2,1)}, u32[]{:S(2)}, u32[]{:S(2)}) collective-permute-start(bf16[4,96,384]{2,1,0:T(8,128)(2,1)} %collective-permute-done.8.refs_10_), channel_id=1, source_target_pairs={{8,0},{0,8},{9,1},{1,9},{10,2},{2,10},{11,3},{3,11},{12,4},{4,12},... | collective-permute-start | bytes 884744 | tf_op jit(solution)/shard_map/ppermute | solution.py:215
  43.7 14.2 %collective-permute-start.15 = (bf16[8,32,384]{2,1,0:T(8,128)(2,1)}, bf16[8,32,384]{2,1,0:T(8,128)(2,1)S(1)}, u32[]{:S(2)}, u32[]{:S(2)}) collective-permute-start(bf16[8,32,384]{2,1,0:T(8,128)(2,1)} %get-tuple-element.70), channel_id=1, source_target_pairs={{2,0},{3,1},{0,2},{1,3},{6,4},{7,5},{4,6},{5,7},{10,8},{11,9},{8,1... | collective-permute-start | bytes 589832 | tf_op jit(solution)/shard_map/ppermute | solution.py:215
  57.8 6.6 %collective-permute-start.18 = (f32[8,1920]{1,0:T(8,128)S(1)}, f32[8,1920]{1,0:T(8,128)S(1)}, u32[]{:S(2)}, u32[]{:S(2)}) collective-permute-start(f32[8,1920]{1,0:T(8,128)S(1)} %get-tuple-element.74.refs_9_), channel_id=1, source_target_pairs={{3,0},{0,1},{1,2},{2,3},{7,4},{4,5},{5,6},{6,7},{11,8},{8,9},{9,10... | collective-permute-start | bytes 184328 | tf_op jit(solution)/shard_map/ppermute | solution.py:215
  58.3 6.1 %collective-permute-start.17 = (f32[8,1920]{1,0:T(8,128)S(1)}, f32[8,1920]{1,0:T(8,128)S(1)}, u32[]{:S(2)}, u32[]{:S(2)}) collective-permute-start(f32[8,1920]{1,0:T(8,128)S(1)} %get-tuple-element.74.refs_9_), channel_id=1, source_target_pairs={{2,0},{3,1},{0,2},{1,3},{6,4},{7,5},{4,6},{5,7},{10,8},{11,9},{8,1... | collective-permute-start | bytes 184328 | tf_op jit(solution)/shard_map/ppermute | solution.py:215
  60.8 4.3 %collective-permute-start.16 = (f32[8,1920]{1,0:T(8,128)S(1)}, f32[8,1920]{1,0:T(8,128)S(1)}, u32[]{:S(2)}, u32[]{:S(2)}) collective-permute-start(f32[8,1920]{1,0:T(8,128)S(1)} %get-tuple-element.74.refs_9_), channel_id=1, source_target_pairs={{1,0},{2,1},{3,2},{0,3},{5,4},{6,5},{7,6},{4,7},{9,8},{10,9},{11,1... | collective-permute-start | bytes 184328 | tf_op jit(solution)/shard_map/ppermute | solution.py:215
  91.5 3.2 %collective-permute-start.19 = (bf16[4,4,96,384]{3,2,1,0:T(8,128)(2,1)S(1)}, bf16[4,4,96,384]{3,2,1,0:T(8,128)(2,1)S(1)}, u32[]{:S(2)}, u32[]{:S(2)}) collective-permute-start(bf16[4,4,96,384]{3,2,1,0:T(8,128)(2,1)S(1)} %get-tuple-element.77), channel_id=1, source_target_pairs={{8,0},{0,8},{9,1},{1,9},{10,2},{2,10},{11,3},{3,11},{12,4},{4,12},... | collective-permute-start | bytes 3538952 | tf_op jit(solution)/shard_map/ppermute | solution.py:215
  91.6 15.6 %collective-permute-start.21 = (bf16[16,32,384]{2,1,0:T(8,128)(2,1)S(1)}, bf16[16,32,384]{2,1,0:T(8,128)(2,1)S(1)}, u32[]{:S(2)}, u32[]{:S(2)}) collective-permute-start(bf16[16,32,384]{2,1,0:T(8,128)(2,1)S(1)} %get-tuple-element.80), channel_id=1, source_target_pairs={{4,0},{0,4},{5,1},{1,5},{6,2},{2,6},{7,3},{3,7},{12,8},{8,12},{13,... | collective-permute-start | bytes 1179656 | tf_op jit(solution)/shard_map/ppermute | solution.py:215
  95.2 16.7 %collective-permute-start.20 = (bf16[4,96,384]{2,1,0:T(8,128)(2,1)S(1)}, bf16[4,96,384]{2,1,0:T(8,128)(2,1)S(1)}, u32[]{:S(2)}, u32[]{:S(2)}) collective-permute-start(bf16[4,96,384]{2,1,0:T(8,128)(2,1)S(1)} %get-tuple-element.79), channel_id=1, source_target_pairs={{0,16},{16,32},{32,48},{48,0},{1,17},{17,33},{33,49},{49,1},{2,18}... | collective-permute-start | bytes 884744 | tf_op jit(solution)/shard_map/ppermute | solution.py:219
  95.3 16.5 %collective-permute-start.23 = (bf16[4,96,384]{2,1,0:T(8,128)(2,1)S(1)}, bf16[4,96,384]{2,1,0:T(8,128)(2,1)S(1)}, u32[]{:S(2)}, u32[]{:S(2)}) collective-permute-start(bf16[4,96,384]{2,1,0:T(8,128)(2,1)S(1)} %get-tuple-element.83), channel_id=1, source_target_pairs={{0,32},{16,48},{32,0},{48,16},{1,33},{17,49},{33,1},{49,17},{2,34}... | collective-permute-start | bytes 884744 | tf_op jit(solution)/shard_map/ppermute | solution.py:219
  96.2 16.3 %collective-permute-start.24 = (bf16[4,96,384]{2,1,0:T(8,128)(2,1)S(1)}, bf16[4,96,384]{2,1,0:T(8,128)(2,1)S(1)}, u32[]{:S(2)}, u32[]{:S(2)}) collective-permute-start(bf16[4,96,384]{2,1,0:T(8,128)(2,1)S(1)} %get-tuple-element.84), channel_id=1, source_target_pairs={{0,48},{16,0},{32,16},{48,32},{1,49},{17,1},{33,17},{49,33},{2,50}... | collective-permute-start | bytes 884744 | tf_op jit(solution)/shard_map/ppermute | solution.py:219
  98.5 8.7 %collective-permute-start.22 = (bf16[8,32,384]{2,1,0:T(8,128)(2,1)S(1)}, bf16[8,32,384]{2,1,0:T(8,128)(2,1)S(1)}, u32[]{:S(2)}, u32[]{:S(2)}) collective-permute-start(bf16[8,32,384]{2,1,0:T(8,128)(2,1)S(1)} %get-tuple-element.81), channel_id=1, source_target_pairs={{0,1},{1,2},{2,3},{3,0},{4,5},{5,6},{6,7},{7,4},{8,9},{9,10},{10,1... | collective-permute-start | bytes 589832 | tf_op jit(solution)/shard_map/ppermute | solution.py:219
  112.6 12.1 %collective-permute-start.27 = (bf16[2,96,384]{2,1,0:T(8,128)(2,1)S(1)}, bf16[2,96,384]{2,1,0:T(8,128)(2,1)S(1)}, u32[]{:S(2)}, u32[]{:S(2)}) collective-permute-start(bf16[2,96,384]{2,1,0:T(8,128)(2,1)S(1)} %slice.77), channel_id=1, source_target_pairs={{0,64},{64,0},{128,192},{192,128},{1,65},{65,1},{129,193},{193,129... | collective-permute-start | bytes 442376 | tf_op jit(solution)/shard_map/ppermute | solution.py:318
  120.8 7.8 %collective-permute-start.25 = (bf16[8,32,384]{2,1,0:T(8,128)(2,1)S(1)}, bf16[8,32,384]{2,1,0:T(8,128)(2,1)S(1)}, u32[]{:S(2)}, u32[]{:S(2)}) collective-permute-start(bf16[8,32,384]{2,1,0:T(8,128)(2,1)S(1)} %get-tuple-element.90), channel_id=1, source_target_pairs={{0,2},{1,3},{2,0},{3,1},{4,6},{5,7},{6,4},{7,5},{8,10},{9,11},{10,... | collective-permute-start | bytes 589832 | tf_op jit(solution)/shard_map/ppermute | solution.py:219
  122.3 8.9 %collective-permute-start.26 = (bf16[8,32,384]{2,1,0:T(8,128)(2,1)S(1)}, bf16[8,32,384]{2,1,0:T(8,128)(2,1)S(1)}, u32[]{:S(2)}, u32[]{:S(2)}) collective-permute-start(bf16[8,32,384]{2,1,0:T(8,128)(2,1)S(1)} %get-tuple-element.91), channel_id=1, source_target_pairs={{0,3},{1,0},{2,1},{3,2},{4,7},{5,4},{6,5},{7,6},{8,11},{9,8},{10,9... | collective-permute-start | bytes 589832 | tf_op jit(solution)/shard_map/ppermute | solution.py:219
  124.8 9.9 %collective-permute-start.28 = (bf16[96,384]{1,0:T(8,128)(2,1)S(1)}, bf16[96,384]{1,0:T(8,128)(2,1)S(1)}, u32[]{:S(2)}, u32[]{:S(2)}) collective-permute-start(bf16[96,384]{1,0:T(8,128)(2,1)S(1)} %get-tuple-element.103), channel_id=1, source_target_pairs={{0,0},{64,64},{128,4},{192,68},{4,128},{68,192},{132,132},{196,196... | collective-permute-start | bytes 221192 | tf_op jit(solution)/shard_map/ppermute | solution.py:322
  128.5 8.3 %collective-permute-start.29 = (bf16[96,384]{1,0:T(8,128)(2,1)S(1)}, bf16[96,384]{1,0:T(8,128)(2,1)S(1)}, u32[]{:S(2)}, u32[]{:S(2)}) collective-permute-start(bf16[96,384]{1,0:T(8,128)(2,1)S(1)} %get-tuple-element.104), channel_id=1, source_target_pairs={{0,4},{64,68},{128,0},{192,64},{4,132},{68,196},{132,128},{196,192... | collective-permute-start | bytes 221192 | tf_op jit(solution)/shard_map/ppermute | solution.py:322
